TPU v7x, 32 devices: a whole 2x2x4 slice. The times are simulated.
32 devices in a mesh: group: 2 (over x), particle: 2 (over core), strip: 8 (over z, y).
Axes of the slice: x: 2, y: 2, z: 4, core: 2. Of those that a mesh axis runs over, the one named last changes fastest.
Arguments:
- ensemble: float32 [16, 3, 64, 4096], P(('group', 'particle'), None, 'strip'), parts along dimension 0, may hold values from -1 to 1
- offspring: int32 [16], P('group'), parts along dimension 0, may hold values from 0 to 2, as said below
- observations: float32 [128, 128], P(('group', 'strip')), parts along dimension 0, may hold values from -6 to 6
- obs_cols: int32 [128, 128], P(('group', 'strip')), parts along dimension 0, may hold values from 0 to 4095
- obs_precision: float32 [128, 128], P(('group', 'strip')), parts along dimension 0, may hold values from 0.3 to 3
Outputs:
- forecast: float32 [16, 3, 64, 4096], P(('group', 'particle'), None, 'strip'), parts along dimension 0
- log_weights: float32 [16], P(('group', 'particle')), parts along dimension 0
There are 2 independent parts, one for each index of `group`. A program takes and returns all parts, laid end to end along the dimension named above; each array names one. Nothing has to cross between parts.
Inputs may be any that keep to these rules, and one draw needn't show every extreme that they name: `offspring`: nonnegative copy counts that sum to 8.
All inputs are finite; a program needn't handle non-finite values.
Results may differ from a plain program's by a relative error of at most 0.00002.
Values sent between devices are 32-bit elements; how exact they have to be, the bound alone decides.
No kernel may reach another device: no remote copies, remote signals or barrier semaphores. Data moves between devices by JAX's collectives and lax.ppermute only.
A program may use at most 64 MiB of HBM per device.

v0:
```python
import jax
import jax.numpy as jnp
from jax import lax
from jax.sharding import PartitionSpec as P

STEPS = 3


DT = 0.4


def with_halo(block, sides, width):
    for axis, dim in sides:
        count = lax.axis_size(axis)
        forward = [(i, i + 1) for i in range(count - 1)]
        forward.append((count - 1, 0))
        backward = [(target, source) for source, target in forward]
        low = lax.ppermute(
            lax.slice_in_dim(block, block.shape[dim] - width, None, axis=dim), axis, forward
        )
        high = lax.ppermute(lax.slice_in_dim(block, 0, width, axis=dim), axis, backward)
        block = jnp.concatenate([low, block, high], axis=dim)
    return block


def tendency(padded, coriolis):
    eta = padded[..., 0, :, :]
    east = padded[..., 1, :, :]
    north = padded[..., 2, :, :]
    depth = 1.0 + eta

    def along_x(field):
        inner = field[..., 1:-1, :]
        return 0.5 * (jnp.roll(inner, -1, axis=-1) - jnp.roll(inner, 1, axis=-1))

    def along_y(field):
        return 0.5 * (field[..., 2:, :] - field[..., :-2, :])

    east_c = east[..., 1:-1, :]
    north_c = north[..., 1:-1, :]
    eta_t = -(along_x(depth * east) + along_y(depth * north))
    east_t = -(east_c * along_x(east) + north_c * along_y(east)) + coriolis * north_c - along_x(eta)
    north_t = (
        -(east_c * along_x(north) + north_c * along_y(north)) - coriolis * east_c - along_y(eta)
    )
    return jnp.stack([eta_t, east_t, north_t], axis=-3)


def coriolis_rows(first_row, count, total_rows):
    rows = (first_row + jnp.arange(count, dtype=jnp.int32)) % total_rows
    rows = rows.astype(jnp.float32)
    return (0.3 + 0.4 * ((rows + 0.5) / total_rows - 0.5))[:, None]


def section_rows(field):
    return with_halo(field, (("strip", 2),), 1)


def local(ensemble, offspring, observations, obs_cols, obs_precision):
    members = ensemble.shape[0]
    strip_rows = ensemble.shape[2]
    strips = lax.axis_size("strip")
    total_rows = strips * strip_rows
    row_start = lax.axis_index("strip") * strip_rows
    total_members = offspring.shape[0]
    cumulative = jnp.cumsum(offspring)
    slots = jnp.arange(total_members, dtype=jnp.int32)
    source = jnp.sum((cumulative[None, :] <= slots[:, None]).astype(jnp.int32), axis=1)
    mine = lax.axis_index("particle") * members + jnp.arange(members, dtype=jnp.int32)
    wanted = jnp.take(source, mine, axis=0)
    everyone = lax.all_gather(ensemble, "particle", axis=0, tiled=True)
    state = jnp.take(everyone, wanted, axis=0)
    coriolis = coriolis_rows(row_start, strip_rows, total_rows)
    for step in range(STEPS):
        first = state + DT * tendency(section_rows(state), coriolis)
        second = 0.75 * state + 0.25 * (first + DT * tendency(section_rows(first), coriolis))
        state = state / 3.0 + 2.0 / 3.0 * (second + DT * tendency(section_rows(second), coriolis))
    eta = state[:, 0]
    index = jnp.broadcast_to(obs_cols[None], (members,) + obs_cols.shape)
    picked = jnp.take_along_axis(eta, index, axis=-1)
    rows = (row_start + jnp.arange(strip_rows, dtype=jnp.int32)).astype(jnp.float32)
    weight = obs_precision * (1.0 + 2.0 * (rows + 0.5) / total_rows)[:, None]
    misfit = observations[None] - picked
    partial_sum = jnp.sum(weight[None] * misfit * misfit, axis=(1, 2))
    total = lax.psum(partial_sum, "strip")
    log_weights = -0.5 * total / (total_rows * obs_cols.shape[1])
    return (state, log_weights)


def solution(mesh):
    in_specs = (
        P(("group", "particle"), None, "strip", None),
        P("group"),
        P(("group", "strip"), None),
        P(("group", "strip"), None),
        P(("group", "strip"), None),
    )
    out_specs = (P(("group", "particle"), None, "strip", None), P(("group", "particle")))
    return jax.shard_map(local, mesh=mesh, in_specs=in_specs, out_specs=out_specs, check_vma=False)
```

profile of v0, /device:TPU:0, one launch (start us, length us, event | category | flops | bytes accessed | tf_op | source)
XLA Modules:
  0.0 227.1 jit_solution(7969208227632684460)
XLA Ops:
  8.9 15.5 %all-gather.2.cloned.1.call-done = f32[8,3,8,4096]{3,2,1,0:T(8,128)} async-done(((f32[4,3,8,4096]{3,2,1,0:T(8,128)}), f32[8,3,8,4096]{3,2,1,0:T(8,128)}) %all-gather.2.cloned.1.call-update) | async-done | bytes 3145744 | tf_op jit(solution)/shard_map/all_gather | solution.py:71
  24.4 2.5 %gather_fusion.1 = f32[4,3,8,4096]{3,2,1,0:T(8,128)S(1)} fusion(f32[8,3,8,4096]{3,2,1,0:T(8,128)} %all-gather.2.cloned.1.call-done, s32[1024]{0:T(1024)S(1)} %pad_clamp_fusion), kind=kCustom, calls=%fused_computation.1 | custom fusion | bytes 3145744 | tf_op jit(solution)/shard_map/jit(_take)/gather | solution.py:72
  27.5 1.8 collective-permute-start
  29.2 3.0 %collective-permute-start.1 = (f32[4,3,1,4096]{3,2,0,1:T(1,128)S(1)}, f32[4,3,1,4096]{3,2,0,1:T(1,128)S(1)}, u32[]{:S(2)}, u32[]{:S(2)}) collective-permute-start(f32[4,3,1,4096]{3,2,0,1:T(1,128)S(1)} %get-tuple-element.64), channel_id=1, source_target_pairs={{1,0},{2,1},{3,2},{4,3},{5,4},{6,5},{7,6},{0,7},{9,8},{10,9},{11,1... | collective-permute-start | bytes 589832 | tf_op jit(solution)/shard_map/ppermute | solution.py:21
  32.2 5.8 %collective-permute-done = f32[4,3,1,4096]{3,2,0,1:T(1,128)S(1)} collective-permute-done((f32[4,3,1,4096]{3,2,0,1:T(1,128)S(1)}, f32[4,3,1,4096]{3,2,0,1:T(1,128)S(1)}, u32[]{:S(2)}, u32[]{:S(2)}) %collective-permute-start) | collective-permute-done | bytes 196640 | tf_op jit(solution)/shard_map/ppermute | solution.py:18
  38.1 2.2 collective-permute-done.1
  44.6 4.4 %collective-permute-start.3 = (f32[4,3,1,4096]{3,2,0,1:T(1,128)S(1)}, f32[4,3,1,4096]{3,2,0,1:T(1,128)S(1)}, u32[]{:S(2)}, u32[]{:S(2)}) collective-permute-start(f32[4,3,1,4096]{3,2,0,1:T(1,128)S(1)} %get-tuple-element.62), channel_id=1, source_target_pairs={{1,0},{2,1},{3,2},{4,3},{5,4},{6,5},{7,6},{0,7},{9,8},{10,9},{11,1... | collective-permute-start | bytes 589832 | tf_op jit(solution)/shard_map/ppermute | solution.py:21
  49.1 4.1 %collective-permute-done.2 = f32[4,3,1,4096]{3,2,0,1:T(1,128)S(1)} collective-permute-done((f32[4,3,1,4096]{3,2,0,1:T(1,128)S(1)}, f32[4,3,1,4096]{3,2,0,1:T(1,128)S(1)}, u32[]{:S(2)}, u32[]{:S(2)}) %collective-permute-start.2) | collective-permute-done | bytes 196640 | tf_op jit(solution)/shard_map/ppermute | solution.py:18
  53.1 2.9 %collective-permute-done.3 = f32[4,3,1,4096]{3,2,0,1:T(1,128)S(1)} collective-permute-done((f32[4,3,1,4096]{3,2,0,1:T(1,128)S(1)}, f32[4,3,1,4096]{3,2,0,1:T(1,128)S(1)}, u32[]{:S(2)}, u32[]{:S(2)}) %collective-permute-start.3) | collective-permute-done | bytes 196640 | tf_op jit(solution)/shard_map/ppermute | solution.py:21
  60.3 4.7 %collective-permute-start.5 = (f32[4,3,1,4096]{3,2,0,1:T(1,128)S(1)}, f32[4,3,1,4096]{3,2,0,1:T(1,128)S(1)}, u32[]{:S(2)}, u32[]{:S(2)}) collective-permute-start(f32[4,3,1,4096]{3,2,0,1:T(1,128)S(1)} %get-tuple-element.60), channel_id=1, source_target_pairs={{1,0},{2,1},{3,2},{4,3},{5,4},{6,5},{7,6},{0,7},{9,8},{10,9},{11,1... | collective-permute-start | bytes 589832 | tf_op jit(solution)/shard_map/ppermute | solution.py:21
  65.0 4.1 %collective-permute-done.4 = f32[4,3,1,4096]{3,2,0,1:T(1,128)S(1)} collective-permute-done((f32[4,3,1,4096]{3,2,0,1:T(1,128)S(1)}, f32[4,3,1,4096]{3,2,0,1:T(1,128)S(1)}, u32[]{:S(2)}, u32[]{:S(2)}) %collective-permute-start.4) | collective-permute-done | bytes 196640 | tf_op jit(solution)/shard_map/ppermute | solution.py:18
  69.0 3.2 %collective-permute-done.5 = f32[4,3,1,4096]{3,2,0,1:T(1,128)S(1)} collective-permute-done((f32[4,3,1,4096]{3,2,0,1:T(1,128)S(1)}, f32[4,3,1,4096]{3,2,0,1:T(1,128)S(1)}, u32[]{:S(2)}, u32[]{:S(2)}) %collective-permute-start.5) | collective-permute-done | bytes 196640 | tf_op jit(solution)/shard_map/ppermute | solution.py:21
  76.4 4.7 %collective-permute-start.7 = (f32[4,3,1,4096]{3,2,0,1:T(1,128)S(1)}, f32[4,3,1,4096]{3,2,0,1:T(1,128)S(1)}, u32[]{:S(2)}, u32[]{:S(2)}) collective-permute-start(f32[4,3,1,4096]{3,2,0,1:T(1,128)S(1)} %get-tuple-element.58), channel_id=1, source_target_pairs={{1,0},{2,1},{3,2},{4,3},{5,4},{6,5},{7,6},{0,7},{9,8},{10,9},{11,1... | collective-permute-start | bytes 589832 | tf_op jit(solution)/shard_map/ppermute | solution.py:21
  81.2 4.1 %collective-permute-done.6 = f32[4,3,1,4096]{3,2,0,1:T(1,128)S(1)} collective-permute-done((f32[4,3,1,4096]{3,2,0,1:T(1,128)S(1)}, f32[4,3,1,4096]{3,2,0,1:T(1,128)S(1)}, u32[]{:S(2)}, u32[]{:S(2)}) %collective-permute-start.6) | collective-permute-done | bytes 196640 | tf_op jit(solution)/shard_map/ppermute | solution.py:18
  85.2 3.2 %collective-permute-done.7 = f32[4,3,1,4096]{3,2,0,1:T(1,128)S(1)} collective-permute-done((f32[4,3,1,4096]{3,2,0,1:T(1,128)S(1)}, f32[4,3,1,4096]{3,2,0,1:T(1,128)S(1)}, u32[]{:S(2)}, u32[]{:S(2)}) %collective-permute-start.7) | collective-permute-done | bytes 196640 | tf_op jit(solution)/shard_map/ppermute | solution.py:21
  92.4 4.7 %collective-permute-start.9 = (f32[4,3,1,4096]{3,2,0,1:T(1,128)S(1)}, f32[4,3,1,4096]{3,2,0,1:T(1,128)S(1)}, u32[]{:S(2)}, u32[]{:S(2)}) collective-permute-start(f32[4,3,1,4096]{3,2,0,1:T(1,128)S(1)} %get-tuple-element.56), channel_id=1, source_target_pairs={{1,0},{2,1},{3,2},{4,3},{5,4},{6,5},{7,6},{0,7},{9,8},{10,9},{11,1... | collective-permute-start | bytes 589832 | tf_op jit(solution)/shard_map/ppermute | solution.py:21
  97.1 4.1 %collective-permute-done.8 = f32[4,3,1,4096]{3,2,0,1:T(1,128)S(1)} collective-permute-done((f32[4,3,1,4096]{3,2,0,1:T(1,128)S(1)}, f32[4,3,1,4096]{3,2,0,1:T(1,128)S(1)}, u32[]{:S(2)}, u32[]{:S(2)}) %collective-permute-start.8) | collective-permute-done | bytes 196640 | tf_op jit(solution)/shard_map/ppermute | solution.py:18
  101.1 1.5 collective-permute-done.9
  107.0 4.5 %collective-permute-start.11 = (f32[4,3,1,4096]{3,2,0,1:T(1,128)S(1)}, f32[4,3,1,4096]{3,2,0,1:T(1,128)S(1)}, u32[]{:S(2)}, u32[]{:S(2)}) collective-permute-start(f32[4,3,1,4096]{3,2,0,1:T(1,128)S(1)} %get-tuple-element.54), channel_id=1, source_target_pairs={{1,0},{2,1},{3,2},{4,3},{5,4},{6,5},{7,6},{0,7},{9,8},{10,9},{11,1... | collective-permute-start | bytes 589832 | tf_op jit(solution)/shard_map/ppermute | solution.py:21
  111.5 3.7 %collective-permute-done.10 = f32[4,3,1,4096]{3,2,0,1:T(1,128)S(1)} collective-permute-done((f32[4,3,1,4096]{3,2,0,1:T(1,128)S(1)}, f32[4,3,1,4096]{3,2,0,1:T(1,128)S(1)}, u32[]{:S(2)}, u32[]{:S(2)}) %collective-permute-start.10) | collective-permute-done | bytes 196640 | tf_op jit(solution)/shard_map/ppermute | solution.py:18
  115.2 2.1 collective-permute-done.11
  121.6 4.7 %collective-permute-start.13 = (f32[4,3,1,4096]{3,2,0,1:T(1,128)S(1)}, f32[4,3,1,4096]{3,2,0,1:T(1,128)S(1)}, u32[]{:S(2)}, u32[]{:S(2)}) collective-permute-start(f32[4,3,1,4096]{3,2,0,1:T(1,128)S(1)} %get-tuple-element.52), channel_id=1, source_target_pairs={{1,0},{2,1},{3,2},{4,3},{5,4},{6,5},{7,6},{0,7},{9,8},{10,9},{11,1... | collective-permute-start | bytes 589832 | tf_op jit(solution)/shard_map/ppermute | solution.py:21
  126.3 4.0 %collective-permute-done.12 = f32[4,3,1,4096]{3,2,0,1:T(1,128)S(1)} collective-permute-done((f32[4,3,1,4096]{3,2,0,1:T(1,128)S(1)}, f32[4,3,1,4096]{3,2,0,1:T(1,128)S(1)}, u32[]{:S(2)}, u32[]{:S(2)}) %collective-permute-start.12) | collective-permute-done | bytes 196640 | tf_op jit(solution)/shard_map/ppermute | solution.py:18
  130.3 3.2 %collective-permute-done.13 = f32[4,3,1,4096]{3,2,0,1:T(1,128)S(1)} collective-permute-done((f32[4,3,1,4096]{3,2,0,1:T(1,128)S(1)}, f32[4,3,1,4096]{3,2,0,1:T(1,128)S(1)}, u32[]{:S(2)}, u32[]{:S(2)}) %collective-permute-start.13) | collective-permute-done | bytes 196640 | tf_op jit(solution)/shard_map/ppermute | solution.py:21
  137.5 4.7 %collective-permute-start.15 = (f32[4,3,1,4096]{3,2,0,1:T(1,128)S(1)}, f32[4,3,1,4096]{3,2,0,1:T(1,128)S(1)}, u32[]{:S(2)}, u32[]{:S(2)}) collective-permute-start(f32[4,3,1,4096]{3,2,0,1:T(1,128)S(1)} %get-tuple-element.50), channel_id=1, source_target_pairs={{1,0},{2,1},{3,2},{4,3},{5,4},{6,5},{7,6},{0,7},{9,8},{10,9},{11,1... | collective-permute-start | bytes 589832 | tf_op jit(solution)/shard_map/ppermute | solution.py:21
  142.2 4.1 %collective-permute-done.14 = f32[4,3,1,4096]{3,2,0,1:T(1,128)S(1)} collective-permute-done((f32[4,3,1,4096]{3,2,0,1:T(1,128)S(1)}, f32[4,3,1,4096]{3,2,0,1:T(1,128)S(1)}, u32[]{:S(2)}, u32[]{:S(2)}) %collective-permute-start.14) | collective-permute-done | bytes 196640 | tf_op jit(solution)/shard_map/ppermute | solution.py:18
  146.3 3.1 %collective-permute-done.15 = f32[4,3,1,4096]{3,2,0,1:T(1,128)S(1)} collective-permute-done((f32[4,3,1,4096]{3,2,0,1:T(1,128)S(1)}, f32[4,3,1,4096]{3,2,0,1:T(1,128)S(1)}, u32[]{:S(2)}, u32[]{:S(2)}) %collective-permute-start.15) | collective-permute-done | bytes 196640 | tf_op jit(solution)/shard_map/ppermute | solution.py:21
  153.5 4.7 %collective-permute-start.17 = (f32[4,3,1,4096]{3,2,0,1:T(1,128)S(1)}, f32[4,3,1,4096]{3,2,0,1:T(1,128)S(1)}, u32[]{:S(2)}, u32[]{:S(2)}) collective-permute-start(f32[4,3,1,4096]{3,2,0,1:T(1,128)S(1)} %get-tuple-element.48), channel_id=1, source_target_pairs={{1,0},{2,1},{3,2},{4,3},{5,4},{6,5},{7,6},{0,7},{9,8},{10,9},{11,1... | collective-permute-start | bytes 589832 | tf_op jit(solution)/shard_map/ppermute | solution.py:21
  158.3 4.0 %collective-permute-done.16 = f32[4,3,1,4096]{3,2,0,1:T(1,128)S(1)} collective-permute-done((f32[4,3,1,4096]{3,2,0,1:T(1,128)S(1)}, f32[4,3,1,4096]{3,2,0,1:T(1,128)S(1)}, u32[]{:S(2)}, u32[]{:S(2)}) %collective-permute-start.16) | collective-permute-done | bytes 196640 | tf_op jit(solution)/shard_map/ppermute | solution.py:18
  162.3 1.7 collective-permute-done.17
  167.9 32.0 %gather_fusion.2 = f32[4096]{0:T(1024)S(1)} fusion(f32[4,8,4096]{2,1,0:T(8,128)S(1)} %slice_bitcast_fusion.27, s32[4096]{0:T(1024)S(1)} %or_bitcast_fusion), kind=kCustom, calls=%fused_computation.2 | custom fusion | bytes 81920 | tf_op jit(solution)/shard_map/jit(take_along_axis)/gather | solution.py:80
  200.0 19.7 %psum.7 = f32[4]{0:T(128)S(1)} all-reduce(f32[4]{0:T(128)S(1)} %fusion.230), channel_id=1, replica_groups=mesh['group'=2,'particle'=2,'strip'=8] {'strip'}, use_global_device_ids=true, to_apply=%region_3.4 | all-reduce | flops 4 | bytes 32 | tf_op jit(solution)/shard_map/psum | solution.py:85
  (178 shorter events, 39.5 us)
Async XLA Ops:
  7.2 0.8 copy-start.4
  7.2 17.2 %all-gather.2.cloned.1.call-start = ((), (), s32[]{:S(2)}) async-start(), calls=%async_computation | async-start | bytes 4718592 | tf_op jit(solution)/shard_map/all_gather | solution.py:71
  27.5 10.6 %collective-permute-start = (f32[4,3,1,4096]{3,2,0,1:T(1,128)S(1)}, f32[4,3,1,4096]{3,2,0,1:T(1,128)S(1)}, u32[]{:S(2)}, u32[]{:S(2)}) collective-permute-start(f32[4,3,1,4096]{3,2,0,1:T(1,128)S(1)} %get-tuple-element.63), channel_id=1, source_target_pairs={{0,1},{1,2},{2,3},{3,4},{4,5},{5,6},{6,7},{7,0},{8,9},{9,10},{10,1... | collective-permute-start | bytes 589832 | tf_op jit(solution)/shard_map/ppermute | solution.py:18
  29.2 11.0 %collective-permute-start.1 = (f32[4,3,1,4096]{3,2,0,1:T(1,128)S(1)}, f32[4,3,1,4096]{3,2,0,1:T(1,128)S(1)}, u32[]{:S(2)}, u32[]{:S(2)}) collective-permute-start(f32[4,3,1,4096]{3,2,0,1:T(1,128)S(1)} %get-tuple-element.64), channel_id=1, source_target_pairs={{1,0},{2,1},{3,2},{4,3},{5,4},{6,5},{7,6},{0,7},{9,8},{10,9},{11,1... | collective-permute-start | bytes 589832 | tf_op jit(solution)/shard_map/ppermute | solution.py:21
  44.3 8.8 %collective-permute-start.2 = (f32[4,3,1,4096]{3,2,0,1:T(1,128)S(1)}, f32[4,3,1,4096]{3,2,0,1:T(1,128)S(1)}, u32[]{:S(2)}, u32[]{:S(2)}) collective-permute-start(f32[4,3,1,4096]{3,2,0,1:T(1,128)S(1)} %get-tuple-element.61), channel_id=1, source_target_pairs={{0,1},{1,2},{2,3},{3,4},{4,5},{5,6},{6,7},{7,0},{8,9},{9,10},{10,1... | collective-permute-start | bytes 589832 | tf_op jit(solution)/shard_map/ppermute | solution.py:18
  44.6 11.4 %collective-permute-start.3 = (f32[4,3,1,4096]{3,2,0,1:T(1,128)S(1)}, f32[4,3,1,4096]{3,2,0,1:T(1,128)S(1)}, u32[]{:S(2)}, u32[]{:S(2)}) collective-permute-start(f32[4,3,1,4096]{3,2,0,1:T(1,128)S(1)} %get-tuple-element.62), channel_id=1, source_target_pairs={{1,0},{2,1},{3,2},{4,3},{5,4},{6,5},{7,6},{0,7},{9,8},{10,9},{11,1... | collective-permute-start | bytes 589832 | tf_op jit(solution)/shard_map/ppermute | solution.py:21
  60.2 8.8 %collective-permute-start.4 = (f32[4,3,1,4096]{3,2,0,1:T(1,128)S(1)}, f32[4,3,1,4096]{3,2,0,1:T(1,128)S(1)}, u32[]{:S(2)}, u32[]{:S(2)}) collective-permute-start(f32[4,3,1,4096]{3,2,0,1:T(1,128)S(1)} %get-tuple-element.59), channel_id=1, source_target_pairs={{0,1},{1,2},{2,3},{3,4},{4,5},{5,6},{6,7},{7,0},{8,9},{9,10},{10,1... | collective-permute-start | bytes 589832 | tf_op jit(solution)/shard_map/ppermute | solution.py:18
  60.3 11.9 %collective-permute-start.5 = (f32[4,3,1,4096]{3,2,0,1:T(1,128)S(1)}, f32[4,3,1,4096]{3,2,0,1:T(1,128)S(1)}, u32[]{:S(2)}, u32[]{:S(2)}) collective-permute-start(f32[4,3,1,4096]{3,2,0,1:T(1,128)S(1)} %get-tuple-element.60), channel_id=1, source_target_pairs={{1,0},{2,1},{3,2},{4,3},{5,4},{6,5},{7,6},{0,7},{9,8},{10,9},{11,1... | collective-permute-start | bytes 589832 | tf_op jit(solution)/shard_map/ppermute | solution.py:21
  76.4 8.8 %collective-permute-start.6 = (f32[4,3,1,4096]{3,2,0,1:T(1,128)S(1)}, f32[4,3,1,4096]{3,2,0,1:T(1,128)S(1)}, u32[]{:S(2)}, u32[]{:S(2)}) collective-permute-start(f32[4,3,1,4096]{3,2,0,1:T(1,128)S(1)} %get-tuple-element.57), channel_id=1, source_target_pairs={{0,1},{1,2},{2,3},{3,4},{4,5},{5,6},{6,7},{7,0},{8,9},{9,10},{10,1... | collective-permute-start | bytes 589832 | tf_op jit(solution)/shard_map/ppermute | solution.py:18
  76.4 11.9 %collective-permute-start.7 = (f32[4,3,1,4096]{3,2,0,1:T(1,128)S(1)}, f32[4,3,1,4096]{3,2,0,1:T(1,128)S(1)}, u32[]{:S(2)}, u32[]{:S(2)}) collective-permute-start(f32[4,3,1,4096]{3,2,0,1:T(1,128)S(1)} %get-tuple-element.58), channel_id=1, source_target_pairs={{1,0},{2,1},{3,2},{4,3},{5,4},{6,5},{7,6},{0,7},{9,8},{10,9},{11,1... | collective-permute-start | bytes 589832 | tf_op jit(solution)/shard_map/ppermute | solution.py:21
  92.3 8.8 %collective-permute-start.8 = (f32[4,3,1,4096]{3,2,0,1:T(1,128)S(1)}, f32[4,3,1,4096]{3,2,0,1:T(1,128)S(1)}, u32[]{:S(2)}, u32[]{:S(2)}) collective-permute-start(f32[4,3,1,4096]{3,2,0,1:T(1,128)S(1)} %get-tuple-element.55), channel_id=1, source_target_pairs={{0,1},{1,2},{2,3},{3,4},{4,5},{5,6},{6,7},{7,0},{8,9},{9,10},{10,1... | collective-permute-start | bytes 589832 | tf_op jit(solution)/shard_map/ppermute | solution.py:18
  92.4 10.2 %collective-permute-start.9 = (f32[4,3,1,4096]{3,2,0,1:T(1,128)S(1)}, f32[4,3,1,4096]{3,2,0,1:T(1,128)S(1)}, u32[]{:S(2)}, u32[]{:S(2)}) collective-permute-start(f32[4,3,1,4096]{3,2,0,1:T(1,128)S(1)} %get-tuple-element.56), channel_id=1, source_target_pairs={{1,0},{2,1},{3,2},{4,3},{5,4},{6,5},{7,6},{0,7},{9,8},{10,9},{11,1... | collective-permute-start | bytes 589832 | tf_op jit(solution)/shard_map/ppermute | solution.py:21
  106.0 5.5 %copy-start.1 = (s32[8,128]{1,0:T(8,128)S(1)}, s32[8,128]{1,0:T(8,128)}, u32[]{:S(2)}) copy-start(s32[8,128]{1,0:T(8,128)} %param.8) | copy-start | bytes 12292
  106.7 8.5 %collective-permute-start.10 = (f32[4,3,1,4096]{3,2,0,1:T(1,128)S(1)}, f32[4,3,1,4096]{3,2,0,1:T(1,128)S(1)}, u32[]{:S(2)}, u32[]{:S(2)}) collective-permute-start(f32[4,3,1,4096]{3,2,0,1:T(1,128)S(1)} %get-tuple-element.53), channel_id=1, source_target_pairs={{0,1},{1,2},{2,3},{3,4},{4,5},{5,6},{6,7},{7,0},{8,9},{9,10},{10,1... | collective-permute-start | bytes 589832 | tf_op jit(solution)/shard_map/ppermute | solution.py:18
  107.0 10.4 %collective-permute-start.11 = (f32[4,3,1,4096]{3,2,0,1:T(1,128)S(1)}, f32[4,3,1,4096]{3,2,0,1:T(1,128)S(1)}, u32[]{:S(2)}, u32[]{:S(2)}) collective-permute-start(f32[4,3,1,4096]{3,2,0,1:T(1,128)S(1)} %get-tuple-element.54), channel_id=1, source_target_pairs={{1,0},{2,1},{3,2},{4,3},{5,4},{6,5},{7,6},{0,7},{9,8},{10,9},{11,1... | collective-permute-start | bytes 589832 | tf_op jit(solution)/shard_map/ppermute | solution.py:21
  121.5 8.8 %collective-permute-start.12 = (f32[4,3,1,4096]{3,2,0,1:T(1,128)S(1)}, f32[4,3,1,4096]{3,2,0,1:T(1,128)S(1)}, u32[]{:S(2)}, u32[]{:S(2)}) collective-permute-start(f32[4,3,1,4096]{3,2,0,1:T(1,128)S(1)} %get-tuple-element.51), channel_id=1, source_target_pairs={{0,1},{1,2},{2,3},{3,4},{4,5},{5,6},{6,7},{7,0},{8,9},{9,10},{10,1... | collective-permute-start | bytes 589832 | tf_op jit(solution)/shard_map/ppermute | solution.py:18
  121.6 11.9 %collective-permute-start.13 = (f32[4,3,1,4096]{3,2,0,1:T(1,128)S(1)}, f32[4,3,1,4096]{3,2,0,1:T(1,128)S(1)}, u32[]{:S(2)}, u32[]{:S(2)}) collective-permute-start(f32[4,3,1,4096]{3,2,0,1:T(1,128)S(1)} %get-tuple-element.52), channel_id=1, source_target_pairs={{1,0},{2,1},{3,2},{4,3},{5,4},{6,5},{7,6},{0,7},{9,8},{10,9},{11,1... | collective-permute-start | bytes 589832 | tf_op jit(solution)/shard_map/ppermute | solution.py:21
  137.4 8.9 %collective-permute-start.14 = (f32[4,3,1,4096]{3,2,0,1:T(1,128)S(1)}, f32[4,3,1,4096]{3,2,0,1:T(1,128)S(1)}, u32[]{:S(2)}, u32[]{:S(2)}) collective-permute-start(f32[4,3,1,4096]{3,2,0,1:T(1,128)S(1)} %get-tuple-element.49), channel_id=1, source_target_pairs={{0,1},{1,2},{2,3},{3,4},{4,5},{5,6},{6,7},{7,0},{8,9},{9,10},{10,1... | collective-permute-start | bytes 589832 | tf_op jit(solution)/shard_map/ppermute | solution.py:18
  137.5 11.9 %collective-permute-start.15 = (f32[4,3,1,4096]{3,2,0,1:T(1,128)S(1)}, f32[4,3,1,4096]{3,2,0,1:T(1,128)S(1)}, u32[]{:S(2)}, u32[]{:S(2)}) collective-permute-start(f32[4,3,1,4096]{3,2,0,1:T(1,128)S(1)} %get-tuple-element.50), channel_id=1, source_target_pairs={{1,0},{2,1},{3,2},{4,3},{5,4},{6,5},{7,6},{0,7},{9,8},{10,9},{11,1... | collective-permute-start | bytes 589832 | tf_op jit(solution)/shard_map/ppermute | solution.py:21
  152.8 5.5 %copy-start.3 = (f32[8,128]{1,0:T(8,128)S(1)}, f32[8,128]{1,0:T(8,128)}, u32[]{:S(2)}) copy-start(f32[8,128]{1,0:T(8,128)} %param.9) | copy-start | bytes 12292
  153.5 8.8 %collective-permute-start.16 = (f32[4,3,1,4096]{3,2,0,1:T(1,128)S(1)}, f32[4,3,1,4096]{3,2,0,1:T(1,128)S(1)}, u32[]{:S(2)}, u32[]{:S(2)}) collective-permute-start(f32[4,3,1,4096]{3,2,0,1:T(1,128)S(1)} %get-tuple-element.47), channel_id=1, source_target_pairs={{0,1},{1,2},{2,3},{3,4},{4,5},{5,6},{6,7},{7,0},{8,9},{9,10},{10,1... | collective-permute-start | bytes 589832 | tf_op jit(solution)/shard_map/ppermute | solution.py:18
  153.5 10.5 %collective-permute-start.17 = (f32[4,3,1,4096]{3,2,0,1:T(1,128)S(1)}, f32[4,3,1,4096]{3,2,0,1:T(1,128)S(1)}, u32[]{:S(2)}, u32[]{:S(2)}) collective-permute-start(f32[4,3,1,4096]{3,2,0,1:T(1,128)S(1)} %get-tuple-element.48), channel_id=1, source_target_pairs={{1,0},{2,1},{3,2},{4,3},{5,4},{6,5},{7,6},{0,7},{9,8},{10,9},{11,1... | collective-permute-start | bytes 589832 | tf_op jit(solution)/shard_map/ppermute | solution.py:21
  167.8 32.1 %copy-start = (f32[4,3,8,4096]{3,2,1,0:T(8,128)}, f32[4,3,8,4096]{3,2,1,0:T(8,128)S(1)}, u32[]{:S(2)}) copy-start(f32[4,3,8,4096]{3,2,1,0:T(8,128)S(1)} %fusion.5) | copy-start | bytes 4718596
  167.9 32.0 %copy-start.2 = (f32[8,128]{1,0:T(8,128)S(1)}, f32[8,128]{1,0:T(8,128)}, u32[]{:S(2)}) copy-start(f32[8,128]{1,0:T(8,128)} %param.7) | copy-start | bytes 12292
Sparse Core Ops, SparseCore 0:
  9.6 14.8 all-gather.1
where the time goes:
time: 227 us
  waiting for transfers between devices  77.2 us (34%)
  local copies, waits for them, and re-layouts  50.8 us (22%)
  starting transfers between devices  43 us (19%)
  other arithmetic  21.5 us (9%)
  blocking collectives  19.7 us (9%)
  between operations  14.9 us (7%)
    ppermute x9, starting transfers between devices, with_halo(): lax.ppermute(lax.slice_in_dim(block, 0, width, axis=dim), axis, backward)  40.2 us
    ppermute x9, waiting for transfers between devices, with_halo(): lax.ppermute(lax.slice_in_dim(block, block.shape[dim] - width, None, axis...  37.9 us
    gather x1, local copies, waits for them, and re-layouts, local(): picked = jnp.take_along_axis(eta, index, axis=-1)  32 us
    ppermute x9, waiting for transfers between devices, with_halo(): lax.ppermute(lax.slice_in_dim(block, 0, width, axis=dim), axis, backward)  23.1 us
    psum x1, blocking collectives, local(): total = lax.psum(partial_sum, 'strip')  19.7 us
    all_gather x1, waiting for transfers between devices, local(): everyone = lax.all_gather(ensemble, 'particle', axis=0, tiled=True)  15.5 us
    slice x70, local copies, waits for them, and re-layouts, along_x(): return 0.5 * (jnp.roll(inner, -1, axis=-1) - jnp.roll(inner, 1, axis=-1))  10 us
    another operation x27, other arithmetic, tendency(): return jnp.stack([eta_t, east_t, north_t], axis=-3)  10 us
  transfers between devices with their start and end apart: 19, of which 19 were waited for; matrix products, arithmetic and copies ran while one was open for 0% of the time, Pallas kernels for 0%

commit v1 on v0

v1 whole, which is shorter than its diff:
```python
import functools

import jax
import jax.numpy as jnp
from jax import lax
from jax.experimental import pallas as pl
from jax.experimental.pallas import tpu as pltpu
from jax.sharding import PartitionSpec as P

STEPS = 3
DT = 0.4
HALF = 0.5 * DT
DEPTH = 3 * STEPS
LANES = 128
TILE = 8
UNROLL = 4

VMEM = pl.BlockSpec(memory_space=pltpu.VMEM)
SMEM = pl.BlockSpec(memory_space=pltpu.SMEM)
ANY = pl.BlockSpec(memory_space=pl.ANY)


def pick_kernel(index_ref, own_ref, other_ref, *rest, count):
    outs, sems = rest[:count], rest[count]
    own = own_ref.shape[0]
    for k in range(count):
        at = index_ref[k]

        @pl.when(at < own)
        def _():
            pltpu.make_async_copy(own_ref.at[jnp.minimum(at, own - 1)], outs[k], sems.at[k]).start()

        @pl.when(at >= own)
        def _():
            pltpu.make_async_copy(
                other_ref.at[jnp.maximum(at - own, 0)], outs[k], sems.at[k]
            ).start()

    for k in range(count):
        pltpu.make_async_copy(own_ref.at[0], outs[k], sems.at[k]).wait()


def pick(index, own, other):
    count = index.shape[0]
    block = jax.ShapeDtypeStruct(own.shape[1:], own.dtype)
    return pl.pallas_call(
        functools.partial(pick_kernel, count=count),
        out_shape=[block] * count,
        in_specs=[SMEM, ANY, ANY],
        out_specs=[ANY] * count,
        scratch_shapes=[pltpu.SemaphoreType.DMA((count,))],
    )(index, own, other)


def pack_kernel(par_ref, own_ref, got_ref, up_ref, down_ref):
    cols = own_ref.shape[2]
    part = cols // TILE

    def fill(top, bottom):
        up_ref[:, :, :cols] = bottom[...]
        down_ref[:, :, :cols] = top[...]
        for f in range(3):
            for q in range(TILE):
                up_ref[f, q : q + 1, cols:] = top[f, TILE - 1 : TILE, q * part : (q + 1) * part]
                down_ref[f, q : q + 1, cols:] = bottom[f, 0:1, q * part : (q + 1) * part]

    @pl.when(par_ref[0] == 0)
    def _():
        fill(own_ref, got_ref)

    @pl.when(par_ref[0] == 1)
    def _():
        fill(got_ref, own_ref)


def pack(par, own, got):
    cols = own.shape[2]
    message = jax.ShapeDtypeStruct((3, TILE, cols + cols // TILE), own.dtype)
    return pl.pallas_call(
        pack_kernel,
        out_shape=[message, message],
        in_specs=[SMEM, VMEM, VMEM],
        out_specs=[VMEM, VMEM],
    )(par, own, got)


BASE = 16
ROWS = 48


def evaluate(src, state, dst, cor_ref, start, tiles, kind):
    ncol = src.shape[1]
    lane = lax.broadcasted_iota(jnp.int32, (TILE, LANES), 1)
    first = lane == 0
    last = lane == LANES - 1

    def one(ct, r0, cor):
        left = (ct + (ncol - 1)) % ncol
        right = (ct + 1) % ncol
        rows = pl.ds(r0, TILE)
        mid, dx, dy = [], [], []
        ee = []
        for f in range(3):
            c = src[f, ct, rows, :]
            e = pltpu.roll(jnp.where(first, src[f, right, rows, :], c), LANES - 1, 1)
            w = pltpu.roll(jnp.where(last, src[f, left, rows, :], c), 1, 1)
            n = src[f, ct, pl.ds(r0 + 1, TILE), :]
            s = src[f, ct, pl.ds(r0 - 1, TILE), :]
            mid.append(c)
            ee.append((e, w, n, s))
        eta, u, v = mid
        (eE, eW, eN, eS), (uE, uW, uN, uS), (vE, vW, vN, vS) = ee
        duy = uN - uS
        dvx = vE - vW
        dux = uE - uW
        dvy = vN - vS
        flow = (dux + dvy) + ((eE * uE - eW * uW) + (eN * vN - eS * vS))
        lu = v * (cor - duy) - u * dux - (eE - eW)
        lv = u * (cor + dvx) + v * dvy + (eN - eS)
        change = (-flow, lu, -lv)
        for f in range(3):
            if kind == 0:
                new = mid[f] + HALF * change[f]
            elif kind == 1:
                new = 0.75 * state[f, ct, rows, :] + (0.25 * mid[f] + (0.25 * HALF) * change[f])
            else:
                new = (1.0 / 3.0) * state[f, ct, rows, :] + (
                    (2.0 / 3.0) * mid[f] + (2.0 / 3.0 * HALF) * change[f]
                )
            dst[f, ct, rows, :] = new

    for t in range(tiles):
        r0 = start + t * TILE
        cor = cor_ref[pl.ds(r0, TILE), :]

        def body(i, carry):
            for k in range(UNROLL):
                one(i * UNROLL + k, r0, cor)
            return carry

        lax.fori_loop(0, ncol // UNROLL, body, 0)


def forecast_kernel(
    scalars, own, got, low, high, obs_own, obs_got, keep, send, misfit, state, s1, s2, cor_ref
):
    cols = own.shape[2]
    ncol = cols // LANES
    per = ncol // TILE
    par = scalars[0]

    def load(top, bottom):
        for f in range(3):
            for ct in range(ncol):
                at = slice(ct * LANES, (ct + 1) * LANES)
                state[f, ct, BASE : BASE + TILE, :] = top[f, :, at]
                state[f, ct, BASE + TILE : BASE + 2 * TILE, :] = bottom[f, :, at]

    @pl.when(par == 0)
    def _():
        load(own, got)

    @pl.when(par == 1)
    def _():
        load(got, own)

    for f in range(3):
        for ct in range(ncol):
            at = slice(ct * LANES, (ct + 1) * LANES)
            state[f, ct, BASE - TILE : BASE, :] = low[f, :, at]
            state[f, ct, BASE + 2 * TILE : BASE + 3 * TILE, :] = high[f, :, at]
            q = ct // per
            at = slice(cols + (ct % per) * LANES, cols + (ct % per + 1) * LANES)
            state[f, ct, BASE - TILE - 1 : BASE - TILE, :] = low[f, q : q + 1, at]
            state[f, ct, BASE + 3 * TILE : BASE + 3 * TILE + 1, :] = high[f, q : q + 1, at]

    total_rows = scalars[2]
    row = lax.broadcasted_iota(jnp.int32, (ROWS, LANES), 0) + (scalars[1] - BASE)
    row = jnp.where(row < 0, row + total_rows, row)
    row = jnp.where(row >= total_rows, row - total_rows, row).astype(jnp.float32)
    rows_f = total_rows.astype(jnp.float32)
    cor_ref[...] = 2.0 * (0.3 + 0.4 * ((row + 0.5) / rows_f - 0.5))

    for k in range(DEPTH):
        reach = DEPTH - 1 - k
        start = BASE - reach
        tiles = (2 * TILE + 2 * reach + TILE - 1) // TILE
        kind = k % 3
        src, dst = ((state, s1), (s1, s2), (s2, state))[kind]
        evaluate(src, state, dst, cor_ref, start, tiles, kind)

    def store(top, bottom):
        for f in range(3):
            for ct in range(ncol):
                at = slice(ct * LANES, (ct + 1) * LANES)
                top[f, :, at] = state[f, ct, BASE : BASE + TILE, :]
                bottom[f, :, at] = state[f, ct, BASE + TILE : BASE + 2 * TILE, :]

    @pl.when(par == 0)
    def _():
        store(keep, send)

    @pl.when(par == 1)
    def _():
        store(send, keep)

    total = jnp.zeros((TILE, LANES), jnp.float32)
    for half in range(2):
        mine = par == half
        obs = [jnp.where(mine, obs_own[k], obs_got[k]) for k in range(3)]
        where = obs[1].astype(jnp.int32)
        tile, lane = where // LANES, where % LANES
        picked = jnp.zeros((TILE, LANES), jnp.float32)
        for ct in range(ncol):
            eta = state[0, ct, BASE + half * TILE : BASE + (half + 1) * TILE, :]
            there = jnp.take_along_axis(eta, lane, axis=1)
            picked = jnp.where(tile == ct, there, picked)
        gap = obs[0] - picked
        total = total + obs[2] * gap * gap
    misfit[...] = total


def forecast(scalars, own, got, low, high, obs_own, obs_got):
    cols = own.shape[2]
    block = jax.ShapeDtypeStruct(own.shape, own.dtype)
    field = pltpu.VMEM((3, cols // LANES, ROWS, LANES), jnp.float32)
    return pl.pallas_call(
        forecast_kernel,
        out_shape=[block, block, jax.ShapeDtypeStruct((TILE, LANES), jnp.float32)],
        in_specs=[SMEM] + [VMEM] * 6,
        out_specs=[VMEM] * 3,
        scratch_shapes=[field, field, field, pltpu.VMEM((ROWS, LANES), jnp.float32)],
        compiler_params=pltpu.CompilerParams(vmem_limit_bytes=32 * 2**20),
    )(scalars, own, got, low, high, obs_own, obs_got)


def local(ensemble, offspring, observations, obs_cols, obs_precision):
    members, _, strip_rows, cols = ensemble.shape
    strips = lax.axis_size("strip")
    total_rows = strips * strip_rows
    strip = lax.axis_index("strip")
    par = strip % 2
    half = members // 2
    swap = [(i, i ^ 1) for i in range(strips)]
    up = [(i, (i + 2) % strips) for i in range(strips)]
    down = [(b, a) for a, b in up]

    total_members = offspring.shape[0]
    cumulative = jnp.cumsum(offspring)
    slots = jnp.arange(total_members, dtype=jnp.int32)
    source = jnp.sum((cumulative[None, :] <= slots[:, None]).astype(jnp.int32), axis=1)
    here = lax.axis_index("particle")

    def crossing(side):
        wanted = lax.dynamic_slice_in_dim(source, (1 - side) * members, members)
        mine = wanted // members == side
        low = jnp.min(jnp.where(mine, wanted, total_members))
        high = jnp.max(jnp.where(mine, wanted, -1))
        base = side * members
        return jnp.clip(low - base, 0, members - 1), jnp.clip(high - base, 0, members - 1)

    low_out, high_out = crossing(here)
    leaving = jnp.concatenate(
        [
            lax.dynamic_slice_in_dim(ensemble, low_out, 1, axis=0),
            lax.dynamic_slice_in_dim(ensemble, high_out, 1, axis=0),
        ]
    )
    arrived = lax.ppermute(leaving, "particle", [(0, 1), (1, 0)])
    low_in, _ = crossing(1 - here)
    wanted = lax.dynamic_slice_in_dim(source, here * members, members)
    local_at = wanted - here * members
    other_at = wanted - (1 - here) * members
    own = wanted // members == here
    index = jnp.where(own, local_at, jnp.where(other_at == low_in, members, members + 1))

    rows = (strip * strip_rows + jnp.arange(strip_rows, dtype=jnp.int32)).astype(jnp.float32)
    weight = obs_precision * (1.0 + 2.0 * (rows + 0.5) / total_rows)[:, None]
    obs_own = jnp.stack([observations, obs_cols.astype(jnp.float32), weight])
    obs_got = lax.ppermute(obs_own, "strip", swap)

    order = jnp.stack([(1 - par) * half + k for k in range(half)] + [par * half + k for k in range(half)])
    blocks = pick(jnp.take(index, order), ensemble, arrived)
    given, kept = blocks[:half], blocks[half:]
    scalars = jnp.stack([par, (strip - par) * strip_rows, jnp.int32(total_rows)]).astype(jnp.int32)

    keeps, backs, sums = [], [], []
    got = [lax.ppermute(g, "strip", swap) for g in given]
    for k in range(half):
        rising, falling = pack(scalars, kept[k], got[k])
        low = lax.ppermute(rising, "strip", up)
        high = lax.ppermute(falling, "strip", down)
        keep, send, misfit = forecast(scalars, kept[k], got[k], low, high, obs_own, obs_got)
        keeps.append(keep)
        backs.append(lax.ppermute(send, "strip", swap))
        sums.append(jnp.sum(misfit))
    total = jnp.stack(sums)
    step = 2
    while step < strips:
        total = total + lax.ppermute(total, "strip", [(i, i ^ step) for i in range(strips)])
        step *= 2
    total_got = lax.ppermute(total, "strip", swap)
    lower = par == 0
    mine, theirs = jnp.stack(keeps), jnp.stack(backs)
    state = jnp.concatenate([jnp.where(lower, mine, theirs), jnp.where(lower, theirs, mine)])
    total = jnp.concatenate([jnp.where(lower, total, total_got), jnp.where(lower, total_got, total)])
    log_weights = -0.5 * total / (total_rows * obs_cols.shape[1])
    return (state, log_weights)


def solution(mesh):
    in_specs = (
        P(("group", "particle"), None, "strip", None),
        P("group"),
        P(("group", "strip"), None),
        P(("group", "strip"), None),
        P(("group", "strip"), None),
    )
    out_specs = (P(("group", "particle"), None, "strip", None), P(("group", "particle")))
    return jax.shard_map(local, mesh=mesh, in_specs=in_specs, out_specs=out_specs, check_vma=False)
```

time: 227 us -> 186 us (0.82)
  Pallas kernels: 0 us -> 112 us
  local copies, waits for them, and re-layouts: 50.8 us -> 5.21 us
  waiting for transfers between devices: 77.2 us -> 37.6 us
  starting transfers between devices: 43 us -> 16 us
  blocking collectives: 19.7 us -> 0 us
  between operations: 14.9 us -> 2.69 us
  other arithmetic: 21.5 us -> 11.6 us
    pallas_call x0 -> x5, Pallas kernels: none -> 112 us  [the longest x2 58.3 us: forecast(): pl.pallas_call(forecast_kernel, out_shape=[block, block, jax.ShapeDtypeSt...]
    gather x3 -> x1, local copies, waits for them, and re-layouts: 35.2 us -> 0.64 us  [local(): blocks = pick(jnp.take(index, order), ensemble, arrived)]
    ppermute x18 -> x13, starting transfers between devices: 42.9 us -> 16 us  [the longest x2 4.07 us: local(): high = lax.ppermute(falling, 'strip', down)]
    ppermute x18 -> x13, waiting for transfers between devices: 61 us -> 37.6 us  [the longest x2 15.4 us: local(): high = lax.ppermute(falling, 'strip', down)]
    psum x1 -> x0, blocking collectives: 19.7 us -> none  [local(): total = lax.psum(partial_sum, 'strip')]
    all_gather x1 -> x0, waiting for transfers between devices: 15.5 us -> none  [local(): everyone = lax.all_gather(ensemble, 'particle', axis=0, tiled=True)]
    slice x78 -> x0, local copies, waits for them, and re-layouts: 12.8 us -> none  [the longest x70 10 us: along_x(): return 0.5 * (jnp.roll(inner, -1, axis=-1) - jnp.roll(inner, 1, axis=-1))]
    another operation x28 -> x6, other arithmetic: 10.2 us -> 2.92 us  [the longest x1 1.35 us: local(): total = jnp.stack(sums)]
  transfers between devices with their start and end apart: 19 -> 13, of which waited for: 19 -> 7; matrix products, arithmetic and copies ran while one was open for 0% -> 4% of each run, Pallas kernels for 0% -> 34%
where the time goes in v1:
time: 186 us; the launch traced here: 185 us
  Pallas kernels  112 us (60%)
  waiting for transfers between devices  37.6 us (20%)
  starting transfers between devices  16 us (9%)
  other arithmetic  11.6 us (6%)
  local copies, waits for them, and re-layouts  5.21 us (3%)
  between operations  2.69 us (1%)
    pallas_call x2, Pallas kernels, forecast(): pl.pallas_call(forecast_kernel, out_shape=[block, block, jax.ShapeDtypeSt...  58.3 us
    pallas_call x1, Pallas kernels, pick(): pl.pallas_call(functools.partial(pick_kernel, count=count), out_shape=[bl...  49.4 us
    ppermute x2, waiting for transfers between devices, local(): high = lax.ppermute(falling, 'strip', down)  15.4 us
    ppermute x2, waiting for transfers between devices, local(): got = [lax.ppermute(g, 'strip', swap) for g in given]  10.4 us
    ppermute x2, waiting for transfers between devices, local(): lax.ppermute(total, 'strip', [(i, i ^ step) for i in range(strips)])  7.09 us
    pallas_call x2, Pallas kernels, pack(): pl.pallas_call(pack_kernel, out_shape=[message, message], in_specs=[SMEM,...  4.32 us
    ppermute x2, starting transfers between devices, local(): high = lax.ppermute(falling, 'strip', down)  4.07 us
    ppermute x2, starting transfers between devices, local(): low = lax.ppermute(rising, 'strip', up)  3.91 us
  transfers between devices with their start and end apart: 13, of which 7 were waited for; matrix products, arithmetic and copies ran while one was open for 4% of the time, Pallas kernels for 34%

profile of v1, /device:TPU:0, one launch (start us, length us, event | category | flops | bytes accessed | tf_op | source)
XLA Modules:
  0.0 185.3 jit_solution(8867580978844169620)
XLA Ops:
  0.6 0.8 reduce-window.8
  1.6 0.8 fusion.2
  3.7 1.2 constant_dynamic-slice_fusion.1
  7.6 0.9 copy-done.7
  8.5 49.4 %shard_map.68 = (f32[3,8,4096]{2,1,0:T(8,128)}, f32[3,8,4096]{2,1,0:T(8,128)}, f32[3,8,4096]{2,1,0:T(8,128)}, f32[3,8,4096]{2,1,0:T(8,128)}) custom-call(s32[4]{0:T(128)} %and_select_fusion.2.index_ref, f32[4,3,8,4096]{3,2,1,0:T(8,128)} %own_ref.1, f32[2,3,8,4096]{3,2,1,0:T(8,128)} %copy-done.7), custom_call_target="tpu_custom_call" | custom-call | tf_op jit(solution)/shard_map/pallas_call | solution.py:46
  57.9 2.8 %collective-permute-start.5 = (f32[3,8,4096]{2,1,0:T(8,128)}, f32[3,8,4096]{2,1,0:T(8,128)S(1)}, u32[]{:S(2)}, u32[]{:S(2)}) collective-permute-start(f32[3,8,4096]{2,1,0:T(8,128)} %get-tuple-element.22), channel_id=1, source_target_pairs={{0,1},{1,0},{2,3},{3,2},{4,5},{5,4},{6,7},{7,6},{8,9},{9,8},{10,11... | collective-permute-start | bytes 1179656 | tf_op jit(solution)/shard_map/ppermute | solution.py:288
  61.4 9.3 %collective-permute-done.5.got_ref.got = f32[3,8,4096]{2,1,0:T(8,128)S(1)} collective-permute-done((f32[3,8,4096]{2,1,0:T(8,128)}, f32[3,8,4096]{2,1,0:T(8,128)S(1)}, u32[]{:S(2)}, u32[]{:S(2)}) %collective-permute-start.5) | collective-permute-done | bytes 393248 | tf_op jit(solution)/shard_map/ppermute | solution.py:288
  70.8 0.8 copy-done.4
  71.5 2.2 %shard_map.71 = (f32[3,8,4608]{2,1,0:T(8,128)}, f32[3,8,4608]{2,1,0:T(8,128)}) custom-call(s32[3]{0:T(128)} %pad_add_fusion.par_ref.scalars, f32[3,8,4096]{2,1,0:T(8,128)} %get-tuple-element.21.own_ref.own, f32[3,8,4096]{2,1,0:T(8,128)} %copy-done.4), custom_call_target="tpu_custom_call" | custom-call | tf_op jit(solution)/shard_map/pallas_call | solution.py:79
  73.7 2.1 %collective-permute-start.6 = (f32[3,8,4608]{2,1,0:T(8,128)}, f32[3,8,4608]{2,1,0:T(8,128)S(1)}, u32[]{:S(2)}, u32[]{:S(2)}) collective-permute-start(f32[3,8,4608]{2,1,0:T(8,128)} %get-tuple-element.23), channel_id=1, source_target_pairs={{0,2},{1,3},{2,4},{3,5},{4,6},{5,7},{6,0},{7,1},{8,10},{9,11},{10,... | collective-permute-start | bytes 1327112 | tf_op jit(solution)/shard_map/ppermute | solution.py:291
  75.8 2.0 %collective-permute-start.7 = (f32[3,8,4608]{2,1,0:T(8,128)}, f32[3,8,4608]{2,1,0:T(8,128)S(1)}, u32[]{:S(2)}, u32[]{:S(2)}) collective-permute-start(f32[3,8,4608]{2,1,0:T(8,128)} %get-tuple-element.24), channel_id=1, source_target_pairs={{2,0},{3,1},{4,2},{5,3},{6,4},{7,5},{0,6},{1,7},{10,8},{11,9},{12,... | collective-permute-start | bytes 1327112 | tf_op jit(solution)/shard_map/ppermute | solution.py:292
  77.9 1.1 collective-permute-done.1.got_ref.got
  79.7 2.1 %shard_map.69 = (f32[3,8,4608]{2,1,0:T(8,128)}, f32[3,8,4608]{2,1,0:T(8,128)}) custom-call(s32[3]{0:T(128)} %pad_add_fusion.par_ref.scalars, f32[3,8,4096]{2,1,0:T(8,128)} %get-tuple-element.16.own_ref.own, f32[3,8,4096]{2,1,0:T(8,128)} %copy-done.1), custom_call_target="tpu_custom_call" | custom-call | tf_op jit(solution)/shard_map/pallas_call | solution.py:79
  81.8 1.8 collective-permute-start.2
  83.6 2.0 %collective-permute-start.3 = (f32[3,8,4608]{2,1,0:T(8,128)}, f32[3,8,4608]{2,1,0:T(8,128)S(1)}, u32[]{:S(2)}, u32[]{:S(2)}) collective-permute-start(f32[3,8,4608]{2,1,0:T(8,128)} %get-tuple-element.19), channel_id=1, source_target_pairs={{2,0},{3,1},{4,2},{5,3},{6,4},{7,5},{0,6},{1,7},{10,8},{11,9},{12,... | collective-permute-start | bytes 1327112 | tf_op jit(solution)/shard_map/ppermute | solution.py:292
  85.7 1.7 collective-permute-start.4
  87.5 2.0 %collective-permute-done.4.obs_got = f32[3,8,128]{2,1,0:T(8,128)S(1)} collective-permute-done((f32[3,8,128]{2,1,0:T(8,128)S(1)}, f32[3,8,128]{2,1,0:T(8,128)S(1)}, u32[]{:S(2)}, u32[]{:S(2)}) %collective-permute-start.4) | collective-permute-done | bytes 12320 | tf_op jit(solution)/shard_map/ppermute | solution.py:280
  89.5 15.4 %collective-permute-done.7.high = f32[3,8,4608]{2,1,0:T(8,128)S(1)} collective-permute-done((f32[3,8,4608]{2,1,0:T(8,128)}, f32[3,8,4608]{2,1,0:T(8,128)S(1)}, u32[]{:S(2)}, u32[]{:S(2)}) %collective-permute-start.7) | collective-permute-done | bytes 442400 | tf_op jit(solution)/shard_map/ppermute | solution.py:292
  104.9 1.0 copy-done.5
  105.9 29.5 %shard_map.72 = (f32[3,8,4096]{2,1,0:T(8,128)S(1)}, f32[3,8,4096]{2,1,0:T(8,128)}, f32[8,128]{1,0:T(8,128)S(1)}) custom-call(s32[3]{0:T(128)S(1)} %copy-done.6, f32[3,8,4096]{2,1,0:T(8,128)S(1)} %copy-done.3, f32[3,8,4096]{2,1,0:T(8,128)S(1)} %copy-done.5, f32[3,8,4608]{2,1,0:T(8,128)S(1)} %collective-permute-done.6.low, ...), custom_call_target="tpu_custom_call" | custom-call | tf_op jit(solution)/shard_map/pallas_call | solution.py:227
  135.3 1.2 collective-permute-start.9
  137.2 28.9 %shard_map.70 = (f32[3,8,4096]{2,1,0:T(8,128)S(1)}, f32[3,8,4096]{2,1,0:T(8,128)S(1)}, f32[8,128]{1,0:T(8,128)S(1)}) custom-call(s32[3]{0:T(128)S(1)} %copy-done.6, f32[3,8,4096]{2,1,0:T(8,128)S(1)} %copy-done, f32[3,8,4096]{2,1,0:T(8,128)S(1)} %copy-done.2, f32[3,8,4608]{2,1,0:T(8,128)S(1)} %collective-permute-done.2.low, ...), custom_call_target="tpu_custom_call" | custom-call | tf_op jit(solution)/shard_map/pallas_call | solution.py:227
  166.7 1.4 pad_maximum_fusion.5
  168.1 0.9 collective-permute-start.8
  168.9 2.7 %collective-permute-done.10 = f32[2]{0:T(128)S(1)} collective-permute-done((f32[2]{0:T(128)S(1)}, f32[2]{0:T(128)S(1)}, u32[]{:S(2)}, u32[]{:S(2)}) %collective-permute-start.10) | collective-permute-done | bytes 40 | tf_op jit(solution)/shard_map/ppermute | solution.py:300
  171.6 1.4 fusion.6
  173.0 4.4 %collective-permute-done.11 = f32[2]{0:T(128)S(1)} collective-permute-done((f32[2]{0:T(128)S(1)}, f32[2]{0:T(128)S(1)}, u32[]{:S(2)}, u32[]{:S(2)}) %collective-permute-start.11) | collective-permute-done | bytes 40 | tf_op jit(solution)/shard_map/ppermute | solution.py:300
  177.4 1.4 fusion.7
  178.7 0.8 collective-permute-start.12
  179.5 2.7 %collective-permute-done.12 = f32[2]{0:T(128)S(1)} collective-permute-done((f32[2]{0:T(128)S(1)}, f32[2]{0:T(128)S(1)}, u32[]{:S(2)}, u32[]{:S(2)}) %collective-permute-start.12) | collective-permute-done | bytes 40 | tf_op jit(solution)/shard_map/ppermute | solution.py:302
  182.9 1.1 fusion.1
  184.0 1.3 pad_maximum_fusion
  (45 shorter events, 5.6 us)
Async XLA Ops:
  4.9 56.5 %copy-start.8 = (s32[8,128]{1,0:T(8,128)S(1)}, s32[8,128]{1,0:T(8,128)}, u32[]{:S(2)}) copy-start(s32[8,128]{1,0:T(8,128)} %param.8) | copy-start | bytes 12292
  5.0 2.6 %collective-permute-start = (f32[2,3,8,4096]{3,2,1,0:T(8,128)S(1)}, f32[2,3,8,4096]{3,2,1,0:T(8,128)S(1)}, u32[]{:S(2)}, u32[]{:S(2)}) collective-permute-start(f32[2,3,8,4096]{3,2,1,0:T(8,128)S(1)} %pad_maximum_fusion.1), channel_id=1, source_target_pairs={{0,8},{8,0},{1,9},{9,1},{2,10},{10,2},{3,11},{11,3},{4,12},{12,4},... | collective-permute-start | bytes 2359304 | tf_op jit(solution)/shard_map/ppermute | solution.py:269
  7.6 78.1 %copy-start.9 = (f32[8,128]{1,0:T(8,128)S(1)}, f32[8,128]{1,0:T(8,128)}, u32[]{:S(2)}) copy-start(f32[8,128]{1,0:T(8,128)} %param.9) | copy-start | bytes 12292
  7.6 78.2 %copy-start.10 = (f32[8,128]{1,0:T(8,128)S(1)}, f32[8,128]{1,0:T(8,128)}, u32[]{:S(2)}) copy-start(f32[8,128]{1,0:T(8,128)} %param.7) | copy-start | bytes 12292
  7.6 0.9 copy-start.7
  57.9 47.0 %copy-start.3 = (f32[3,8,4096]{2,1,0:T(8,128)S(1)}, f32[3,8,4096]{2,1,0:T(8,128)}, u32[]{:S(2)}) copy-start(f32[3,8,4096]{2,1,0:T(8,128)} %get-tuple-element.21.own_ref.own) | copy-start | bytes 1179652
  57.9 12.8 %collective-permute-start.5 = (f32[3,8,4096]{2,1,0:T(8,128)}, f32[3,8,4096]{2,1,0:T(8,128)S(1)}, u32[]{:S(2)}, u32[]{:S(2)}) collective-permute-start(f32[3,8,4096]{2,1,0:T(8,128)} %get-tuple-element.22), channel_id=1, source_target_pairs={{0,1},{1,0},{2,3},{3,2},{4,5},{5,4},{6,7},{7,6},{8,9},{9,8},{10,11... | collective-permute-start | bytes 1179656 | tf_op jit(solution)/shard_map/ppermute | solution.py:288
  60.7 18.2 %collective-permute-start.1 = (f32[3,8,4096]{2,1,0:T(8,128)}, f32[3,8,4096]{2,1,0:T(8,128)S(1)}, u32[]{:S(2)}, u32[]{:S(2)}) collective-permute-start(f32[3,8,4096]{2,1,0:T(8,128)} %get-tuple-element.17), channel_id=1, source_target_pairs={{0,1},{1,0},{2,3},{3,2},{4,5},{5,4},{6,7},{7,6},{8,9},{9,8},{10,11... | collective-permute-start | bytes 1179656 | tf_op jit(solution)/shard_map/ppermute | solution.py:288
  61.4 43.5 %copy-start.6 = (s32[3]{0:T(128)S(1)}, s32[3]{0:T(128)}, u32[]{:S(2)}) copy-start(s32[3]{0:T(128)} %pad_add_fusion.par_ref.scalars) | copy-start | bytes 40
  70.8 0.8 copy-start.4
  71.5 65.7 %copy-start = (f32[3,8,4096]{2,1,0:T(8,128)S(1)}, f32[3,8,4096]{2,1,0:T(8,128)}, u32[]{:S(2)}) copy-start(f32[3,8,4096]{2,1,0:T(8,128)} %get-tuple-element.16.own_ref.own) | copy-start | bytes 1179652
  73.7 15.7 %collective-permute-start.6 = (f32[3,8,4608]{2,1,0:T(8,128)}, f32[3,8,4608]{2,1,0:T(8,128)S(1)}, u32[]{:S(2)}, u32[]{:S(2)}) collective-permute-start(f32[3,8,4608]{2,1,0:T(8,128)} %get-tuple-element.23), channel_id=1, source_target_pairs={{0,2},{1,3},{2,4},{3,5},{4,6},{5,7},{6,0},{7,1},{8,10},{9,11},{10,... | collective-permute-start | bytes 1327112 | tf_op jit(solution)/shard_map/ppermute | solution.py:291
  75.8 29.0 %collective-permute-start.7 = (f32[3,8,4608]{2,1,0:T(8,128)}, f32[3,8,4608]{2,1,0:T(8,128)S(1)}, u32[]{:S(2)}, u32[]{:S(2)}) collective-permute-start(f32[3,8,4608]{2,1,0:T(8,128)} %get-tuple-element.24), channel_id=1, source_target_pairs={{2,0},{3,1},{4,2},{5,3},{6,4},{7,5},{0,6},{1,7},{10,8},{11,9},{12,... | collective-permute-start | bytes 1327112 | tf_op jit(solution)/shard_map/ppermute | solution.py:292
  78.9 0.7 copy-start.1
  81.8 55.4 %copy-start.2 = (f32[3,8,4096]{2,1,0:T(8,128)S(1)}, f32[3,8,4096]{2,1,0:T(8,128)}, u32[]{:S(2)}) copy-start(f32[3,8,4096]{2,1,0:T(8,128)} %copy-done.1) | copy-start | bytes 1179652
  81.8 55.4 %collective-permute-start.2 = (f32[3,8,4608]{2,1,0:T(8,128)}, f32[3,8,4608]{2,1,0:T(8,128)S(1)}, u32[]{:S(2)}, u32[]{:S(2)}) collective-permute-start(f32[3,8,4608]{2,1,0:T(8,128)} %get-tuple-element.18), channel_id=1, source_target_pairs={{0,2},{1,3},{2,4},{3,5},{4,6},{5,7},{6,0},{7,1},{8,10},{9,11},{10,... | collective-permute-start | bytes 1327112 | tf_op jit(solution)/shard_map/ppermute | solution.py:291
  83.6 53.6 %collective-permute-start.3 = (f32[3,8,4608]{2,1,0:T(8,128)}, f32[3,8,4608]{2,1,0:T(8,128)S(1)}, u32[]{:S(2)}, u32[]{:S(2)}) collective-permute-start(f32[3,8,4608]{2,1,0:T(8,128)} %get-tuple-element.19), channel_id=1, source_target_pairs={{2,0},{3,1},{4,2},{5,3},{6,4},{7,5},{0,6},{1,7},{10,8},{11,9},{12,... | collective-permute-start | bytes 1327112 | tf_op jit(solution)/shard_map/ppermute | solution.py:292
  85.7 3.7 %collective-permute-start.4 = (f32[3,8,128]{2,1,0:T(8,128)S(1)}, f32[3,8,128]{2,1,0:T(8,128)S(1)}, u32[]{:S(2)}, u32[]{:S(2)}) collective-permute-start(f32[3,8,128]{2,1,0:T(8,128)S(1)} %pad_maximum_fusion.4.obs_own), channel_id=1, source_target_pairs={{0,1},{1,0},{2,3},{3,2},{4,5},{5,4},{6,7},{7,6},{8,9},{9,8},{10,11... | collective-permute-start | bytes 36872 | tf_op jit(solution)/shard_map/ppermute | solution.py:280
  104.9 1.0 copy-start.5
  135.3 47.5 %collective-permute-start.9 = (f32[3,8,4096]{2,1,0:T(8,128)}, f32[3,8,4096]{2,1,0:T(8,128)}, u32[]{:S(2)}, u32[]{:S(2)}) collective-permute-start(f32[3,8,4096]{2,1,0:T(8,128)} %get-tuple-element.27), channel_id=1, source_target_pairs={{0,1},{1,0},{2,3},{3,2},{4,5},{5,4},{6,7},{7,6},{8,9},{9,8},{10,11... | collective-permute-start | bytes 1179656 | tf_op jit(solution)/shard_map/ppermute | solution.py:295
  168.0 3.5 %collective-permute-start.10 = (f32[2]{0:T(128)S(1)}, f32[2]{0:T(128)S(1)}, u32[]{:S(2)}, u32[]{:S(2)}) collective-permute-start(f32[2]{0:T(128)S(1)} %pad_maximum_fusion.5), channel_id=1, source_target_pairs={{0,2},{1,3},{2,0},{3,1},{4,6},{5,7},{6,4},{7,5},{8,10},{9,11},{10,... | collective-permute-start | bytes 32 | tf_op jit(solution)/shard_map/ppermute | solution.py:300
  168.1 14.8 %collective-permute-start.8 = (f32[3,8,4096]{2,1,0:T(8,128)S(1)}, f32[3,8,4096]{2,1,0:T(8,128)S(1)}, u32[]{:S(2)}, u32[]{:S(2)}) collective-permute-start(f32[3,8,4096]{2,1,0:T(8,128)S(1)} %get-tuple-element.26), channel_id=1, source_target_pairs={{0,1},{1,0},{2,3},{3,2},{4,5},{5,4},{6,7},{7,6},{8,9},{9,8},{10,11... | collective-permute-start | bytes 1179656 | tf_op jit(solution)/shard_map/ppermute | solution.py:295
  172.9 4.4 %collective-permute-start.11 = (f32[2]{0:T(128)S(1)}, f32[2]{0:T(128)S(1)}, u32[]{:S(2)}, u32[]{:S(2)}) collective-permute-start(f32[2]{0:T(128)S(1)} %fusion.6), channel_id=1, source_target_pairs={{0,4},{1,5},{2,6},{3,7},{4,0},{5,1},{6,2},{7,3},{8,12},{9,13},{10,... | collective-permute-start | bytes 32 | tf_op jit(solution)/shard_map/ppermute | solution.py:300
  178.7 3.5 %collective-permute-start.12 = (f32[2]{0:T(128)S(1)}, f32[2]{0:T(128)S(1)}, u32[]{:S(2)}, u32[]{:S(2)}) collective-permute-start(f32[2]{0:T(128)S(1)} %fusion.7), channel_id=1, source_target_pairs={{0,1},{1,0},{2,3},{3,2},{4,5},{5,4},{6,7},{7,6},{8,9},{9,8},{10,11... | collective-permute-start | bytes 32 | tf_op jit(solution)/shard_map/ppermute | solution.py:302

commit v2 on v0

v2 whole, which is shorter than its diff:
```python
import functools

import jax
import jax.numpy as jnp
from jax import lax
from jax.experimental import pallas as pl
from jax.experimental.pallas import tpu as pltpu
from jax.sharding import PartitionSpec as P

STEPS = 3
DT = 0.4
HALF = 0.5 * DT
DEPTH = 3 * STEPS
LANES = 128
TILE = 8
BASE = 16
ROWS = 48

VMEM = pl.BlockSpec(memory_space=pltpu.VMEM)
SMEM = pl.BlockSpec(memory_space=pltpu.SMEM)


def cost(us):
    return pl.CostEstimate(flops=0, bytes_accessed=int(us * 3.0e6), transcendentals=0)


def halves(ncol):
    cut = ncol // 2 + 2
    return (
        (list(range(cut)), list(range(cut)), list(range(1, cut - 1))),
        (
            list(range(cut, ncol)),
            list(range(cut - 2, ncol)) + [0, 1],
            list(range(cut - 1, ncol)) + [0],
        ),
    )


def at(i):
    return slice(i * LANES, (i + 1) * LANES)


def leave_kernel(offspring, ensemble, leaving, index):
    members = ensemble.shape[0]
    total = offspring.shape[0]
    here = lax.axis_index("particle")
    cumulative = []
    for i in range(total):
        cumulative.append(offspring[i] + (cumulative[-1] if i else 0))

    def source(j):
        return sum((c <= j).astype(jnp.int32) for c in cumulative)

    def span(side):
        base = side * members
        low, high = jnp.int32(members), jnp.int32(-1)
        for k in range(members):
            s = source((1 - side) * members + k) - base
            mine = (s >= 0) & (s < members)
            low = jnp.minimum(low, jnp.where(mine, s, members))
            high = jnp.maximum(high, jnp.where(mine, s, -1))
        return jnp.clip(low, 0, members - 1), jnp.clip(high, 0, members - 1)

    low, high = span(here)
    leaving[0] = ensemble[low]
    leaving[1] = ensemble[high]
    there, _ = span(1 - here)
    for k in range(members):
        s = source(here * members + k)
        own = s - here * members
        other = s - (1 - here) * members
        inside = (own >= 0) & (own < members)
        index[k] = jnp.where(inside, own, jnp.where(other == there, members, members + 1))


def leave(offspring, ensemble):
    return pl.pallas_call(
        leave_kernel,
        out_shape=[
            jax.ShapeDtypeStruct((2,) + ensemble.shape[1:], ensemble.dtype),
            jax.ShapeDtypeStruct((ensemble.shape[0],), jnp.int32),
        ],
        in_specs=[SMEM, VMEM],
        out_specs=[VMEM, SMEM],
    )(offspring, ensemble)


def pick_kernel(index, own, other, *outs, parts):
    members = own.shape[0]
    half = members // 2
    par = lax.axis_index("strip") % 2
    kept, given = outs[:half], outs[half:]

    def copy(slot, write):
        i = index[slot]

        @pl.when(i < members)
        def _():
            write(own, jnp.minimum(i, members - 1))

        @pl.when(i >= members)
        def _():
            write(other, jnp.maximum(i - members, 0))

    for k in range(half):

        def whole(ref, i):
            kept[k][...] = ref[i]

        def split(ref, i):
            for p, (first, count) in enumerate(parts):
                given[k * len(parts) + p][...] = ref[i, :, :, pl.ds(first, count)]

        copy((1 - par) * half + k, split)
        copy(par * half + k, whole)


def pick(index, own, other, parts):
    half = own.shape[0] // 2
    whole = jax.ShapeDtypeStruct(own.shape[1:], own.dtype)
    pieces = [jax.ShapeDtypeStruct(own.shape[1:3] + (c,), own.dtype) for _, c in parts]
    outs = [whole] * half + pieces * half
    got = pl.pallas_call(
        functools.partial(pick_kernel, parts=parts),
        out_shape=outs,
        in_specs=[SMEM, VMEM, VMEM],
        out_specs=[VMEM] * len(outs),
    )(index, own, other)
    return got[:half], [got[half + k * len(parts) : half + (k + 1) * len(parts)] for k in range(half)]


def pack_kernel(own_ref, got_ref, up_ref, down_ref, *, sent):
    par = lax.axis_index("strip") % 2
    count = len(sent)
    wide = count * LANES
    per = -(-count // TILE)
    first = sent[0] * LANES
    own = own_ref.at[:, :, pl.ds(first, wide)]

    def fill(top, bottom):
        up_ref[:, :, :wide] = bottom[...]
        down_ref[:, :, :wide] = top[...]
        for i in range(count):
            q, lanes = i // per, slice(wide + (i % per) * LANES, wide + (i % per + 1) * LANES)
            up_ref[:, q : q + 1, lanes] = top[:, TILE - 1 : TILE, at(i)]
            down_ref[:, q : q + 1, lanes] = bottom[:, 0:1, at(i)]

    @pl.when(par == 0)
    def _():
        fill(own, got_ref)

    @pl.when(par == 1)
    def _():
        fill(got_ref, own)


def pack(own, got, sent):
    per = -(-len(sent) // TILE)
    message = jax.ShapeDtypeStruct((3, TILE, (len(sent) + per) * LANES), own.dtype)
    return pl.pallas_call(
        functools.partial(pack_kernel, sent=sent),
        out_shape=[message, message],
        in_specs=[VMEM, VMEM],
        out_specs=[VMEM, VMEM],
        cost_estimate=cost(1.5),
    )(own, got)


def evaluate(src, state, dst, cor_ref, start, tiles, kind):
    ncol = src.shape[1]
    lane = lax.broadcasted_iota(jnp.int32, (TILE, LANES), 1)
    first = lane == 0
    last = lane == LANES - 1

    def body(t, carry):
        r0 = start + t * TILE
        rows = pl.ds(r0, TILE)
        cor = cor_ref[rows, :]
        for ct in range(ncol):
            mid, around = [], []
            for f in range(3):
                c = src[f, ct, rows, :]
                e = pltpu.roll(
                    jnp.where(first, src[f, (ct + 1) % ncol, rows, :], c), LANES - 1, 1
                )
                w = pltpu.roll(jnp.where(last, src[f, (ct - 1) % ncol, rows, :], c), 1, 1)
                n = src[f, ct, pl.ds(r0 + 1, TILE), :]
                s = src[f, ct, pl.ds(r0 - 1, TILE), :]
                mid.append(c)
                around.append((e, w, n, s))
            eta, u, v = mid
            (eE, eW, eN, eS), (uE, uW, uN, uS), (vE, vW, vN, vS) = around
            duy = uN - uS
            dvx = vE - vW
            dux = uE - uW
            dvy = vN - vS
            flow = (dux + dvy) + ((eE * uE - eW * uW) + (eN * vN - eS * vS))
            lu = v * (cor - duy) - u * dux - (eE - eW)
            lv = u * (cor + dvx) + v * dvy + (eN - eS)
            change = (-flow, lu, -lv)
            for f in range(3):
                if kind == 0:
                    new = mid[f] + HALF * change[f]
                elif kind == 1:
                    new = 0.75 * state[f, ct, rows, :] + (0.25 * mid[f] + (0.25 * HALF) * change[f])
                else:
                    new = (1.0 / 3.0) * state[f, ct, rows, :] + (
                        (2.0 / 3.0) * mid[f] + (2.0 / 3.0 * HALF) * change[f]
                    )
                dst[f, ct, rows, :] = new
        return carry

    lax.fori_loop(0, tiles, body, 0)


def forecast_kernel(*refs, worked, kept, ncol, place, total_rows, slot, slots):
    parts = max(p for p, _ in place) + 1
    own, refs = refs[0], refs[1:]
    got, low, high = refs[:parts], refs[parts : 2 * parts], refs[2 * parts : 3 * parts]
    obs_own, obs_got, keep, send, misfit, state, s1, s2, cor_ref = refs[3 * parts :]
    strip = lax.axis_index("strip")
    par = strip % 2

    def load(own_row, got_row):
        for i, ct in enumerate(worked):
            p, j = place[i]
            state[:, i, own_row : own_row + TILE, :] = own[:, :, at(ct)]
            state[:, i, got_row : got_row + TILE, :] = got[p][:, :, at(j)]

    @pl.when(par == 0)
    def _():
        load(BASE, BASE + TILE)

    @pl.when(par == 1)
    def _():
        load(BASE + TILE, BASE)

    for i in range(len(worked)):
        p, j = place[i]
        state[:, i, BASE - TILE : BASE, :] = low[p][:, :, at(j)]
        state[:, i, BASE + 2 * TILE : BASE + 3 * TILE, :] = high[p][:, :, at(j)]
        count = got[p].shape[2] // LANES
        per = -(-count // TILE)
        q, lanes = j // per, at(count + j % per)
        state[:, i, BASE - TILE - 1 : BASE - TILE, :] = low[p][:, q : q + 1, lanes]
        state[:, i, BASE + 3 * TILE : BASE + 3 * TILE + 1, :] = high[p][:, q : q + 1, lanes]

    row = lax.broadcasted_iota(jnp.int32, (ROWS, LANES), 0) + ((strip - par) * TILE - BASE)
    row = jnp.where(row < 0, row + total_rows, row)
    row = jnp.where(row >= total_rows, row - total_rows, row).astype(jnp.float32)
    cor_ref[...] = 2.0 * (0.3 + 0.4 * ((row + 0.5) / total_rows - 0.5))

    for k in range(DEPTH):
        reach = DEPTH - 1 - k
        tiles = (2 * TILE + 2 * reach + TILE - 1) // TILE
        kind = k % 3
        src, dst = ((state, s1), (s1, s2), (s2, state))[kind]
        evaluate(src, state, dst, cor_ref, BASE - reach, tiles, kind)

    def store(keep_row, send_row):
        for j, ct in enumerate(kept):
            i = worked.index(ct)
            keep[:, :, at(j)] = state[:, i, keep_row : keep_row + TILE, :]
            send[:, :, at(j)] = state[:, i, send_row : send_row + TILE, :]

    @pl.when(par == 0)
    def _():
        store(BASE, BASE + TILE)

    @pl.when(par == 1)
    def _():
        store(BASE + TILE, BASE)

    total = jnp.zeros((TILE, LANES), jnp.float32)
    for side in range(2):
        mine = par == side
        obs = [jnp.where(mine, obs_own[k], obs_got[k]) for k in range(3)]
        where = obs[1].astype(jnp.int32)
        tile, lane = where // LANES, where % LANES
        picked = jnp.zeros((TILE, LANES), jnp.float32)
        here = jnp.zeros((TILE, LANES), jnp.bool_)
        for ct in kept:
            i = worked.index(ct)
            eta = state[0, i, BASE + side * TILE : BASE + (side + 1) * TILE, :]
            found = tile == ct
            picked = jnp.where(found, jnp.take_along_axis(eta, lane, axis=1), picked)
            here = here | found
        gap = obs[0] - picked
        total = total + jnp.where(here, obs[2] * gap * gap, 0.0)
    at_slot = lax.broadcasted_iota(jnp.int32, (TILE, LANES), 0) == par * (slots // 2) + slot
    misfit[...] = jnp.where(at_slot, jnp.sum(total), 0.0)


def forecast(own, got, low, high, obs_own, obs_got, piece, ncol, slot, slots, total_rows):
    parts = halves(ncol)
    sent, worked, kept = parts[piece]
    place = []
    for ct in worked:
        p = 0 if ct in parts[0][0] else 1
        place.append((p, parts[p][0].index(ct)))
    block = jax.ShapeDtypeStruct((3, TILE, len(kept) * LANES), own.dtype)
    field = pltpu.VMEM((3, len(worked), ROWS, LANES), jnp.float32)
    args = [own, *got, *low, *high, obs_own, obs_got]
    return pl.pallas_call(
        functools.partial(
            forecast_kernel,
            worked=worked,
            kept=kept,
            ncol=ncol,
            place=place,
            total_rows=total_rows,
            slot=slot,
            slots=slots,
        ),
        out_shape=[block, block, jax.ShapeDtypeStruct((TILE, LANES), jnp.float32)],
        in_specs=[VMEM] * len(args),
        out_specs=[VMEM] * 3,
        scratch_shapes=[field, field, field, pltpu.VMEM((ROWS, LANES), jnp.float32)],
        compiler_params=pltpu.CompilerParams(vmem_limit_bytes=24 * 2**20),
        cost_estimate=cost(7.0),
    )(*args)


def gather_kernel(*refs, ncol):
    out = refs[-1]
    parts = halves(ncol)
    half = out.shape[0] // 2
    par = lax.axis_index("strip") % 2
    n = len(parts)
    for k in range(half):
        for p, (_, _, kept) in enumerate(parts):
            mine, theirs = refs[k * n + p], refs[half * n + k * n + p]
            for j, ct in enumerate(kept):
                out[par * half + k, :, :, at(ct)] = mine[:, :, at(j)]
                out[(1 - par) * half + k, :, :, at(ct)] = theirs[:, :, at(j)]


def gather(keeps, backs, ncol):
    pieces = [x for k in keeps for x in k] + [x for k in backs for x in k]
    return pl.pallas_call(
        functools.partial(gather_kernel, ncol=ncol),
        out_shape=jax.ShapeDtypeStruct((2 * len(keeps), 3, TILE, ncol * LANES), jnp.float32),
        in_specs=[VMEM] * len(pieces),
        out_specs=VMEM,
    )(*pieces)


def local(ensemble, offspring, observations, obs_cols, obs_precision):
    members, _, strip_rows, cols = ensemble.shape
    strips = lax.axis_size("strip")
    total_rows = strips * strip_rows
    strip = lax.axis_index("strip")
    half = members // 2
    ncol = cols // LANES
    parts = halves(ncol)
    swap = [(i, i ^ 1) for i in range(strips)]
    up = [(i, (i + 2) % strips) for i in range(strips)]
    down = [(b, a) for a, b in up]

    leaving, index = leave(offspring, ensemble)
    arrived = lax.ppermute(leaving, "particle", [(0, 1), (1, 0)])
    spans = [(sent[0] * LANES, len(sent) * LANES) for sent, _, _ in parts]
    kept, given = pick(index, ensemble, arrived, spans)

    got = [[lax.ppermute(g, "strip", swap) for g in slot] for slot in given]

    rows = (strip * strip_rows + jnp.arange(strip_rows, dtype=jnp.int32)).astype(jnp.float32)
    weight = obs_precision * (1.0 + 2.0 * (rows + 0.5) / total_rows)[:, None]
    obs_own = jnp.stack([observations, obs_cols.astype(jnp.float32), weight])
    obs_got = lax.ppermute(obs_own, "strip", swap)

    keeps, backs, total = [], [], None
    for k in range(half):
        low, high = [], []
        keeps.append([])
        backs.append([])
        for p, (sent, _, _) in enumerate(parts):
            rising, falling = pack(kept[k], got[k][p], sent)
            low.append(lax.ppermute(rising, "strip", up))
            high.append(lax.ppermute(falling, "strip", down))
            keep, send, misfit = forecast(
                kept[k], got[k][: p + 1], low, high, obs_own, obs_got, p, ncol, k, members, total_rows
            )
            keeps[k].append(keep)
            backs[k].append(lax.ppermute(send, "strip", swap))
            total = misfit if total is None else total + misfit
    step = 1
    while step < strips:
        total = total + lax.ppermute(total, "strip", [(i, i ^ step) for i in range(strips)])
        step *= 2
    state = gather(keeps, backs, ncol)
    log_weights = (-0.5 / (total_rows * obs_cols.shape[1])) * total[:members, 0]
    return (state, log_weights)


def solution(mesh):
    in_specs = (
        P(("group", "particle"), None, "strip", None),
        P("group"),
        P(("group", "strip"), None),
        P(("group", "strip"), None),
        P(("group", "strip"), None),
    )
    out_specs = (P(("group", "particle"), None, "strip", None), P(("group", "particle")))
    return jax.shard_map(local, mesh=mesh, in_specs=in_specs, out_specs=out_specs, check_vma=False)
```

time: 227 us -> 97.4 us (0.43)
  waiting for transfers between devices: 77.2 us -> 16.3 us
  local copies, waits for them, and re-layouts: 50.8 us -> 5.69 us
  Pallas kernels: 0 us -> 39.9 us
  other arithmetic: 21.5 us -> 0.73 us
  blocking collectives: 19.7 us -> 0 us
  between operations: 14.9 us -> 0.86 us
  starting transfers between devices: 43 us -> 33.7 us
    ppermute x18 -> x21, waiting for transfers between devices: 61 us -> 16.3 us  [the longest x3 8.48 us: local(): lax.ppermute(total, 'strip', [(i, i ^ step) for i in range(strips)])]
    pallas_call x0 -> x11, Pallas kernels: none -> 39.9 us  [the longest x4 24.2 us: forecast(): pl.pallas_call(functools.partial(forecast_kernel, worked=worked, kept=kep...]
    gather x3 -> x0, local copies, waits for them, and re-layouts: 35.2 us -> none  [the longest x1 32 us: local(): picked = jnp.take_along_axis(eta, index, axis=-1)]
    psum x1 -> x0, blocking collectives: 19.7 us -> none  [local(): total = lax.psum(partial_sum, 'strip')]
    all_gather x1 -> x0, waiting for transfers between devices: 15.5 us -> none  [local(): everyone = lax.all_gather(ensemble, 'particle', axis=0, tiled=True)]
    slice x78 -> x0, local copies, waits for them, and re-layouts: 12.8 us -> none  [the longest x70 10 us: along_x(): return 0.5 * (jnp.roll(inner, -1, axis=-1) - jnp.roll(inner, 1, axis=-1))]
    another operation x28 -> x3, other arithmetic: 10.2 us -> 0.08 us  [local(): obs_own = jnp.stack([observations, obs_cols.astype(jnp.float32), weight])]
    ppermute x18 -> x21, starting transfers between devices: 42.9 us -> 33.7 us  [the longest x4 10.3 us: local(): high.append(lax.ppermute(falling, 'strip', down))]
  transfers between devices with their start and end apart: 19 -> 21, of which waited for: 19 -> 8; matrix products, arithmetic and copies ran while one was open for 0% -> 1% of each run, Pallas kernels for 0% -> 33%
where the time goes in v2:
time: 97.4 us; the launch traced here: 97.1 us
  Pallas kernels  39.9 us (41%)
  starting transfers between devices  33.7 us (35%)
  waiting for transfers between devices  16.3 us (17%)
  local copies, waits for them, and re-layouts  5.69 us (6%)
    pallas_call x4, Pallas kernels, forecast(): pl.pallas_call(functools.partial(forecast_kernel, worked=worked, kept=kep...  24.2 us
    ppermute x4, starting transfers between devices, local(): high.append(lax.ppermute(falling, 'strip', down))  10.3 us
    ppermute x3, waiting for transfers between devices, local(): lax.ppermute(total, 'strip', [(i, i ^ step) for i in range(strips)])  8.48 us
    pallas_call x4, Pallas kernels, pack(): pl.pallas_call(functools.partial(pack_kernel, sent=sent), out_shape=[mess...  7.56 us
    unnamed x44, local copies, waits for them, and re-layouts  5.69 us
    ppermute x3, starting transfers between devices, local(): lax.ppermute(total, 'strip', [(i, i ^ step) for i in range(strips)])  5.64 us
    ppermute x4, starting transfers between devices, local(): low.append(lax.ppermute(rising, 'strip', up))  5.64 us
    ppermute x4, starting transfers between devices, local(): backs[k].append(lax.ppermute(send, 'strip', swap))  5.01 us
  transfers between devices with their start and end apart: 21, of which 8 were waited for; matrix products, arithmetic and copies ran while one was open for 1% of the time, Pallas kernels for 33%

profile of v2, /device:TPU:0, one launch (start us, length us, event | category | flops | bytes accessed | tf_op | source)
XLA Modules:
  0.0 97.1 jit_solution(5845314075990618745)
XLA Ops:
  0.6 2.4 %shard_map.68 = (f32[2,3,8,4096]{3,2,1,0:T(8,128)}, s32[4]{0:T(128)}) custom-call(s32[8]{0:T(128)} %offspring.1, f32[4,3,8,4096]{3,2,1,0:T(8,128)} %own.1), custom_call_target="tpu_custom_call" | custom-call | tf_op jit(solution)/shard_map/pallas_call | solution.py:77
  3.7 2.0 %collective-permute-done.other = f32[2,3,8,4096]{3,2,1,0:T(8,128)S(1)} collective-permute-done((f32[2,3,8,4096]{3,2,1,0:T(8,128)}, f32[2,3,8,4096]{3,2,1,0:T(8,128)S(1)}, u32[]{:S(2)}, u32[]{:S(2)}) %collective-permute-start) | collective-permute-done | bytes 786464 | tf_op jit(solution)/shard_map/ppermute | solution.py:361
  6.6 3.0 %shard_map.69 = (f32[3,8,4096]{2,1,0:T(8,128)}, f32[3,8,4096]{2,1,0:T(8,128)}, f32[3,8,2304]{2,1,0:T(8,128)}, f32[3,8,1792]{2,1,0:T(8,128)}, f32[3,8,2304]{2,1,0:T(8,128)}, /*index=5*/f32[3,8,1792]{2,1,0:T(8,128)}) custom-call(s32[4]{0:T(128)} %get-tuple-element.30.index, f32[4,3,8,4096]{3,2,1,0:T(8,128)} %own.1, f32[2,3,8,4096]{3,2,1,0:T(8,128)} %copy-done.14), custom_call_target="tpu_custom_call" | custom-call | tf_op jit(solution)/shard_map/pallas_call | solution.py:123
  9.6 2.9 %collective-permute-start.11 = (f32[3,8,1792]{2,1,0:T(8,128)}, f32[3,8,1792]{2,1,0:T(8,128)S(1)}, u32[]{:S(2)}, u32[]{:S(2)}) collective-permute-start(f32[3,8,1792]{2,1,0:T(8,128)} %get-tuple-element.46), channel_id=1, source_target_pairs={{0,1},{1,0},{2,3},{3,2},{4,5},{5,4},{6,7},{7,6},{8,9},{9,8},{10,11... | collective-permute-start | bytes 516104 | tf_op jit(solution)/shard_map/ppermute | solution.py:365
  12.5 2.0 %collective-permute-start.5 = (f32[3,8,1792]{2,1,0:T(8,128)}, f32[3,8,1792]{2,1,0:T(8,128)S(1)}, u32[]{:S(2)}, u32[]{:S(2)}) collective-permute-start(f32[3,8,1792]{2,1,0:T(8,128)} %get-tuple-element.37), channel_id=1, source_target_pairs={{0,1},{1,0},{2,3},{3,2},{4,5},{5,4},{6,7},{7,6},{8,9},{9,8},{10,11... | collective-permute-start | bytes 516104 | tf_op jit(solution)/shard_map/ppermute | solution.py:365
  14.6 3.3 %collective-permute-done.11.got_ref.refs_2_ = f32[3,8,1792]{2,1,0:T(8,128)S(1)} collective-permute-done((f32[3,8,1792]{2,1,0:T(8,128)}, f32[3,8,1792]{2,1,0:T(8,128)S(1)}, u32[]{:S(2)}, u32[]{:S(2)}) %collective-permute-start.11) | collective-permute-done | bytes 172064 | tf_op jit(solution)/shard_map/ppermute | solution.py:365
  18.5 1.9 %shard_map.76 = (f32[3,8,2048]{2,1,0:T(8,128)}, f32[3,8,2048]{2,1,0:T(8,128)}) custom-call(f32[3,8,4096]{2,1,0:T(8,128)} %get-tuple-element.41.own_ref.refs_0_, f32[3,8,1792]{2,1,0:T(8,128)} %copy-done.8), custom_call_target="tpu_custom_call" | custom-call | bytes 4500000 | tf_op jit(solution)/shard_map/pallas_call | solution.py:160
  20.4 2.1 %collective-permute-start.12 = (f32[3,8,2048]{2,1,0:T(8,128)}, f32[3,8,2048]{2,1,0:T(8,128)S(1)}, u32[]{:S(2)}, u32[]{:S(2)}) collective-permute-start(f32[3,8,2048]{2,1,0:T(8,128)} %get-tuple-element.47), channel_id=1, source_target_pairs={{0,2},{1,3},{2,4},{3,5},{4,6},{5,7},{6,0},{7,1},{8,10},{9,11},{10,... | collective-permute-start | bytes 589832 | tf_op jit(solution)/shard_map/ppermute | solution.py:379
  23.3 1.9 %shard_map.74 = (f32[3,8,2688]{2,1,0:T(8,128)}, f32[3,8,2688]{2,1,0:T(8,128)}) custom-call(f32[3,8,4096]{2,1,0:T(8,128)} %get-tuple-element.41.own_ref.refs_0_, f32[3,8,2304]{2,1,0:T(8,128)} %copy-done.4), custom_call_target="tpu_custom_call" | custom-call | bytes 4500000 | tf_op jit(solution)/shard_map/pallas_call | solution.py:160
  25.2 2.1 %collective-permute-start.9 = (f32[3,8,2688]{2,1,0:T(8,128)}, f32[3,8,2688]{2,1,0:T(8,128)S(1)}, u32[]{:S(2)}, u32[]{:S(2)}) collective-permute-start(f32[3,8,2688]{2,1,0:T(8,128)} %get-tuple-element.43), channel_id=1, source_target_pairs={{0,2},{1,3},{2,4},{3,5},{4,6},{5,7},{6,0},{7,1},{8,10},{9,11},{10,... | collective-permute-start | bytes 774152 | tf_op jit(solution)/shard_map/ppermute | solution.py:379
  27.3 1.5 %collective-permute-start.4 = (f32[3,8,128]{2,1,0:T(8,128)S(1)}, f32[3,8,128]{2,1,0:T(8,128)S(1)}, u32[]{:S(2)}, u32[]{:S(2)}) collective-permute-start(f32[3,8,128]{2,1,0:T(8,128)S(1)} %pad_maximum_fusion.refs_4_.refs_7_), channel_id=1, source_target_pairs={{0,1},{1,0},{2,3},{3,2},{4,5},{5,4},{6,7},{7,6},{8,9},{9,8},{10,11... | collective-permute-start | bytes 36872 | tf_op jit(solution)/shard_map/ppermute | solution.py:370
  28.9 2.2 %collective-permute-done.4.refs_5_.refs_8_ = f32[3,8,128]{2,1,0:T(8,128)S(1)} collective-permute-done((f32[3,8,128]{2,1,0:T(8,128)S(1)}, f32[3,8,128]{2,1,0:T(8,128)S(1)}, u32[]{:S(2)}, u32[]{:S(2)}) %collective-permute-start.4) | collective-permute-done | bytes 12320 | tf_op jit(solution)/shard_map/ppermute | solution.py:370
  31.0 3.6 %collective-permute-start.13 = (f32[3,8,2048]{2,1,0:T(8,128)}, f32[3,8,2048]{2,1,0:T(8,128)S(1)}, u32[]{:S(2)}, u32[]{:S(2)}) collective-permute-start(f32[3,8,2048]{2,1,0:T(8,128)} %get-tuple-element.48), channel_id=1, source_target_pairs={{2,0},{3,1},{4,2},{5,3},{6,4},{7,5},{0,6},{1,7},{10,8},{11,9},{12,... | collective-permute-start | bytes 589832 | tf_op jit(solution)/shard_map/ppermute | solution.py:380
  35.3 1.9 %shard_map.70 = (f32[3,8,2688]{2,1,0:T(8,128)}, f32[3,8,2688]{2,1,0:T(8,128)}) custom-call(f32[3,8,4096]{2,1,0:T(8,128)} %get-tuple-element.32.own_ref.refs_0_, f32[3,8,2304]{2,1,0:T(8,128)} %copy-done.2), custom_call_target="tpu_custom_call" | custom-call | bytes 4500000 | tf_op jit(solution)/shard_map/pallas_call | solution.py:160
  37.2 1.3 %collective-permute-start.2 = (f32[3,8,2688]{2,1,0:T(8,128)}, f32[3,8,2688]{2,1,0:T(8,128)S(1)}, u32[]{:S(2)}, u32[]{:S(2)}) collective-permute-start(f32[3,8,2688]{2,1,0:T(8,128)} %get-tuple-element.34), channel_id=1, source_target_pairs={{0,2},{1,3},{2,4},{3,5},{4,6},{5,7},{6,0},{7,1},{8,10},{9,11},{10,... | collective-permute-start | bytes 774152 | tf_op jit(solution)/shard_map/ppermute | solution.py:379
  38.6 2.5 %collective-permute-start.3 = (f32[3,8,2688]{2,1,0:T(8,128)}, f32[3,8,2688]{2,1,0:T(8,128)S(1)}, u32[]{:S(2)}, u32[]{:S(2)}) collective-permute-start(f32[3,8,2688]{2,1,0:T(8,128)} %get-tuple-element.35), channel_id=1, source_target_pairs={{2,0},{3,1},{4,2},{5,3},{6,4},{7,5},{0,6},{1,7},{10,8},{11,9},{12,... | collective-permute-start | bytes 774152 | tf_op jit(solution)/shard_map/ppermute | solution.py:380
  41.0 1.9 %shard_map.72 = (f32[3,8,2048]{2,1,0:T(8,128)}, f32[3,8,2048]{2,1,0:T(8,128)}) custom-call(f32[3,8,4096]{2,1,0:T(8,128)} %get-tuple-element.32.own_ref.refs_0_, f32[3,8,1792]{2,1,0:T(8,128)} %copy-done.6), custom_call_target="tpu_custom_call" | custom-call | bytes 4500000 | tf_op jit(solution)/shard_map/pallas_call | solution.py:160
  43.0 3.8 %collective-permute-start.7 = (f32[3,8,2048]{2,1,0:T(8,128)}, f32[3,8,2048]{2,1,0:T(8,128)S(1)}, u32[]{:S(2)}, u32[]{:S(2)}) collective-permute-start(f32[3,8,2048]{2,1,0:T(8,128)} %get-tuple-element.39), channel_id=1, source_target_pairs={{2,0},{3,1},{4,2},{5,3},{6,4},{7,5},{0,6},{1,7},{10,8},{11,9},{12,... | collective-permute-start | bytes 589832 | tf_op jit(solution)/shard_map/ppermute | solution.py:380
  47.7 6.1 %shard_map.77 = (f32[3,8,2048]{2,1,0:T(8,128)S(1)}, f32[3,8,2048]{2,1,0:T(8,128)S(1)}, f32[8,128]{1,0:T(8,128)S(1)}) custom-call(f32[3,8,4096]{2,1,0:T(8,128)S(1)} %copy-done.1, f32[3,8,2304]{2,1,0:T(8,128)S(1)} %copy-done.5, f32[3,8,1792]{2,1,0:T(8,128)S(1)} %copy-done.9, f32[3,8,2688]{2,1,0:T(8,128)S(1)} %collective-permute-done.9.refs_2_.refs_3_, ...), custom_call_target="tpu_custom_call" | custom-call | bytes 21000000 | tf_op jit(solution)/shard_map/pallas_call | solution.py:304
  53.8 1.6 %collective-permute-start.17 = (f32[3,8,2048]{2,1,0:T(8,128)S(1)}, f32[3,8,2048]{2,1,0:T(8,128)S(1)}, u32[]{:S(2)}, u32[]{:S(2)}) collective-permute-start(f32[3,8,2048]{2,1,0:T(8,128)S(1)} %get-tuple-element.53), channel_id=1, source_target_pairs={{0,1},{1,0},{2,3},{3,2},{4,5},{5,4},{6,7},{7,6},{8,9},{9,8},{10,11... | collective-permute-start | bytes 589832 | tf_op jit(solution)/shard_map/ppermute | solution.py:385
  55.4 6.0 %shard_map.75 = (f32[3,8,2048]{2,1,0:T(8,128)S(1)}, f32[3,8,2048]{2,1,0:T(8,128)S(1)}, f32[8,128]{1,0:T(8,128)S(1)}) custom-call(f32[3,8,4096]{2,1,0:T(8,128)S(1)} %copy-done.1, f32[3,8,2304]{2,1,0:T(8,128)S(1)} %copy-done.5, f32[3,8,2688]{2,1,0:T(8,128)S(1)} %collective-permute-done.9.refs_2_.refs_3_, ...), custom_call_target="tpu_custom_call" | custom-call | bytes 21000000 | tf_op jit(solution)/shard_map/pallas_call | solution.py:304
  62.1 1.3 %collective-permute-start.16 = (f32[3,8,2048]{2,1,0:T(8,128)S(1)}, f32[3,8,2048]{2,1,0:T(8,128)S(1)}, u32[]{:S(2)}, u32[]{:S(2)}) collective-permute-start(f32[3,8,2048]{2,1,0:T(8,128)S(1)} %get-tuple-element.52), channel_id=1, source_target_pairs={{0,1},{1,0},{2,3},{3,2},{4,5},{5,4},{6,7},{7,6},{8,9},{9,8},{10,11... | collective-permute-start | bytes 589832 | tf_op jit(solution)/shard_map/ppermute | solution.py:385
  63.7 6.1 %shard_map.73 = (f32[3,8,2048]{2,1,0:T(8,128)S(1)}, f32[3,8,2048]{2,1,0:T(8,128)S(1)}, f32[8,128]{1,0:T(8,128)S(1)}) custom-call(f32[3,8,4096]{2,1,0:T(8,128)S(1)} %copy-done, f32[3,8,2304]{2,1,0:T(8,128)S(1)} %copy-done.3, f32[3,8,1792]{2,1,0:T(8,128)S(1)} %copy-done.7, f32[3,8,2688]{2,1,0:T(8,128)S(1)} %collective-permute-done.2.refs_2_.refs_3_, ...), custom_call_target="tpu_custom_call" | custom-call | bytes 21000000 | tf_op jit(solution)/shard_map/pallas_call | solution.py:304
  69.8 1.5 %collective-permute-start.15 = (f32[3,8,2048]{2,1,0:T(8,128)S(1)}, f32[3,8,2048]{2,1,0:T(8,128)S(1)}, u32[]{:S(2)}, u32[]{:S(2)}) collective-permute-start(f32[3,8,2048]{2,1,0:T(8,128)S(1)} %get-tuple-element.51), channel_id=1, source_target_pairs={{0,1},{1,0},{2,3},{3,2},{4,5},{5,4},{6,7},{7,6},{8,9},{9,8},{10,11... | collective-permute-start | bytes 589832 | tf_op jit(solution)/shard_map/ppermute | solution.py:385
  71.4 6.0 %shard_map.71 = (f32[3,8,2048]{2,1,0:T(8,128)S(1)}, f32[3,8,2048]{2,1,0:T(8,128)S(1)}, f32[8,128]{1,0:T(8,128)S(1)}) custom-call(f32[3,8,4096]{2,1,0:T(8,128)S(1)} %copy-done, f32[3,8,2304]{2,1,0:T(8,128)S(1)} %copy-done.3, f32[3,8,2688]{2,1,0:T(8,128)S(1)} %collective-permute-done.2.refs_2_.refs_3_, ...), custom_call_target="tpu_custom_call" | custom-call | bytes 21000000 | tf_op jit(solution)/shard_map/pallas_call | solution.py:304
  78.7 1.5 %collective-permute-start.18 = (f32[8,128]{1,0:T(8,128)S(1)}, f32[8,128]{1,0:T(8,128)S(1)}, u32[]{:S(2)}, u32[]{:S(2)}) collective-permute-start(f32[8,128]{1,0:T(8,128)S(1)} %add_add_fusion), channel_id=1, source_target_pairs={{0,1},{1,0},{2,3},{3,2},{4,5},{5,4},{6,7},{7,6},{8,9},{9,8},{10,11... | collective-permute-start | bytes 12296 | tf_op jit(solution)/shard_map/ppermute | solution.py:389
  80.2 4.2 %collective-permute-done.18 = f32[8,128]{1,0:T(8,128)S(1)} collective-permute-done((f32[8,128]{1,0:T(8,128)S(1)}, f32[8,128]{1,0:T(8,128)S(1)}, u32[]{:S(2)}, u32[]{:S(2)}) %collective-permute-start.18) | collective-permute-done | bytes 4128 | tf_op jit(solution)/shard_map/ppermute | solution.py:389
  84.4 2.3 %collective-permute-start.19 = (f32[8,128]{1,0:T(8,128)S(1)}, f32[8,128]{1,0:T(8,128)S(1)}, u32[]{:S(2)}, u32[]{:S(2)}) collective-permute-start(f32[8,128]{1,0:T(8,128)S(1)} %add.49), channel_id=1, source_target_pairs={{0,2},{1,3},{2,0},{3,1},{4,6},{5,7},{6,4},{7,5},{8,10},{9,11},{10,... | collective-permute-start | bytes 12296 | tf_op jit(solution)/shard_map/ppermute | solution.py:389
  86.7 1.6 %collective-permute-done.19 = f32[8,128]{1,0:T(8,128)S(1)} collective-permute-done((f32[8,128]{1,0:T(8,128)S(1)}, f32[8,128]{1,0:T(8,128)S(1)}, u32[]{:S(2)}, u32[]{:S(2)}) %collective-permute-start.19) | collective-permute-done | bytes 4128 | tf_op jit(solution)/shard_map/ppermute | solution.py:389
  88.3 1.8 %collective-permute-start.20 = (f32[8,128]{1,0:T(8,128)S(1)}, f32[8,128]{1,0:T(8,128)S(1)}, u32[]{:S(2)}, u32[]{:S(2)}) collective-permute-start(f32[8,128]{1,0:T(8,128)S(1)} %add.50), channel_id=1, source_target_pairs={{0,4},{1,5},{2,6},{3,7},{4,0},{5,1},{6,2},{7,3},{8,12},{9,13},{10,... | collective-permute-start | bytes 12296 | tf_op jit(solution)/shard_map/ppermute | solution.py:389
  90.2 2.7 %collective-permute-done.20 = f32[8,128]{1,0:T(8,128)S(1)} collective-permute-done((f32[8,128]{1,0:T(8,128)S(1)}, f32[8,128]{1,0:T(8,128)S(1)}, u32[]{:S(2)}, u32[]{:S(2)}) %collective-permute-start.20) | collective-permute-done | bytes 4128 | tf_op jit(solution)/shard_map/ppermute | solution.py:389
  94.4 2.7 %shard_map.78 = f32[4,3,8,4096]{3,2,1,0:T(8,128)} custom-call(f32[3,8,2048]{2,1,0:T(8,128)} %copy-done.13, f32[3,8,2048]{2,1,0:T(8,128)} %copy-done.12, f32[3,8,2048]{2,1,0:T(8,128)} %copy-done.11, f32[3,8,2048]{2,1,0:T(8,128)} %copy-done.10, f32[3,8,2048]{2,1,0:T(8,128)} %copy-done.18, f32[3,8,2048]{2,1,0:T(8,128)} %copy-done.17, f32[3,8,2048]{2,1,0:T(8,128)} %copy-done.16, ...), custom_call_target="tpu_custom_call" | custom-call | tf_op jit(solution)/shard_map/pallas_call | solution.py:340
  (74 shorter events, 8.5 us)
Async XLA Ops:
  0.6 3.0 %copy-start.19 = (f32[8,128]{1,0:T(8,128)S(1)}, f32[8,128]{1,0:T(8,128)}, u32[]{:S(2)}) copy-start(f32[8,128]{1,0:T(8,128)} %param.9) | copy-start | bytes 12292
  3.1 9.5 %copy-start.20 = (s32[8,128]{1,0:T(8,128)S(1)}, s32[8,128]{1,0:T(8,128)}, u32[]{:S(2)}) copy-start(s32[8,128]{1,0:T(8,128)} %param.8) | copy-start | bytes 12292
  3.1 2.6 %collective-permute-start = (f32[2,3,8,4096]{3,2,1,0:T(8,128)}, f32[2,3,8,4096]{3,2,1,0:T(8,128)S(1)}, u32[]{:S(2)}, u32[]{:S(2)}) collective-permute-start(f32[2,3,8,4096]{3,2,1,0:T(8,128)} %get-tuple-element.31), channel_id=1, source_target_pairs={{0,8},{8,0},{1,9},{9,1},{2,10},{10,2},{3,11},{11,3},{4,12},{12,4},... | collective-permute-start | bytes 2359304 | tf_op jit(solution)/shard_map/ppermute | solution.py:361
  6.6 20.7 %copy-start.21 = (f32[8,128]{1,0:T(8,128)S(1)}, f32[8,128]{1,0:T(8,128)}, u32[]{:S(2)}) copy-start(f32[8,128]{1,0:T(8,128)} %param.7) | copy-start | bytes 12292
  9.6 37.2 %copy-start.1 = (f32[3,8,4096]{2,1,0:T(8,128)S(1)}, f32[3,8,4096]{2,1,0:T(8,128)}, u32[]{:S(2)}) copy-start(f32[3,8,4096]{2,1,0:T(8,128)} %get-tuple-element.41.own_ref.refs_0_) | copy-start | bytes 1179652
  9.6 8.3 %collective-permute-start.11 = (f32[3,8,1792]{2,1,0:T(8,128)}, f32[3,8,1792]{2,1,0:T(8,128)S(1)}, u32[]{:S(2)}, u32[]{:S(2)}) collective-permute-start(f32[3,8,1792]{2,1,0:T(8,128)} %get-tuple-element.46), channel_id=1, source_target_pairs={{0,1},{1,0},{2,3},{3,2},{4,5},{5,4},{6,7},{7,6},{8,9},{9,8},{10,11... | collective-permute-start | bytes 516104 | tf_op jit(solution)/shard_map/ppermute | solution.py:365
  12.5 10.1 %collective-permute-start.8 = (f32[3,8,2304]{2,1,0:T(8,128)}, f32[3,8,2304]{2,1,0:T(8,128)S(1)}, u32[]{:S(2)}, u32[]{:S(2)}) collective-permute-start(f32[3,8,2304]{2,1,0:T(8,128)} %get-tuple-element.42), channel_id=1, source_target_pairs={{0,1},{1,0},{2,3},{3,2},{4,5},{5,4},{6,7},{7,6},{8,9},{9,8},{10,11... | collective-permute-start | bytes 663560 | tf_op jit(solution)/shard_map/ppermute | solution.py:365
  12.5 24.7 %collective-permute-start.5 = (f32[3,8,1792]{2,1,0:T(8,128)}, f32[3,8,1792]{2,1,0:T(8,128)S(1)}, u32[]{:S(2)}, u32[]{:S(2)}) collective-permute-start(f32[3,8,1792]{2,1,0:T(8,128)} %get-tuple-element.37), channel_id=1, source_target_pairs={{0,1},{1,0},{2,3},{3,2},{4,5},{5,4},{6,7},{7,6},{8,9},{9,8},{10,11... | collective-permute-start | bytes 516104 | tf_op jit(solution)/shard_map/ppermute | solution.py:365
  14.5 20.1 %collective-permute-start.1 = (f32[3,8,2304]{2,1,0:T(8,128)}, f32[3,8,2304]{2,1,0:T(8,128)S(1)}, u32[]{:S(2)}, u32[]{:S(2)}) collective-permute-start(f32[3,8,2304]{2,1,0:T(8,128)} %get-tuple-element.33), channel_id=1, source_target_pairs={{0,1},{1,0},{2,3},{3,2},{4,5},{5,4},{6,7},{7,6},{8,9},{9,8},{10,11... | collective-permute-start | bytes 663560 | tf_op jit(solution)/shard_map/ppermute | solution.py:365
  20.4 26.4 %copy-start.9 = (f32[3,8,1792]{2,1,0:T(8,128)S(1)}, f32[3,8,1792]{2,1,0:T(8,128)}, u32[]{:S(2)}) copy-start(f32[3,8,1792]{2,1,0:T(8,128)} %copy-done.8) | copy-start | bytes 516100
  20.4 18.2 %collective-permute-start.12 = (f32[3,8,2048]{2,1,0:T(8,128)}, f32[3,8,2048]{2,1,0:T(8,128)S(1)}, u32[]{:S(2)}, u32[]{:S(2)}) collective-permute-start(f32[3,8,2048]{2,1,0:T(8,128)} %get-tuple-element.47), channel_id=1, source_target_pairs={{0,2},{1,3},{2,4},{3,5},{4,6},{5,7},{6,0},{7,1},{8,10},{9,11},{10,... | collective-permute-start | bytes 589832 | tf_op jit(solution)/shard_map/ppermute | solution.py:379
  25.2 17.8 %collective-permute-start.9 = (f32[3,8,2688]{2,1,0:T(8,128)}, f32[3,8,2688]{2,1,0:T(8,128)S(1)}, u32[]{:S(2)}, u32[]{:S(2)}) collective-permute-start(f32[3,8,2688]{2,1,0:T(8,128)} %get-tuple-element.43), channel_id=1, source_target_pairs={{0,2},{1,3},{2,4},{3,5},{4,6},{5,7},{6,0},{7,1},{8,10},{9,11},{10,... | collective-permute-start | bytes 774152 | tf_op jit(solution)/shard_map/ppermute | solution.py:379
  27.3 3.7 %collective-permute-start.4 = (f32[3,8,128]{2,1,0:T(8,128)S(1)}, f32[3,8,128]{2,1,0:T(8,128)S(1)}, u32[]{:S(2)}, u32[]{:S(2)}) collective-permute-start(f32[3,8,128]{2,1,0:T(8,128)S(1)} %pad_maximum_fusion.refs_4_.refs_7_), channel_id=1, source_target_pairs={{0,1},{1,0},{2,3},{3,2},{4,5},{5,4},{6,7},{7,6},{8,9},{9,8},{10,11... | collective-permute-start | bytes 36872 | tf_op jit(solution)/shard_map/ppermute | solution.py:370
  31.0 11.9 %collective-permute-start.13 = (f32[3,8,2048]{2,1,0:T(8,128)}, f32[3,8,2048]{2,1,0:T(8,128)S(1)}, u32[]{:S(2)}, u32[]{:S(2)}) collective-permute-start(f32[3,8,2048]{2,1,0:T(8,128)} %get-tuple-element.48), channel_id=1, source_target_pairs={{2,0},{3,1},{4,2},{5,3},{6,4},{7,5},{0,6},{1,7},{10,8},{11,9},{12,... | collective-permute-start | bytes 589832 | tf_op jit(solution)/shard_map/ppermute | solution.py:380
  34.6 12.2 %collective-permute-start.10 = (f32[3,8,2688]{2,1,0:T(8,128)}, f32[3,8,2688]{2,1,0:T(8,128)S(1)}, u32[]{:S(2)}, u32[]{:S(2)}) collective-permute-start(f32[3,8,2688]{2,1,0:T(8,128)} %get-tuple-element.44), channel_id=1, source_target_pairs={{2,0},{3,1},{4,2},{5,3},{6,4},{7,5},{0,6},{1,7},{10,8},{11,9},{12,... | collective-permute-start | bytes 774152 | tf_op jit(solution)/shard_map/ppermute | solution.py:380
  37.2 3.8 %copy-start.6 = (f32[3,8,1792]{2,1,0:T(8,128)}, f32[3,8,1792]{2,1,0:T(8,128)S(1)}, u32[]{:S(2)}) copy-start(f32[3,8,1792]{2,1,0:T(8,128)S(1)} %collective-permute-done.5.got_ref.refs_2_) | copy-start | bytes 516100
  37.2 26.5 %collective-permute-start.2 = (f32[3,8,2688]{2,1,0:T(8,128)}, f32[3,8,2688]{2,1,0:T(8,128)S(1)}, u32[]{:S(2)}, u32[]{:S(2)}) collective-permute-start(f32[3,8,2688]{2,1,0:T(8,128)} %get-tuple-element.34), channel_id=1, source_target_pairs={{0,2},{1,3},{2,4},{3,5},{4,6},{5,7},{6,0},{7,1},{8,10},{9,11},{10,... | collective-permute-start | bytes 774152 | tf_op jit(solution)/shard_map/ppermute | solution.py:379
  38.6 25.2 %collective-permute-start.3 = (f32[3,8,2688]{2,1,0:T(8,128)}, f32[3,8,2688]{2,1,0:T(8,128)S(1)}, u32[]{:S(2)}, u32[]{:S(2)}) collective-permute-start(f32[3,8,2688]{2,1,0:T(8,128)} %get-tuple-element.35), channel_id=1, source_target_pairs={{2,0},{3,1},{4,2},{5,3},{6,4},{7,5},{0,6},{1,7},{10,8},{11,9},{12,... | collective-permute-start | bytes 774152 | tf_op jit(solution)/shard_map/ppermute | solution.py:380
  42.9 20.8 %copy-start = (f32[3,8,4096]{2,1,0:T(8,128)S(1)}, f32[3,8,4096]{2,1,0:T(8,128)}, u32[]{:S(2)}) copy-start(f32[3,8,4096]{2,1,0:T(8,128)} %get-tuple-element.32.own_ref.refs_0_) | copy-start | bytes 1179652
  42.9 20.8 %copy-start.3 = (f32[3,8,2304]{2,1,0:T(8,128)S(1)}, f32[3,8,2304]{2,1,0:T(8,128)}, u32[]{:S(2)}) copy-start(f32[3,8,2304]{2,1,0:T(8,128)} %copy-done.2) | copy-start | bytes 663556
  42.9 19.2 %collective-permute-start.6 = (f32[3,8,2048]{2,1,0:T(8,128)}, f32[3,8,2048]{2,1,0:T(8,128)S(1)}, u32[]{:S(2)}, u32[]{:S(2)}) collective-permute-start(f32[3,8,2048]{2,1,0:T(8,128)} %get-tuple-element.38), channel_id=1, source_target_pairs={{0,2},{1,3},{2,4},{3,5},{4,6},{5,7},{6,0},{7,1},{8,10},{9,11},{10,... | collective-permute-start | bytes 589832 | tf_op jit(solution)/shard_map/ppermute | solution.py:379
  43.0 20.7 %collective-permute-start.7 = (f32[3,8,2048]{2,1,0:T(8,128)}, f32[3,8,2048]{2,1,0:T(8,128)S(1)}, u32[]{:S(2)}, u32[]{:S(2)}) collective-permute-start(f32[3,8,2048]{2,1,0:T(8,128)} %get-tuple-element.39), channel_id=1, source_target_pairs={{2,0},{3,1},{4,2},{5,3},{6,4},{7,5},{0,6},{1,7},{10,8},{11,9},{12,... | collective-permute-start | bytes 589832 | tf_op jit(solution)/shard_map/ppermute | solution.py:380
  47.7 16.0 %copy-start.7 = (f32[3,8,1792]{2,1,0:T(8,128)S(1)}, f32[3,8,1792]{2,1,0:T(8,128)}, u32[]{:S(2)}) copy-start(f32[3,8,1792]{2,1,0:T(8,128)} %copy-done.6) | copy-start | bytes 516100
  53.8 9.9 %copy-start.10 = (f32[3,8,2048]{2,1,0:T(8,128)}, f32[3,8,2048]{2,1,0:T(8,128)S(1)}, u32[]{:S(2)}) copy-start(f32[3,8,2048]{2,1,0:T(8,128)S(1)} %get-tuple-element.49.refs_3_) | copy-start | bytes 589828
  53.8 39.6 %collective-permute-start.17 = (f32[3,8,2048]{2,1,0:T(8,128)S(1)}, f32[3,8,2048]{2,1,0:T(8,128)S(1)}, u32[]{:S(2)}, u32[]{:S(2)}) collective-permute-start(f32[3,8,2048]{2,1,0:T(8,128)S(1)} %get-tuple-element.53), channel_id=1, source_target_pairs={{0,1},{1,0},{2,3},{3,2},{4,5},{5,4},{6,7},{7,6},{8,9},{9,8},{10,11... | collective-permute-start | bytes 589832 | tf_op jit(solution)/shard_map/ppermute | solution.py:385
  62.1 31.3 %collective-permute-start.16 = (f32[3,8,2048]{2,1,0:T(8,128)S(1)}, f32[3,8,2048]{2,1,0:T(8,128)S(1)}, u32[]{:S(2)}, u32[]{:S(2)}) collective-permute-start(f32[3,8,2048]{2,1,0:T(8,128)S(1)} %get-tuple-element.52), channel_id=1, source_target_pairs={{0,1},{1,0},{2,3},{3,2},{4,5},{5,4},{6,7},{7,6},{8,9},{9,8},{10,11... | collective-permute-start | bytes 589832 | tf_op jit(solution)/shard_map/ppermute | solution.py:385
  69.8 7.6 %copy-start.12 = (f32[3,8,2048]{2,1,0:T(8,128)}, f32[3,8,2048]{2,1,0:T(8,128)S(1)}, u32[]{:S(2)}) copy-start(f32[3,8,2048]{2,1,0:T(8,128)S(1)} %get-tuple-element.40.refs_1_) | copy-start | bytes 589828
  69.8 23.6 %collective-permute-start.15 = (f32[3,8,2048]{2,1,0:T(8,128)S(1)}, f32[3,8,2048]{2,1,0:T(8,128)S(1)}, u32[]{:S(2)}, u32[]{:S(2)}) collective-permute-start(f32[3,8,2048]{2,1,0:T(8,128)S(1)} %get-tuple-element.51), channel_id=1, source_target_pairs={{0,1},{1,0},{2,3},{3,2},{4,5},{5,4},{6,7},{7,6},{8,9},{9,8},{10,11... | collective-permute-start | bytes 589832 | tf_op jit(solution)/shard_map/ppermute | solution.py:385
  78.1 15.4 %collective-permute-start.14 = (f32[3,8,2048]{2,1,0:T(8,128)S(1)}, f32[3,8,2048]{2,1,0:T(8,128)S(1)}, u32[]{:S(2)}, u32[]{:S(2)}) collective-permute-start(f32[3,8,2048]{2,1,0:T(8,128)S(1)} %get-tuple-element.50), channel_id=1, source_target_pairs={{0,1},{1,0},{2,3},{3,2},{4,5},{5,4},{6,7},{7,6},{8,9},{9,8},{10,11... | collective-permute-start | bytes 589832 | tf_op jit(solution)/shard_map/ppermute | solution.py:385
  78.7 5.7 %collective-permute-start.18 = (f32[8,128]{1,0:T(8,128)S(1)}, f32[8,128]{1,0:T(8,128)S(1)}, u32[]{:S(2)}, u32[]{:S(2)}) collective-permute-start(f32[8,128]{1,0:T(8,128)S(1)} %add_add_fusion), channel_id=1, source_target_pairs={{0,1},{1,0},{2,3},{3,2},{4,5},{5,4},{6,7},{7,6},{8,9},{9,8},{10,11... | collective-permute-start | bytes 12296 | tf_op jit(solution)/shard_map/ppermute | solution.py:389
  84.4 3.9 %collective-permute-start.19 = (f32[8,128]{1,0:T(8,128)S(1)}, f32[8,128]{1,0:T(8,128)S(1)}, u32[]{:S(2)}, u32[]{:S(2)}) collective-permute-start(f32[8,128]{1,0:T(8,128)S(1)} %add.49), channel_id=1, source_target_pairs={{0,2},{1,3},{2,0},{3,1},{4,6},{5,7},{6,4},{7,5},{8,10},{9,11},{10,... | collective-permute-start | bytes 12296 | tf_op jit(solution)/shard_map/ppermute | solution.py:389
  88.3 4.5 %collective-permute-start.20 = (f32[8,128]{1,0:T(8,128)S(1)}, f32[8,128]{1,0:T(8,128)S(1)}, u32[]{:S(2)}, u32[]{:S(2)}) collective-permute-start(f32[8,128]{1,0:T(8,128)S(1)} %add.50), channel_id=1, source_target_pairs={{0,4},{1,5},{2,6},{3,7},{4,0},{5,1},{6,2},{7,3},{8,12},{9,13},{10,... | collective-permute-start | bytes 12296 | tf_op jit(solution)/shard_map/ppermute | solution.py:389
  (11 other events, 8.4 us)

commit v3 on v2

v3 whole, which is shorter than its diff:
```python
import functools

import jax
import jax.numpy as jnp
from jax import lax
from jax.experimental import pallas as pl
from jax.experimental.pallas import tpu as pltpu
from jax.sharding import PartitionSpec as P

STEPS = 3
DT = 0.4
HALF = 0.5 * DT
DEPTH = 3 * STEPS
LANES = 128
TILE = 8
BASE = 16
ROWS = 48

VMEM = pl.BlockSpec(memory_space=pltpu.VMEM)
SMEM = pl.BlockSpec(memory_space=pltpu.SMEM)
ANY = pl.BlockSpec(memory_space=pl.ANY)


def cost(us):
    return pl.CostEstimate(flops=0, bytes_accessed=int(us * 3.0e6), transcendentals=0)


def plan(ncol, slot, slots):
    every = list(range(ncol))
    if slot < slots - 1:
        return ((every, every, every),)
    cut = ncol // 2 + 2
    return (
        (every[:cut], every[:cut], every[1 : cut - 1]),
        (every[cut:], every[cut - 2 :] + [0, 1], every[cut - 1 :] + [0]),
    )


def at(i):
    return slice(i * LANES, (i + 1) * LANES)


def index_kernel(offspring, index):
    members = index.shape[0]
    here = lax.axis_index("particle")
    cumulative = []
    for i in range(offspring.shape[0]):
        cumulative.append(offspring[i] + (cumulative[-1] if i else 0))
    for k in range(members):
        j = here * members + k
        s = sum((c <= j).astype(jnp.int32) for c in cumulative)
        own = s - here * members
        other = s - (1 - here) * members
        inside = (own >= 0) & (own < members)
        index[k] = jnp.clip(jnp.where(inside, own, members + other), 0, 2 * members - 1)


def sources(offspring, members):
    return pl.pallas_call(
        index_kernel,
        out_shape=jax.ShapeDtypeStruct((members,), jnp.int32),
        in_specs=[SMEM],
        out_specs=SMEM,
    )(offspring)


def fetch(index, slot, own, other, spans, outs, sems):
    members = own.shape[0]
    i = index[slot]

    @pl.when(i < members)
    def _():
        for n, (first, count) in enumerate(spans):
            pltpu.make_async_copy(
                own.at[jnp.minimum(i, members - 1), :, :, pl.ds(first, count)], outs[n], sems.at[n]
            ).start()

    @pl.when(i >= members)
    def _():
        for n, (first, count) in enumerate(spans):
            pltpu.make_async_copy(
                other.at[jnp.maximum(i - members, 0), :, :, pl.ds(first, count)], outs[n], sems.at[n]
            ).start()


def arrive(own, spans, outs, sems):
    for n, (first, count) in enumerate(spans):
        pltpu.make_async_copy(own.at[0, :, :, pl.ds(first, count)], outs[n], sems.at[n]).wait()


def pick_kernel(index, own, other, *refs, slot, spans, before):
    n = len(spans)
    members = own.shape[0]
    half = members // 2
    par = lax.axis_index("strip") % 2
    earlier, refs = refs[: 2 * before], refs[2 * before :]
    kept, given, refs = refs[:n], refs[n : 2 * n], refs[2 * n :]
    sems = refs[-1]
    fetch(index, (1 - par) * half + slot, own, other, spans, given, sems.at[0])
    fetch(index, par * half + slot, own, other, spans, kept, sems.at[1])
    arrive(own, spans, given, sems.at[0])
    arrive(own, spans, kept, sems.at[1])
    if slot < half - 1:
        return
    near, far = refs[0], refs[1]
    ncol = own.shape[3] // LANES
    per = ncol // 4

    def edges(row):
        for ref, blocks, these in (
            (near, earlier[:before], kept),
            (far, earlier[before:], given),
        ):
            for k in range(half):
                for f in range(3):
                    for ct in range(ncol):
                        if k < before:
                            block, j = blocks[k], ct
                        else:
                            m = 0
                            while ct * LANES >= spans[m][0] + spans[m][1]:
                                m += 1
                            block, j = these[m], ct - spans[m][0] // LANES
                        q = (k * 3 + f) * 4 + ct // per
                        ref[q : q + 1, at(ct % per)] = block[f, row : row + 1, at(j)]

    @pl.when(par == 0)
    def _():
        edges(TILE - 1)

    @pl.when(par == 1)
    def _():
        edges(0)


def pick(index, own, other, slot, slots, spans, earlier):
    shape, kind = own.shape[1:3], own.dtype
    outs = [jax.ShapeDtypeStruct(shape + (c,), kind) for _, c in spans] * 2
    if slot == slots - 1:
        outs += [jax.ShapeDtypeStruct((12 * slots, own.shape[3] // 4), kind)] * 2
    return pl.pallas_call(
        functools.partial(pick_kernel, slot=slot, spans=spans, before=len(earlier) // 2),
        out_shape=outs,
        in_specs=[SMEM, ANY, ANY] + [VMEM] * len(earlier),
        out_specs=[VMEM] * len(outs),
        scratch_shapes=[pltpu.SemaphoreType.DMA((2, len(spans)))],
    )(index, own, other, *earlier)


def evaluate(src, state, dst, cor_ref, start, tiles, kind):
    ncol = src.shape[1]
    lane = lax.broadcasted_iota(jnp.int32, (TILE, LANES), 1)
    first = lane == 0
    last = lane == LANES - 1

    def body(t, carry):
        r0 = start + t * TILE
        rows = pl.ds(r0, TILE)
        cor = cor_ref[rows, :]
        for ct in range(ncol):
            mid, around = [], []
            for f in range(3):
                c = src[f, ct, rows, :]
                e = pltpu.roll(
                    jnp.where(first, src[f, (ct + 1) % ncol, rows, :], c), LANES - 1, 1
                )
                w = pltpu.roll(jnp.where(last, src[f, (ct - 1) % ncol, rows, :], c), 1, 1)
                n = src[f, ct, pl.ds(r0 + 1, TILE), :]
                s = src[f, ct, pl.ds(r0 - 1, TILE), :]
                mid.append(c)
                around.append((e, w, n, s))
            eta, u, v = mid
            (eE, eW, eN, eS), (uE, uW, uN, uS), (vE, vW, vN, vS) = around
            duy = uN - uS
            dvx = vE - vW
            dux = uE - uW
            dvy = vN - vS
            flow = (dux + dvy) + ((eE * uE - eW * uW) + (eN * vN - eS * vS))
            lu = v * (cor - duy) - u * dux - (eE - eW)
            lv = u * (cor + dvx) + v * dvy + (eN - eS)
            change = (-flow, lu, -lv)
            for f in range(3):
                if kind == 0:
                    new = mid[f] + HALF * change[f]
                elif kind == 1:
                    new = 0.75 * state[f, ct, rows, :] + (0.25 * mid[f] + (0.25 * HALF) * change[f])
                else:
                    new = (1.0 / 3.0) * state[f, ct, rows, :] + (
                        (2.0 / 3.0) * mid[f] + (2.0 / 3.0 * HALF) * change[f]
                    )
                dst[f, ct, rows, :] = new
        return carry

    lax.fori_loop(0, tiles, body, 0)


def forecast_kernel(*refs, worked, kept, place, parts, slot, slots, ncol, total_rows):
    own, got, direct, passed = (refs[n * parts : (n + 1) * parts] for n in range(4))
    near, far, obs_own, obs_got, keep, send, misfit, state, s1, s2, cor_ref = refs[4 * parts :]
    strip = lax.axis_index("strip")
    par = strip % 2
    per = ncol // 4

    def load(own_row, got_row, direct_row, passed_row, near_row, far_row):
        for i, ct in enumerate(worked):
            p, j = place[i]
            for ref, row in (
                (own, own_row),
                (got, got_row),
                (direct, direct_row),
                (passed, passed_row),
            ):
                state[:, i, row : row + TILE, :] = ref[p][:, :, at(j)]
            for ref, row in ((near, near_row), (far, far_row)):
                for f in range(3):
                    q = (slot * 3 + f) * 4 + ct // per
                    state[f, i, row : row + 1, :] = ref[q : q + 1, at(ct % per)]

    above, below = BASE - TILE, BASE + 2 * TILE

    @pl.when(par == 0)
    def _():
        load(BASE, BASE + TILE, below, above, above - 1, below + TILE)

    @pl.when(par == 1)
    def _():
        load(BASE + TILE, BASE, above, below, below + TILE, above - 1)

    row = lax.broadcasted_iota(jnp.int32, (ROWS, LANES), 0) + ((strip - par) * TILE - BASE)
    row = jnp.where(row < 0, row + total_rows, row)
    row = jnp.where(row >= total_rows, row - total_rows, row).astype(jnp.float32)
    cor_ref[...] = 2.0 * (0.3 + 0.4 * ((row + 0.5) / total_rows - 0.5))

    for k in range(DEPTH):
        reach = DEPTH - 1 - k
        tiles = (2 * TILE + 2 * reach + TILE - 1) // TILE
        kind = k % 3
        src, dst = ((state, s1), (s1, s2), (s2, state))[kind]
        evaluate(src, state, dst, cor_ref, BASE - reach, tiles, kind)

    def store(keep_row, send_row):
        for j, ct in enumerate(kept):
            i = worked.index(ct)
            keep[:, :, at(j)] = state[:, i, keep_row : keep_row + TILE, :]
            send[:, :, at(j)] = state[:, i, send_row : send_row + TILE, :]

    @pl.when(par == 0)
    def _():
        store(BASE, BASE + TILE)

    @pl.when(par == 1)
    def _():
        store(BASE + TILE, BASE)

    total = jnp.zeros((TILE, LANES), jnp.float32)
    for side in range(2):
        mine = par == side
        obs = [jnp.where(mine, obs_own[k], obs_got[k]) for k in range(3)]
        where = obs[1].astype(jnp.int32)
        tile, lane = where // LANES, where % LANES
        picked = jnp.zeros((TILE, LANES), jnp.float32)
        here = jnp.zeros((TILE, LANES), jnp.bool_)
        for ct in kept:
            i = worked.index(ct)
            eta = state[0, i, BASE + side * TILE : BASE + (side + 1) * TILE, :]
            found = tile == ct
            picked = jnp.where(found, jnp.take_along_axis(eta, lane, axis=1), picked)
            here = here | found
        gap = obs[0] - picked
        total = total + jnp.where(here, obs[2] * gap * gap, 0.0)
    at_slot = lax.broadcasted_iota(jnp.int32, (TILE, LANES), 0) == par * slots + slot
    misfit[...] = jnp.where(at_slot, jnp.sum(total), 0.0)


def forecast(own, got, direct, passed, near, far, obs_own, obs_got, piece, slot, slots, ncol, total_rows):
    parts = plan(ncol, slot, slots)
    _, worked, kept = parts[piece]
    place = []
    for ct in worked:
        p = 0 if ct in parts[0][0] else 1
        place.append((p, parts[p][0].index(ct)))
    block = jax.ShapeDtypeStruct((3, TILE, len(kept) * LANES), jnp.float32)
    field = pltpu.VMEM((3, len(worked), ROWS, LANES), jnp.float32)
    args = [*own, *got, *direct, *passed, near, far, obs_own, obs_got]
    return pl.pallas_call(
        functools.partial(
            forecast_kernel,
            worked=worked,
            kept=kept,
            place=place,
            parts=len(own),
            slot=slot,
            slots=slots,
            ncol=ncol,
            total_rows=total_rows,
        ),
        out_shape=[block, block, jax.ShapeDtypeStruct((TILE, LANES), jnp.float32)],
        in_specs=[VMEM] * len(args),
        out_specs=[VMEM] * 3,
        scratch_shapes=[field, field, field, pltpu.VMEM((ROWS, LANES), jnp.float32)],
        compiler_params=pltpu.CompilerParams(vmem_limit_bytes=24 * 2**20),
        cost_estimate=cost(7.0 * len(worked) / 18),
    )(*args)


def gather_kernel(*refs, ncol, slots, pieces):
    out = refs[-1]
    par = lax.axis_index("strip") % 2
    for n, (k, p) in enumerate(pieces):
        mine, theirs = refs[2 * n], refs[2 * n + 1]
        for j, ct in enumerate(plan(ncol, k, slots)[p][2]):
            out[par * slots + k, :, :, at(ct)] = mine[:, :, at(j)]
            out[(1 - par) * slots + k, :, :, at(ct)] = theirs[:, :, at(j)]


def gather(blocks, pieces, ncol, slots):
    args = [b for pair in blocks for b in pair]
    return pl.pallas_call(
        functools.partial(gather_kernel, ncol=ncol, slots=slots, pieces=pieces),
        out_shape=jax.ShapeDtypeStruct((2 * slots, 3, TILE, ncol * LANES), jnp.float32),
        in_specs=[VMEM] * len(args),
        out_specs=VMEM,
    )(*args)


def finish_kernel(before, mine, theirs, out, sems, *, runs, slot, slots):
    par = lax.axis_index("strip") % 2
    copies = []
    for n, (first, start, count) in enumerate(runs):
        for m, (ref, row) in enumerate(
            ((mine, par * slots + slot), (theirs, (1 - par) * slots + slot))
        ):
            copies.append(
                pltpu.make_async_copy(
                    ref.at[:, :, pl.ds(first * LANES, count * LANES)],
                    out.at[row, :, :, pl.ds(start * LANES, count * LANES)],
                    sems.at[2 * n + m],
                )
            )
    for c in copies:
        c.start()
    for c in copies:
        c.wait()


def finish(before, mine, theirs, slot, slots, piece, ncol):
    kept = plan(ncol, slot, slots)[piece][2]
    runs = []
    for j, ct in enumerate(kept):
        if j and ct == kept[j - 1] + 1:
            first, start, count = runs[-1]
            runs[-1] = (first, start, count + 1)
        else:
            runs.append((j, ct, 1))
    return pl.pallas_call(
        functools.partial(finish_kernel, runs=runs, slot=slot, slots=slots),
        out_shape=jax.ShapeDtypeStruct(before.shape, before.dtype),
        in_specs=[ANY, VMEM, VMEM],
        out_specs=ANY,
        scratch_shapes=[pltpu.SemaphoreType.DMA((2 * len(runs),))],
        input_output_aliases={0: 0},
    )(before, mine, theirs)


def local(ensemble, offspring, observations, obs_cols, obs_precision):
    members, _, strip_rows, cols = ensemble.shape
    strips = lax.axis_size("strip")
    total_rows = strips * strip_rows
    strip = lax.axis_index("strip")
    half = members // 2
    ncol = cols // LANES

    def moved(even, odd):
        return [(i, (i + (odd if i % 2 else even)) % strips) for i in range(strips)]

    swap = moved(1, -1)
    straight = moved(-2, 2)
    onward = moved(2, -2)
    cross = moved(3, -3)

    arrived = lax.ppermute(ensemble, "particle", [(0, 1), (1, 0)])
    index = sources(offspring, members)

    rows = (strip * strip_rows + jnp.arange(strip_rows, dtype=jnp.int32)).astype(jnp.float32)
    weight = obs_precision * (1.0 + 2.0 * (rows + 0.5) / total_rows)[:, None]
    obs_own = jnp.stack([observations, obs_cols.astype(jnp.float32), weight])

    kept, given, got, direct, passed = [], [], [], [], []
    earlier = []
    for k in range(half):
        parts = plan(ncol, k, half)
        spans = [(sent[0] * LANES, len(sent) * LANES) for sent, _, _ in parts]
        out = pick(index, ensemble, arrived, k, half, spans, [e[0] for e in kept + given])
        n = len(parts)
        kept.append(out[:n])
        given.append(out[n : 2 * n])
        rest = out[2 * n :]
    near = lax.ppermute(rest[0], "strip", onward)
    far = lax.ppermute(rest[1], "strip", cross)
    for k in range(half):
        got.append([lax.ppermute(g, "strip", swap) for g in given[k]])
        direct.append([lax.ppermute(b, "strip", straight) for b in kept[k]])
        passed.append([lax.ppermute(g, "strip", onward) for g in got[k]])
    obs_got = lax.ppermute(obs_own, "strip", swap)

    blocks, pieces, total = [], [], None
    for k in range(half):
        for p in range(len(plan(ncol, k, half))):
            keep, send, misfit = forecast(
                kept[k][: p + 1],
                got[k][: p + 1],
                direct[k][: p + 1],
                passed[k][: p + 1],
                near,
                far,
                obs_own,
                obs_got,
                p,
                k,
                half,
                ncol,
                total_rows,
            )
            blocks.append((keep, lax.ppermute(send, "strip", swap)))
            pieces.append((k, p))
            total = misfit if total is None else total + misfit
    step = 2
    while step < strips:
        total = total + lax.ppermute(total, "strip", [(i, i ^ step) for i in range(strips)])
        step *= 2
    total = total + lax.ppermute(total, "strip", swap)
    state = gather(blocks[:-1], pieces[:-1], ncol, half)
    state = finish(state, *blocks[-1], half - 1, half, pieces[-1][1], ncol)
    log_weights = (-0.5 / (total_rows * obs_cols.shape[1])) * total[:members, 0]
    return (state, log_weights)


def solution(mesh):
    in_specs = (
        P(("group", "particle"), None, "strip", None),
        P("group"),
        P(("group", "strip"), None),
        P(("group", "strip"), None),
        P(("group", "strip"), None),
    )
    out_specs = (P(("group", "particle"), None, "strip", None), P(("group", "particle")))
    return jax.shard_map(local, mesh=mesh, in_specs=in_specs, out_specs=out_specs, check_vma=False)
```

time: 97.4 us -> 91.1 us (0.935)
  Pallas kernels: 39.9 us -> 32.9 us
  waiting for transfers between devices: 16.3 us -> 22.4 us
  starting transfers between devices: 33.7 us -> 29.9 us
  local copies, waits for them, and re-layouts: 5.69 us -> 4.07 us
    ppermute x17 -> x16, waiting for transfers between devices: 5.63 us -> 14.3 us  [the longest x1 6.12 us: local(): far = lax.ppermute(rest[1], 'strip', cross)]
    ppermute x3 -> x2, starting transfers between devices: 5.64 us -> 1.59 us  [local(): lax.ppermute(total, 'strip', [(i, i ^ step) for i in range(strips)])]
    pallas_call x7 -> x5, Pallas kernels: 15.7 us -> 11.8 us  [the longest x2 6.32 us: pick(): pl.pallas_call(functools.partial(pick_kernel, slot=slot, spans=spans, bef...]
    pallas_call x4 -> x3, Pallas kernels: 24.2 us -> 21.1 us  [forecast(): pl.pallas_call(functools.partial(forecast_kernel, worked=worked, kept=kep...]
    ppermute x1, starting transfers between devices: 1.54 us -> 3.54 us  [local(): obs_got = lax.ppermute(obs_own, 'strip', swap)]
    ppermute x3 -> x2, waiting for transfers between devices: 8.48 us -> 6.52 us  [local(): lax.ppermute(total, 'strip', [(i, i ^ step) for i in range(strips)])]
    ppermute x17 -> x16, starting transfers between devices: 26.5 us -> 24.8 us  [the longest x3 10.5 us: local(): direct.append([lax.ppermute(b, 'strip', straight) for b in kept[k]])]
    unnamed x44 -> x26, local copies, waits for them, and re-layouts: 5.69 us -> 4.07 us
  transfers between devices with their start and end apart: 21 -> 19, of which waited for: 8 -> 8; matrix products, arithmetic and copies ran while one was open for 1% -> 1% of each run, Pallas kernels for 33% -> 31%
where the time goes in v3:
time: 91.1 us; the launch traced here: 90.8 us
  Pallas kernels  32.9 us (36%)
  starting transfers between devices  29.9 us (33%)
  waiting for transfers between devices  22.4 us (25%)
  local copies, waits for them, and re-layouts  4.07 us (4%)
    pallas_call x3, Pallas kernels, forecast(): pl.pallas_call(functools.partial(forecast_kernel, worked=worked, kept=kep...  21.1 us
    ppermute x3, starting transfers between devices, local(): direct.append([lax.ppermute(b, 'strip', straight) for b in kept[k]])  10.5 us
    ppermute x2, waiting for transfers between devices, local(): lax.ppermute(total, 'strip', [(i, i ^ step) for i in range(strips)])  6.52 us
    pallas_call x2, Pallas kernels, pick(): pl.pallas_call(functools.partial(pick_kernel, slot=slot, spans=spans, bef...  6.32 us
    ppermute x1, waiting for transfers between devices, local(): far = lax.ppermute(rest[1], 'strip', cross)  6.12 us
    ppermute x3, starting transfers between devices, local(): got.append([lax.ppermute(g, 'strip', swap) for g in given[k]])  5.49 us
    ppermute x3, starting transfers between devices, local(): blocks.append((keep, lax.ppermute(send, 'strip', swap)))  4.54 us
    unnamed x26, local copies, waits for them, and re-layouts  4.07 us
  transfers between devices with their start and end apart: 19, of which 8 were waited for; matrix products, arithmetic and copies ran while one was open for 1% of the time, Pallas kernels for 31%

profile of v3, /device:TPU:0, one launch (start us, length us, event | category | flops | bytes accessed | tf_op | source)
XLA Modules:
  0.0 90.8 jit_solution(9436906451571164866)
XLA Ops:
  1.1 1.2 %shard_map.68.index = s32[4]{0:T(128)} custom-call(s32[8]{0:T(128)} %offspring.1), custom_call_target="tpu_custom_call" | custom-call | tf_op jit(solution)/shard_map/pallas_call | solution.py:59
  2.4 2.0 %collective-permute-done.other = f32[4,3,8,4096]{3,2,1,0:T(8,128)S(1)} collective-permute-done((f32[4,3,8,4096]{3,2,1,0:T(8,128)}, f32[4,3,8,4096]{3,2,1,0:T(8,128)S(1)}, u32[]{:S(2)}, u32[]{:S(2)}) %collective-permute-start) | collective-permute-done | bytes 1572896 | tf_op jit(solution)/shard_map/ppermute | solution.py:381
  4.4 1.1 %copy-done.6 = f32[4,3,8,4096]{3,2,1,0:T(8,128)} copy-done((f32[4,3,8,4096]{3,2,1,0:T(8,128)}, f32[4,3,8,4096]{3,2,1,0:T(8,128)S(1)}, u32[]{:S(2)}) %copy-start.6) | copy-done | bytes 1572888
  5.5 2.7 %shard_map.69 = (f32[3,8,4096]{2,1,0:T(8,128)}, f32[3,8,4096]{2,1,0:T(8,128)}) custom-call(s32[4]{0:T(128)} %shard_map.68.index, f32[4,3,8,4096]{3,2,1,0:T(8,128)} %own.3, f32[4,3,8,4096]{3,2,1,0:T(8,128)} %copy-done.6), custom_call_target="tpu_custom_call" | custom-call | tf_op jit(solution)/shard_map/pallas_call | solution.py:141
  8.3 3.0 %collective-permute-start.1 = (f32[3,8,4096]{2,1,0:T(8,128)}, f32[3,8,4096]{2,1,0:T(8,128)S(1)}, u32[]{:S(2)}, u32[]{:S(2)}) collective-permute-start(f32[3,8,4096]{2,1,0:T(8,128)} %get-tuple-element.20.refs_1_), channel_id=1, source_target_pairs={{0,1},{1,0},{2,3},{3,2},{4,5},{5,4},{6,7},{7,6},{8,9},{9,8},{10,11... | collective-permute-start | bytes 1179656 | tf_op jit(solution)/shard_map/ppermute | solution.py:401
  11.3 3.6 %collective-permute-start.2 = (f32[3,8,4096]{2,1,0:T(8,128)}, f32[3,8,4096]{2,1,0:T(8,128)S(1)}, u32[]{:S(2)}, u32[]{:S(2)}) collective-permute-start(f32[3,8,4096]{2,1,0:T(8,128)} %get-tuple-element.19.refs_0_), channel_id=1, source_target_pairs={{0,6},{1,3},{2,0},{3,5},{4,2},{5,7},{6,4},{7,1},{8,14},{9,11},{10,... | collective-permute-start | bytes 1179656 | tf_op jit(solution)/shard_map/ppermute | solution.py:402
  14.9 3.6 %shard_map.70 = (f32[3,8,2304]{2,1,0:T(8,128)}, f32[3,8,1792]{2,1,0:T(8,128)}, f32[3,8,2304]{2,1,0:T(8,128)}, f32[3,8,1792]{2,1,0:T(8,128)}, f32[24,1024]{1,0:T(8,128)}, /*index=5*/f32[24,1024]{1,0:T(8,128)}) custom-call(s32[4]{0:T(128)} %shard_map.68.index, f32[4,3,8,4096]{3,2,1,0:T(8,128)} %own.3, f32[4,3,8,4096]{3,2,1,0:T(8,128)} %copy-done.6, ...), custom_call_target="tpu_custom_call" | custom-call | tf_op jit(solution)/shard_map/pallas_call | solution.py:141
  19.1 1.9 %collective-permute-done.1.refs_1_ = f32[3,8,4096]{2,1,0:T(8,128)S(1)} collective-permute-done((f32[3,8,4096]{2,1,0:T(8,128)}, f32[3,8,4096]{2,1,0:T(8,128)S(1)}, u32[]{:S(2)}, u32[]{:S(2)}) %collective-permute-start.1) | collective-permute-done | bytes 393248 | tf_op jit(solution)/shard_map/ppermute | solution.py:401
  21.0 2.4 %collective-permute-start.3 = (f32[3,8,4096]{2,1,0:T(8,128)S(1)}, f32[3,8,4096]{2,1,0:T(8,128)S(1)}, u32[]{:S(2)}, u32[]{:S(2)}) collective-permute-start(f32[3,8,4096]{2,1,0:T(8,128)S(1)} %collective-permute-done.1.refs_1_), channel_id=1, source_target_pairs={{0,2},{1,7},{2,4},{3,1},{4,6},{5,3},{6,0},{7,5},{8,10},{9,15},{10,... | collective-permute-start | bytes 1179656 | tf_op jit(solution)/shard_map/ppermute | solution.py:403
  23.4 3.5 %collective-permute-start.6 = (f32[3,8,128]{2,1,0:T(8,128)S(1)}, f32[3,8,128]{2,1,0:T(8,128)S(1)}, u32[]{:S(2)}, u32[]{:S(2)}) collective-permute-start(f32[3,8,128]{2,1,0:T(8,128)S(1)} %pad_maximum_fusion.refs_6_.refs_10_), channel_id=1, source_target_pairs={{0,1},{1,0},{2,3},{3,2},{4,5},{5,4},{6,7},{7,6},{8,9},{9,8},{10,11... | collective-permute-start | bytes 36872 | tf_op jit(solution)/shard_map/ppermute | solution.py:404
  27.0 1.7 %collective-permute-done.6.refs_7_.refs_11_ = f32[3,8,128]{2,1,0:T(8,128)S(1)} collective-permute-done((f32[3,8,128]{2,1,0:T(8,128)S(1)}, f32[3,8,128]{2,1,0:T(8,128)S(1)}, u32[]{:S(2)}, u32[]{:S(2)}) %collective-permute-start.6) | collective-permute-done | bytes 12320 | tf_op jit(solution)/shard_map/ppermute | solution.py:404
  28.7 2.0 %collective-permute-start.12 = (f32[3,8,1792]{2,1,0:T(8,128)}, f32[3,8,1792]{2,1,0:T(8,128)S(1)}, u32[]{:S(2)}, u32[]{:S(2)}) collective-permute-start(f32[3,8,1792]{2,1,0:T(8,128)} %get-tuple-element.30), channel_id=1, source_target_pairs={{0,1},{1,0},{2,3},{3,2},{4,5},{5,4},{6,7},{7,6},{8,9},{9,8},{10,11... | collective-permute-start | bytes 516104 | tf_op jit(solution)/shard_map/ppermute | solution.py:401
  30.7 6.1 %collective-permute-done.5.refs_5_.refs_9_ = f32[24,1024]{1,0:T(8,128)S(1)} collective-permute-done((f32[24,1024]{1,0:T(8,128)}, f32[24,1024]{1,0:T(8,128)S(1)}, u32[]{:S(2)}, u32[]{:S(2)}) %collective-permute-start.5) | collective-permute-done | bytes 98336 | tf_op jit(solution)/shard_map/ppermute | solution.py:399
  36.8 3.0 %collective-permute-start.9 = (f32[3,8,2304]{2,1,0:T(8,128)}, f32[3,8,2304]{2,1,0:T(8,128)S(1)}, u32[]{:S(2)}, u32[]{:S(2)}) collective-permute-start(f32[3,8,2304]{2,1,0:T(8,128)} %get-tuple-element.25.refs_0_), channel_id=1, source_target_pairs={{0,6},{1,3},{2,0},{3,5},{4,2},{5,7},{6,4},{7,1},{8,14},{9,11},{10,... | collective-permute-start | bytes 663560 | tf_op jit(solution)/shard_map/ppermute | solution.py:402
  39.9 3.8 %collective-permute-start.13 = (f32[3,8,1792]{2,1,0:T(8,128)}, f32[3,8,1792]{2,1,0:T(8,128)S(1)}, u32[]{:S(2)}, u32[]{:S(2)}) collective-permute-start(f32[3,8,1792]{2,1,0:T(8,128)} %get-tuple-element.29.refs_1_), channel_id=1, source_target_pairs={{0,6},{1,3},{2,0},{3,5},{4,2},{5,7},{6,4},{7,1},{8,14},{9,11},{10,... | collective-permute-start | bytes 516104 | tf_op jit(solution)/shard_map/ppermute | solution.py:402
  43.7 8.9 %shard_map.71 = (f32[3,8,4096]{2,1,0:T(8,128)S(1)}, f32[3,8,4096]{2,1,0:T(8,128)S(1)}, f32[8,128]{1,0:T(8,128)S(1)}) custom-call(f32[3,8,4096]{2,1,0:T(8,128)S(1)} %copy-done, f32[3,8,4096]{2,1,0:T(8,128)S(1)} %collective-permute-done.1.refs_1_, f32[3,8,4096]{2,1,0:T(8,128)S(1)} %collective-permute-done.2.refs_2_, ...), custom_call_target="tpu_custom_call" | custom-call | bytes 37333332 | tf_op jit(solution)/shard_map/pallas_call | solution.py:285
  52.6 0.7 copy-done.2
  53.3 2.4 %collective-permute-start.7 = (f32[3,8,4096]{2,1,0:T(8,128)S(1)}, f32[3,8,4096]{2,1,0:T(8,128)S(1)}, u32[]{:S(2)}, u32[]{:S(2)}) collective-permute-start(f32[3,8,4096]{2,1,0:T(8,128)S(1)} %get-tuple-element.24), channel_id=1, source_target_pairs={{0,1},{1,0},{2,3},{3,2},{4,5},{5,4},{6,7},{7,6},{8,9},{9,8},{10,11... | collective-permute-start | bytes 1179656 | tf_op jit(solution)/shard_map/ppermute | solution.py:424
  55.8 1.9 %collective-permute-done.14.refs_7_ = f32[3,8,1792]{2,1,0:T(8,128)S(1)} collective-permute-done((f32[3,8,1792]{2,1,0:T(8,128)S(1)}, f32[3,8,1792]{2,1,0:T(8,128)S(1)}, u32[]{:S(2)}, u32[]{:S(2)}) %collective-permute-start.14) | collective-permute-done | bytes 172064 | tf_op jit(solution)/shard_map/ppermute | solution.py:403
  57.7 6.1 %shard_map.74 = (f32[3,8,2048]{2,1,0:T(8,128)S(1)}, f32[3,8,2048]{2,1,0:T(8,128)S(1)}, f32[8,128]{1,0:T(8,128)S(1)}) custom-call(f32[3,8,2304]{2,1,0:T(8,128)S(1)} %copy-done.1, f32[3,8,1792]{2,1,0:T(8,128)S(1)} %copy-done.5, f32[3,8,2304]{2,1,0:T(8,128)S(1)} %collective-permute-done.8.refs_1_.refs_2_, f32[3,8,1792]{2,1,0:T(8,128)S(1)} %collective-permute-done.12.refs_3_, ...), custom_call_target="tpu_custom_call" | custom-call | bytes 21000000 | tf_op jit(solution)/shard_map/pallas_call | solution.py:285
  63.8 1.3 %collective-permute-start.15 = (f32[3,8,2048]{2,1,0:T(8,128)S(1)}, f32[3,8,2048]{2,1,0:T(8,128)S(1)}, u32[]{:S(2)}, u32[]{:S(2)}) collective-permute-start(f32[3,8,2048]{2,1,0:T(8,128)S(1)} %get-tuple-element.32), channel_id=1, source_target_pairs={{0,1},{1,0},{2,3},{3,2},{4,5},{5,4},{6,7},{7,6},{8,9},{9,8},{10,11... | collective-permute-start | bytes 589832 | tf_op jit(solution)/shard_map/ppermute | solution.py:424
  65.2 6.1 %shard_map.72 = (f32[3,8,2048]{2,1,0:T(8,128)S(1)}, f32[3,8,2048]{2,1,0:T(8,128)S(1)}, f32[8,128]{1,0:T(8,128)S(1)}) custom-call(f32[3,8,2304]{2,1,0:T(8,128)S(1)} %copy-done.1, f32[3,8,2304]{2,1,0:T(8,128)S(1)} %collective-permute-done.8.refs_1_.refs_2_, f32[3,8,2304]{2,1,0:T(8,128)S(1)} %collective-permute-done.9.refs_2_.refs_4_, ...), custom_call_target="tpu_custom_call" | custom-call | bytes 21000000 | tf_op jit(solution)/shard_map/pallas_call | solution.py:285
  71.3 0.7 copy-done.4
  72.0 0.7 collective-permute-start.11
  73.3 3.0 %collective-permute-done.16 = f32[8,128]{1,0:T(8,128)S(1)} collective-permute-done((f32[8,128]{1,0:T(8,128)S(1)}, f32[8,128]{1,0:T(8,128)S(1)}, u32[]{:S(2)}, u32[]{:S(2)}) %collective-permute-start.16) | collective-permute-done | bytes 4128 | tf_op jit(solution)/shard_map/ppermute | solution.py:429
  76.3 1.0 %collective-permute-start.17 = (f32[8,128]{1,0:T(8,128)S(1)}, f32[8,128]{1,0:T(8,128)S(1)}, u32[]{:S(2)}, u32[]{:S(2)}) collective-permute-start(f32[8,128]{1,0:T(8,128)S(1)} %add.45), channel_id=1, source_target_pairs={{0,4},{1,5},{2,6},{3,7},{4,0},{5,1},{6,2},{7,3},{8,12},{9,13},{10,... | collective-permute-start | bytes 12296 | tf_op jit(solution)/shard_map/ppermute | solution.py:429
  77.3 3.5 %collective-permute-done.17 = f32[8,128]{1,0:T(8,128)S(1)} collective-permute-done((f32[8,128]{1,0:T(8,128)S(1)}, f32[8,128]{1,0:T(8,128)S(1)}, u32[]{:S(2)}, u32[]{:S(2)}) %collective-permute-start.17) | collective-permute-done | bytes 4128 | tf_op jit(solution)/shard_map/ppermute | solution.py:429
  80.8 1.3 %collective-permute-start.18 = (f32[8,128]{1,0:T(8,128)S(1)}, f32[8,128]{1,0:T(8,128)S(1)}, u32[]{:S(2)}, u32[]{:S(2)}) collective-permute-start(f32[8,128]{1,0:T(8,128)S(1)} %add.46), channel_id=1, source_target_pairs={{0,1},{1,0},{2,3},{3,2},{4,5},{5,4},{6,7},{7,6},{8,9},{9,8},{10,11... | collective-permute-start | bytes 12296 | tf_op jit(solution)/shard_map/ppermute | solution.py:431
  82.1 2.3 %collective-permute-done.18 = f32[8,128]{1,0:T(8,128)S(1)} collective-permute-done((f32[8,128]{1,0:T(8,128)S(1)}, f32[8,128]{1,0:T(8,128)S(1)}, u32[]{:S(2)}, u32[]{:S(2)}) %collective-permute-start.18) | collective-permute-done | bytes 4128 | tf_op jit(solution)/shard_map/ppermute | solution.py:431
  85.9 2.5 %shard_map.73.before = f32[4,3,8,4096]{3,2,1,0:T(8,128)} custom-call(f32[3,8,4096]{2,1,0:T(8,128)} %copy-done.2, f32[3,8,4096]{2,1,0:T(8,128)} %copy-done.7, f32[3,8,2048]{2,1,0:T(8,128)} %copy-done.4, f32[3,8,2048]{2,1,0:T(8,128)} %copy-done.9), custom_call_target="tpu_custom_call" | custom-call | tf_op jit(solution)/shard_map/pallas_call | solution.py:318
  88.4 0.7 copy-done.8
  89.0 1.8 %shard_map.75 = f32[4,3,8,4096]{3,2,1,0:T(8,128)} custom-call(f32[4,3,8,4096]{3,2,1,0:T(8,128)} %shard_map.73.before, f32[3,8,2048]{2,1,0:T(8,128)} %copy-done.3, f32[3,8,2048]{2,1,0:T(8,128)} %copy-done.8), custom_call_target="tpu_custom_call", output_to_operand_aliasing={{}: (0, {})} | custom-call | tf_op jit(solution)/shard_map/pallas_call | solution.py:355
  (49 shorter events, 3.3 us)
Async XLA Ops:
  0.6 3.8 %collective-permute-start = (f32[4,3,8,4096]{3,2,1,0:T(8,128)}, f32[4,3,8,4096]{3,2,1,0:T(8,128)S(1)}, u32[]{:S(2)}, u32[]{:S(2)}) collective-permute-start(f32[4,3,8,4096]{3,2,1,0:T(8,128)} %own.3), channel_id=1, source_target_pairs={{0,8},{8,0},{1,9},{9,1},{2,10},{10,2},{3,11},{11,3},{4,12},{12,4},... | collective-permute-start | bytes 4718600 | tf_op jit(solution)/shard_map/ppermute | solution.py:381
  2.4 8.8 %copy-start.10 = (f32[8,128]{1,0:T(8,128)S(1)}, f32[8,128]{1,0:T(8,128)}, u32[]{:S(2)}) copy-start(f32[8,128]{1,0:T(8,128)} %param.9) | copy-start | bytes 12292
  2.4 12.5 %copy-start.11 = (s32[8,128]{1,0:T(8,128)S(1)}, s32[8,128]{1,0:T(8,128)}, u32[]{:S(2)}) copy-start(s32[8,128]{1,0:T(8,128)} %param.8) | copy-start | bytes 12292
  4.4 1.1 %copy-start.6 = (f32[4,3,8,4096]{3,2,1,0:T(8,128)}, f32[4,3,8,4096]{3,2,1,0:T(8,128)S(1)}, u32[]{:S(2)}) copy-start(f32[4,3,8,4096]{3,2,1,0:T(8,128)S(1)} %collective-permute-done.other) | copy-start | bytes 4718596
  8.3 12.7 %collective-permute-start.1 = (f32[3,8,4096]{2,1,0:T(8,128)}, f32[3,8,4096]{2,1,0:T(8,128)S(1)}, u32[]{:S(2)}, u32[]{:S(2)}) collective-permute-start(f32[3,8,4096]{2,1,0:T(8,128)} %get-tuple-element.20.refs_1_), channel_id=1, source_target_pairs={{0,1},{1,0},{2,3},{3,2},{4,5},{5,4},{6,7},{7,6},{8,9},{9,8},{10,11... | collective-permute-start | bytes 1179656 | tf_op jit(solution)/shard_map/ppermute | solution.py:401
  11.3 32.4 %collective-permute-start.2 = (f32[3,8,4096]{2,1,0:T(8,128)}, f32[3,8,4096]{2,1,0:T(8,128)S(1)}, u32[]{:S(2)}, u32[]{:S(2)}) collective-permute-start(f32[3,8,4096]{2,1,0:T(8,128)} %get-tuple-element.19.refs_0_), channel_id=1, source_target_pairs={{0,6},{1,3},{2,0},{3,5},{4,2},{5,7},{6,4},{7,1},{8,14},{9,11},{10,... | collective-permute-start | bytes 1179656 | tf_op jit(solution)/shard_map/ppermute | solution.py:402
  14.9 8.5 %copy-start.12 = (f32[8,128]{1,0:T(8,128)S(1)}, f32[8,128]{1,0:T(8,128)}, u32[]{:S(2)}) copy-start(f32[8,128]{1,0:T(8,128)} %param.7) | copy-start | bytes 12292
  14.9 28.8 %copy-start = (f32[3,8,4096]{2,1,0:T(8,128)S(1)}, f32[3,8,4096]{2,1,0:T(8,128)}, u32[]{:S(2)}) copy-start(f32[3,8,4096]{2,1,0:T(8,128)} %get-tuple-element.19.refs_0_) | copy-start | bytes 1179652
  18.5 39.2 %copy-start.1 = (f32[3,8,2304]{2,1,0:T(8,128)S(1)}, f32[3,8,2304]{2,1,0:T(8,128)}, u32[]{:S(2)}) copy-start(f32[3,8,2304]{2,1,0:T(8,128)} %get-tuple-element.25.refs_0_) | copy-start | bytes 663556
  18.5 39.2 %copy-start.5 = (f32[3,8,1792]{2,1,0:T(8,128)S(1)}, f32[3,8,1792]{2,1,0:T(8,128)}, u32[]{:S(2)}) copy-start(f32[3,8,1792]{2,1,0:T(8,128)} %get-tuple-element.29.refs_1_) | copy-start | bytes 516100
  18.5 12.2 %collective-permute-start.4 = (f32[24,1024]{1,0:T(8,128)}, f32[24,1024]{1,0:T(8,128)S(1)}, u32[]{:S(2)}, u32[]{:S(2)}) collective-permute-start(f32[24,1024]{1,0:T(8,128)} %get-tuple-element.21), channel_id=1, source_target_pairs={{0,2},{1,7},{2,4},{3,1},{4,6},{5,3},{6,0},{7,5},{8,10},{9,15},{10,... | collective-permute-start | bytes 294920 | tf_op jit(solution)/shard_map/ppermute | solution.py:398
  18.6 21.3 %collective-permute-start.8 = (f32[3,8,2304]{2,1,0:T(8,128)}, f32[3,8,2304]{2,1,0:T(8,128)S(1)}, u32[]{:S(2)}, u32[]{:S(2)}) collective-permute-start(f32[3,8,2304]{2,1,0:T(8,128)} %get-tuple-element.26), channel_id=1, source_target_pairs={{0,1},{1,0},{2,3},{3,2},{4,5},{5,4},{6,7},{7,6},{8,9},{9,8},{10,11... | collective-permute-start | bytes 663560 | tf_op jit(solution)/shard_map/ppermute | solution.py:401
  21.0 22.7 %collective-permute-start.3 = (f32[3,8,4096]{2,1,0:T(8,128)S(1)}, f32[3,8,4096]{2,1,0:T(8,128)S(1)}, u32[]{:S(2)}, u32[]{:S(2)}) collective-permute-start(f32[3,8,4096]{2,1,0:T(8,128)S(1)} %collective-permute-done.1.refs_1_), channel_id=1, source_target_pairs={{0,2},{1,7},{2,4},{3,1},{4,6},{5,3},{6,0},{7,5},{8,10},{9,15},{10,... | collective-permute-start | bytes 1179656 | tf_op jit(solution)/shard_map/ppermute | solution.py:403
  23.4 5.2 %collective-permute-start.6 = (f32[3,8,128]{2,1,0:T(8,128)S(1)}, f32[3,8,128]{2,1,0:T(8,128)S(1)}, u32[]{:S(2)}, u32[]{:S(2)}) collective-permute-start(f32[3,8,128]{2,1,0:T(8,128)S(1)} %pad_maximum_fusion.refs_6_.refs_10_), channel_id=1, source_target_pairs={{0,1},{1,0},{2,3},{3,2},{4,5},{5,4},{6,7},{7,6},{8,9},{9,8},{10,11... | collective-permute-start | bytes 36872 | tf_op jit(solution)/shard_map/ppermute | solution.py:404
  28.7 11.2 %collective-permute-start.12 = (f32[3,8,1792]{2,1,0:T(8,128)}, f32[3,8,1792]{2,1,0:T(8,128)S(1)}, u32[]{:S(2)}, u32[]{:S(2)}) collective-permute-start(f32[3,8,1792]{2,1,0:T(8,128)} %get-tuple-element.30), channel_id=1, source_target_pairs={{0,1},{1,0},{2,3},{3,2},{4,5},{5,4},{6,7},{7,6},{8,9},{9,8},{10,11... | collective-permute-start | bytes 516104 | tf_op jit(solution)/shard_map/ppermute | solution.py:401
  30.7 6.1 %collective-permute-start.5 = (f32[24,1024]{1,0:T(8,128)}, f32[24,1024]{1,0:T(8,128)S(1)}, u32[]{:S(2)}, u32[]{:S(2)}) collective-permute-start(f32[24,1024]{1,0:T(8,128)} %get-tuple-element.22), channel_id=1, source_target_pairs={{0,3},{1,6},{2,5},{3,0},{4,7},{5,2},{6,1},{7,4},{8,11},{9,14},{10,... | collective-permute-start | bytes 294920 | tf_op jit(solution)/shard_map/ppermute | solution.py:399
  36.8 19.0 %collective-permute-start.9 = (f32[3,8,2304]{2,1,0:T(8,128)}, f32[3,8,2304]{2,1,0:T(8,128)S(1)}, u32[]{:S(2)}, u32[]{:S(2)}) collective-permute-start(f32[3,8,2304]{2,1,0:T(8,128)} %get-tuple-element.25.refs_0_), channel_id=1, source_target_pairs={{0,6},{1,3},{2,0},{3,5},{4,2},{5,7},{6,4},{7,1},{8,14},{9,11},{10,... | collective-permute-start | bytes 663560 | tf_op jit(solution)/shard_map/ppermute | solution.py:402
  39.9 17.9 %collective-permute-start.10 = (f32[3,8,2304]{2,1,0:T(8,128)S(1)}, f32[3,8,2304]{2,1,0:T(8,128)S(1)}, u32[]{:S(2)}, u32[]{:S(2)}) collective-permute-start(f32[3,8,2304]{2,1,0:T(8,128)S(1)} %collective-permute-done.8.refs_1_.refs_2_), channel_id=1, source_target_pairs={{0,2},{1,7},{2,4},{3,1},{4,6},{5,3},{6,0},{7,5},{8,10},{9,15},{10,... | collective-permute-start | bytes 663560 | tf_op jit(solution)/shard_map/ppermute | solution.py:403
  39.9 15.9 %collective-permute-start.13 = (f32[3,8,1792]{2,1,0:T(8,128)}, f32[3,8,1792]{2,1,0:T(8,128)S(1)}, u32[]{:S(2)}, u32[]{:S(2)}) collective-permute-start(f32[3,8,1792]{2,1,0:T(8,128)} %get-tuple-element.29.refs_1_), channel_id=1, source_target_pairs={{0,6},{1,3},{2,0},{3,5},{4,2},{5,7},{6,4},{7,1},{8,14},{9,11},{10,... | collective-permute-start | bytes 516104 | tf_op jit(solution)/shard_map/ppermute | solution.py:402
  43.7 14.0 %collective-permute-start.14 = (f32[3,8,1792]{2,1,0:T(8,128)S(1)}, f32[3,8,1792]{2,1,0:T(8,128)S(1)}, u32[]{:S(2)}, u32[]{:S(2)}) collective-permute-start(f32[3,8,1792]{2,1,0:T(8,128)S(1)} %collective-permute-done.12.refs_3_), channel_id=1, source_target_pairs={{0,2},{1,7},{2,4},{3,1},{4,6},{5,3},{6,0},{7,5},{8,10},{9,15},{10,... | collective-permute-start | bytes 516104 | tf_op jit(solution)/shard_map/ppermute | solution.py:403
  52.6 0.7 copy-start.2
  53.3 31.7 %collective-permute-start.7 = (f32[3,8,4096]{2,1,0:T(8,128)S(1)}, f32[3,8,4096]{2,1,0:T(8,128)S(1)}, u32[]{:S(2)}, u32[]{:S(2)}) collective-permute-start(f32[3,8,4096]{2,1,0:T(8,128)S(1)} %get-tuple-element.24), channel_id=1, source_target_pairs={{0,1},{1,0},{2,3},{3,2},{4,5},{5,4},{6,7},{7,6},{8,9},{9,8},{10,11... | collective-permute-start | bytes 1179656 | tf_op jit(solution)/shard_map/ppermute | solution.py:424
  63.8 7.4 %copy-start.3 = (f32[3,8,2048]{2,1,0:T(8,128)}, f32[3,8,2048]{2,1,0:T(8,128)S(1)}, u32[]{:S(2)}) copy-start(f32[3,8,2048]{2,1,0:T(8,128)S(1)} %get-tuple-element.31.mine) | copy-start | bytes 589828
  63.8 24.5 %collective-permute-start.15 = (f32[3,8,2048]{2,1,0:T(8,128)S(1)}, f32[3,8,2048]{2,1,0:T(8,128)S(1)}, u32[]{:S(2)}, u32[]{:S(2)}) collective-permute-start(f32[3,8,2048]{2,1,0:T(8,128)S(1)} %get-tuple-element.32), channel_id=1, source_target_pairs={{0,1},{1,0},{2,3},{3,2},{4,5},{5,4},{6,7},{7,6},{8,9},{9,8},{10,11... | collective-permute-start | bytes 589832 | tf_op jit(solution)/shard_map/ppermute | solution.py:424
  71.3 0.7 copy-start.4
  72.0 13.1 %collective-permute-start.11 = (f32[3,8,2048]{2,1,0:T(8,128)S(1)}, f32[3,8,2048]{2,1,0:T(8,128)S(1)}, u32[]{:S(2)}, u32[]{:S(2)}) collective-permute-start(f32[3,8,2048]{2,1,0:T(8,128)S(1)} %get-tuple-element.28), channel_id=1, source_target_pairs={{0,1},{1,0},{2,3},{3,2},{4,5},{5,4},{6,7},{7,6},{8,9},{9,8},{10,11... | collective-permute-start | bytes 589832 | tf_op jit(solution)/shard_map/ppermute | solution.py:424
  72.7 3.6 %collective-permute-start.16 = (f32[8,128]{1,0:T(8,128)S(1)}, f32[8,128]{1,0:T(8,128)S(1)}, u32[]{:S(2)}, u32[]{:S(2)}) collective-permute-start(f32[8,128]{1,0:T(8,128)S(1)} %add_add_fusion), channel_id=1, source_target_pairs={{0,2},{1,3},{2,0},{3,1},{4,6},{5,7},{6,4},{7,5},{8,10},{9,11},{10,... | collective-permute-start | bytes 12296 | tf_op jit(solution)/shard_map/ppermute | solution.py:429
  76.3 4.5 %collective-permute-start.17 = (f32[8,128]{1,0:T(8,128)S(1)}, f32[8,128]{1,0:T(8,128)S(1)}, u32[]{:S(2)}, u32[]{:S(2)}) collective-permute-start(f32[8,128]{1,0:T(8,128)S(1)} %add.45), channel_id=1, source_target_pairs={{0,4},{1,5},{2,6},{3,7},{4,0},{5,1},{6,2},{7,3},{8,12},{9,13},{10,... | collective-permute-start | bytes 12296 | tf_op jit(solution)/shard_map/ppermute | solution.py:429
  80.8 3.6 %collective-permute-start.18 = (f32[8,128]{1,0:T(8,128)S(1)}, f32[8,128]{1,0:T(8,128)S(1)}, u32[]{:S(2)}, u32[]{:S(2)}) collective-permute-start(f32[8,128]{1,0:T(8,128)S(1)} %add.46), channel_id=1, source_target_pairs={{0,1},{1,0},{2,3},{3,2},{4,5},{5,4},{6,7},{7,6},{8,9},{9,8},{10,11... | collective-permute-start | bytes 12296 | tf_op jit(solution)/shard_map/ppermute | solution.py:431
  85.1 0.7 copy-start.9
  85.1 0.8 copy-start.7
  88.4 0.7 copy-start.8

commit v4 on v3

--- a/solution.py
+++ b/solution.py
@@ -15,6 +15,8 @@
 TILE = 8
 BASE = 16
 ROWS = 48
+SMALL = 12 * 2**20
+WORK = 0.005
 
 VMEM = pl.BlockSpec(memory_space=pltpu.VMEM)
 SMEM = pl.BlockSpec(memory_space=pltpu.SMEM)
@@ -34,6 +36,10 @@
         (every[:cut], every[:cut], every[1 : cut - 1]),
         (every[cut:], every[cut - 2 :] + [0, 1], every[cut - 1 :] + [0]),
     )
+
+
+def after(arrays, first):
+    return lax.optimization_barrier((tuple(arrays), first))[0]
 
 
 def at(i):
@@ -64,87 +70,71 @@
     )(offspring)
 
 
-def fetch(index, slot, own, other, spans, outs, sems):
-    members = own.shape[0]
-    i = index[slot]
-
-    @pl.when(i < members)
-    def _():
-        for n, (first, count) in enumerate(spans):
-            pltpu.make_async_copy(
-                own.at[jnp.minimum(i, members - 1), :, :, pl.ds(first, count)], outs[n], sems.at[n]
-            ).start()
-
-    @pl.when(i >= members)
-    def _():
-        for n, (first, count) in enumerate(spans):
-            pltpu.make_async_copy(
-                other.at[jnp.maximum(i - members, 0), :, :, pl.ds(first, count)], outs[n], sems.at[n]
-            ).start()
-
-
-def arrive(own, spans, outs, sems):
-    for n, (first, count) in enumerate(spans):
-        pltpu.make_async_copy(own.at[0, :, :, pl.ds(first, count)], outs[n], sems.at[n]).wait()
-
-
-def pick_kernel(index, own, other, *refs, slot, spans, before):
-    n = len(spans)
+def pick_kernel(index, own, other, *outs, spans):
     members = own.shape[0]
     half = members // 2
     par = lax.axis_index("strip") % 2
-    earlier, refs = refs[: 2 * before], refs[2 * before :]
-    kept, given, refs = refs[:n], refs[n : 2 * n], refs[2 * n :]
-    sems = refs[-1]
-    fetch(index, (1 - par) * half + slot, own, other, spans, given, sems.at[0])
-    fetch(index, par * half + slot, own, other, spans, kept, sems.at[1])
-    arrive(own, spans, given, sems.at[0])
-    arrive(own, spans, kept, sems.at[1])
-    if slot < half - 1:
-        return
-    near, far = refs[0], refs[1]
-    ncol = own.shape[3] // LANES
-    per = ncol // 4
-
-    def edges(row):
-        for ref, blocks, these in (
-            (near, earlier[:before], kept),
-            (far, earlier[before:], given),
-        ):
-            for k in range(half):
+    refs, kept, given = list(outs), [], []
+    for s in spans:
+        kept.append([refs.pop(0) for _ in s])
+        given.append([refs.pop(0) for _ in s])
+    near, far = refs
+    wide = own.shape[3] // TILE
+
+    def copy(slot, k, pieces, edge):
+        i = index[slot]
+
+        def write(ref, m):
+            for (first, count), out in zip(spans[k], pieces):
+                out[...] = ref[m, :, :, pl.ds(first, count)]
+
+            def edges(row):
                 for f in range(3):
-                    for ct in range(ncol):
-                        if k < before:
-                            block, j = blocks[k], ct
-                        else:
-                            m = 0
-                            while ct * LANES >= spans[m][0] + spans[m][1]:
-                                m += 1
-                            block, j = these[m], ct - spans[m][0] // LANES
-                        q = (k * 3 + f) * 4 + ct // per
-                        ref[q : q + 1, at(ct % per)] = block[f, row : row + 1, at(j)]
-
-    @pl.when(par == 0)
-    def _():
-        edges(TILE - 1)
-
-    @pl.when(par == 1)
-    def _():
-        edges(0)
-
-
-def pick(index, own, other, slot, slots, spans, earlier):
+                    for q in range(TILE):
+                        edge[k * 3 + f, q : q + 1, :] = ref[
+                            m, f, row : row + 1, q * wide : (q + 1) * wide
+                        ]
+
+            @pl.when(par == 0)
+            def _():
+                edges(TILE - 1)
+
+            @pl.when(par == 1)
+            def _():
+                edges(0)
+
+        @pl.when(i < members)
+        def _():
+            write(own, jnp.minimum(i, members - 1))
+
+        @pl.when(i >= members)
+        def _():
+            write(other, jnp.maximum(i - members, 0))
+
+    for k in range(half):
+        copy((1 - par) * half + k, k, given[k], far)
+        copy(par * half + k, k, kept[k], near)
+
+
+def pick(index, own, other, spans):
     shape, kind = own.shape[1:3], own.dtype
-    outs = [jax.ShapeDtypeStruct(shape + (c,), kind) for _, c in spans] * 2
-    if slot == slots - 1:
-        outs += [jax.ShapeDtypeStruct((12 * slots, own.shape[3] // 4), kind)] * 2
-    return pl.pallas_call(
-        functools.partial(pick_kernel, slot=slot, spans=spans, before=len(earlier) // 2),
+    outs = []
+    for s in spans:
+        outs += [jax.ShapeDtypeStruct(shape + (c,), kind) for _, c in s] * 2
+    outs += [jax.ShapeDtypeStruct((3 * len(spans), TILE, own.shape[3] // TILE), kind)] * 2
+    out = pl.pallas_call(
+        functools.partial(pick_kernel, spans=spans),
         out_shape=outs,
-        in_specs=[SMEM, ANY, ANY] + [VMEM] * len(earlier),
+        in_specs=[SMEM, VMEM, VMEM],
         out_specs=[VMEM] * len(outs),
-        scratch_shapes=[pltpu.SemaphoreType.DMA((2, len(spans)))],
-    )(index, own, other, *earlier)
+        compiler_params=pltpu.CompilerParams(vmem_limit_bytes=SMALL),
+    )(index, own, other)
+    kept, given = [], []
+    for s in spans:
+        kept.append(out[: len(s)])
+        given.append(out[len(s) : 2 * len(s)])
+        out = out[2 * len(s) :]
+    return kept, given, out[0], out[1]
 
 
 def evaluate(src, state, dst, cor_ref, start, tiles, kind):
@@ -199,7 +189,7 @@
     near, far, obs_own, obs_got, keep, send, misfit, state, s1, s2, cor_ref = refs[4 * parts :]
     strip = lax.axis_index("strip")
     par = strip % 2
-    per = ncol // 4
+    per = ncol // TILE
 
     def load(own_row, got_row, direct_row, passed_row, near_row, far_row):
         for i, ct in enumerate(worked):
@@ -212,9 +202,10 @@
             ):
                 state[:, i, row : row + TILE, :] = ref[p][:, :, at(j)]
             for ref, row in ((near, near_row), (far, far_row)):
-                for f in range(3):
-                    q = (slot * 3 + f) * 4 + ct // per
-                    state[f, i, row : row + 1, :] = ref[q : q + 1, at(ct % per)]
+                q = ct // per
+                state[:, i, row : row + 1, :] = ref[
+                    slot * 3 : slot * 3 + 3, q : q + 1, at(ct % per)
+                ]
 
     above, below = BASE - TILE, BASE + 2 * TILE
 
@@ -299,7 +290,7 @@
         out_specs=[VMEM] * 3,
         scratch_shapes=[field, field, field, pltpu.VMEM((ROWS, LANES), jnp.float32)],
         compiler_params=pltpu.CompilerParams(vmem_limit_bytes=24 * 2**20),
-        cost_estimate=cost(7.0 * len(worked) / 18),
+        cost_estimate=cost(WORK * len(worked)),
     )(*args)
 
 
@@ -320,46 +311,9 @@
         out_shape=jax.ShapeDtypeStruct((2 * slots, 3, TILE, ncol * LANES), jnp.float32),
         in_specs=[VMEM] * len(args),
         out_specs=VMEM,
+        compiler_params=pltpu.CompilerParams(vmem_limit_bytes=SMALL),
+        cost_estimate=cost(0.1),
     )(*args)
-
-
-def finish_kernel(before, mine, theirs, out, sems, *, runs, slot, slots):
-    par = lax.axis_index("strip") % 2
-    copies = []
-    for n, (first, start, count) in enumerate(runs):
-        for m, (ref, row) in enumerate(
-            ((mine, par * slots + slot), (theirs, (1 - par) * slots + slot))
-        ):
-            copies.append(
-                pltpu.make_async_copy(
-                    ref.at[:, :, pl.ds(first * LANES, count * LANES)],
-                    out.at[row, :, :, pl.ds(start * LANES, count * LANES)],
-                    sems.at[2 * n + m],
-                )
-            )
-    for c in copies:
-        c.start()
-    for c in copies:
-        c.wait()
-
-
-def finish(before, mine, theirs, slot, slots, piece, ncol):
-    kept = plan(ncol, slot, slots)[piece][2]
-    runs = []
-    for j, ct in enumerate(kept):
-        if j and ct == kept[j - 1] + 1:
-            first, start, count = runs[-1]
-            runs[-1] = (first, start, count + 1)
-        else:
-            runs.append((j, ct, 1))
-    return pl.pallas_call(
-        functools.partial(finish_kernel, runs=runs, slot=slot, slots=slots),
-        out_shape=jax.ShapeDtypeStruct(before.shape, before.dtype),
-        in_specs=[ANY, VMEM, VMEM],
-        out_specs=ANY,
-        scratch_shapes=[pltpu.SemaphoreType.DMA((2 * len(runs),))],
-        input_output_aliases={0: 0},
-    )(before, mine, theirs)
 
 
 def local(ensemble, offspring, observations, obs_cols, obs_precision):
@@ -385,22 +339,38 @@
     weight = obs_precision * (1.0 + 2.0 * (rows + 0.5) / total_rows)[:, None]
     obs_own = jnp.stack([observations, obs_cols.astype(jnp.float32), weight])
 
-    kept, given, got, direct, passed = [], [], [], [], []
-    earlier = []
+    spans = [
+        [(sent[0] * LANES, len(sent) * LANES) for sent, _, _ in plan(ncol, k, half)]
+        for k in range(half)
+    ]
+    kept, given, near, far = pick(index, ensemble, arrived, spans)
+    near = lax.ppermute(near, "strip", onward)
+    far = lax.ppermute(far, "strip", cross)
+
+    got, direct, passed = [], [], []
+    swapped = None
     for k in range(half):
-        parts = plan(ncol, k, half)
-        spans = [(sent[0] * LANES, len(sent) * LANES) for sent, _, _ in parts]
-        out = pick(index, ensemble, arrived, k, half, spans, [e[0] for e in kept + given])
-        n = len(parts)
-        kept.append(out[:n])
-        given.append(out[n : 2 * n])
-        rest = out[2 * n :]
-    near = lax.ppermute(rest[0], "strip", onward)
-    far = lax.ppermute(rest[1], "strip", cross)
-    for k in range(half):
-        got.append([lax.ppermute(g, "strip", swap) for g in given[k]])
-        direct.append([lax.ppermute(b, "strip", straight) for b in kept[k]])
-        passed.append([lax.ppermute(g, "strip", onward) for g in got[k]])
+        got.append([])
+        direct.append([])
+        passed.append([])
+        for p in range(len(spans[k])):
+            giving, keeping = given[k][p], kept[k][p]
+            if k > 0:
+                (giving,) = after((giving,), swapped)
+                (keeping,) = after((keeping,), passed[0][0] if p else (near, far))
+            swapped = lax.ppermute(giving, "strip", swap)
+            got[k].append(swapped)
+            direct[k].append(lax.ppermute(keeping, "strip", straight))
+            goes = swapped
+            if k == 0:
+                (goes,) = after((goes,), direct[0][0])
+            elif p > 0:
+                (goes,) = after((goes,), passed[0][0])
+            passed[k].append(lax.ppermute(goes, "strip", onward))
+    obs_got = lax.ppermute(obs_own, "strip", swap)
+
+    obs_got = lax.ppermute(obs_own, "strip", swap)
+
     obs_got = lax.ppermute(obs_own, "strip", swap)
 
     blocks, pieces, total = [], [], None
@@ -424,13 +394,18 @@
             blocks.append((keep, lax.ppermute(send, "strip", swap)))
             pieces.append((k, p))
             total = misfit if total is None else total + misfit
-    step = 2
-    while step < strips:
-        total = total + lax.ppermute(total, "strip", [(i, i ^ step) for i in range(strips)])
-        step *= 2
+    (total,) = after((total,), [b[1] for b in blocks[:-1]])
+    if strips == 8:
+        turn = [lax.ppermute(total, "strip", moved(step, step)) for step in (2, 4, 6)]
+        total = (total + turn[1]) + (turn[0] + turn[2])
+    else:
+        step = 2
+        while step < strips:
+            total = total + lax.ppermute(total, "strip", [(i, i ^ step) for i in range(strips)])
+            step *= 2
     total = total + lax.ppermute(total, "strip", swap)
-    state = gather(blocks[:-1], pieces[:-1], ncol, half)
-    state = finish(state, *blocks[-1], half - 1, half, pieces[-1][1], ncol)
+    state = gather(blocks, pieces, ncol, half)
+    (total,) = after((total,), state)
     log_weights = (-0.5 / (total_rows * obs_cols.shape[1])) * total[:members, 0]
     return (state, log_weights)
 

time: 91.1 us -> 82.5 us (0.906)
  Pallas kernels: 32.9 us -> 24.3 us
  local copies, waits for them, and re-layouts: 4.07 us -> 2.07 us
  starting transfers between devices: 29.9 us -> 31.1 us
  waiting for transfers between devices: 22.4 us -> 23.4 us
    pallas_call x3 -> x1, Pallas kernels: 8.11 us -> 0.78 us  [pick(): pl.pallas_call(functools.partial(pick_kernel, spans=spans), out_shape=out...]
    ppermute x13 -> x14, waiting for transfers between devices: 16.5 us -> 20.9 us  [the longest x3 8.65 us: local(): swapped = lax.ppermute(giving, 'strip', swap)]
    unnamed x26 -> x10, local copies, waits for them, and re-layouts: 4.07 us -> 2.07 us
    ppermute x1, waiting for transfers between devices: 2.33 us -> 0.48 us  [local(): total = total + lax.ppermute(total, 'strip', swap)]
    ppermute x1, waiting for transfers between devices: 1.67 us -> 0.01 us  [local(): obs_got = lax.ppermute(obs_own, 'strip', swap)]
    pallas_call x1, Pallas kernels: 2.45 us -> 1.26 us  [gather(): pl.pallas_call(functools.partial(gather_kernel, ncol=ncol, slots=slots, p...]
    ppermute x13 -> x14, starting transfers between devices: 20 us -> 21.1 us  [the longest x3 7.23 us: local(): swapped = lax.ppermute(giving, 'strip', swap)]
  transfers between devices with their start and end apart: 19 -> 20, of which waited for: 8 -> 7; matrix products, arithmetic and copies ran while one was open for 1% -> 0% of each run, Pallas kernels for 31% -> 29%
where the time goes in v4:
time: 82.5 us; the launch traced here: 82.3 us
  starting transfers between devices  31.1 us (38%)
  Pallas kernels  24.3 us (29%)
  waiting for transfers between devices  23.4 us (28%)
  local copies, waits for them, and re-layouts  2.07 us (3%)
    pallas_call x3, Pallas kernels, forecast(): pl.pallas_call(functools.partial(forecast_kernel, worked=worked, kept=kep...  21 us
    ppermute x3, waiting for transfers between devices, local(): swapped = lax.ppermute(giving, 'strip', swap)  8.65 us
    ppermute x3, starting transfers between devices, local(): swapped = lax.ppermute(giving, 'strip', swap)  7.23 us
    ppermute x1, waiting for transfers between devices, local(): near = lax.ppermute(near, 'strip', onward)  6.63 us
    ppermute x3, starting transfers between devices, local(): direct[k].append(lax.ppermute(keeping, 'strip', straight))  6.6 us
    ppermute x3, starting transfers between devices, local(): blocks.append((keep, lax.ppermute(send, 'strip', swap)))  4.02 us
    ppermute x3, starting transfers between devices, local(): lax.ppermute(total, 'strip', moved(step, step))  3.88 us
    ppermute x1, starting transfers between devices, local(): obs_got = lax.ppermute(obs_own, 'strip', swap)  3.66 us
  transfers between devices with their start and end apart: 20, of which 7 were waited for; matrix products, arithmetic and copies ran while one was open for 0% of the time, Pallas kernels for 29%

profile of v4, /device:TPU:0, one launch (start us, length us, event | category | flops | bytes accessed | tf_op | source)
XLA Modules:
  0.0 82.3 jit_solution(8334352521222157206)
XLA Ops:
  0.6 0.5 collective-permute-start
  1.1 1.2 %shard_map.68.index = s32[4]{0:T(128)} custom-call(s32[8]{0:T(128)} %offspring.1), custom_call_target="tpu_custom_call" | custom-call | tf_op jit(solution)/shard_map/pallas_call | solution.py:65
  2.4 2.0 %collective-permute-done.other = f32[4,3,8,4096]{3,2,1,0:T(8,128)S(1)} collective-permute-done((f32[4,3,8,4096]{3,2,1,0:T(8,128)}, f32[4,3,8,4096]{3,2,1,0:T(8,128)S(1)}, u32[]{:S(2)}, u32[]{:S(2)}) %collective-permute-start) | collective-permute-done | bytes 1572896 | tf_op jit(solution)/shard_map/ppermute | solution.py:335
  4.4 1.4 %copy-done = f32[4,3,8,4096]{3,2,1,0:T(8,128)S(1)} copy-done((f32[4,3,8,4096]{3,2,1,0:T(8,128)S(1)}, f32[4,3,8,4096]{3,2,1,0:T(8,128)}, u32[]{:S(2)}) %copy-start) | copy-done | bytes 1572888
  5.8 0.7 copy-done.1
  6.5 0.8 shard_map.69
  7.3 2.9 %collective-permute-start.1 = (f32[3,8,4096]{2,1,0:T(8,128)S(1)}, f32[3,8,4096]{2,1,0:T(8,128)S(1)}, u32[]{:S(2)}, u32[]{:S(2)}) collective-permute-start(f32[3,8,4096]{2,1,0:T(8,128)S(1)} %get-tuple-element.28), channel_id=1, source_target_pairs={{0,1},{1,0},{2,3},{3,2},{4,5},{5,4},{6,7},{7,6},{8,9},{9,8},{10,11... | collective-permute-start | bytes 1179656 | tf_op jit(solution)/shard_map/ppermute | solution.py:361
  10.2 3.6 %collective-permute-start.2 = (f32[3,8,4096]{2,1,0:T(8,128)S(1)}, f32[3,8,4096]{2,1,0:T(8,128)S(1)}, u32[]{:S(2)}, u32[]{:S(2)}) collective-permute-start(f32[3,8,4096]{2,1,0:T(8,128)S(1)} %get-tuple-element.27.refs_0_), channel_id=1, source_target_pairs={{0,6},{1,3},{2,0},{3,5},{4,2},{5,7},{6,4},{7,1},{8,14},{9,11},{10,... | collective-permute-start | bytes 1179656 | tf_op jit(solution)/shard_map/ppermute | solution.py:363
  13.8 5.8 %collective-permute-done.1.refs_1_ = f32[3,8,4096]{2,1,0:T(8,128)S(1)} collective-permute-done((f32[3,8,4096]{2,1,0:T(8,128)S(1)}, f32[3,8,4096]{2,1,0:T(8,128)S(1)}, u32[]{:S(2)}, u32[]{:S(2)}) %collective-permute-start.1) | collective-permute-done | bytes 393248 | tf_op jit(solution)/shard_map/ppermute | solution.py:361
  19.6 3.0 %collective-permute-done.2.refs_2_ = f32[3,8,4096]{2,1,0:T(8,128)S(1)} collective-permute-done((f32[3,8,4096]{2,1,0:T(8,128)S(1)}, f32[3,8,4096]{2,1,0:T(8,128)S(1)}, u32[]{:S(2)}, u32[]{:S(2)}) %collective-permute-start.2) | collective-permute-done | bytes 393248 | tf_op jit(solution)/shard_map/ppermute | solution.py:363
  22.6 2.5 %collective-permute-start.8 = (f32[3,8,2304]{2,1,0:T(8,128)S(1)}, f32[3,8,2304]{2,1,0:T(8,128)S(1)}, u32[]{:S(2)}, u32[]{:S(2)}) collective-permute-start(f32[3,8,2304]{2,1,0:T(8,128)S(1)} %get-tuple-element.36), channel_id=1, source_target_pairs={{0,1},{1,0},{2,3},{3,2},{4,5},{5,4},{6,7},{7,6},{8,9},{9,8},{10,11... | collective-permute-start | bytes 663560 | tf_op jit(solution)/shard_map/ppermute | solution.py:361
  25.3 0.3 collective-permute-start.4
  25.5 1.2 %collective-permute-start.5 = (f32[6,8,512]{2,1,0:T(8,128)S(1)}, f32[6,8,512]{2,1,0:T(8,128)S(1)}, u32[]{:S(2)}, u32[]{:S(2)}) collective-permute-start(f32[6,8,512]{2,1,0:T(8,128)S(1)} %get-tuple-element.31), channel_id=1, source_target_pairs={{0,3},{1,6},{2,5},{3,0},{4,7},{5,2},{6,1},{7,4},{8,11},{9,14},{10,... | collective-permute-start | bytes 294920 | tf_op jit(solution)/shard_map/ppermute | solution.py:348
  26.7 2.8 %collective-permute-done.8.refs_1_.refs_2_ = f32[3,8,2304]{2,1,0:T(8,128)S(1)} collective-permute-done((f32[3,8,2304]{2,1,0:T(8,128)S(1)}, f32[3,8,2304]{2,1,0:T(8,128)S(1)}, u32[]{:S(2)}, u32[]{:S(2)}) %collective-permute-start.8) | collective-permute-done | bytes 221216 | tf_op jit(solution)/shard_map/ppermute | solution.py:361
  29.6 1.7 %collective-permute-start.12 = (f32[3,8,1792]{2,1,0:T(8,128)S(1)}, f32[3,8,1792]{2,1,0:T(8,128)S(1)}, u32[]{:S(2)}, u32[]{:S(2)}) collective-permute-start(f32[3,8,1792]{2,1,0:T(8,128)S(1)} %get-tuple-element.42), channel_id=1, source_target_pairs={{0,1},{1,0},{2,3},{3,2},{4,5},{5,4},{6,7},{7,6},{8,9},{9,8},{10,11... | collective-permute-start | bytes 516104 | tf_op jit(solution)/shard_map/ppermute | solution.py:361
  31.3 6.6 %collective-permute-done.4.refs_4_.refs_8_ = f32[6,8,512]{2,1,0:T(8,128)S(1)} collective-permute-done((f32[6,8,512]{2,1,0:T(8,128)S(1)}, f32[6,8,512]{2,1,0:T(8,128)S(1)}, u32[]{:S(2)}, u32[]{:S(2)}) %collective-permute-start.4) | collective-permute-done | bytes 98336 | tf_op jit(solution)/shard_map/ppermute | solution.py:347
  38.0 2.8 %collective-permute-start.9 = (f32[3,8,2304]{2,1,0:T(8,128)S(1)}, f32[3,8,2304]{2,1,0:T(8,128)S(1)}, u32[]{:S(2)}, u32[]{:S(2)}) collective-permute-start(f32[3,8,2304]{2,1,0:T(8,128)S(1)} %get-tuple-element.37.refs_0_), channel_id=1, source_target_pairs={{0,6},{1,3},{2,0},{3,5},{4,2},{5,7},{6,4},{7,1},{8,14},{9,11},{10,... | collective-permute-start | bytes 663560 | tf_op jit(solution)/shard_map/ppermute | solution.py:363
  40.7 3.7 %collective-permute-start.6 = (f32[3,8,128]{2,1,0:T(8,128)S(1)}, f32[3,8,128]{2,1,0:T(8,128)S(1)}, u32[]{:S(2)}, u32[]{:S(2)}) collective-permute-start(f32[3,8,128]{2,1,0:T(8,128)S(1)} %pad_maximum_fusion.refs_6_.refs_10_), channel_id=1, source_target_pairs={{0,1},{1,0},{2,3},{3,2},{4,5},{5,4},{6,7},{7,6},{8,9},{9,8},{10,11... | collective-permute-start | bytes 36872 | tf_op jit(solution)/shard_map/ppermute | solution.py:374
  44.4 0.2 collective-permute-start.13
  44.6 1.8 %collective-permute-start.14 = (f32[3,8,1792]{2,1,0:T(8,128)S(1)}, f32[3,8,1792]{2,1,0:T(8,128)S(1)}, u32[]{:S(2)}, u32[]{:S(2)}) collective-permute-start(f32[3,8,1792]{2,1,0:T(8,128)S(1)} %collective-permute-done.12.refs_3_), channel_id=1, source_target_pairs={{0,2},{1,7},{2,4},{3,1},{4,6},{5,3},{6,0},{7,5},{8,10},{9,15},{10,... | collective-permute-start | bytes 516104 | tf_op jit(solution)/shard_map/ppermute | solution.py:369
  46.4 8.9 %shard_map.70 = (f32[3,8,4096]{2,1,0:T(8,128)S(1)}, f32[3,8,4096]{2,1,0:T(8,128)S(1)}, f32[8,128]{1,0:T(8,128)S(1)}) custom-call(f32[3,8,4096]{2,1,0:T(8,128)S(1)} %get-tuple-element.27.refs_0_, f32[3,8,4096]{2,1,0:T(8,128)S(1)} %collective-permute-done.1.refs_1_, f32[3,8,4096]{2,1,0:T(8,128)S(1)} %collective-permute-done.2.refs_2_, ...), custom_call_target="tpu_custom_call" | custom-call | bytes 480000 | tf_op jit(solution)/shard_map/pallas_call | solution.py:276
  55.3 1.9 %collective-permute-start.7 = (f32[3,8,4096]{2,1,0:T(8,128)S(1)}, f32[3,8,4096]{2,1,0:T(8,128)S(1)}, u32[]{:S(2)}, u32[]{:S(2)}) collective-permute-start(f32[3,8,4096]{2,1,0:T(8,128)S(1)} %get-tuple-element.33), channel_id=1, source_target_pairs={{0,1},{1,0},{2,3},{3,2},{4,5},{5,4},{6,7},{7,6},{8,9},{9,8},{10,11... | collective-permute-start | bytes 1179656 | tf_op jit(solution)/shard_map/ppermute | solution.py:394
  57.3 6.1 %shard_map.71 = (f32[3,8,2048]{2,1,0:T(8,128)S(1)}, f32[3,8,2048]{2,1,0:T(8,128)S(1)}, f32[8,128]{1,0:T(8,128)S(1)}) custom-call(f32[3,8,2304]{2,1,0:T(8,128)S(1)} %get-tuple-element.37.refs_0_, f32[3,8,2304]{2,1,0:T(8,128)S(1)} %collective-permute-done.8.refs_1_.refs_2_, f32[3,8,2304]{2,1,0:T(8,128)S(1)} %collective-permute-done.9.refs_2_.refs_4_, ...), custom_call_target="tpu_custom_call" | custom-call | bytes 270000 | tf_op jit(solution)/shard_map/pallas_call | solution.py:276
  63.3 0.2 collective-permute-start.11
  63.6 6.1 %shard_map.72 = (f32[3,8,2048]{2,1,0:T(8,128)S(1)}, f32[3,8,2048]{2,1,0:T(8,128)S(1)}, f32[8,128]{1,0:T(8,128)S(1)}) custom-call(f32[3,8,2304]{2,1,0:T(8,128)S(1)} %get-tuple-element.37.refs_0_, f32[3,8,1792]{2,1,0:T(8,128)S(1)} %get-tuple-element.43.refs_1_, f32[3,8,2304]{2,1,0:T(8,128)S(1)} %collective-permute-done.8.refs_1_.refs_2_, ...), custom_call_target="tpu_custom_call" | custom-call | bytes 270000 | tf_op jit(solution)/shard_map/pallas_call | solution.py:276
  69.8 3.8 %collective-permute-start.18 = (f32[8,128]{1,0:T(8,128)S(1)}, f32[8,128]{1,0:T(8,128)S(1)}, u32[]{:S(2)}, u32[]{:S(2)}) collective-permute-start(f32[8,128]{1,0:T(8,128)S(1)} %add_add_fusion.1), channel_id=1, source_target_pairs={{0,6},{1,7},{2,0},{3,1},{4,2},{5,3},{6,4},{7,5},{8,14},{9,15},{10,... | collective-permute-start | bytes 12296 | tf_op jit(solution)/shard_map/ppermute | solution.py:399
  73.6 1.9 %collective-permute-start.15 = (f32[3,8,2048]{2,1,0:T(8,128)S(1)}, f32[3,8,2048]{2,1,0:T(8,128)S(1)}, u32[]{:S(2)}, u32[]{:S(2)}) collective-permute-start(f32[3,8,2048]{2,1,0:T(8,128)S(1)} %get-tuple-element.46), channel_id=1, source_target_pairs={{0,1},{1,0},{2,3},{3,2},{4,5},{5,4},{6,7},{7,6},{8,9},{9,8},{10,11... | collective-permute-start | bytes 589832 | tf_op jit(solution)/shard_map/ppermute | solution.py:394
  75.4 2.6 %collective-permute-done.16 = f32[8,128]{1,0:T(8,128)S(1)} collective-permute-done((f32[8,128]{1,0:T(8,128)S(1)}, f32[8,128]{1,0:T(8,128)S(1)}, u32[]{:S(2)}, u32[]{:S(2)}) %collective-permute-start.16) | collective-permute-done | bytes 4128 | tf_op jit(solution)/shard_map/ppermute | solution.py:399
  78.1 1.9 %collective-permute-start.19 = (f32[8,128]{1,0:T(8,128)S(1)}, f32[8,128]{1,0:T(8,128)S(1)}, u32[]{:S(2)}, u32[]{:S(2)}) collective-permute-start(f32[8,128]{1,0:T(8,128)S(1)} %add_add_fusion), channel_id=1, source_target_pairs={{0,1},{1,0},{2,3},{3,2},{4,5},{5,4},{6,7},{7,6},{8,9},{9,8},{10,11... | collective-permute-start | bytes 12296 | tf_op jit(solution)/shard_map/ppermute | solution.py:406
  80.0 1.3 %shard_map.73 = f32[4,3,8,4096]{3,2,1,0:T(8,128)} custom-call(f32[3,8,4096]{2,1,0:T(8,128)S(1)} %get-tuple-element.32.refs_0_, f32[3,8,4096]{2,1,0:T(8,128)S(1)} %collective-permute-done.7.refs_1_, f32[3,8,2048]{2,1,0:T(8,128)S(1)} %get-tuple-element.38.refs_2_, f32[3,8,2048]{2,1,0:T(8,128)S(1)} %collective-permute-done.11.refs_3_, ...), custom_call_target="tpu_custom_call" | custom-call | bytes 300000 | tf_op jit(solution)/shard_map/pallas_call | solution.py:309
  81.2 0.5 collective-permute-done.19
  81.7 0.6 multiply_reduce_fusion
  (32 shorter events, 0.3 us)
Async XLA Ops:
  0.6 3.8 %collective-permute-start = (f32[4,3,8,4096]{3,2,1,0:T(8,128)}, f32[4,3,8,4096]{3,2,1,0:T(8,128)S(1)}, u32[]{:S(2)}, u32[]{:S(2)}) collective-permute-start(f32[4,3,8,4096]{3,2,1,0:T(8,128)} %own.1), channel_id=1, source_target_pairs={{0,8},{8,0},{1,9},{9,1},{2,10},{10,2},{3,11},{11,3},{4,12},{12,4},... | collective-permute-start | bytes 4718600 | tf_op jit(solution)/shard_map/ppermute | solution.py:335
  4.4 1.4 %copy-start = (f32[4,3,8,4096]{3,2,1,0:T(8,128)S(1)}, f32[4,3,8,4096]{3,2,1,0:T(8,128)}, u32[]{:S(2)}) copy-start(f32[4,3,8,4096]{3,2,1,0:T(8,128)} %own.1) | copy-start | bytes 4718596
  5.8 0.7 copy-start.1
  6.5 18.7 %copy-start.2 = (f32[8,128]{1,0:T(8,128)S(1)}, f32[8,128]{1,0:T(8,128)}, u32[]{:S(2)}) copy-start(f32[8,128]{1,0:T(8,128)} %param.9) | copy-start | bytes 12292
  6.5 24.9 %copy-start.3 = (s32[8,128]{1,0:T(8,128)S(1)}, s32[8,128]{1,0:T(8,128)}, u32[]{:S(2)}) copy-start(s32[8,128]{1,0:T(8,128)} %param.8) | copy-start | bytes 12292
  6.5 34.3 %copy-start.4 = (f32[8,128]{1,0:T(8,128)S(1)}, f32[8,128]{1,0:T(8,128)}, u32[]{:S(2)}) copy-start(f32[8,128]{1,0:T(8,128)} %param.7) | copy-start | bytes 12292
  7.3 12.4 %collective-permute-start.1 = (f32[3,8,4096]{2,1,0:T(8,128)S(1)}, f32[3,8,4096]{2,1,0:T(8,128)S(1)}, u32[]{:S(2)}, u32[]{:S(2)}) collective-permute-start(f32[3,8,4096]{2,1,0:T(8,128)S(1)} %get-tuple-element.28), channel_id=1, source_target_pairs={{0,1},{1,0},{2,3},{3,2},{4,5},{5,4},{6,7},{7,6},{8,9},{9,8},{10,11... | collective-permute-start | bytes 1179656 | tf_op jit(solution)/shard_map/ppermute | solution.py:361
  10.2 12.4 %collective-permute-start.2 = (f32[3,8,4096]{2,1,0:T(8,128)S(1)}, f32[3,8,4096]{2,1,0:T(8,128)S(1)}, u32[]{:S(2)}, u32[]{:S(2)}) collective-permute-start(f32[3,8,4096]{2,1,0:T(8,128)S(1)} %get-tuple-element.27.refs_0_), channel_id=1, source_target_pairs={{0,6},{1,3},{2,0},{3,5},{4,2},{5,7},{6,4},{7,1},{8,14},{9,11},{10,... | collective-permute-start | bytes 1179656 | tf_op jit(solution)/shard_map/ppermute | solution.py:363
  22.6 21.8 %collective-permute-start.3 = (f32[3,8,4096]{2,1,0:T(8,128)S(1)}, f32[3,8,4096]{2,1,0:T(8,128)S(1)}, u32[]{:S(2)}, u32[]{:S(2)}) collective-permute-start(f32[3,8,4096]{2,1,0:T(8,128)S(1)} %collective-permute-done.1.refs_1_), channel_id=1, source_target_pairs={{0,2},{1,7},{2,4},{3,1},{4,6},{5,3},{6,0},{7,5},{8,10},{9,15},{10,... | collective-permute-start | bytes 1179656 | tf_op jit(solution)/shard_map/ppermute | solution.py:369
  22.6 6.9 %collective-permute-start.8 = (f32[3,8,2304]{2,1,0:T(8,128)S(1)}, f32[3,8,2304]{2,1,0:T(8,128)S(1)}, u32[]{:S(2)}, u32[]{:S(2)}) collective-permute-start(f32[3,8,2304]{2,1,0:T(8,128)S(1)} %get-tuple-element.36), channel_id=1, source_target_pairs={{0,1},{1,0},{2,3},{3,2},{4,5},{5,4},{6,7},{7,6},{8,9},{9,8},{10,11... | collective-permute-start | bytes 663560 | tf_op jit(solution)/shard_map/ppermute | solution.py:361
  25.3 12.7 %collective-permute-start.4 = (f32[6,8,512]{2,1,0:T(8,128)S(1)}, f32[6,8,512]{2,1,0:T(8,128)S(1)}, u32[]{:S(2)}, u32[]{:S(2)}) collective-permute-start(f32[6,8,512]{2,1,0:T(8,128)S(1)} %get-tuple-element.30), channel_id=1, source_target_pairs={{0,2},{1,7},{2,4},{3,1},{4,6},{5,3},{6,0},{7,5},{8,10},{9,15},{10,... | collective-permute-start | bytes 294920 | tf_op jit(solution)/shard_map/ppermute | solution.py:347
  25.5 12.4 %collective-permute-start.5 = (f32[6,8,512]{2,1,0:T(8,128)S(1)}, f32[6,8,512]{2,1,0:T(8,128)S(1)}, u32[]{:S(2)}, u32[]{:S(2)}) collective-permute-start(f32[6,8,512]{2,1,0:T(8,128)S(1)} %get-tuple-element.31), channel_id=1, source_target_pairs={{0,3},{1,6},{2,5},{3,0},{4,7},{5,2},{6,1},{7,4},{8,11},{9,14},{10,... | collective-permute-start | bytes 294920 | tf_op jit(solution)/shard_map/ppermute | solution.py:348
  29.6 15.1 %collective-permute-start.12 = (f32[3,8,1792]{2,1,0:T(8,128)S(1)}, f32[3,8,1792]{2,1,0:T(8,128)S(1)}, u32[]{:S(2)}, u32[]{:S(2)}) collective-permute-start(f32[3,8,1792]{2,1,0:T(8,128)S(1)} %get-tuple-element.42), channel_id=1, source_target_pairs={{0,1},{1,0},{2,3},{3,2},{4,5},{5,4},{6,7},{7,6},{8,9},{9,8},{10,11... | collective-permute-start | bytes 516104 | tf_op jit(solution)/shard_map/ppermute | solution.py:361
  38.0 19.3 %collective-permute-start.9 = (f32[3,8,2304]{2,1,0:T(8,128)S(1)}, f32[3,8,2304]{2,1,0:T(8,128)S(1)}, u32[]{:S(2)}, u32[]{:S(2)}) collective-permute-start(f32[3,8,2304]{2,1,0:T(8,128)S(1)} %get-tuple-element.37.refs_0_), channel_id=1, source_target_pairs={{0,6},{1,3},{2,0},{3,5},{4,2},{5,7},{6,4},{7,1},{8,14},{9,11},{10,... | collective-permute-start | bytes 663560 | tf_op jit(solution)/shard_map/ppermute | solution.py:363
  40.7 16.5 %collective-permute-start.10 = (f32[3,8,2304]{2,1,0:T(8,128)S(1)}, f32[3,8,2304]{2,1,0:T(8,128)S(1)}, u32[]{:S(2)}, u32[]{:S(2)}) collective-permute-start(f32[3,8,2304]{2,1,0:T(8,128)S(1)} %collective-permute-done.8.refs_1_.refs_2_), channel_id=1, source_target_pairs={{0,2},{1,7},{2,4},{3,1},{4,6},{5,3},{6,0},{7,5},{8,10},{9,15},{10,... | collective-permute-start | bytes 663560 | tf_op jit(solution)/shard_map/ppermute | solution.py:369
  40.7 5.7 %collective-permute-start.6 = (f32[3,8,128]{2,1,0:T(8,128)S(1)}, f32[3,8,128]{2,1,0:T(8,128)S(1)}, u32[]{:S(2)}, u32[]{:S(2)}) collective-permute-start(f32[3,8,128]{2,1,0:T(8,128)S(1)} %pad_maximum_fusion.refs_6_.refs_10_), channel_id=1, source_target_pairs={{0,1},{1,0},{2,3},{3,2},{4,5},{5,4},{6,7},{7,6},{8,9},{9,8},{10,11... | collective-permute-start | bytes 36872 | tf_op jit(solution)/shard_map/ppermute | solution.py:374
  44.4 19.2 %collective-permute-start.13 = (f32[3,8,1792]{2,1,0:T(8,128)S(1)}, f32[3,8,1792]{2,1,0:T(8,128)S(1)}, u32[]{:S(2)}, u32[]{:S(2)}) collective-permute-start(f32[3,8,1792]{2,1,0:T(8,128)S(1)} %get-tuple-element.43.refs_1_), channel_id=1, source_target_pairs={{0,6},{1,3},{2,0},{3,5},{4,2},{5,7},{6,4},{7,1},{8,14},{9,11},{10,... | collective-permute-start | bytes 516104 | tf_op jit(solution)/shard_map/ppermute | solution.py:363
  44.6 18.9 %collective-permute-start.14 = (f32[3,8,1792]{2,1,0:T(8,128)S(1)}, f32[3,8,1792]{2,1,0:T(8,128)S(1)}, u32[]{:S(2)}, u32[]{:S(2)}) collective-permute-start(f32[3,8,1792]{2,1,0:T(8,128)S(1)} %collective-permute-done.12.refs_3_), channel_id=1, source_target_pairs={{0,2},{1,7},{2,4},{3,1},{4,6},{5,3},{6,0},{7,5},{8,10},{9,15},{10,... | collective-permute-start | bytes 516104 | tf_op jit(solution)/shard_map/ppermute | solution.py:369
  55.3 14.4 %collective-permute-start.7 = (f32[3,8,4096]{2,1,0:T(8,128)S(1)}, f32[3,8,4096]{2,1,0:T(8,128)S(1)}, u32[]{:S(2)}, u32[]{:S(2)}) collective-permute-start(f32[3,8,4096]{2,1,0:T(8,128)S(1)} %get-tuple-element.33), channel_id=1, source_target_pairs={{0,1},{1,0},{2,3},{3,2},{4,5},{5,4},{6,7},{7,6},{8,9},{9,8},{10,11... | collective-permute-start | bytes 1179656 | tf_op jit(solution)/shard_map/ppermute | solution.py:394
  63.3 6.3 %collective-permute-start.11 = (f32[3,8,2048]{2,1,0:T(8,128)S(1)}, f32[3,8,2048]{2,1,0:T(8,128)S(1)}, u32[]{:S(2)}, u32[]{:S(2)}) collective-permute-start(f32[3,8,2048]{2,1,0:T(8,128)S(1)} %get-tuple-element.39), channel_id=1, source_target_pairs={{0,1},{1,0},{2,3},{3,2},{4,5},{5,4},{6,7},{7,6},{8,9},{9,8},{10,11... | collective-permute-start | bytes 589832 | tf_op jit(solution)/shard_map/ppermute | solution.py:394
  69.7 5.7 %collective-permute-start.17 = (f32[8,128]{1,0:T(8,128)S(1)}, f32[8,128]{1,0:T(8,128)S(1)}, u32[]{:S(2)}, u32[]{:S(2)}) collective-permute-start(f32[8,128]{1,0:T(8,128)S(1)} %add_add_fusion.1), channel_id=1, source_target_pairs={{0,2},{1,3},{2,4},{3,5},{4,6},{5,7},{6,0},{7,1},{8,10},{9,11},{10,... | collective-permute-start | bytes 12296 | tf_op jit(solution)/shard_map/ppermute | solution.py:399
  69.8 5.7 %collective-permute-start.18 = (f32[8,128]{1,0:T(8,128)S(1)}, f32[8,128]{1,0:T(8,128)S(1)}, u32[]{:S(2)}, u32[]{:S(2)}) collective-permute-start(f32[8,128]{1,0:T(8,128)S(1)} %add_add_fusion.1), channel_id=1, source_target_pairs={{0,6},{1,7},{2,0},{3,1},{4,2},{5,3},{6,4},{7,5},{8,14},{9,15},{10,... | collective-permute-start | bytes 12296 | tf_op jit(solution)/shard_map/ppermute | solution.py:399
  73.6 4.5 %collective-permute-start.16 = (f32[8,128]{1,0:T(8,128)S(1)}, f32[8,128]{1,0:T(8,128)S(1)}, u32[]{:S(2)}, u32[]{:S(2)}) collective-permute-start(f32[8,128]{1,0:T(8,128)S(1)} %add_add_fusion.1), channel_id=1, source_target_pairs={{0,4},{1,5},{2,6},{3,7},{4,0},{5,1},{6,2},{7,3},{8,12},{9,13},{10,... | collective-permute-start | bytes 12296 | tf_op jit(solution)/shard_map/ppermute | solution.py:399
  73.6 6.4 %collective-permute-start.15 = (f32[3,8,2048]{2,1,0:T(8,128)S(1)}, f32[3,8,2048]{2,1,0:T(8,128)S(1)}, u32[]{:S(2)}, u32[]{:S(2)}) collective-permute-start(f32[3,8,2048]{2,1,0:T(8,128)S(1)} %get-tuple-element.46), channel_id=1, source_target_pairs={{0,1},{1,0},{2,3},{3,2},{4,5},{5,4},{6,7},{7,6},{8,9},{9,8},{10,11... | collective-permute-start | bytes 589832 | tf_op jit(solution)/shard_map/ppermute | solution.py:394
  78.1 3.6 %collective-permute-start.19 = (f32[8,128]{1,0:T(8,128)S(1)}, f32[8,128]{1,0:T(8,128)S(1)}, u32[]{:S(2)}, u32[]{:S(2)}) collective-permute-start(f32[8,128]{1,0:T(8,128)S(1)} %add_add_fusion), channel_id=1, source_target_pairs={{0,1},{1,0},{2,3},{3,2},{4,5},{5,4},{6,7},{7,6},{8,9},{9,8},{10,11... | collective-permute-start | bytes 12296 | tf_op jit(solution)/shard_map/ppermute | solution.py:406

commit v5 on v4

--- a/solution.py
+++ b/solution.py
@@ -46,7 +46,7 @@
     return slice(i * LANES, (i + 1) * LANES)
 
 
-def index_kernel(offspring, index):
+def index_kernel(offspring, ensemble, index):
     members = index.shape[0]
     here = lax.axis_index("particle")
     cumulative = []
@@ -61,13 +61,15 @@
         index[k] = jnp.clip(jnp.where(inside, own, members + other), 0, 2 * members - 1)
 
 
-def sources(offspring, members):
+def sources(offspring, ensemble):
+    members = ensemble.shape[0]
     return pl.pallas_call(
         index_kernel,
         out_shape=jax.ShapeDtypeStruct((members,), jnp.int32),
-        in_specs=[SMEM],
+        in_specs=[SMEM, VMEM],
         out_specs=SMEM,
-    )(offspring)
+        compiler_params=pltpu.CompilerParams(vmem_limit_bytes=SMALL),
+    )(offspring, ensemble)
 
 
 def pick_kernel(index, own, other, *outs, spans):
@@ -259,7 +261,7 @@
             here = here | found
         gap = obs[0] - picked
         total = total + jnp.where(here, obs[2] * gap * gap, 0.0)
-    at_slot = lax.broadcasted_iota(jnp.int32, (TILE, LANES), 0) == par * slots + slot
+    at_slot = lax.broadcasted_iota(jnp.int32, (TILE, LANES), 1) == par * slots + slot
     misfit[...] = jnp.where(at_slot, jnp.sum(total), 0.0)
 
 
@@ -333,7 +335,7 @@
     cross = moved(3, -3)
 
     arrived = lax.ppermute(ensemble, "particle", [(0, 1), (1, 0)])
-    index = sources(offspring, members)
+    index = sources(offspring, ensemble)
 
     rows = (strip * strip_rows + jnp.arange(strip_rows, dtype=jnp.int32)).astype(jnp.float32)
     weight = obs_precision * (1.0 + 2.0 * (rows + 0.5) / total_rows)[:, None]
@@ -348,25 +350,26 @@
     far = lax.ppermute(far, "strip", cross)
 
     got, direct, passed = [], [], []
-    swapped = None
+    swapped, held = None, (near, far)
     for k in range(half):
         got.append([])
         direct.append([])
         passed.append([])
         for p in range(len(spans[k])):
             giving, keeping = given[k][p], kept[k][p]
-            if k > 0:
+            if swapped is not None:
                 (giving,) = after((giving,), swapped)
-                (keeping,) = after((keeping,), passed[0][0] if p else (near, far))
+            if k > 0 and p > 0:
+                (keeping,) = after((keeping,), direct[k][p - 1])
             swapped = lax.ppermute(giving, "strip", swap)
             got[k].append(swapped)
             direct[k].append(lax.ppermute(keeping, "strip", straight))
-            goes = swapped
-            if k == 0:
-                (goes,) = after((goes,), direct[0][0])
-            elif p > 0:
-                (goes,) = after((goes,), passed[0][0])
+            (goes,) = after((swapped,), (direct[k][p], held))
             passed[k].append(lax.ppermute(goes, "strip", onward))
+            if k > 0:
+                held = passed[0][-1]
+    obs_got = lax.ppermute(obs_own, "strip", swap)
+
     obs_got = lax.ppermute(obs_own, "strip", swap)
 
     obs_got = lax.ppermute(obs_own, "strip", swap)
@@ -406,7 +409,7 @@
     total = total + lax.ppermute(total, "strip", swap)
     state = gather(blocks, pieces, ncol, half)
     (total,) = after((total,), state)
-    log_weights = (-0.5 / (total_rows * obs_cols.shape[1])) * total[:members, 0]
+    log_weights = (-0.5 / (total_rows * obs_cols.shape[1])) * total[0, :members]
     return (state, log_weights)
 
 

time: 82.5 us -> 81 us (0.982)
  waiting for transfers between devices: 23.4 us -> 21.4 us
    ppermute x3, waiting for transfers between devices: 8.65 us -> 0.01 us  [local(): swapped = lax.ppermute(giving, 'strip', swap)]
    ppermute x3, starting transfers between devices: 6.6 us -> 11.8 us  [local(): direct[k].append(lax.ppermute(keeping, 'strip', straight))]
    ppermute x3, waiting for transfers between devices: 2.96 us -> 7.36 us  [local(): direct[k].append(lax.ppermute(keeping, 'strip', straight))]
    ppermute x1, starting transfers between devices: 3.66 us -> 1.02 us  [local(): obs_got = lax.ppermute(obs_own, 'strip', swap)]
    ppermute x1, waiting for transfers between devices: 6.63 us -> 8.77 us  [local(): near = lax.ppermute(near, 'strip', onward)]
    ppermute x1, waiting for transfers between devices: 2 us -> 0.01 us  [local(): arrived = lax.ppermute(ensemble, 'particle', [(0, 1), (1, 0)])]
    ppermute x3, starting transfers between devices: 7.23 us -> 5.63 us  [local(): swapped = lax.ppermute(giving, 'strip', swap)]
    ppermute x1, starting transfers between devices: 1.18 us -> 0.01 us  [local(): far = lax.ppermute(far, 'strip', cross)]
where the time goes in v5:
time: 81 us; the launch traced here: 80.8 us
  starting transfers between devices  31.6 us (39%)
  Pallas kernels  24.3 us (30%)
  waiting for transfers between devices  21.4 us (26%)
  local copies, waits for them, and re-layouts  2.24 us (3%)
    pallas_call x3, Pallas kernels, forecast(): pl.pallas_call(functools.partial(forecast_kernel, worked=worked, kept=kep...  21.1 us
    ppermute x3, starting transfers between devices, local(): direct[k].append(lax.ppermute(keeping, 'strip', straight))  11.8 us
    ppermute x1, waiting for transfers between devices, local(): near = lax.ppermute(near, 'strip', onward)  8.77 us
    ppermute x3, waiting for transfers between devices, local(): direct[k].append(lax.ppermute(keeping, 'strip', straight))  7.36 us
    ppermute x3, starting transfers between devices, local(): swapped = lax.ppermute(giving, 'strip', swap)  5.63 us
    ppermute x3, starting transfers between devices, local(): lax.ppermute(total, 'strip', moved(step, step))  4.29 us
    ppermute x3, starting transfers between devices, local(): blocks.append((keep, lax.ppermute(send, 'strip', swap)))  4.18 us
    ppermute x3, waiting for transfers between devices, local(): lax.ppermute(total, 'strip', moved(step, step))  2.76 us
  transfers between devices with their start and end apart: 20, of which 7 were waited for; matrix products, arithmetic and copies ran while one was open for 0% of the time, Pallas kernels for 29%

profile of v5, /device:TPU:0, one launch (start us, length us, event | category | flops | bytes accessed | tf_op | source)
XLA Modules:
  0.0 80.8 jit_solution(7355684729592196159)
XLA Ops:
  0.6 0.5 collective-permute-start
  1.1 1.4 %copy-done = f32[4,3,8,4096]{3,2,1,0:T(8,128)S(1)} copy-done((f32[4,3,8,4096]{3,2,1,0:T(8,128)S(1)}, f32[4,3,8,4096]{3,2,1,0:T(8,128)}, u32[]{:S(2)}) %copy-start) | copy-done | bytes 1572888
  2.6 0.7 copy-done.2
  3.2 1.2 %shard_map.68.index = s32[4]{0:T(128)S(1)} custom-call(s32[8]{0:T(128)S(1)} %copy-done.2, f32[4,3,8,4096]{3,2,1,0:T(8,128)S(1)} %copy-done), custom_call_target="tpu_custom_call" | custom-call | tf_op jit(solution)/shard_map/pallas_call | solution.py:66
  4.6 0.8 shard_map.69
  5.4 2.7 %collective-permute-start.1 = (f32[3,8,4096]{2,1,0:T(8,128)S(1)}, f32[3,8,4096]{2,1,0:T(8,128)S(1)}, u32[]{:S(2)}, u32[]{:S(2)}) collective-permute-start(f32[3,8,4096]{2,1,0:T(8,128)S(1)} %get-tuple-element.28), channel_id=1, source_target_pairs={{0,1},{1,0},{2,3},{3,2},{4,5},{5,4},{6,7},{7,6},{8,9},{9,8},{10,11... | collective-permute-start | bytes 1179656 | tf_op jit(solution)/shard_map/ppermute | solution.py:364
  8.1 3.6 %collective-permute-start.2 = (f32[3,8,4096]{2,1,0:T(8,128)S(1)}, f32[3,8,4096]{2,1,0:T(8,128)S(1)}, u32[]{:S(2)}, u32[]{:S(2)}) collective-permute-start(f32[3,8,4096]{2,1,0:T(8,128)S(1)} %get-tuple-element.27.refs_0_), channel_id=1, source_target_pairs={{0,6},{1,3},{2,0},{3,5},{4,2},{5,7},{6,4},{7,1},{8,14},{9,11},{10,... | collective-permute-start | bytes 1179656 | tf_op jit(solution)/shard_map/ppermute | solution.py:366
  11.8 3.9 %collective-permute-start.9 = (f32[3,8,2304]{2,1,0:T(8,128)S(1)}, f32[3,8,2304]{2,1,0:T(8,128)S(1)}, u32[]{:S(2)}, u32[]{:S(2)}) collective-permute-start(f32[3,8,2304]{2,1,0:T(8,128)S(1)} %get-tuple-element.34.refs_0_), channel_id=1, source_target_pairs={{0,6},{1,3},{2,0},{3,5},{4,2},{5,7},{6,4},{7,1},{8,14},{9,11},{10,... | collective-permute-start | bytes 663560 | tf_op jit(solution)/shard_map/ppermute | solution.py:366
  15.6 8.8 %collective-permute-done.3.refs_4_.refs_8_ = f32[6,8,512]{2,1,0:T(8,128)S(1)} collective-permute-done((f32[6,8,512]{2,1,0:T(8,128)S(1)}, f32[6,8,512]{2,1,0:T(8,128)S(1)}, u32[]{:S(2)}, u32[]{:S(2)}) %collective-permute-start.3) | collective-permute-done | bytes 98336 | tf_op jit(solution)/shard_map/ppermute | solution.py:349
  24.4 1.1 %collective-permute-done.4.refs_5_.refs_9_ = f32[6,8,512]{2,1,0:T(8,128)S(1)} collective-permute-done((f32[6,8,512]{2,1,0:T(8,128)S(1)}, f32[6,8,512]{2,1,0:T(8,128)S(1)}, u32[]{:S(2)}, u32[]{:S(2)}) %collective-permute-start.4) | collective-permute-done | bytes 98336 | tf_op jit(solution)/shard_map/ppermute | solution.py:350
  25.5 0.8 %collective-permute-start.5 = (f32[3,8,4096]{2,1,0:T(8,128)S(1)}, f32[3,8,4096]{2,1,0:T(8,128)S(1)}, u32[]{:S(2)}, u32[]{:S(2)}) collective-permute-start(f32[3,8,4096]{2,1,0:T(8,128)S(1)} %collective-permute-done.1.refs_1_), channel_id=1, source_target_pairs={{0,2},{1,7},{2,4},{3,1},{4,6},{5,3},{6,0},{7,5},{8,10},{9,15},{10,... | collective-permute-start | bytes 1179656 | tf_op jit(solution)/shard_map/ppermute | solution.py:368
  26.4 2.5 %collective-permute-start.8 = (f32[3,8,2304]{2,1,0:T(8,128)S(1)}, f32[3,8,2304]{2,1,0:T(8,128)S(1)}, u32[]{:S(2)}, u32[]{:S(2)}) collective-permute-start(f32[3,8,2304]{2,1,0:T(8,128)S(1)} %get-tuple-element.36), channel_id=1, source_target_pairs={{0,1},{1,0},{2,3},{3,2},{4,5},{5,4},{6,7},{7,6},{8,9},{9,8},{10,11... | collective-permute-start | bytes 663560 | tf_op jit(solution)/shard_map/ppermute | solution.py:364
  28.9 1.4 %collective-permute-done.9.refs_2_.refs_4_ = f32[3,8,2304]{2,1,0:T(8,128)S(1)} collective-permute-done((f32[3,8,2304]{2,1,0:T(8,128)S(1)}, f32[3,8,2304]{2,1,0:T(8,128)S(1)}, u32[]{:S(2)}, u32[]{:S(2)}) %collective-permute-start.9) | collective-permute-done | bytes 221216 | tf_op jit(solution)/shard_map/ppermute | solution.py:366
  30.3 4.3 %collective-permute-start.13 = (f32[3,8,1792]{2,1,0:T(8,128)S(1)}, f32[3,8,1792]{2,1,0:T(8,128)S(1)}, u32[]{:S(2)}, u32[]{:S(2)}) collective-permute-start(f32[3,8,1792]{2,1,0:T(8,128)S(1)} %get-tuple-element.43.refs_1_), channel_id=1, source_target_pairs={{0,6},{1,3},{2,0},{3,5},{4,2},{5,7},{6,4},{7,1},{8,14},{9,11},{10,... | collective-permute-start | bytes 516104 | tf_op jit(solution)/shard_map/ppermute | solution.py:366
  34.6 0.4 collective-permute-start.12
  35.0 1.3 %collective-permute-start.10 = (f32[3,8,2304]{2,1,0:T(8,128)S(1)}, f32[3,8,2304]{2,1,0:T(8,128)S(1)}, u32[]{:S(2)}, u32[]{:S(2)}) collective-permute-start(f32[3,8,2304]{2,1,0:T(8,128)S(1)} %collective-permute-done.8.refs_1_.refs_2_), channel_id=1, source_target_pairs={{0,2},{1,7},{2,4},{3,1},{4,6},{5,3},{6,0},{7,5},{8,10},{9,15},{10,... | collective-permute-start | bytes 663560 | tf_op jit(solution)/shard_map/ppermute | solution.py:368
  36.3 1.0 %collective-permute-start.6 = (f32[3,8,128]{2,1,0:T(8,128)S(1)}, f32[3,8,128]{2,1,0:T(8,128)S(1)}, u32[]{:S(2)}, u32[]{:S(2)}) collective-permute-start(f32[3,8,128]{2,1,0:T(8,128)S(1)} %pad_maximum_fusion.refs_6_.refs_10_), channel_id=1, source_target_pairs={{0,1},{1,0},{2,3},{3,2},{4,5},{5,4},{6,7},{7,6},{8,9},{9,8},{10,11... | collective-permute-start | bytes 36872 | tf_op jit(solution)/shard_map/ppermute | solution.py:377
  37.3 6.0 %collective-permute-done.13.refs_5_ = f32[3,8,1792]{2,1,0:T(8,128)S(1)} collective-permute-done((f32[3,8,1792]{2,1,0:T(8,128)S(1)}, f32[3,8,1792]{2,1,0:T(8,128)S(1)}, u32[]{:S(2)}, u32[]{:S(2)}) %collective-permute-start.13) | collective-permute-done | bytes 172064 | tf_op jit(solution)/shard_map/ppermute | solution.py:366
  43.3 0.3 collective-permute-start.14
  43.6 8.9 %shard_map.70 = (f32[3,8,4096]{2,1,0:T(8,128)S(1)}, f32[3,8,4096]{2,1,0:T(8,128)S(1)}, f32[8,128]{1,0:T(8,128)S(1)}) custom-call(f32[3,8,4096]{2,1,0:T(8,128)S(1)} %get-tuple-element.27.refs_0_, f32[3,8,4096]{2,1,0:T(8,128)S(1)} %collective-permute-done.1.refs_1_, f32[3,8,4096]{2,1,0:T(8,128)S(1)} %collective-permute-done.2.refs_2_, ...), custom_call_target="tpu_custom_call" | custom-call | bytes 480000 | tf_op jit(solution)/shard_map/pallas_call | solution.py:278
  52.5 2.8 %collective-permute-start.7 = (f32[3,8,4096]{2,1,0:T(8,128)S(1)}, f32[3,8,4096]{2,1,0:T(8,128)S(1)}, u32[]{:S(2)}, u32[]{:S(2)}) collective-permute-start(f32[3,8,4096]{2,1,0:T(8,128)S(1)} %get-tuple-element.33), channel_id=1, source_target_pairs={{0,1},{1,0},{2,3},{3,2},{4,5},{5,4},{6,7},{7,6},{8,9},{9,8},{10,11... | collective-permute-start | bytes 1179656 | tf_op jit(solution)/shard_map/ppermute | solution.py:397
  55.3 6.1 %shard_map.71 = (f32[3,8,2048]{2,1,0:T(8,128)S(1)}, f32[3,8,2048]{2,1,0:T(8,128)S(1)}, f32[8,128]{1,0:T(8,128)S(1)}) custom-call(f32[3,8,2304]{2,1,0:T(8,128)S(1)} %get-tuple-element.34.refs_0_, f32[3,8,2304]{2,1,0:T(8,128)S(1)} %collective-permute-done.8.refs_1_.refs_2_, f32[3,8,2304]{2,1,0:T(8,128)S(1)} %collective-permute-done.9.refs_2_.refs_4_, ...), custom_call_target="tpu_custom_call" | custom-call | bytes 270000 | tf_op jit(solution)/shard_map/pallas_call | solution.py:278
  61.5 6.1 %shard_map.72 = (f32[3,8,2048]{2,1,0:T(8,128)S(1)}, f32[3,8,2048]{2,1,0:T(8,128)S(1)}, f32[8,128]{1,0:T(8,128)S(1)}) custom-call(f32[3,8,2304]{2,1,0:T(8,128)S(1)} %get-tuple-element.34.refs_0_, f32[3,8,1792]{2,1,0:T(8,128)S(1)} %get-tuple-element.43.refs_1_, f32[3,8,2304]{2,1,0:T(8,128)S(1)} %collective-permute-done.8.refs_1_.refs_2_, ...), custom_call_target="tpu_custom_call" | custom-call | bytes 270000 | tf_op jit(solution)/shard_map/pallas_call | solution.py:278
  67.6 0.7 collective-permute-done.11.refs_3_
  68.4 3.8 %collective-permute-start.18 = (f32[8,128]{1,0:T(8,128)S(1)}, f32[8,128]{1,0:T(8,128)S(1)}, u32[]{:S(2)}, u32[]{:S(2)}) collective-permute-start(f32[8,128]{1,0:T(8,128)S(1)} %add_add_fusion.1), channel_id=1, source_target_pairs={{0,6},{1,7},{2,0},{3,1},{4,2},{5,3},{6,4},{7,5},{8,14},{9,15},{10,... | collective-permute-start | bytes 12296 | tf_op jit(solution)/shard_map/ppermute | solution.py:402
  72.2 0.5 collective-permute-start.16
  72.7 1.3 %collective-permute-start.15 = (f32[3,8,2048]{2,1,0:T(8,128)S(1)}, f32[3,8,2048]{2,1,0:T(8,128)S(1)}, u32[]{:S(2)}, u32[]{:S(2)}) collective-permute-start(f32[3,8,2048]{2,1,0:T(8,128)S(1)} %get-tuple-element.46), channel_id=1, source_target_pairs={{0,1},{1,0},{2,3},{3,2},{4,5},{5,4},{6,7},{7,6},{8,9},{9,8},{10,11... | collective-permute-start | bytes 589832 | tf_op jit(solution)/shard_map/ppermute | solution.py:397
  74.0 2.8 %collective-permute-done.16 = f32[8,128]{1,0:T(8,128)S(1)} collective-permute-done((f32[8,128]{1,0:T(8,128)S(1)}, f32[8,128]{1,0:T(8,128)S(1)}, u32[]{:S(2)}, u32[]{:S(2)}) %collective-permute-start.16) | collective-permute-done | bytes 4128 | tf_op jit(solution)/shard_map/ppermute | solution.py:402
  76.7 1.7 %collective-permute-start.19 = (f32[8,128]{1,0:T(8,128)S(1)}, f32[8,128]{1,0:T(8,128)S(1)}, u32[]{:S(2)}, u32[]{:S(2)}) collective-permute-start(f32[8,128]{1,0:T(8,128)S(1)} %add_add_fusion), channel_id=1, source_target_pairs={{0,1},{1,0},{2,3},{3,2},{4,5},{5,4},{6,7},{7,6},{8,9},{9,8},{10,11... | collective-permute-start | bytes 12296 | tf_op jit(solution)/shard_map/ppermute | solution.py:409
  78.5 1.3 %shard_map.73 = f32[4,3,8,4096]{3,2,1,0:T(8,128)} custom-call(f32[3,8,4096]{2,1,0:T(8,128)S(1)} %get-tuple-element.32.refs_0_, f32[3,8,4096]{2,1,0:T(8,128)S(1)} %collective-permute-done.7.refs_1_, f32[3,8,2048]{2,1,0:T(8,128)S(1)} %get-tuple-element.38.refs_2_, f32[3,8,2048]{2,1,0:T(8,128)S(1)} %collective-permute-done.11.refs_3_, ...), custom_call_target="tpu_custom_call" | custom-call | bytes 300000 | tf_op jit(solution)/shard_map/pallas_call | solution.py:311
  79.7 0.6 collective-permute-done.19
  80.3 0.5 multiply_bitcast_fusion.1
  (34 shorter events, 0.4 us)
Async XLA Ops:
  0.6 3.8 %collective-permute-start = (f32[4,3,8,4096]{3,2,1,0:T(8,128)}, f32[4,3,8,4096]{3,2,1,0:T(8,128)S(1)}, u32[]{:S(2)}, u32[]{:S(2)}) collective-permute-start(f32[4,3,8,4096]{3,2,1,0:T(8,128)} %own.1), channel_id=1, source_target_pairs={{0,8},{8,0},{1,9},{9,1},{2,10},{10,2},{3,11},{11,3},{4,12},{12,4},... | collective-permute-start | bytes 4718600 | tf_op jit(solution)/shard_map/ppermute | solution.py:337
  1.1 1.4 %copy-start = (f32[4,3,8,4096]{3,2,1,0:T(8,128)S(1)}, f32[4,3,8,4096]{3,2,1,0:T(8,128)}, u32[]{:S(2)}) copy-start(f32[4,3,8,4096]{3,2,1,0:T(8,128)} %own.1) | copy-start | bytes 4718596
  2.6 0.7 copy-start.2
  3.2 1.4 %copy-start.1 = (f32[4,3,8,4096]{3,2,1,0:T(8,128)S(1)}, f32[4,3,8,4096]{3,2,1,0:T(8,128)}, u32[]{:S(2)}) copy-start(f32[4,3,8,4096]{3,2,1,0:T(8,128)} %own.1) | copy-start | bytes 4718596
  4.4 24.4 %copy-start.3 = (f32[8,128]{1,0:T(8,128)S(1)}, f32[8,128]{1,0:T(8,128)}, u32[]{:S(2)}) copy-start(f32[8,128]{1,0:T(8,128)} %param.9) | copy-start | bytes 12292
  4.4 30.6 %copy-start.4 = (s32[8,128]{1,0:T(8,128)S(1)}, s32[8,128]{1,0:T(8,128)}, u32[]{:S(2)}) copy-start(s32[8,128]{1,0:T(8,128)} %param.8) | copy-start | bytes 12292
  4.4 31.8 %copy-start.5 = (f32[8,128]{1,0:T(8,128)S(1)}, f32[8,128]{1,0:T(8,128)}, u32[]{:S(2)}) copy-start(f32[8,128]{1,0:T(8,128)} %param.7) | copy-start | bytes 12292
  5.4 20.1 %collective-permute-start.1 = (f32[3,8,4096]{2,1,0:T(8,128)S(1)}, f32[3,8,4096]{2,1,0:T(8,128)S(1)}, u32[]{:S(2)}, u32[]{:S(2)}) collective-permute-start(f32[3,8,4096]{2,1,0:T(8,128)S(1)} %get-tuple-element.28), channel_id=1, source_target_pairs={{0,1},{1,0},{2,3},{3,2},{4,5},{5,4},{6,7},{7,6},{8,9},{9,8},{10,11... | collective-permute-start | bytes 1179656 | tf_op jit(solution)/shard_map/ppermute | solution.py:364
  8.1 17.4 %collective-permute-start.2 = (f32[3,8,4096]{2,1,0:T(8,128)S(1)}, f32[3,8,4096]{2,1,0:T(8,128)S(1)}, u32[]{:S(2)}, u32[]{:S(2)}) collective-permute-start(f32[3,8,4096]{2,1,0:T(8,128)S(1)} %get-tuple-element.27.refs_0_), channel_id=1, source_target_pairs={{0,6},{1,3},{2,0},{3,5},{4,2},{5,7},{6,4},{7,1},{8,14},{9,11},{10,... | collective-permute-start | bytes 1179656 | tf_op jit(solution)/shard_map/ppermute | solution.py:366
  11.7 12.7 %collective-permute-start.3 = (f32[6,8,512]{2,1,0:T(8,128)S(1)}, f32[6,8,512]{2,1,0:T(8,128)S(1)}, u32[]{:S(2)}, u32[]{:S(2)}) collective-permute-start(f32[6,8,512]{2,1,0:T(8,128)S(1)} %get-tuple-element.29), channel_id=1, source_target_pairs={{0,2},{1,7},{2,4},{3,1},{4,6},{5,3},{6,0},{7,5},{8,10},{9,15},{10,... | collective-permute-start | bytes 294920 | tf_op jit(solution)/shard_map/ppermute | solution.py:349
  11.7 13.7 %collective-permute-start.4 = (f32[6,8,512]{2,1,0:T(8,128)S(1)}, f32[6,8,512]{2,1,0:T(8,128)S(1)}, u32[]{:S(2)}, u32[]{:S(2)}) collective-permute-start(f32[6,8,512]{2,1,0:T(8,128)S(1)} %get-tuple-element.30), channel_id=1, source_target_pairs={{0,3},{1,6},{2,5},{3,0},{4,7},{5,2},{6,1},{7,4},{8,11},{9,14},{10,... | collective-permute-start | bytes 294920 | tf_op jit(solution)/shard_map/ppermute | solution.py:350
  11.8 18.5 %collective-permute-start.9 = (f32[3,8,2304]{2,1,0:T(8,128)S(1)}, f32[3,8,2304]{2,1,0:T(8,128)S(1)}, u32[]{:S(2)}, u32[]{:S(2)}) collective-permute-start(f32[3,8,2304]{2,1,0:T(8,128)S(1)} %get-tuple-element.34.refs_0_), channel_id=1, source_target_pairs={{0,6},{1,3},{2,0},{3,5},{4,2},{5,7},{6,4},{7,1},{8,14},{9,11},{10,... | collective-permute-start | bytes 663560 | tf_op jit(solution)/shard_map/ppermute | solution.py:366
  25.5 17.8 %collective-permute-start.5 = (f32[3,8,4096]{2,1,0:T(8,128)S(1)}, f32[3,8,4096]{2,1,0:T(8,128)S(1)}, u32[]{:S(2)}, u32[]{:S(2)}) collective-permute-start(f32[3,8,4096]{2,1,0:T(8,128)S(1)} %collective-permute-done.1.refs_1_), channel_id=1, source_target_pairs={{0,2},{1,7},{2,4},{3,1},{4,6},{5,3},{6,0},{7,5},{8,10},{9,15},{10,... | collective-permute-start | bytes 1179656 | tf_op jit(solution)/shard_map/ppermute | solution.py:368
  26.4 8.2 %collective-permute-start.8 = (f32[3,8,2304]{2,1,0:T(8,128)S(1)}, f32[3,8,2304]{2,1,0:T(8,128)S(1)}, u32[]{:S(2)}, u32[]{:S(2)}) collective-permute-start(f32[3,8,2304]{2,1,0:T(8,128)S(1)} %get-tuple-element.36), channel_id=1, source_target_pairs={{0,1},{1,0},{2,3},{3,2},{4,5},{5,4},{6,7},{7,6},{8,9},{9,8},{10,11... | collective-permute-start | bytes 663560 | tf_op jit(solution)/shard_map/ppermute | solution.py:364
  30.3 13.0 %collective-permute-start.13 = (f32[3,8,1792]{2,1,0:T(8,128)S(1)}, f32[3,8,1792]{2,1,0:T(8,128)S(1)}, u32[]{:S(2)}, u32[]{:S(2)}) collective-permute-start(f32[3,8,1792]{2,1,0:T(8,128)S(1)} %get-tuple-element.43.refs_1_), channel_id=1, source_target_pairs={{0,6},{1,3},{2,0},{3,5},{4,2},{5,7},{6,4},{7,1},{8,14},{9,11},{10,... | collective-permute-start | bytes 516104 | tf_op jit(solution)/shard_map/ppermute | solution.py:366
  34.6 8.7 %collective-permute-start.12 = (f32[3,8,1792]{2,1,0:T(8,128)S(1)}, f32[3,8,1792]{2,1,0:T(8,128)S(1)}, u32[]{:S(2)}, u32[]{:S(2)}) collective-permute-start(f32[3,8,1792]{2,1,0:T(8,128)S(1)} %get-tuple-element.42), channel_id=1, source_target_pairs={{0,1},{1,0},{2,3},{3,2},{4,5},{5,4},{6,7},{7,6},{8,9},{9,8},{10,11... | collective-permute-start | bytes 516104 | tf_op jit(solution)/shard_map/ppermute | solution.py:364
  35.0 20.3 %collective-permute-start.10 = (f32[3,8,2304]{2,1,0:T(8,128)S(1)}, f32[3,8,2304]{2,1,0:T(8,128)S(1)}, u32[]{:S(2)}, u32[]{:S(2)}) collective-permute-start(f32[3,8,2304]{2,1,0:T(8,128)S(1)} %collective-permute-done.8.refs_1_.refs_2_), channel_id=1, source_target_pairs={{0,2},{1,7},{2,4},{3,1},{4,6},{5,3},{6,0},{7,5},{8,10},{9,15},{10,... | collective-permute-start | bytes 663560 | tf_op jit(solution)/shard_map/ppermute | solution.py:368
  36.3 7.3 %collective-permute-start.6 = (f32[3,8,128]{2,1,0:T(8,128)S(1)}, f32[3,8,128]{2,1,0:T(8,128)S(1)}, u32[]{:S(2)}, u32[]{:S(2)}) collective-permute-start(f32[3,8,128]{2,1,0:T(8,128)S(1)} %pad_maximum_fusion.refs_6_.refs_10_), channel_id=1, source_target_pairs={{0,1},{1,0},{2,3},{3,2},{4,5},{5,4},{6,7},{7,6},{8,9},{9,8},{10,11... | collective-permute-start | bytes 36872 | tf_op jit(solution)/shard_map/ppermute | solution.py:377
  43.3 18.3 %collective-permute-start.14 = (f32[3,8,1792]{2,1,0:T(8,128)S(1)}, f32[3,8,1792]{2,1,0:T(8,128)S(1)}, u32[]{:S(2)}, u32[]{:S(2)}) collective-permute-start(f32[3,8,1792]{2,1,0:T(8,128)S(1)} %collective-permute-done.12.refs_3_), channel_id=1, source_target_pairs={{0,2},{1,7},{2,4},{3,1},{4,6},{5,3},{6,0},{7,5},{8,10},{9,15},{10,... | collective-permute-start | bytes 516104 | tf_op jit(solution)/shard_map/ppermute | solution.py:368
  52.5 15.8 %collective-permute-start.7 = (f32[3,8,4096]{2,1,0:T(8,128)S(1)}, f32[3,8,4096]{2,1,0:T(8,128)S(1)}, u32[]{:S(2)}, u32[]{:S(2)}) collective-permute-start(f32[3,8,4096]{2,1,0:T(8,128)S(1)} %get-tuple-element.33), channel_id=1, source_target_pairs={{0,1},{1,0},{2,3},{3,2},{4,5},{5,4},{6,7},{7,6},{8,9},{9,8},{10,11... | collective-permute-start | bytes 1179656 | tf_op jit(solution)/shard_map/ppermute | solution.py:397
  61.4 7.0 %collective-permute-start.11 = (f32[3,8,2048]{2,1,0:T(8,128)S(1)}, f32[3,8,2048]{2,1,0:T(8,128)S(1)}, u32[]{:S(2)}, u32[]{:S(2)}) collective-permute-start(f32[3,8,2048]{2,1,0:T(8,128)S(1)} %get-tuple-element.39), channel_id=1, source_target_pairs={{0,1},{1,0},{2,3},{3,2},{4,5},{5,4},{6,7},{7,6},{8,9},{9,8},{10,11... | collective-permute-start | bytes 589832 | tf_op jit(solution)/shard_map/ppermute | solution.py:397
  68.4 5.6 %collective-permute-start.17 = (f32[8,128]{1,0:T(8,128)S(1)}, f32[8,128]{1,0:T(8,128)S(1)}, u32[]{:S(2)}, u32[]{:S(2)}) collective-permute-start(f32[8,128]{1,0:T(8,128)S(1)} %add_add_fusion.1), channel_id=1, source_target_pairs={{0,2},{1,3},{2,4},{3,5},{4,6},{5,7},{6,0},{7,1},{8,10},{9,11},{10,... | collective-permute-start | bytes 12296 | tf_op jit(solution)/shard_map/ppermute | solution.py:402
  68.4 5.6 %collective-permute-start.18 = (f32[8,128]{1,0:T(8,128)S(1)}, f32[8,128]{1,0:T(8,128)S(1)}, u32[]{:S(2)}, u32[]{:S(2)}) collective-permute-start(f32[8,128]{1,0:T(8,128)S(1)} %add_add_fusion.1), channel_id=1, source_target_pairs={{0,6},{1,7},{2,0},{3,1},{4,2},{5,3},{6,4},{7,5},{8,14},{9,15},{10,... | collective-permute-start | bytes 12296 | tf_op jit(solution)/shard_map/ppermute | solution.py:402
  72.2 4.5 %collective-permute-start.16 = (f32[8,128]{1,0:T(8,128)S(1)}, f32[8,128]{1,0:T(8,128)S(1)}, u32[]{:S(2)}, u32[]{:S(2)}) collective-permute-start(f32[8,128]{1,0:T(8,128)S(1)} %add_add_fusion.1), channel_id=1, source_target_pairs={{0,4},{1,5},{2,6},{3,7},{4,0},{5,1},{6,2},{7,3},{8,12},{9,13},{10,... | collective-permute-start | bytes 12296 | tf_op jit(solution)/shard_map/ppermute | solution.py:402
  72.7 5.8 %collective-permute-start.15 = (f32[3,8,2048]{2,1,0:T(8,128)S(1)}, f32[3,8,2048]{2,1,0:T(8,128)S(1)}, u32[]{:S(2)}, u32[]{:S(2)}) collective-permute-start(f32[3,8,2048]{2,1,0:T(8,128)S(1)} %get-tuple-element.46), channel_id=1, source_target_pairs={{0,1},{1,0},{2,3},{3,2},{4,5},{5,4},{6,7},{7,6},{8,9},{9,8},{10,11... | collective-permute-start | bytes 589832 | tf_op jit(solution)/shard_map/ppermute | solution.py:397
  76.7 3.6 %collective-permute-start.19 = (f32[8,128]{1,0:T(8,128)S(1)}, f32[8,128]{1,0:T(8,128)S(1)}, u32[]{:S(2)}, u32[]{:S(2)}) collective-permute-start(f32[8,128]{1,0:T(8,128)S(1)} %add_add_fusion), channel_id=1, source_target_pairs={{0,1},{1,0},{2,3},{3,2},{4,5},{5,4},{6,7},{7,6},{8,9},{9,8},{10,11... | collective-permute-start | bytes 12296 | tf_op jit(solution)/shard_map/ppermute | solution.py:409

commit v6 on v5

--- a/solution.py
+++ b/solution.py
@@ -29,8 +29,6 @@
 
 def plan(ncol, slot, slots):
     every = list(range(ncol))
-    if slot < slots - 1:
-        return ((every, every, every),)
     cut = ncol // 2 + 2
     return (
         (every[:cut], every[:cut], every[1 : cut - 1]),
@@ -78,7 +76,7 @@
     par = lax.axis_index("strip") % 2
     refs, kept, given = list(outs), [], []
     for s in spans:
-        kept.append([refs.pop(0) for _ in s])
+        kept.append([refs.pop(0)])
         given.append([refs.pop(0) for _ in s])
     near, far = refs
     wide = own.shape[3] // TILE
@@ -87,8 +85,11 @@
         i = index[slot]
 
         def write(ref, m):
-            for (first, count), out in zip(spans[k], pieces):
-                out[...] = ref[m, :, :, pl.ds(first, count)]
+            if len(pieces) == 1:
+                pieces[0][...] = ref[m]
+            else:
+                for (first, count), out in zip(spans[k], pieces):
+                    out[...] = ref[m, :, :, pl.ds(first, count)]
 
             def edges(row):
                 for f in range(3):
@@ -122,7 +123,7 @@
     shape, kind = own.shape[1:3], own.dtype
     outs = []
     for s in spans:
-        outs += [jax.ShapeDtypeStruct(shape + (c,), kind) for _, c in s] * 2
+        outs += [jax.ShapeDtypeStruct(shape + (c,), kind) for c in [own.shape[3]] + [c for _, c in s]]
     outs += [jax.ShapeDtypeStruct((3 * len(spans), TILE, own.shape[3] // TILE), kind)] * 2
     out = pl.pallas_call(
         functools.partial(pick_kernel, spans=spans),
@@ -133,9 +134,9 @@
     )(index, own, other)
     kept, given = [], []
     for s in spans:
-        kept.append(out[: len(s)])
-        given.append(out[len(s) : 2 * len(s)])
-        out = out[2 * len(s) :]
+        kept.append(out[0])
+        given.append(out[1 : 1 + len(s)])
+        out = out[1 + len(s) :]
     return kept, given, out[0], out[1]
 
 
@@ -187,8 +188,9 @@
 
 
 def forecast_kernel(*refs, worked, kept, place, parts, slot, slots, ncol, total_rows):
-    own, got, direct, passed = (refs[n * parts : (n + 1) * parts] for n in range(4))
-    near, far, obs_own, obs_got, keep, send, misfit, state, s1, s2, cor_ref = refs[4 * parts :]
+    own, direct, refs = refs[0], refs[1], refs[2:]
+    got, passed = refs[:parts], refs[parts : 2 * parts]
+    near, far, obs_own, obs_got, keep, send, misfit, state, s1, s2, cor_ref = refs[2 * parts :]
     strip = lax.axis_index("strip")
     par = strip % 2
     per = ncol // TILE
@@ -196,13 +198,13 @@
     def load(own_row, got_row, direct_row, passed_row, near_row, far_row):
         for i, ct in enumerate(worked):
             p, j = place[i]
-            for ref, row in (
-                (own, own_row),
-                (got, got_row),
-                (direct, direct_row),
-                (passed, passed_row),
+            for ref, row, place_at in (
+                (own, own_row, ct),
+                (got[p], got_row, j),
+                (direct, direct_row, ct),
+                (passed[p], passed_row, j),
             ):
-                state[:, i, row : row + TILE, :] = ref[p][:, :, at(j)]
+                state[:, i, row : row + TILE, :] = ref[:, :, at(place_at)]
             for ref, row in ((near, near_row), (far, far_row)):
                 q = ct // per
                 state[:, i, row : row + 1, :] = ref[
@@ -274,14 +276,14 @@
         place.append((p, parts[p][0].index(ct)))
     block = jax.ShapeDtypeStruct((3, TILE, len(kept) * LANES), jnp.float32)
     field = pltpu.VMEM((3, len(worked), ROWS, LANES), jnp.float32)
-    args = [*own, *got, *direct, *passed, near, far, obs_own, obs_got]
+    args = [own, direct, *got, *passed, near, far, obs_own, obs_got]
     return pl.pallas_call(
         functools.partial(
             forecast_kernel,
             worked=worked,
             kept=kept,
             place=place,
-            parts=len(own),
+            parts=len(got),
             slot=slot,
             slots=slots,
             ncol=ncol,
@@ -349,54 +351,36 @@
     near = lax.ppermute(near, "strip", onward)
     far = lax.ppermute(far, "strip", cross)
 
-    got, direct, passed = [], [], []
-    swapped, held = None, (near, far)
-    for k in range(half):
-        got.append([])
-        direct.append([])
-        passed.append([])
-        for p in range(len(spans[k])):
-            giving, keeping = given[k][p], kept[k][p]
-            if swapped is not None:
-                (giving,) = after((giving,), swapped)
-            if k > 0 and p > 0:
-                (keeping,) = after((keeping,), direct[k][p - 1])
-            swapped = lax.ppermute(giving, "strip", swap)
-            got[k].append(swapped)
-            direct[k].append(lax.ppermute(keeping, "strip", straight))
-            (goes,) = after((swapped,), (direct[k][p], held))
-            passed[k].append(lax.ppermute(goes, "strip", onward))
-            if k > 0:
-                held = passed[0][-1]
     obs_got = lax.ppermute(obs_own, "strip", swap)
 
-    obs_got = lax.ppermute(obs_own, "strip", swap)
-
-    obs_got = lax.ppermute(obs_own, "strip", swap)
-
-    obs_got = lax.ppermute(obs_own, "strip", swap)
-
-    blocks, pieces, total = [], [], None
-    for k in range(half):
-        for p in range(len(plan(ncol, k, half))):
-            keep, send, misfit = forecast(
-                kept[k][: p + 1],
-                got[k][: p + 1],
-                direct[k][: p + 1],
-                passed[k][: p + 1],
-                near,
-                far,
-                obs_own,
-                obs_got,
-                p,
-                k,
-                half,
-                ncol,
-                total_rows,
-            )
-            blocks.append((keep, lax.ppermute(send, "strip", swap)))
-            pieces.append((k, p))
-            total = misfit if total is None else total + misfit
+    pieces = [(k, p) for k in range(half) for p in range(len(spans[k]))]
+    got, passed, direct = [[] for _ in range(half)], [[] for _ in range(half)], []
+    swapped, last, blocks, misfits = [], [], [], []
+    for n, (k, p) in enumerate(pieces):
+        giving, keeping = given[k][p], kept[k]
+        if p == 0:
+            if k:
+                (keeping,) = after((keeping,), last[n - 2])
+            direct.append(lax.ppermute(keeping, "strip", straight))
+        if n == 1:
+            (giving,) = after((giving,), (swapped[0], direct[0], near, far, obs_got))
+        elif n == 2:
+            (giving,) = after((giving,), (swapped[1], last[0]))
+        elif n:
+            (giving,) = after((giving,), (swapped[-1], misfits[n - 3]))
+        swapped.append(lax.ppermute(giving, "strip", swap))
+        goes = swapped[n]
+        if n > 1:
+            (goes,) = after((goes,), misfits[n - 2])
+        last.append(lax.ppermute(goes, "strip", onward))
+        got[k].append(swapped[n])
+        passed[k].append(last[n])
+        keep, send, misfit = forecast(
+            kept[k], got[k], direct[k], passed[k], near, far, obs_own, obs_got, p, k, half, ncol, total_rows
+        )
+        blocks.append((keep, lax.ppermute(send, "strip", swap)))
+        misfits.append(misfit)
+    total = sum(misfits[1:], misfits[0])
     (total,) = after((total,), [b[1] for b in blocks[:-1]])
     if strips == 8:
         turn = [lax.ppermute(total, "strip", moved(step, step)) for step in (2, 4, 6)]
@@ -406,9 +390,10 @@
         while step < strips:
             total = total + lax.ppermute(total, "strip", [(i, i ^ step) for i in range(strips)])
             step *= 2
-    total = total + lax.ppermute(total, "strip", swap)
+    theirs = lax.ppermute(total, "strip", swap)
     state = gather(blocks, pieces, ncol, half)
-    (total,) = after((total,), state)
+    theirs, total = after((theirs, total), state)
+    total = total + theirs
     log_weights = (-0.5 / (total_rows * obs_cols.shape[1])) * total[0, :members]
     return (state, log_weights)
 

time: 81 us -> 86 us (1.062)
  Pallas kernels: 24.3 us -> 27.5 us
  waiting for transfers between devices: 21.4 us -> 23.5 us
    ppermute x10 -> x11, waiting for transfers between devices: 7.97 us -> 16.1 us  [the longest x4 9.74 us: local(): last.append(lax.ppermute(goes, 'strip', onward))]
    ppermute x1, waiting for transfers between devices: 8.77 us -> 1.22 us  [local(): near = lax.ppermute(near, 'strip', onward)]
    ppermute x10 -> x11, starting transfers between devices: 21.6 us -> 15.9 us  [the longest x2 12.3 us: local(): direct.append(lax.ppermute(keeping, 'strip', straight))]
    pallas_call x3 -> x4, Pallas kernels: 21.1 us -> 24.3 us  [forecast(): pl.pallas_call(functools.partial(forecast_kernel, worked=worked, kept=kep...]
    ppermute x1, starting transfers between devices: 0.01 us -> 2.43 us  [local(): far = lax.ppermute(far, 'strip', cross)]
    ppermute x3, waiting for transfers between devices: 2.76 us -> 0.74 us  [local(): lax.ppermute(total, 'strip', moved(step, step))]
    ppermute x1, waiting for transfers between devices: 0.01 us -> 1.95 us  [local(): obs_got = lax.ppermute(obs_own, 'strip', swap)]
    ppermute x1, waiting for transfers between devices: 1.1 us -> 2.51 us  [local(): far = lax.ppermute(far, 'strip', cross)]
  transfers between devices with their start and end apart: 20 -> 22, of which waited for: 7 -> 9; matrix products, arithmetic and copies ran while one was open for 0% -> 0% of each run, Pallas kernels for 29% -> 31%
where the time goes in v6:
time: 86 us; the launch traced here: 85.8 us
  starting transfers between devices  31.2 us (36%)
  Pallas kernels  27.5 us (32%)
  waiting for transfers between devices  23.5 us (27%)
  local copies, waits for them, and re-layouts  2.22 us (3%)
    pallas_call x4, Pallas kernels, forecast(): pl.pallas_call(functools.partial(forecast_kernel, worked=worked, kept=kep...  24.3 us
    ppermute x2, starting transfers between devices, local(): direct.append(lax.ppermute(keeping, 'strip', straight))  12.3 us
    ppermute x4, waiting for transfers between devices, local(): last.append(lax.ppermute(goes, 'strip', onward))  9.74 us
    ppermute x4, waiting for transfers between devices, local(): swapped.append(lax.ppermute(giving, 'strip', swap))  6.35 us
    ppermute x3, starting transfers between devices, local(): lax.ppermute(total, 'strip', moved(step, step))  5.21 us
    ppermute x4, starting transfers between devices, local(): blocks.append((keep, lax.ppermute(send, 'strip', swap)))  4.22 us
    ppermute x1, waiting for transfers between devices, local(): far = lax.ppermute(far, 'strip', cross)  2.51 us
    ppermute x1, starting transfers between devices, local(): far = lax.ppermute(far, 'strip', cross)  2.43 us
  transfers between devices with their start and end apart: 22, of which 9 were waited for; matrix products, arithmetic and copies ran while one was open for 0% of the time, Pallas kernels for 31%

profile of v6, /device:TPU:0, one launch (start us, length us, event | category | flops | bytes accessed | tf_op | source)
XLA Modules:
  0.0 85.8 jit_solution(3938730767424947435)
XLA Ops:
  0.6 0.5 collective-permute-start
  1.1 1.4 %copy-done = f32[4,3,8,4096]{3,2,1,0:T(8,128)S(1)} copy-done((f32[4,3,8,4096]{3,2,1,0:T(8,128)S(1)}, f32[4,3,8,4096]{3,2,1,0:T(8,128)}, u32[]{:S(2)}) %copy-start) | copy-done | bytes 1572888
  2.6 0.7 copy-done.2
  3.2 1.2 %shard_map.68.index = s32[4]{0:T(128)S(1)} custom-call(s32[8]{0:T(128)S(1)} %copy-done.2, f32[4,3,8,4096]{3,2,1,0:T(8,128)S(1)} %copy-done), custom_call_target="tpu_custom_call" | custom-call | tf_op jit(solution)/shard_map/pallas_call | solution.py:64
  4.6 0.8 shard_map.69
  5.4 4.8 %collective-permute-start.1 = (f32[3,8,4096]{2,1,0:T(8,128)S(1)}, f32[3,8,4096]{2,1,0:T(8,128)S(1)}, u32[]{:S(2)}, u32[]{:S(2)}) collective-permute-start(f32[3,8,4096]{2,1,0:T(8,128)S(1)} %get-tuple-element.31.refs_0_), channel_id=1, source_target_pairs={{0,6},{1,3},{2,0},{3,5},{4,2},{5,7},{6,4},{7,1},{8,14},{9,11},{10,... | collective-permute-start | bytes 1179656 | tf_op jit(solution)/shard_map/ppermute | solution.py:364
  10.3 1.1 %collective-permute-start.4 = (f32[6,8,512]{2,1,0:T(8,128)S(1)}, f32[6,8,512]{2,1,0:T(8,128)S(1)}, u32[]{:S(2)}, u32[]{:S(2)}) collective-permute-start(f32[6,8,512]{2,1,0:T(8,128)S(1)} %get-tuple-element.33), channel_id=1, source_target_pairs={{0,2},{1,7},{2,4},{3,1},{4,6},{5,3},{6,0},{7,5},{8,10},{9,15},{10,... | collective-permute-start | bytes 294920 | tf_op jit(solution)/shard_map/ppermute | solution.py:351
  11.4 2.4 %collective-permute-start.5 = (f32[6,8,512]{2,1,0:T(8,128)S(1)}, f32[6,8,512]{2,1,0:T(8,128)S(1)}, u32[]{:S(2)}, u32[]{:S(2)}) collective-permute-start(f32[6,8,512]{2,1,0:T(8,128)S(1)} %get-tuple-element.34), channel_id=1, source_target_pairs={{0,3},{1,6},{2,5},{3,0},{4,7},{5,2},{6,1},{7,4},{8,11},{9,14},{10,... | collective-permute-start | bytes 294920 | tf_op jit(solution)/shard_map/ppermute | solution.py:352
  13.8 3.9 %collective-permute-done.2.refs_2_ = f32[3,8,2304]{2,1,0:T(8,128)S(1)} collective-permute-done((f32[3,8,2304]{2,1,0:T(8,128)S(1)}, f32[3,8,2304]{2,1,0:T(8,128)S(1)}, u32[]{:S(2)}, u32[]{:S(2)}) %collective-permute-start.2) | collective-permute-done | bytes 221216 | tf_op jit(solution)/shard_map/ppermute | solution.py:371
  17.7 1.8 %collective-permute-start.6 = (f32[3,8,128]{2,1,0:T(8,128)S(1)}, f32[3,8,128]{2,1,0:T(8,128)S(1)}, u32[]{:S(2)}, u32[]{:S(2)}) collective-permute-start(f32[3,8,128]{2,1,0:T(8,128)S(1)} %pad_maximum_fusion.refs_6_.refs_8_), channel_id=1, source_target_pairs={{0,1},{1,0},{2,3},{3,2},{4,5},{5,4},{6,7},{7,6},{8,9},{9,8},{10,11... | collective-permute-start | bytes 36872 | tf_op jit(solution)/shard_map/ppermute | solution.py:354
  19.5 2.0 %collective-permute-done.6.refs_7_.refs_9_ = f32[3,8,128]{2,1,0:T(8,128)S(1)} collective-permute-done((f32[3,8,128]{2,1,0:T(8,128)S(1)}, f32[3,8,128]{2,1,0:T(8,128)S(1)}, u32[]{:S(2)}, u32[]{:S(2)}) %collective-permute-start.6) | collective-permute-done | bytes 12320 | tf_op jit(solution)/shard_map/ppermute | solution.py:354
  21.5 1.2 %collective-permute-done.4.refs_4_.refs_6_ = f32[6,8,512]{2,1,0:T(8,128)S(1)} collective-permute-done((f32[6,8,512]{2,1,0:T(8,128)S(1)}, f32[6,8,512]{2,1,0:T(8,128)S(1)}, u32[]{:S(2)}, u32[]{:S(2)}) %collective-permute-start.4) | collective-permute-done | bytes 98336 | tf_op jit(solution)/shard_map/ppermute | solution.py:351
  22.7 2.5 %collective-permute-done.5.refs_5_.refs_7_ = f32[6,8,512]{2,1,0:T(8,128)S(1)} collective-permute-done((f32[6,8,512]{2,1,0:T(8,128)S(1)}, f32[6,8,512]{2,1,0:T(8,128)S(1)}, u32[]{:S(2)}, u32[]{:S(2)}) %collective-permute-start.5) | collective-permute-done | bytes 98336 | tf_op jit(solution)/shard_map/ppermute | solution.py:352
  25.2 1.1 %collective-permute-start.8 = (f32[3,8,1792]{2,1,0:T(8,128)S(1)}, f32[3,8,1792]{2,1,0:T(8,128)S(1)}, u32[]{:S(2)}, u32[]{:S(2)}) collective-permute-start(f32[3,8,1792]{2,1,0:T(8,128)S(1)} %get-tuple-element.38), channel_id=1, source_target_pairs={{0,1},{1,0},{2,3},{3,2},{4,5},{5,4},{6,7},{7,6},{8,9},{9,8},{10,11... | collective-permute-start | bytes 516104 | tf_op jit(solution)/shard_map/ppermute | solution.py:371
  26.3 2.7 %collective-permute-done.3.refs_3_.refs_4_ = f32[3,8,2304]{2,1,0:T(8,128)S(1)} collective-permute-done((f32[3,8,2304]{2,1,0:T(8,128)S(1)}, f32[3,8,2304]{2,1,0:T(8,128)S(1)}, u32[]{:S(2)}, u32[]{:S(2)}) %collective-permute-start.3) | collective-permute-done | bytes 221216 | tf_op jit(solution)/shard_map/ppermute | solution.py:375
  29.0 2.4 %collective-permute-done.8.refs_3_ = f32[3,8,1792]{2,1,0:T(8,128)S(1)} collective-permute-done((f32[3,8,1792]{2,1,0:T(8,128)S(1)}, f32[3,8,1792]{2,1,0:T(8,128)S(1)}, u32[]{:S(2)}, u32[]{:S(2)}) %collective-permute-start.8) | collective-permute-done | bytes 172064 | tf_op jit(solution)/shard_map/ppermute | solution.py:371
  31.7 7.5 %collective-permute-start.11 = (f32[3,8,4096]{2,1,0:T(8,128)S(1)}, f32[3,8,4096]{2,1,0:T(8,128)S(1)}, u32[]{:S(2)}, u32[]{:S(2)}) collective-permute-start(f32[3,8,4096]{2,1,0:T(8,128)S(1)} %get-tuple-element.42.refs_0_), channel_id=1, source_target_pairs={{0,6},{1,3},{2,0},{3,5},{4,2},{5,7},{6,4},{7,1},{8,14},{9,11},{10,... | collective-permute-start | bytes 1179656 | tf_op jit(solution)/shard_map/ppermute | solution.py:364
  39.2 6.1 %shard_map.70 = (f32[3,8,2048]{2,1,0:T(8,128)S(1)}, f32[3,8,2048]{2,1,0:T(8,128)S(1)}, f32[8,128]{1,0:T(8,128)S(1)}) custom-call(f32[3,8,4096]{2,1,0:T(8,128)S(1)} %get-tuple-element.31.refs_0_, f32[3,8,4096]{2,1,0:T(8,128)S(1)} %collective-permute-done.1.refs_1_, f32[3,8,2304]{2,1,0:T(8,128)S(1)} %collective-permute-done.2.refs_2_, ...), custom_call_target="tpu_custom_call" | custom-call | bytes 270000 | tf_op jit(solution)/shard_map/pallas_call | solution.py:280
  45.5 7.0 %collective-permute-done.9.refs_5_ = f32[3,8,1792]{2,1,0:T(8,128)S(1)} collective-permute-done((f32[3,8,1792]{2,1,0:T(8,128)S(1)}, f32[3,8,1792]{2,1,0:T(8,128)S(1)}, u32[]{:S(2)}, u32[]{:S(2)}) %collective-permute-start.9) | collective-permute-done | bytes 172064 | tf_op jit(solution)/shard_map/ppermute | solution.py:375
  52.5 6.1 %shard_map.71 = (f32[3,8,2048]{2,1,0:T(8,128)S(1)}, f32[3,8,2048]{2,1,0:T(8,128)S(1)}, f32[8,128]{1,0:T(8,128)S(1)}) custom-call(f32[3,8,4096]{2,1,0:T(8,128)S(1)} %get-tuple-element.31.refs_0_, f32[3,8,4096]{2,1,0:T(8,128)S(1)} %collective-permute-done.1.refs_1_, f32[3,8,2304]{2,1,0:T(8,128)S(1)} %collective-permute-done.2.refs_2_, ...), custom_call_target="tpu_custom_call" | custom-call | bytes 270000 | tf_op jit(solution)/shard_map/pallas_call | solution.py:280
  58.8 2.0 %collective-permute-start.10 = (f32[3,8,2048]{2,1,0:T(8,128)S(1)}, f32[3,8,2048]{2,1,0:T(8,128)S(1)}, u32[]{:S(2)}, u32[]{:S(2)}) collective-permute-start(f32[3,8,2048]{2,1,0:T(8,128)S(1)} %get-tuple-element.40), channel_id=1, source_target_pairs={{0,1},{1,0},{2,3},{3,2},{4,5},{5,4},{6,7},{7,6},{8,9},{9,8},{10,11... | collective-permute-start | bytes 589832 | tf_op jit(solution)/shard_map/ppermute | solution.py:381
  60.8 6.1 %shard_map.72 = (f32[3,8,2048]{2,1,0:T(8,128)S(1)}, f32[3,8,2048]{2,1,0:T(8,128)S(1)}, f32[8,128]{1,0:T(8,128)S(1)}) custom-call(f32[3,8,4096]{2,1,0:T(8,128)S(1)} %get-tuple-element.42.refs_0_, f32[3,8,4096]{2,1,0:T(8,128)S(1)} %collective-permute-done.11.refs_1_, f32[3,8,2304]{2,1,0:T(8,128)S(1)} %collective-permute-done.12.refs_2_, ...), custom_call_target="tpu_custom_call" | custom-call | bytes 270000 | tf_op jit(solution)/shard_map/pallas_call | solution.py:280
  67.0 6.1 %shard_map.73 = (f32[3,8,2048]{2,1,0:T(8,128)S(1)}, f32[3,8,2048]{2,1,0:T(8,128)S(1)}, f32[8,128]{1,0:T(8,128)S(1)}) custom-call(f32[3,8,4096]{2,1,0:T(8,128)S(1)} %get-tuple-element.42.refs_0_, f32[3,8,4096]{2,1,0:T(8,128)S(1)} %collective-permute-done.11.refs_1_, f32[3,8,2304]{2,1,0:T(8,128)S(1)} %collective-permute-done.12.refs_2_, ...), custom_call_target="tpu_custom_call" | custom-call | bytes 270000 | tf_op jit(solution)/shard_map/pallas_call | solution.py:280
  73.2 1.4 %collective-permute-start.18 = (f32[8,128]{1,0:T(8,128)S(1)}, f32[8,128]{1,0:T(8,128)S(1)}, u32[]{:S(2)}, u32[]{:S(2)}) collective-permute-start(f32[8,128]{1,0:T(8,128)S(1)} %add_add_fusion.1), channel_id=1, source_target_pairs={{0,4},{1,5},{2,6},{3,7},{4,0},{5,1},{6,2},{7,3},{8,12},{9,13},{10,... | collective-permute-start | bytes 12296 | tf_op jit(solution)/shard_map/ppermute | solution.py:386
  74.6 2.9 %collective-permute-start.19 = (f32[8,128]{1,0:T(8,128)S(1)}, f32[8,128]{1,0:T(8,128)S(1)}, u32[]{:S(2)}, u32[]{:S(2)}) collective-permute-start(f32[8,128]{1,0:T(8,128)S(1)} %add_add_fusion.1), channel_id=1, source_target_pairs={{0,2},{1,3},{2,4},{3,5},{4,6},{5,7},{6,0},{7,1},{8,10},{9,11},{10,... | collective-permute-start | bytes 12296 | tf_op jit(solution)/shard_map/ppermute | solution.py:386
  77.5 0.9 %collective-permute-start.20 = (f32[8,128]{1,0:T(8,128)S(1)}, f32[8,128]{1,0:T(8,128)S(1)}, u32[]{:S(2)}, u32[]{:S(2)}) collective-permute-start(f32[8,128]{1,0:T(8,128)S(1)} %add_add_fusion.1), channel_id=1, source_target_pairs={{0,6},{1,7},{2,0},{3,1},{4,2},{5,3},{6,4},{7,5},{8,14},{9,15},{10,... | collective-permute-start | bytes 12296 | tf_op jit(solution)/shard_map/ppermute | solution.py:386
  78.4 2.0 %collective-permute-start.17 = (f32[3,8,2048]{2,1,0:T(8,128)S(1)}, f32[3,8,2048]{2,1,0:T(8,128)S(1)}, u32[]{:S(2)}, u32[]{:S(2)}) collective-permute-start(f32[3,8,2048]{2,1,0:T(8,128)S(1)} %get-tuple-element.54), channel_id=1, source_target_pairs={{0,1},{1,0},{2,3},{3,2},{4,5},{5,4},{6,7},{7,6},{8,9},{9,8},{10,11... | collective-permute-start | bytes 589832 | tf_op jit(solution)/shard_map/ppermute | solution.py:381
  80.4 0.7 collective-permute-done.20
  81.1 2.0 %collective-permute-start.21 = (f32[8,128]{1,0:T(8,128)S(1)}, f32[8,128]{1,0:T(8,128)S(1)}, u32[]{:S(2)}, u32[]{:S(2)}) collective-permute-start(f32[8,128]{1,0:T(8,128)S(1)} %add_add_fusion), channel_id=1, source_target_pairs={{0,1},{1,0},{2,3},{3,2},{4,5},{5,4},{6,7},{7,6},{8,9},{9,8},{10,11... | collective-permute-start | bytes 12296 | tf_op jit(solution)/shard_map/ppermute | solution.py:393
  83.1 0.9 %collective-permute-done.17.refs_7_ = f32[3,8,2048]{2,1,0:T(8,128)S(1)} collective-permute-done((f32[3,8,2048]{2,1,0:T(8,128)S(1)}, f32[3,8,2048]{2,1,0:T(8,128)S(1)}, u32[]{:S(2)}, u32[]{:S(2)}) %collective-permute-start.17) | collective-permute-done | bytes 196640 | tf_op jit(solution)/shard_map/ppermute | solution.py:381
  84.1 1.3 %shard_map.74 = f32[4,3,8,4096]{3,2,1,0:T(8,128)} custom-call(f32[3,8,2048]{2,1,0:T(8,128)S(1)} %get-tuple-element.35.refs_0_, f32[3,8,2048]{2,1,0:T(8,128)S(1)} %collective-permute-done.7.refs_1_, f32[3,8,2048]{2,1,0:T(8,128)S(1)} %get-tuple-element.39.refs_2_, f32[3,8,2048]{2,1,0:T(8,128)S(1)} %collective-permute-done.10.refs_3_, ...), custom_call_target="tpu_custom_call" | custom-call | bytes 300000 | tf_op jit(solution)/shard_map/pallas_call | solution.py:313
  85.3 0.5 multiply_bitcast_fusion.1
  (39 shorter events, 1.0 us)
Async XLA Ops:
  0.6 3.8 %collective-permute-start = (f32[4,3,8,4096]{3,2,1,0:T(8,128)}, f32[4,3,8,4096]{3,2,1,0:T(8,128)S(1)}, u32[]{:S(2)}, u32[]{:S(2)}) collective-permute-start(f32[4,3,8,4096]{3,2,1,0:T(8,128)} %own.1), channel_id=1, source_target_pairs={{0,8},{8,0},{1,9},{9,1},{2,10},{10,2},{3,11},{11,3},{4,12},{12,4},... | collective-permute-start | bytes 4718600 | tf_op jit(solution)/shard_map/ppermute | solution.py:339
  1.1 1.4 %copy-start = (f32[4,3,8,4096]{3,2,1,0:T(8,128)S(1)}, f32[4,3,8,4096]{3,2,1,0:T(8,128)}, u32[]{:S(2)}) copy-start(f32[4,3,8,4096]{3,2,1,0:T(8,128)} %own.1) | copy-start | bytes 4718596
  2.6 0.7 copy-start.2
  3.2 1.4 %copy-start.1 = (f32[4,3,8,4096]{3,2,1,0:T(8,128)S(1)}, f32[4,3,8,4096]{3,2,1,0:T(8,128)}, u32[]{:S(2)}) copy-start(f32[4,3,8,4096]{3,2,1,0:T(8,128)} %own.1) | copy-start | bytes 4718596
  4.4 5.8 %copy-start.3 = (f32[8,128]{1,0:T(8,128)S(1)}, f32[8,128]{1,0:T(8,128)}, u32[]{:S(2)}) copy-start(f32[8,128]{1,0:T(8,128)} %param.9) | copy-start | bytes 12292
  4.4 5.9 %copy-start.4 = (s32[8,128]{1,0:T(8,128)S(1)}, s32[8,128]{1,0:T(8,128)}, u32[]{:S(2)}) copy-start(s32[8,128]{1,0:T(8,128)} %param.8) | copy-start | bytes 12292
  4.5 13.2 %copy-start.5 = (f32[8,128]{1,0:T(8,128)S(1)}, f32[8,128]{1,0:T(8,128)}, u32[]{:S(2)}) copy-start(f32[8,128]{1,0:T(8,128)} %param.7) | copy-start | bytes 12292
  5.4 19.8 %collective-permute-start.1 = (f32[3,8,4096]{2,1,0:T(8,128)S(1)}, f32[3,8,4096]{2,1,0:T(8,128)S(1)}, u32[]{:S(2)}, u32[]{:S(2)}) collective-permute-start(f32[3,8,4096]{2,1,0:T(8,128)S(1)} %get-tuple-element.31.refs_0_), channel_id=1, source_target_pairs={{0,6},{1,3},{2,0},{3,5},{4,2},{5,7},{6,4},{7,1},{8,14},{9,11},{10,... | collective-permute-start | bytes 1179656 | tf_op jit(solution)/shard_map/ppermute | solution.py:364
  10.3 7.4 %collective-permute-start.2 = (f32[3,8,2304]{2,1,0:T(8,128)S(1)}, f32[3,8,2304]{2,1,0:T(8,128)S(1)}, u32[]{:S(2)}, u32[]{:S(2)}) collective-permute-start(f32[3,8,2304]{2,1,0:T(8,128)S(1)} %get-tuple-element.32), channel_id=1, source_target_pairs={{0,1},{1,0},{2,3},{3,2},{4,5},{5,4},{6,7},{7,6},{8,9},{9,8},{10,11... | collective-permute-start | bytes 663560 | tf_op jit(solution)/shard_map/ppermute | solution.py:371
  10.3 12.4 %collective-permute-start.4 = (f32[6,8,512]{2,1,0:T(8,128)S(1)}, f32[6,8,512]{2,1,0:T(8,128)S(1)}, u32[]{:S(2)}, u32[]{:S(2)}) collective-permute-start(f32[6,8,512]{2,1,0:T(8,128)S(1)} %get-tuple-element.33), channel_id=1, source_target_pairs={{0,2},{1,7},{2,4},{3,1},{4,6},{5,3},{6,0},{7,5},{8,10},{9,15},{10,... | collective-permute-start | bytes 294920 | tf_op jit(solution)/shard_map/ppermute | solution.py:351
  11.4 13.8 %collective-permute-start.5 = (f32[6,8,512]{2,1,0:T(8,128)S(1)}, f32[6,8,512]{2,1,0:T(8,128)S(1)}, u32[]{:S(2)}, u32[]{:S(2)}) collective-permute-start(f32[6,8,512]{2,1,0:T(8,128)S(1)} %get-tuple-element.34), channel_id=1, source_target_pairs={{0,3},{1,6},{2,5},{3,0},{4,7},{5,2},{6,1},{7,4},{8,11},{9,14},{10,... | collective-permute-start | bytes 294920 | tf_op jit(solution)/shard_map/ppermute | solution.py:352
  17.7 11.3 %collective-permute-start.3 = (f32[3,8,2304]{2,1,0:T(8,128)S(1)}, f32[3,8,2304]{2,1,0:T(8,128)S(1)}, u32[]{:S(2)}, u32[]{:S(2)}) collective-permute-start(f32[3,8,2304]{2,1,0:T(8,128)S(1)} %collective-permute-done.2.refs_2_), channel_id=1, source_target_pairs={{0,2},{1,7},{2,4},{3,1},{4,6},{5,3},{6,0},{7,5},{8,10},{9,15},{10,... | collective-permute-start | bytes 663560 | tf_op jit(solution)/shard_map/ppermute | solution.py:375
  17.7 3.8 %collective-permute-start.6 = (f32[3,8,128]{2,1,0:T(8,128)S(1)}, f32[3,8,128]{2,1,0:T(8,128)S(1)}, u32[]{:S(2)}, u32[]{:S(2)}) collective-permute-start(f32[3,8,128]{2,1,0:T(8,128)S(1)} %pad_maximum_fusion.refs_6_.refs_8_), channel_id=1, source_target_pairs={{0,1},{1,0},{2,3},{3,2},{4,5},{5,4},{6,7},{7,6},{8,9},{9,8},{10,11... | collective-permute-start | bytes 36872 | tf_op jit(solution)/shard_map/ppermute | solution.py:354
  25.2 6.2 %collective-permute-start.8 = (f32[3,8,1792]{2,1,0:T(8,128)S(1)}, f32[3,8,1792]{2,1,0:T(8,128)S(1)}, u32[]{:S(2)}, u32[]{:S(2)}) collective-permute-start(f32[3,8,1792]{2,1,0:T(8,128)S(1)} %get-tuple-element.38), channel_id=1, source_target_pairs={{0,1},{1,0},{2,3},{3,2},{4,5},{5,4},{6,7},{7,6},{8,9},{9,8},{10,11... | collective-permute-start | bytes 516104 | tf_op jit(solution)/shard_map/ppermute | solution.py:371
  31.4 14.0 %collective-permute-start.12 = (f32[3,8,2304]{2,1,0:T(8,128)S(1)}, f32[3,8,2304]{2,1,0:T(8,128)S(1)}, u32[]{:S(2)}, u32[]{:S(2)}) collective-permute-start(f32[3,8,2304]{2,1,0:T(8,128)S(1)} %get-tuple-element.44), channel_id=1, source_target_pairs={{0,1},{1,0},{2,3},{3,2},{4,5},{5,4},{6,7},{7,6},{8,9},{9,8},{10,11... | collective-permute-start | bytes 663560 | tf_op jit(solution)/shard_map/ppermute | solution.py:371
  31.7 29.1 %collective-permute-start.11 = (f32[3,8,4096]{2,1,0:T(8,128)S(1)}, f32[3,8,4096]{2,1,0:T(8,128)S(1)}, u32[]{:S(2)}, u32[]{:S(2)}) collective-permute-start(f32[3,8,4096]{2,1,0:T(8,128)S(1)} %get-tuple-element.42.refs_0_), channel_id=1, source_target_pairs={{0,6},{1,3},{2,0},{3,5},{4,2},{5,7},{6,4},{7,1},{8,14},{9,11},{10,... | collective-permute-start | bytes 1179656 | tf_op jit(solution)/shard_map/ppermute | solution.py:364
  45.3 7.3 %collective-permute-start.9 = (f32[3,8,1792]{2,1,0:T(8,128)S(1)}, f32[3,8,1792]{2,1,0:T(8,128)S(1)}, u32[]{:S(2)}, u32[]{:S(2)}) collective-permute-start(f32[3,8,1792]{2,1,0:T(8,128)S(1)} %collective-permute-done.8.refs_3_), channel_id=1, source_target_pairs={{0,2},{1,7},{2,4},{3,1},{4,6},{5,3},{6,0},{7,5},{8,10},{9,15},{10,... | collective-permute-start | bytes 516104 | tf_op jit(solution)/shard_map/ppermute | solution.py:375
  45.4 13.3 %collective-permute-start.15 = (f32[3,8,1792]{2,1,0:T(8,128)S(1)}, f32[3,8,1792]{2,1,0:T(8,128)S(1)}, u32[]{:S(2)}, u32[]{:S(2)}) collective-permute-start(f32[3,8,1792]{2,1,0:T(8,128)S(1)} %get-tuple-element.50), channel_id=1, source_target_pairs={{0,1},{1,0},{2,3},{3,2},{4,5},{5,4},{6,7},{7,6},{8,9},{9,8},{10,11... | collective-permute-start | bytes 516104 | tf_op jit(solution)/shard_map/ppermute | solution.py:371
  45.4 15.4 %collective-permute-start.13 = (f32[3,8,2304]{2,1,0:T(8,128)S(1)}, f32[3,8,2304]{2,1,0:T(8,128)S(1)}, u32[]{:S(2)}, u32[]{:S(2)}) collective-permute-start(f32[3,8,2304]{2,1,0:T(8,128)S(1)} %collective-permute-done.12.refs_2_), channel_id=1, source_target_pairs={{0,2},{1,7},{2,4},{3,1},{4,6},{5,3},{6,0},{7,5},{8,10},{9,15},{10,... | collective-permute-start | bytes 663560 | tf_op jit(solution)/shard_map/ppermute | solution.py:375
  58.6 8.4 %collective-permute-start.16 = (f32[3,8,1792]{2,1,0:T(8,128)S(1)}, f32[3,8,1792]{2,1,0:T(8,128)S(1)}, u32[]{:S(2)}, u32[]{:S(2)}) collective-permute-start(f32[3,8,1792]{2,1,0:T(8,128)S(1)} %collective-permute-done.15.refs_3_), channel_id=1, source_target_pairs={{0,2},{1,7},{2,4},{3,1},{4,6},{5,3},{6,0},{7,5},{8,10},{9,15},{10,... | collective-permute-start | bytes 516104 | tf_op jit(solution)/shard_map/ppermute | solution.py:375
  58.7 14.4 %collective-permute-start.7 = (f32[3,8,2048]{2,1,0:T(8,128)S(1)}, f32[3,8,2048]{2,1,0:T(8,128)S(1)}, u32[]{:S(2)}, u32[]{:S(2)}) collective-permute-start(f32[3,8,2048]{2,1,0:T(8,128)S(1)} %get-tuple-element.36), channel_id=1, source_target_pairs={{0,1},{1,0},{2,3},{3,2},{4,5},{5,4},{6,7},{7,6},{8,9},{9,8},{10,11... | collective-permute-start | bytes 589832 | tf_op jit(solution)/shard_map/ppermute | solution.py:381
  58.8 14.4 %collective-permute-start.10 = (f32[3,8,2048]{2,1,0:T(8,128)S(1)}, f32[3,8,2048]{2,1,0:T(8,128)S(1)}, u32[]{:S(2)}, u32[]{:S(2)}) collective-permute-start(f32[3,8,2048]{2,1,0:T(8,128)S(1)} %get-tuple-element.40), channel_id=1, source_target_pairs={{0,1},{1,0},{2,3},{3,2},{4,5},{5,4},{6,7},{7,6},{8,9},{9,8},{10,11... | collective-permute-start | bytes 589832 | tf_op jit(solution)/shard_map/ppermute | solution.py:381
  66.9 6.3 %collective-permute-start.14 = (f32[3,8,2048]{2,1,0:T(8,128)S(1)}, f32[3,8,2048]{2,1,0:T(8,128)S(1)}, u32[]{:S(2)}, u32[]{:S(2)}) collective-permute-start(f32[3,8,2048]{2,1,0:T(8,128)S(1)} %get-tuple-element.48), channel_id=1, source_target_pairs={{0,1},{1,0},{2,3},{3,2},{4,5},{5,4},{6,7},{7,6},{8,9},{9,8},{10,11... | collective-permute-start | bytes 589832 | tf_op jit(solution)/shard_map/ppermute | solution.py:381
  73.2 7.2 %collective-permute-start.18 = (f32[8,128]{1,0:T(8,128)S(1)}, f32[8,128]{1,0:T(8,128)S(1)}, u32[]{:S(2)}, u32[]{:S(2)}) collective-permute-start(f32[8,128]{1,0:T(8,128)S(1)} %add_add_fusion.1), channel_id=1, source_target_pairs={{0,4},{1,5},{2,6},{3,7},{4,0},{5,1},{6,2},{7,3},{8,12},{9,13},{10,... | collective-permute-start | bytes 12296 | tf_op jit(solution)/shard_map/ppermute | solution.py:386
  74.6 5.8 %collective-permute-start.19 = (f32[8,128]{1,0:T(8,128)S(1)}, f32[8,128]{1,0:T(8,128)S(1)}, u32[]{:S(2)}, u32[]{:S(2)}) collective-permute-start(f32[8,128]{1,0:T(8,128)S(1)} %add_add_fusion.1), channel_id=1, source_target_pairs={{0,2},{1,3},{2,4},{3,5},{4,6},{5,7},{6,0},{7,1},{8,10},{9,11},{10,... | collective-permute-start | bytes 12296 | tf_op jit(solution)/shard_map/ppermute | solution.py:386
  77.5 3.6 %collective-permute-start.20 = (f32[8,128]{1,0:T(8,128)S(1)}, f32[8,128]{1,0:T(8,128)S(1)}, u32[]{:S(2)}, u32[]{:S(2)}) collective-permute-start(f32[8,128]{1,0:T(8,128)S(1)} %add_add_fusion.1), channel_id=1, source_target_pairs={{0,6},{1,7},{2,0},{3,1},{4,2},{5,3},{6,4},{7,5},{8,14},{9,15},{10,... | collective-permute-start | bytes 12296 | tf_op jit(solution)/shard_map/ppermute | solution.py:386
  78.4 5.7 %collective-permute-start.17 = (f32[3,8,2048]{2,1,0:T(8,128)S(1)}, f32[3,8,2048]{2,1,0:T(8,128)S(1)}, u32[]{:S(2)}, u32[]{:S(2)}) collective-permute-start(f32[3,8,2048]{2,1,0:T(8,128)S(1)} %get-tuple-element.54), channel_id=1, source_target_pairs={{0,1},{1,0},{2,3},{3,2},{4,5},{5,4},{6,7},{7,6},{8,9},{9,8},{10,11... | collective-permute-start | bytes 589832 | tf_op jit(solution)/shard_map/ppermute | solution.py:381
  81.1 4.2 %collective-permute-start.21 = (f32[8,128]{1,0:T(8,128)S(1)}, f32[8,128]{1,0:T(8,128)S(1)}, u32[]{:S(2)}, u32[]{:S(2)}) collective-permute-start(f32[8,128]{1,0:T(8,128)S(1)} %add_add_fusion), channel_id=1, source_target_pairs={{0,1},{1,0},{2,3},{3,2},{4,5},{5,4},{6,7},{7,6},{8,9},{9,8},{10,11... | collective-permute-start | bytes 12296 | tf_op jit(solution)/shard_map/ppermute | solution.py:393

commit v7 on v6

--- a/solution.py
+++ b/solution.py
@@ -29,6 +29,8 @@
 
 def plan(ncol, slot, slots):
     every = list(range(ncol))
+    if slot < slots - 1:
+        return ((every, every, every),)
     cut = ncol // 2 + 2
     return (
         (every[:cut], every[:cut], every[1 : cut - 1]),
@@ -354,29 +356,33 @@
     obs_got = lax.ppermute(obs_own, "strip", swap)
 
     pieces = [(k, p) for k in range(half) for p in range(len(spans[k]))]
-    got, passed, direct = [[] for _ in range(half)], [[] for _ in range(half)], []
-    swapped, last, blocks, misfits = [], [], [], []
-    for n, (k, p) in enumerate(pieces):
-        giving, keeping = given[k][p], kept[k]
-        if p == 0:
-            if k:
-                (keeping,) = after((keeping,), last[n - 2])
-            direct.append(lax.ppermute(keeping, "strip", straight))
-        if n == 1:
-            (giving,) = after((giving,), (swapped[0], direct[0], near, far, obs_got))
-        elif n == 2:
-            (giving,) = after((giving,), (swapped[1], last[0]))
-        elif n:
-            (giving,) = after((giving,), (swapped[-1], misfits[n - 3]))
-        swapped.append(lax.ppermute(giving, "strip", swap))
-        goes = swapped[n]
-        if n > 1:
-            (goes,) = after((goes,), misfits[n - 2])
-        last.append(lax.ppermute(goes, "strip", onward))
-        got[k].append(swapped[n])
-        passed[k].append(last[n])
+    got, passed, direct, blocks, misfits = [], [], [], [], []
+    first = None
+    for k in range(half):
+        giving, keeping = tuple(given[k]), kept[k]
+        if k:
+            *giving, keeping = after((*giving, keeping), first)
+        direct.append(lax.ppermute(keeping, "strip", straight))
+        got.append([lax.ppermute(g, "strip", swap) for g in giving])
+        passed.append([lax.ppermute(g, "strip", onward) for g in got[k]])
+        if first is None:
+            first = (direct[0], got[0], near, far, obs_got)
+    for k, p in pieces:
+        (own,) = after((kept[k],), got[-1])
         keep, send, misfit = forecast(
-            kept[k], got[k], direct[k], passed[k], near, far, obs_own, obs_got, p, k, half, ncol, total_rows
+            own,
+            got[k][: p + 1],
+            direct[k],
+            passed[k][: p + 1],
+            near,
+            far,
+            obs_own,
+            obs_got,
+            p,
+            k,
+            half,
+            ncol,
+            total_rows,
         )
         blocks.append((keep, lax.ppermute(send, "strip", swap)))
         misfits.append(misfit)

time: 86 us -> 76.5 us (0.89)
  waiting for transfers between devices: 23.5 us -> 16 us
  Pallas kernels: 27.5 us -> 24.2 us
  starting transfers between devices: 31.2 us -> 32.6 us
    ppermute x8 -> x6, starting transfers between devices: 1.6 us -> 7.25 us  [the longest x3 5.06 us: local(): got.append([lax.ppermute(g, 'strip', swap) for g in giving])]
    ppermute x8 -> x6, waiting for transfers between devices: 16.1 us -> 10.9 us  [the longest x3 10.9 us: local(): got.append([lax.ppermute(g, 'strip', swap) for g in giving])]
    pallas_call x4 -> x3, Pallas kernels: 24.3 us -> 21 us  [forecast(): pl.pallas_call(functools.partial(forecast_kernel, worked=worked, kept=kep...]
    ppermute x1, starting transfers between devices: 2.43 us -> 0.07 us  [local(): far = lax.ppermute(far, 'strip', cross)]
    ppermute x1, waiting for transfers between devices: 2.51 us -> 0.38 us  [local(): far = lax.ppermute(far, 'strip', cross)]
    ppermute x1, starting transfers between devices: 1.81 us -> 3.74 us  [local(): obs_got = lax.ppermute(obs_own, 'strip', swap)]
    ppermute x3, waiting for transfers between devices: 0.74 us -> 2.52 us  [local(): lax.ppermute(total, 'strip', moved(step, step))]
    ppermute x2, starting transfers between devices: 12.3 us -> 10.6 us  [local(): direct.append(lax.ppermute(keeping, 'strip', straight))]
  transfers between devices with their start and end apart: 22 -> 19, of which waited for: 9 -> 6; matrix products, arithmetic and copies ran while one was open for 0% -> 0% of each run, Pallas kernels for 31% -> 31%
where the time goes in v7:
time: 76.5 us; the launch traced here: 76.4 us
  starting transfers between devices  32.6 us (43%)
  Pallas kernels  24.2 us (32%)
  waiting for transfers between devices  16 us (21%)
  local copies, waits for them, and re-layouts  2.24 us (3%)
    pallas_call x3, Pallas kernels, forecast(): pl.pallas_call(functools.partial(forecast_kernel, worked=worked, kept=kep...  21 us
    ppermute x3, waiting for transfers between devices, local(): got.append([lax.ppermute(g, 'strip', swap) for g in giving])  10.9 us
    ppermute x2, starting transfers between devices, local(): direct.append(lax.ppermute(keeping, 'strip', straight))  10.6 us
    ppermute x3, starting transfers between devices, local(): got.append([lax.ppermute(g, 'strip', swap) for g in giving])  5.06 us
    ppermute x3, starting transfers between devices, local(): blocks.append((keep, lax.ppermute(send, 'strip', swap)))  4.36 us
    ppermute x3, starting transfers between devices, local(): lax.ppermute(total, 'strip', moved(step, step))  4.05 us
    ppermute x1, starting transfers between devices, local(): obs_got = lax.ppermute(obs_own, 'strip', swap)  3.74 us
    ppermute x3, waiting for transfers between devices, local(): lax.ppermute(total, 'strip', moved(step, step))  2.52 us
  transfers between devices with their start and end apart: 19, of which 6 were waited for; matrix products, arithmetic and copies ran while one was open for 0% of the time, Pallas kernels for 31%

profile of v7, /device:TPU:0, one launch (start us, length us, event | category | flops | bytes accessed | tf_op | source)
XLA Modules:
  0.0 76.4 jit_solution(4024610963967831363)
XLA Ops:
  0.6 0.5 collective-permute-start
  1.1 1.4 %copy-done = f32[4,3,8,4096]{3,2,1,0:T(8,128)S(1)} copy-done((f32[4,3,8,4096]{3,2,1,0:T(8,128)S(1)}, f32[4,3,8,4096]{3,2,1,0:T(8,128)}, u32[]{:S(2)}) %copy-start) | copy-done | bytes 1572888
  2.6 0.7 copy-done.2
  3.2 1.2 %shard_map.68.index = s32[4]{0:T(128)S(1)} custom-call(s32[8]{0:T(128)S(1)} %copy-done.2, f32[4,3,8,4096]{3,2,1,0:T(8,128)S(1)} %copy-done), custom_call_target="tpu_custom_call" | custom-call | tf_op jit(solution)/shard_map/pallas_call | solution.py:66
  4.5 0.2 copy-done.1
  4.6 0.8 %shard_map.69 = (f32[3,8,4096]{2,1,0:T(8,128)S(1)}, f32[3,8,4096]{2,1,0:T(8,128)S(1)}, f32[3,8,4096]{2,1,0:T(8,128)S(1)}, f32[3,8,2304]{2,1,0:T(8,128)S(1)}, f32...) custom-call(s32[4]{0:T(128)S(1)} %shard_map.68.index, f32[4,3,8,4096]{3,2,1,0:T(8,128)S(1)} %copy-done.1, ...), custom_call_target="tpu_custom_call" | custom-call | tf_op jit(solution)/shard_map/pallas_call | solution.py:130
  5.4 2.7 %collective-permute-start.2 = (f32[3,8,4096]{2,1,0:T(8,128)S(1)}, f32[3,8,4096]{2,1,0:T(8,128)S(1)}, u32[]{:S(2)}, u32[]{:S(2)}) collective-permute-start(f32[3,8,4096]{2,1,0:T(8,128)S(1)} %get-tuple-element.30), channel_id=1, source_target_pairs={{0,1},{1,0},{2,3},{3,2},{4,5},{5,4},{6,7},{7,6},{8,9},{9,8},{10,11... | collective-permute-start | bytes 1179656 | tf_op jit(solution)/shard_map/ppermute | solution.py:366
  8.1 3.6 %collective-permute-start.1 = (f32[3,8,4096]{2,1,0:T(8,128)S(1)}, f32[3,8,4096]{2,1,0:T(8,128)S(1)}, u32[]{:S(2)}, u32[]{:S(2)}) collective-permute-start(f32[3,8,4096]{2,1,0:T(8,128)S(1)} %get-tuple-element.35.refs_0_), channel_id=1, source_target_pairs={{0,6},{1,3},{2,0},{3,5},{4,2},{5,7},{6,4},{7,1},{8,14},{9,11},{10,... | collective-permute-start | bytes 1179656 | tf_op jit(solution)/shard_map/ppermute | solution.py:365
  11.8 0.1 multiply_bitcast_fusion
  11.9 5.9 %collective-permute-done.2.refs_2_ = f32[3,8,4096]{2,1,0:T(8,128)S(1)} collective-permute-done((f32[3,8,4096]{2,1,0:T(8,128)S(1)}, f32[3,8,4096]{2,1,0:T(8,128)S(1)}, u32[]{:S(2)}, u32[]{:S(2)}) %collective-permute-start.2) | collective-permute-done | bytes 393248 | tf_op jit(solution)/shard_map/ppermute | solution.py:366
  17.8 1.8 %collective-permute-start.8 = (f32[3,8,4096]{2,1,0:T(8,128)S(1)}, f32[3,8,4096]{2,1,0:T(8,128)S(1)}, u32[]{:S(2)}, u32[]{:S(2)}) collective-permute-start(f32[3,8,4096]{2,1,0:T(8,128)S(1)} %collective-permute-done.2.refs_2_), channel_id=1, source_target_pairs={{0,2},{1,7},{2,4},{3,1},{4,6},{5,3},{6,0},{7,5},{8,10},{9,15},{10,... | collective-permute-start | bytes 1179656 | tf_op jit(solution)/shard_map/ppermute | solution.py:367
  19.6 3.7 %collective-permute-start.5 = (f32[3,8,128]{2,1,0:T(8,128)S(1)}, f32[3,8,128]{2,1,0:T(8,128)S(1)}, u32[]{:S(2)}, u32[]{:S(2)}) collective-permute-start(f32[3,8,128]{2,1,0:T(8,128)S(1)} %pad_maximum_fusion.refs_6_.refs_8_), channel_id=1, source_target_pairs={{0,1},{1,0},{2,3},{3,2},{4,5},{5,4},{6,7},{7,6},{8,9},{9,8},{10,11... | collective-permute-start | bytes 36872 | tf_op jit(solution)/shard_map/ppermute | solution.py:356
  23.3 1.8 %collective-permute-done.5.refs_7_.refs_9_ = f32[3,8,128]{2,1,0:T(8,128)S(1)} collective-permute-done((f32[3,8,128]{2,1,0:T(8,128)S(1)}, f32[3,8,128]{2,1,0:T(8,128)S(1)}, u32[]{:S(2)}, u32[]{:S(2)}) %collective-permute-start.5) | collective-permute-done | bytes 12320 | tf_op jit(solution)/shard_map/ppermute | solution.py:356
  25.1 0.4 collective-permute-done.4.refs_5_.refs_7_
  25.5 2.3 %collective-permute-start.6 = (f32[3,8,2304]{2,1,0:T(8,128)S(1)}, f32[3,8,2304]{2,1,0:T(8,128)S(1)}, u32[]{:S(2)}, u32[]{:S(2)}) collective-permute-start(f32[3,8,2304]{2,1,0:T(8,128)S(1)} %get-tuple-element.33), channel_id=1, source_target_pairs={{0,1},{1,0},{2,3},{3,2},{4,5},{5,4},{6,7},{7,6},{8,9},{9,8},{10,11... | collective-permute-start | bytes 663560 | tf_op jit(solution)/shard_map/ppermute | solution.py:366
  27.8 7.0 %collective-permute-start.10 = (f32[3,8,4096]{2,1,0:T(8,128)S(1)}, f32[3,8,4096]{2,1,0:T(8,128)S(1)}, u32[]{:S(2)}, u32[]{:S(2)}) collective-permute-start(f32[3,8,4096]{2,1,0:T(8,128)S(1)} %get-tuple-element.39.refs_0_), channel_id=1, source_target_pairs={{0,6},{1,3},{2,0},{3,5},{4,2},{5,7},{6,4},{7,1},{8,14},{9,11},{10,... | collective-permute-start | bytes 1179656 | tf_op jit(solution)/shard_map/ppermute | solution.py:365
  34.8 0.4 collective-permute-start.11
  35.2 5.0 %collective-permute-done.7.refs_3_ = f32[3,8,1792]{2,1,0:T(8,128)S(1)} collective-permute-done((f32[3,8,1792]{2,1,0:T(8,128)S(1)}, f32[3,8,1792]{2,1,0:T(8,128)S(1)}, u32[]{:S(2)}, u32[]{:S(2)}) %collective-permute-start.7) | collective-permute-done | bytes 172064 | tf_op jit(solution)/shard_map/ppermute | solution.py:366
  40.2 8.9 %shard_map.70 = (f32[3,8,4096]{2,1,0:T(8,128)S(1)}, f32[3,8,4096]{2,1,0:T(8,128)S(1)}, f32[8,128]{1,0:T(8,128)S(1)}) custom-call(f32[3,8,4096]{2,1,0:T(8,128)S(1)} %get-tuple-element.35.refs_0_, f32[3,8,4096]{2,1,0:T(8,128)S(1)} %collective-permute-done.1.refs_1_, f32[3,8,4096]{2,1,0:T(8,128)S(1)} %collective-permute-done.2.refs_2_, ...), custom_call_target="tpu_custom_call" | custom-call | bytes 480000 | tf_op jit(solution)/shard_map/pallas_call | solution.py:282
  49.1 2.4 %collective-permute-start.9 = (f32[3,8,4096]{2,1,0:T(8,128)S(1)}, f32[3,8,4096]{2,1,0:T(8,128)S(1)}, u32[]{:S(2)}, u32[]{:S(2)}) collective-permute-start(f32[3,8,4096]{2,1,0:T(8,128)S(1)} %get-tuple-element.37), channel_id=1, source_target_pairs={{0,1},{1,0},{2,3},{3,2},{4,5},{5,4},{6,7},{7,6},{8,9},{9,8},{10,11... | collective-permute-start | bytes 1179656 | tf_op jit(solution)/shard_map/ppermute | solution.py:387
  51.5 6.1 %shard_map.71 = (f32[3,8,2048]{2,1,0:T(8,128)S(1)}, f32[3,8,2048]{2,1,0:T(8,128)S(1)}, f32[8,128]{1,0:T(8,128)S(1)}) custom-call(f32[3,8,4096]{2,1,0:T(8,128)S(1)} %get-tuple-element.39.refs_0_, f32[3,8,4096]{2,1,0:T(8,128)S(1)} %collective-permute-done.10.refs_1_, f32[3,8,2304]{2,1,0:T(8,128)S(1)} %collective-permute-done.6.refs_2_, ...), custom_call_target="tpu_custom_call" | custom-call | bytes 270000 | tf_op jit(solution)/shard_map/pallas_call | solution.py:282
  57.6 0.1 collective-permute-start.12
  57.7 6.1 %shard_map.72 = (f32[3,8,2048]{2,1,0:T(8,128)S(1)}, f32[3,8,2048]{2,1,0:T(8,128)S(1)}, f32[8,128]{1,0:T(8,128)S(1)}) custom-call(f32[3,8,4096]{2,1,0:T(8,128)S(1)} %get-tuple-element.39.refs_0_, f32[3,8,4096]{2,1,0:T(8,128)S(1)} %collective-permute-done.10.refs_1_, f32[3,8,2304]{2,1,0:T(8,128)S(1)} %collective-permute-done.6.refs_2_, ...), custom_call_target="tpu_custom_call" | custom-call | bytes 270000 | tf_op jit(solution)/shard_map/pallas_call | solution.py:282
  63.8 0.2 collective-permute-start.16
  64.1 3.6 %collective-permute-start.17 = (f32[8,128]{1,0:T(8,128)S(1)}, f32[8,128]{1,0:T(8,128)S(1)}, u32[]{:S(2)}, u32[]{:S(2)}) collective-permute-start(f32[8,128]{1,0:T(8,128)S(1)} %add_add_fusion.1), channel_id=1, source_target_pairs={{0,6},{1,7},{2,0},{3,1},{4,2},{5,3},{6,4},{7,5},{8,14},{9,15},{10,... | collective-permute-start | bytes 12296 | tf_op jit(solution)/shard_map/ppermute | solution.py:392
  67.7 0.2 collective-permute-start.15
  67.9 1.8 %collective-permute-start.14 = (f32[3,8,2048]{2,1,0:T(8,128)S(1)}, f32[3,8,2048]{2,1,0:T(8,128)S(1)}, u32[]{:S(2)}, u32[]{:S(2)}) collective-permute-start(f32[3,8,2048]{2,1,0:T(8,128)S(1)} %get-tuple-element.43), channel_id=1, source_target_pairs={{0,1},{1,0},{2,3},{3,2},{4,5},{5,4},{6,7},{7,6},{8,9},{9,8},{10,11... | collective-permute-start | bytes 589832 | tf_op jit(solution)/shard_map/ppermute | solution.py:387
  69.7 2.5 %collective-permute-done.15 = f32[8,128]{1,0:T(8,128)S(1)} collective-permute-done((f32[8,128]{1,0:T(8,128)S(1)}, f32[8,128]{1,0:T(8,128)S(1)}, u32[]{:S(2)}, u32[]{:S(2)}) %collective-permute-start.15) | collective-permute-done | bytes 4128 | tf_op jit(solution)/shard_map/ppermute | solution.py:392
  72.2 2.0 %collective-permute-start.18 = (f32[8,128]{1,0:T(8,128)S(1)}, f32[8,128]{1,0:T(8,128)S(1)}, u32[]{:S(2)}, u32[]{:S(2)}) collective-permute-start(f32[8,128]{1,0:T(8,128)S(1)} %add_add_fusion), channel_id=1, source_target_pairs={{0,1},{1,0},{2,3},{3,2},{4,5},{5,4},{6,7},{7,6},{8,9},{9,8},{10,11... | collective-permute-start | bytes 12296 | tf_op jit(solution)/shard_map/ppermute | solution.py:399
  74.2 1.3 %shard_map.73 = f32[4,3,8,4096]{3,2,1,0:T(8,128)} custom-call(f32[3,8,4096]{2,1,0:T(8,128)S(1)} %get-tuple-element.36.refs_0_, f32[3,8,4096]{2,1,0:T(8,128)S(1)} %collective-permute-done.9.refs_1_, f32[3,8,2048]{2,1,0:T(8,128)S(1)} %get-tuple-element.40.refs_2_, f32[3,8,2048]{2,1,0:T(8,128)S(1)} %collective-permute-done.12.refs_3_, ...), custom_call_target="tpu_custom_call" | custom-call | bytes 300000 | tf_op jit(solution)/shard_map/pallas_call | solution.py:315
  75.5 0.4 collective-permute-done.18
  75.8 0.5 multiply_bitcast_fusion.1
  (32 shorter events, 0.2 us)
Async XLA Ops:
  0.6 3.8 %collective-permute-start = (f32[4,3,8,4096]{3,2,1,0:T(8,128)}, f32[4,3,8,4096]{3,2,1,0:T(8,128)S(1)}, u32[]{:S(2)}, u32[]{:S(2)}) collective-permute-start(f32[4,3,8,4096]{3,2,1,0:T(8,128)} %own.1), channel_id=1, source_target_pairs={{0,8},{8,0},{1,9},{9,1},{2,10},{10,2},{3,11},{11,3},{4,12},{12,4},... | collective-permute-start | bytes 4718600 | tf_op jit(solution)/shard_map/ppermute | solution.py:341
  1.1 1.4 %copy-start = (f32[4,3,8,4096]{3,2,1,0:T(8,128)S(1)}, f32[4,3,8,4096]{3,2,1,0:T(8,128)}, u32[]{:S(2)}) copy-start(f32[4,3,8,4096]{3,2,1,0:T(8,128)} %own.1) | copy-start | bytes 4718596
  2.6 0.7 copy-start.2
  3.2 1.4 %copy-start.1 = (f32[4,3,8,4096]{3,2,1,0:T(8,128)S(1)}, f32[4,3,8,4096]{3,2,1,0:T(8,128)}, u32[]{:S(2)}) copy-start(f32[4,3,8,4096]{3,2,1,0:T(8,128)} %own.1) | copy-start | bytes 4718596
  4.4 3.7 %copy-start.3 = (s32[8,128]{1,0:T(8,128)S(1)}, s32[8,128]{1,0:T(8,128)}, u32[]{:S(2)}) copy-start(s32[8,128]{1,0:T(8,128)} %param.8) | copy-start | bytes 12292
  4.4 7.3 %copy-start.4 = (f32[8,128]{1,0:T(8,128)S(1)}, f32[8,128]{1,0:T(8,128)}, u32[]{:S(2)}) copy-start(f32[8,128]{1,0:T(8,128)} %param.9) | copy-start | bytes 12292
  4.4 15.1 %copy-start.5 = (f32[8,128]{1,0:T(8,128)S(1)}, f32[8,128]{1,0:T(8,128)}, u32[]{:S(2)}) copy-start(f32[8,128]{1,0:T(8,128)} %param.7) | copy-start | bytes 12292
  5.4 12.4 %collective-permute-start.2 = (f32[3,8,4096]{2,1,0:T(8,128)S(1)}, f32[3,8,4096]{2,1,0:T(8,128)S(1)}, u32[]{:S(2)}, u32[]{:S(2)}) collective-permute-start(f32[3,8,4096]{2,1,0:T(8,128)S(1)} %get-tuple-element.30), channel_id=1, source_target_pairs={{0,1},{1,0},{2,3},{3,2},{4,5},{5,4},{6,7},{7,6},{8,9},{9,8},{10,11... | collective-permute-start | bytes 1179656 | tf_op jit(solution)/shard_map/ppermute | solution.py:366
  8.1 17.4 %collective-permute-start.1 = (f32[3,8,4096]{2,1,0:T(8,128)S(1)}, f32[3,8,4096]{2,1,0:T(8,128)S(1)}, u32[]{:S(2)}, u32[]{:S(2)}) collective-permute-start(f32[3,8,4096]{2,1,0:T(8,128)S(1)} %get-tuple-element.35.refs_0_), channel_id=1, source_target_pairs={{0,6},{1,3},{2,0},{3,5},{4,2},{5,7},{6,4},{7,1},{8,14},{9,11},{10,... | collective-permute-start | bytes 1179656 | tf_op jit(solution)/shard_map/ppermute | solution.py:365
  11.8 13.3 %collective-permute-start.3 = (f32[6,8,512]{2,1,0:T(8,128)S(1)}, f32[6,8,512]{2,1,0:T(8,128)S(1)}, u32[]{:S(2)}, u32[]{:S(2)}) collective-permute-start(f32[6,8,512]{2,1,0:T(8,128)S(1)} %get-tuple-element.31), channel_id=1, source_target_pairs={{0,2},{1,7},{2,4},{3,1},{4,6},{5,3},{6,0},{7,5},{8,10},{9,15},{10,... | collective-permute-start | bytes 294920 | tf_op jit(solution)/shard_map/ppermute | solution.py:353
  11.8 13.7 %collective-permute-start.4 = (f32[6,8,512]{2,1,0:T(8,128)S(1)}, f32[6,8,512]{2,1,0:T(8,128)S(1)}, u32[]{:S(2)}, u32[]{:S(2)}) collective-permute-start(f32[6,8,512]{2,1,0:T(8,128)S(1)} %get-tuple-element.32), channel_id=1, source_target_pairs={{0,3},{1,6},{2,5},{3,0},{4,7},{5,2},{6,1},{7,4},{8,11},{9,14},{10,... | collective-permute-start | bytes 294920 | tf_op jit(solution)/shard_map/ppermute | solution.py:354
  17.8 22.5 %collective-permute-start.8 = (f32[3,8,4096]{2,1,0:T(8,128)S(1)}, f32[3,8,4096]{2,1,0:T(8,128)S(1)}, u32[]{:S(2)}, u32[]{:S(2)}) collective-permute-start(f32[3,8,4096]{2,1,0:T(8,128)S(1)} %collective-permute-done.2.refs_2_), channel_id=1, source_target_pairs={{0,2},{1,7},{2,4},{3,1},{4,6},{5,3},{6,0},{7,5},{8,10},{9,15},{10,... | collective-permute-start | bytes 1179656 | tf_op jit(solution)/shard_map/ppermute | solution.py:367
  19.6 5.5 %collective-permute-start.5 = (f32[3,8,128]{2,1,0:T(8,128)S(1)}, f32[3,8,128]{2,1,0:T(8,128)S(1)}, u32[]{:S(2)}, u32[]{:S(2)}) collective-permute-start(f32[3,8,128]{2,1,0:T(8,128)S(1)} %pad_maximum_fusion.refs_6_.refs_8_), channel_id=1, source_target_pairs={{0,1},{1,0},{2,3},{3,2},{4,5},{5,4},{6,7},{7,6},{8,9},{9,8},{10,11... | collective-permute-start | bytes 36872 | tf_op jit(solution)/shard_map/ppermute | solution.py:356
  25.5 9.3 %collective-permute-start.6 = (f32[3,8,2304]{2,1,0:T(8,128)S(1)}, f32[3,8,2304]{2,1,0:T(8,128)S(1)}, u32[]{:S(2)}, u32[]{:S(2)}) collective-permute-start(f32[3,8,2304]{2,1,0:T(8,128)S(1)} %get-tuple-element.33), channel_id=1, source_target_pairs={{0,1},{1,0},{2,3},{3,2},{4,5},{5,4},{6,7},{7,6},{8,9},{9,8},{10,11... | collective-permute-start | bytes 663560 | tf_op jit(solution)/shard_map/ppermute | solution.py:366
  27.8 23.7 %collective-permute-start.10 = (f32[3,8,4096]{2,1,0:T(8,128)S(1)}, f32[3,8,4096]{2,1,0:T(8,128)S(1)}, u32[]{:S(2)}, u32[]{:S(2)}) collective-permute-start(f32[3,8,4096]{2,1,0:T(8,128)S(1)} %get-tuple-element.39.refs_0_), channel_id=1, source_target_pairs={{0,6},{1,3},{2,0},{3,5},{4,2},{5,7},{6,4},{7,1},{8,14},{9,11},{10,... | collective-permute-start | bytes 1179656 | tf_op jit(solution)/shard_map/ppermute | solution.py:365
  34.8 5.4 %collective-permute-start.7 = (f32[3,8,1792]{2,1,0:T(8,128)S(1)}, f32[3,8,1792]{2,1,0:T(8,128)S(1)}, u32[]{:S(2)}, u32[]{:S(2)}) collective-permute-start(f32[3,8,1792]{2,1,0:T(8,128)S(1)} %get-tuple-element.34), channel_id=1, source_target_pairs={{0,1},{1,0},{2,3},{3,2},{4,5},{5,4},{6,7},{7,6},{8,9},{9,8},{10,11... | collective-permute-start | bytes 516104 | tf_op jit(solution)/shard_map/ppermute | solution.py:366
  34.8 16.7 %collective-permute-start.11 = (f32[3,8,2304]{2,1,0:T(8,128)S(1)}, f32[3,8,2304]{2,1,0:T(8,128)S(1)}, u32[]{:S(2)}, u32[]{:S(2)}) collective-permute-start(f32[3,8,2304]{2,1,0:T(8,128)S(1)} %collective-permute-done.6.refs_2_), channel_id=1, source_target_pairs={{0,2},{1,7},{2,4},{3,1},{4,6},{5,3},{6,0},{7,5},{8,10},{9,15},{10,... | collective-permute-start | bytes 663560 | tf_op jit(solution)/shard_map/ppermute | solution.py:367
  40.2 17.5 %collective-permute-start.13 = (f32[3,8,1792]{2,1,0:T(8,128)S(1)}, f32[3,8,1792]{2,1,0:T(8,128)S(1)}, u32[]{:S(2)}, u32[]{:S(2)}) collective-permute-start(f32[3,8,1792]{2,1,0:T(8,128)S(1)} %collective-permute-done.7.refs_3_), channel_id=1, source_target_pairs={{0,2},{1,7},{2,4},{3,1},{4,6},{5,3},{6,0},{7,5},{8,10},{9,15},{10,... | collective-permute-start | bytes 516104 | tf_op jit(solution)/shard_map/ppermute | solution.py:367
  49.1 14.7 %collective-permute-start.9 = (f32[3,8,4096]{2,1,0:T(8,128)S(1)}, f32[3,8,4096]{2,1,0:T(8,128)S(1)}, u32[]{:S(2)}, u32[]{:S(2)}) collective-permute-start(f32[3,8,4096]{2,1,0:T(8,128)S(1)} %get-tuple-element.37), channel_id=1, source_target_pairs={{0,1},{1,0},{2,3},{3,2},{4,5},{5,4},{6,7},{7,6},{8,9},{9,8},{10,11... | collective-permute-start | bytes 1179656 | tf_op jit(solution)/shard_map/ppermute | solution.py:387
  57.6 6.2 %collective-permute-start.12 = (f32[3,8,2048]{2,1,0:T(8,128)S(1)}, f32[3,8,2048]{2,1,0:T(8,128)S(1)}, u32[]{:S(2)}, u32[]{:S(2)}) collective-permute-start(f32[3,8,2048]{2,1,0:T(8,128)S(1)} %get-tuple-element.41), channel_id=1, source_target_pairs={{0,1},{1,0},{2,3},{3,2},{4,5},{5,4},{6,7},{7,6},{8,9},{9,8},{10,11... | collective-permute-start | bytes 589832 | tf_op jit(solution)/shard_map/ppermute | solution.py:387
  63.8 5.9 %collective-permute-start.16 = (f32[8,128]{1,0:T(8,128)S(1)}, f32[8,128]{1,0:T(8,128)S(1)}, u32[]{:S(2)}, u32[]{:S(2)}) collective-permute-start(f32[8,128]{1,0:T(8,128)S(1)} %add_add_fusion.1), channel_id=1, source_target_pairs={{0,2},{1,3},{2,4},{3,5},{4,6},{5,7},{6,0},{7,1},{8,10},{9,11},{10,... | collective-permute-start | bytes 12296 | tf_op jit(solution)/shard_map/ppermute | solution.py:392
  64.1 5.6 %collective-permute-start.17 = (f32[8,128]{1,0:T(8,128)S(1)}, f32[8,128]{1,0:T(8,128)S(1)}, u32[]{:S(2)}, u32[]{:S(2)}) collective-permute-start(f32[8,128]{1,0:T(8,128)S(1)} %add_add_fusion.1), channel_id=1, source_target_pairs={{0,6},{1,7},{2,0},{3,1},{4,2},{5,3},{6,4},{7,5},{8,14},{9,15},{10,... | collective-permute-start | bytes 12296 | tf_op jit(solution)/shard_map/ppermute | solution.py:392
  67.7 4.5 %collective-permute-start.15 = (f32[8,128]{1,0:T(8,128)S(1)}, f32[8,128]{1,0:T(8,128)S(1)}, u32[]{:S(2)}, u32[]{:S(2)}) collective-permute-start(f32[8,128]{1,0:T(8,128)S(1)} %add_add_fusion.1), channel_id=1, source_target_pairs={{0,4},{1,5},{2,6},{3,7},{4,0},{5,1},{6,2},{7,3},{8,12},{9,13},{10,... | collective-permute-start | bytes 12296 | tf_op jit(solution)/shard_map/ppermute | solution.py:392
  67.9 6.3 %collective-permute-start.14 = (f32[3,8,2048]{2,1,0:T(8,128)S(1)}, f32[3,8,2048]{2,1,0:T(8,128)S(1)}, u32[]{:S(2)}, u32[]{:S(2)}) collective-permute-start(f32[3,8,2048]{2,1,0:T(8,128)S(1)} %get-tuple-element.43), channel_id=1, source_target_pairs={{0,1},{1,0},{2,3},{3,2},{4,5},{5,4},{6,7},{7,6},{8,9},{9,8},{10,11... | collective-permute-start | bytes 589832 | tf_op jit(solution)/shard_map/ppermute | solution.py:387
  72.2 3.6 %collective-permute-start.18 = (f32[8,128]{1,0:T(8,128)S(1)}, f32[8,128]{1,0:T(8,128)S(1)}, u32[]{:S(2)}, u32[]{:S(2)}) collective-permute-start(f32[8,128]{1,0:T(8,128)S(1)} %add_add_fusion), channel_id=1, source_target_pairs={{0,1},{1,0},{2,3},{3,2},{4,5},{5,4},{6,7},{7,6},{8,9},{9,8},{10,11... | collective-permute-start | bytes 12296 | tf_op jit(solution)/shard_map/ppermute | solution.py:399

commit v8 on v7

--- a/solution.py
+++ b/solution.py
@@ -72,7 +72,7 @@
     )(offspring, ensemble)
 
 
-def pick_kernel(index, own, other, *outs, spans):
+def pick_kernel(index, own, other, seen, columns, precision, *outs, spans, total_rows):
     members = own.shape[0]
     half = members // 2
     par = lax.axis_index("strip") % 2
@@ -80,15 +80,21 @@
     for s in spans:
         kept.append([refs.pop(0)])
         given.append([refs.pop(0) for _ in s])
-    near, far = refs
-    wide = own.shape[3] // TILE
+    near, far, obs = refs
+    cols = own.shape[3]
+    wide = cols // TILE
+    row = lax.broadcasted_iota(jnp.int32, precision.shape, 0) + lax.axis_index("strip") * TILE
+    weight = precision[...] * (1.0 + 2.0 * (row.astype(jnp.float32) + 0.5) / total_rows)
+    for n, part in enumerate((seen[...], columns[...].astype(jnp.float32), weight)):
+        obs[n] = part
+        given[0][0][n, :, cols:] = part
 
     def copy(slot, k, pieces, edge):
         i = index[slot]
 
         def write(ref, m):
             if len(pieces) == 1:
-                pieces[0][...] = ref[m]
+                pieces[0][:, :, :cols] = ref[m]
             else:
                 for (first, count), out in zip(spans[k], pieces):
                     out[...] = ref[m, :, :, pl.ds(first, count)]
@@ -121,25 +127,29 @@
         copy(par * half + k, k, kept[k], near)
 
 
-def pick(index, own, other, spans):
+def pick(index, own, other, seen, columns, precision, spans, total_rows):
     shape, kind = own.shape[1:3], own.dtype
     outs = []
     for s in spans:
-        outs += [jax.ShapeDtypeStruct(shape + (c,), kind) for c in [own.shape[3]] + [c for _, c in s]]
+        widths = [own.shape[3]] + [c for _, c in s]
+        if not outs:
+            widths[1] += seen.shape[1]
+        outs += [jax.ShapeDtypeStruct(shape + (c,), kind) for c in widths]
     outs += [jax.ShapeDtypeStruct((3 * len(spans), TILE, own.shape[3] // TILE), kind)] * 2
+    outs.append(jax.ShapeDtypeStruct((3,) + seen.shape, kind))
     out = pl.pallas_call(
-        functools.partial(pick_kernel, spans=spans),
+        functools.partial(pick_kernel, spans=spans, total_rows=total_rows),
         out_shape=outs,
-        in_specs=[SMEM, VMEM, VMEM],
+        in_specs=[SMEM] + [VMEM] * 5,
         out_specs=[VMEM] * len(outs),
         compiler_params=pltpu.CompilerParams(vmem_limit_bytes=SMALL),
-    )(index, own, other)
+    )(index, own, other, seen, columns, precision)
     kept, given = [], []
     for s in spans:
         kept.append(out[0])
         given.append(out[1 : 1 + len(s)])
         out = out[1 + len(s) :]
-    return kept, given, out[0], out[1]
+    return kept, given, out[0], out[1], out[2]
 
 
 def evaluate(src, state, dst, cor_ref, start, tiles, kind):
@@ -193,6 +203,7 @@
     own, direct, refs = refs[0], refs[1], refs[2:]
     got, passed = refs[:parts], refs[parts : 2 * parts]
     near, far, obs_own, obs_got, keep, send, misfit, state, s1, s2, cor_ref = refs[2 * parts :]
+    behind = obs_got.shape[2] - LANES
     strip = lax.axis_index("strip")
     par = strip % 2
     per = ncol // TILE
@@ -252,7 +263,7 @@
     total = jnp.zeros((TILE, LANES), jnp.float32)
     for side in range(2):
         mine = par == side
-        obs = [jnp.where(mine, obs_own[k], obs_got[k]) for k in range(3)]
+        obs = [jnp.where(mine, obs_own[k], obs_got[k, :, behind:]) for k in range(3)]
         where = obs[1].astype(jnp.int32)
         tile, lane = where // LANES, where % LANES
         picked = jnp.zeros((TILE, LANES), jnp.float32)
@@ -341,32 +352,28 @@
     arrived = lax.ppermute(ensemble, "particle", [(0, 1), (1, 0)])
     index = sources(offspring, ensemble)
 
-    rows = (strip * strip_rows + jnp.arange(strip_rows, dtype=jnp.int32)).astype(jnp.float32)
-    weight = obs_precision * (1.0 + 2.0 * (rows + 0.5) / total_rows)[:, None]
-    obs_own = jnp.stack([observations, obs_cols.astype(jnp.float32), weight])
-
     spans = [
         [(sent[0] * LANES, len(sent) * LANES) for sent, _, _ in plan(ncol, k, half)]
         for k in range(half)
     ]
-    kept, given, near, far = pick(index, ensemble, arrived, spans)
+    kept, given, near, far, obs_own = pick(
+        index, ensemble, arrived, observations, obs_cols, obs_precision, spans, total_rows
+    )
     near = lax.ppermute(near, "strip", onward)
     far = lax.ppermute(far, "strip", cross)
 
-    obs_got = lax.ppermute(obs_own, "strip", swap)
 
     pieces = [(k, p) for k in range(half) for p in range(len(spans[k]))]
     got, passed, direct, blocks, misfits = [], [], [], [], []
-    first = None
     for k in range(half):
         giving, keeping = tuple(given[k]), kept[k]
         if k:
-            *giving, keeping = after((*giving, keeping), first)
+            giving = after(giving, got[0])
+            (keeping,) = after((keeping,), (direct[0], got[0], near, far))
         direct.append(lax.ppermute(keeping, "strip", straight))
         got.append([lax.ppermute(g, "strip", swap) for g in giving])
         passed.append([lax.ppermute(g, "strip", onward) for g in got[k]])
-        if first is None:
-            first = (direct[0], got[0], near, far, obs_got)
+    obs_got = got[0][0]
     for k, p in pieces:
         (own,) = after((kept[k],), got[-1])
         keep, send, misfit = forecast(
@@ -396,6 +403,7 @@
         while step < strips:
             total = total + lax.ppermute(total, "strip", [(i, i ^ step) for i in range(strips)])
             step *= 2
+    (total,) = after((total,), blocks[-1][1])
     theirs = lax.ppermute(total, "strip", swap)
     state = gather(blocks, pieces, ncol, half)
     theirs, total = after((theirs, total), state)

time: 76.5 us -> 85.7 us (1.12)
  waiting for transfers between devices: 16 us -> 28.7 us
  starting transfers between devices: 32.6 us -> 26.1 us
  local copies, waits for them, and re-layouts: 2.24 us -> 4.32 us
    ppermute x1, waiting for transfers between devices: 0.01 us -> 8.98 us  [local(): near = lax.ppermute(near, 'strip', onward)]
    ppermute x1 -> x0, starting transfers between devices: 3.74 us -> none  [local(): obs_got = lax.ppermute(obs_own, 'strip', swap)]
    ppermute x1, starting transfers between devices: 0.07 us -> 3.42 us  [local(): far = lax.ppermute(far, 'strip', cross)]
    ppermute x3, waiting for transfers between devices: 2.52 us -> 4.74 us  [local(): lax.ppermute(total, 'strip', moved(step, step))]
    ppermute x3, starting transfers between devices: 4.36 us -> 2.2 us  [local(): blocks.append((keep, lax.ppermute(send, 'strip', swap)))]
    unnamed x12, local copies, waits for them, and re-layouts: 2.24 us -> 4.32 us
    ppermute x3, starting transfers between devices: 5.06 us -> 3.03 us  [local(): got.append([lax.ppermute(g, 'strip', swap) for g in giving])]
    ppermute x1, waiting for transfers between devices: 0.36 us -> 2.3 us  [local(): theirs = lax.ppermute(total, 'strip', swap)]
  transfers between devices with their start and end apart: 19 -> 18, of which waited for: 6 -> 8; matrix products, arithmetic and copies ran while one was open for 0% -> 0% of each run, Pallas kernels for 31% -> 28%
where the time goes in v8:
time: 85.7 us; the launch traced here: 84.7 us
  waiting for transfers between devices  28.7 us (33%)
  starting transfers between devices  26.1 us (30%)
  Pallas kernels  24.3 us (28%)
  local copies, waits for them, and re-layouts  4.32 us (5%)
    pallas_call x3, Pallas kernels, forecast(): pl.pallas_call(functools.partial(forecast_kernel, worked=worked, kept=kep...  21.1 us
    ppermute x3, waiting for transfers between devices, local(): got.append([lax.ppermute(g, 'strip', swap) for g in giving])  11.7 us
    ppermute x2, starting transfers between devices, local(): direct.append(lax.ppermute(keeping, 'strip', straight))  9 us
    ppermute x1, waiting for transfers between devices, local(): near = lax.ppermute(near, 'strip', onward)  8.98 us
    ppermute x3, waiting for transfers between devices, local(): lax.ppermute(total, 'strip', moved(step, step))  4.74 us
    ppermute x3, starting transfers between devices, local(): lax.ppermute(total, 'strip', moved(step, step))  4.5 us
    unnamed x12, local copies, waits for them, and re-layouts  4.32 us
    ppermute x1, starting transfers between devices, local(): far = lax.ppermute(far, 'strip', cross)  3.42 us
  transfers between devices with their start and end apart: 18, of which 8 were waited for; matrix products, arithmetic and copies ran while one was open for 0% of the time, Pallas kernels for 28%

profile of v8, /device:TPU:0, one launch (start us, length us, event | category | flops | bytes accessed | tf_op | source)
XLA Modules:
  0.0 84.7 jit_solution(8045892127071494793)
XLA Ops:
  0.6 0.5 collective-permute-start
  1.1 1.4 %copy-done = f32[4,3,8,4096]{3,2,1,0:T(8,128)S(1)} copy-done((f32[4,3,8,4096]{3,2,1,0:T(8,128)S(1)}, f32[4,3,8,4096]{3,2,1,0:T(8,128)}, u32[]{:S(2)}) %copy-start) | copy-done | bytes 1572888
  2.6 0.7 copy-done.5
  3.2 1.2 %shard_map.68.index = s32[4]{0:T(128)S(1)} custom-call(s32[8]{0:T(128)S(1)} %copy-done.5, f32[4,3,8,4096]{3,2,1,0:T(8,128)S(1)} %copy-done), custom_call_target="tpu_custom_call" | custom-call | tf_op jit(solution)/shard_map/pallas_call | solution.py:66
  4.4 0.2 copy-done.1
  4.6 0.7 copy-done.2
  5.3 0.7 copy-done.3
  6.0 0.7 copy-done.4
  6.7 0.8 shard_map.69
  7.5 2.7 %collective-permute-start.1 = (f32[3,8,4224]{2,1,0:T(8,128)S(1)}, f32[3,8,4224]{2,1,0:T(8,128)S(1)}, u32[]{:S(2)}, u32[]{:S(2)}) collective-permute-start(f32[3,8,4224]{2,1,0:T(8,128)S(1)} %get-tuple-element.31), channel_id=1, source_target_pairs={{0,1},{1,0},{2,3},{3,2},{4,5},{5,4},{6,7},{7,6},{8,9},{9,8},{10,11... | collective-permute-start | bytes 1216520 | tf_op jit(solution)/shard_map/ppermute | solution.py:374
  10.2 3.6 %collective-permute-start.4 = (f32[3,8,4096]{2,1,0:T(8,128)S(1)}, f32[3,8,4096]{2,1,0:T(8,128)S(1)}, u32[]{:S(2)}, u32[]{:S(2)}) collective-permute-start(f32[3,8,4096]{2,1,0:T(8,128)S(1)} %get-tuple-element.34.refs_0_), channel_id=1, source_target_pairs={{0,6},{1,3},{2,0},{3,5},{4,2},{5,7},{6,4},{7,1},{8,14},{9,11},{10,... | collective-permute-start | bytes 1179656 | tf_op jit(solution)/shard_map/ppermute | solution.py:373
  13.8 6.3 %collective-permute-done.1.refs_2_.refs_7_.refs_9_ = f32[3,8,4224]{2,1,0:T(8,128)S(1)} collective-permute-done((f32[3,8,4224]{2,1,0:T(8,128)S(1)}, f32[3,8,4224]{2,1,0:T(8,128)S(1)}, u32[]{:S(2)}, u32[]{:S(2)}) %collective-permute-start.1) | collective-permute-done | bytes 405536 | tf_op jit(solution)/shard_map/ppermute | solution.py:374
  20.1 1.8 %collective-permute-start.5 = (f32[3,8,4224]{2,1,0:T(8,128)S(1)}, f32[3,8,4224]{2,1,0:T(8,128)S(1)}, u32[]{:S(2)}, u32[]{:S(2)}) collective-permute-start(f32[3,8,4224]{2,1,0:T(8,128)S(1)} %collective-permute-done.1.refs_2_.refs_7_.refs_9_), channel_id=1, source_target_pairs={{0,2},{1,7},{2,4},{3,1},{4,6},{5,3},{6,0},{7,5},{8,10},{9,15},{10,... | collective-permute-start | bytes 1216520 | tf_op jit(solution)/shard_map/ppermute | solution.py:375
  21.9 1.6 %collective-permute-start.6 = (f32[6,8,512]{2,1,0:T(8,128)S(1)}, f32[6,8,512]{2,1,0:T(8,128)S(1)}, u32[]{:S(2)}, u32[]{:S(2)}) collective-permute-start(f32[6,8,512]{2,1,0:T(8,128)S(1)} %get-tuple-element.35), channel_id=1, source_target_pairs={{0,2},{1,7},{2,4},{3,1},{4,6},{5,3},{6,0},{7,5},{8,10},{9,15},{10,... | collective-permute-start | bytes 294920 | tf_op jit(solution)/shard_map/ppermute | solution.py:362
  23.5 3.4 %collective-permute-start.7 = (f32[6,8,512]{2,1,0:T(8,128)S(1)}, f32[6,8,512]{2,1,0:T(8,128)S(1)}, u32[]{:S(2)}, u32[]{:S(2)}) collective-permute-start(f32[6,8,512]{2,1,0:T(8,128)S(1)} %get-tuple-element.36), channel_id=1, source_target_pairs={{0,3},{1,6},{2,5},{3,0},{4,7},{5,2},{6,1},{7,4},{8,11},{9,14},{10,... | collective-permute-start | bytes 294920 | tf_op jit(solution)/shard_map/ppermute | solution.py:363
  26.9 0.3 collective-permute-start.2
  27.2 9.0 %collective-permute-done.6.refs_4_.refs_6_ = f32[6,8,512]{2,1,0:T(8,128)S(1)} collective-permute-done((f32[6,8,512]{2,1,0:T(8,128)S(1)}, f32[6,8,512]{2,1,0:T(8,128)S(1)}, u32[]{:S(2)}, u32[]{:S(2)}) %collective-permute-start.6) | collective-permute-done | bytes 98336 | tf_op jit(solution)/shard_map/ppermute | solution.py:362
  36.3 5.4 %collective-permute-start.9 = (f32[3,8,4096]{2,1,0:T(8,128)S(1)}, f32[3,8,4096]{2,1,0:T(8,128)S(1)}, u32[]{:S(2)}, u32[]{:S(2)}) collective-permute-start(f32[3,8,4096]{2,1,0:T(8,128)S(1)} %get-tuple-element.42.refs_0_), channel_id=1, source_target_pairs={{0,6},{1,3},{2,0},{3,5},{4,2},{5,7},{6,4},{7,1},{8,14},{9,11},{10,... | collective-permute-start | bytes 1179656 | tf_op jit(solution)/shard_map/ppermute | solution.py:373
  41.7 5.4 %collective-permute-done.3.refs_3_ = f32[3,8,1792]{2,1,0:T(8,128)S(1)} collective-permute-done((f32[3,8,1792]{2,1,0:T(8,128)S(1)}, f32[3,8,1792]{2,1,0:T(8,128)S(1)}, u32[]{:S(2)}, u32[]{:S(2)}) %collective-permute-start.3) | collective-permute-done | bytes 172064 | tf_op jit(solution)/shard_map/ppermute | solution.py:374
  47.1 8.9 %shard_map.70 = (f32[3,8,4096]{2,1,0:T(8,128)S(1)}, f32[3,8,4096]{2,1,0:T(8,128)S(1)}, f32[8,128]{1,0:T(8,128)S(1)}) custom-call(f32[3,8,4096]{2,1,0:T(8,128)S(1)} %get-tuple-element.34.refs_0_, f32[3,8,4096]{2,1,0:T(8,128)S(1)} %collective-permute-done.4.refs_1_, f32[3,8,4224]{2,1,0:T(8,128)S(1)} %collective-permute-done.1.refs_2_.refs_7_.refs_9_, ...), custom_call_target="tpu_custom_call" | custom-call | bytes 480000 | tf_op jit(solution)/shard_map/pallas_call | solution.py:293
  56.0 0.9 %collective-permute-start.8 = (f32[3,8,4096]{2,1,0:T(8,128)S(1)}, f32[3,8,4096]{2,1,0:T(8,128)S(1)}, u32[]{:S(2)}, u32[]{:S(2)}) collective-permute-start(f32[3,8,4096]{2,1,0:T(8,128)S(1)} %get-tuple-element.39), channel_id=1, source_target_pairs={{0,1},{1,0},{2,3},{3,2},{4,5},{5,4},{6,7},{7,6},{8,9},{9,8},{10,11... | collective-permute-start | bytes 1179656 | tf_op jit(solution)/shard_map/ppermute | solution.py:394
  56.9 6.1 %shard_map.71 = (f32[3,8,2048]{2,1,0:T(8,128)S(1)}, f32[3,8,2048]{2,1,0:T(8,128)S(1)}, f32[8,128]{1,0:T(8,128)S(1)}) custom-call(f32[3,8,4096]{2,1,0:T(8,128)S(1)} %get-tuple-element.42.refs_0_, f32[3,8,4096]{2,1,0:T(8,128)S(1)} %collective-permute-done.9.refs_1_, f32[3,8,2304]{2,1,0:T(8,128)S(1)} %collective-permute-done.2.refs_2_, ...), custom_call_target="tpu_custom_call" | custom-call | bytes 270000 | tf_op jit(solution)/shard_map/pallas_call | solution.py:293
  63.0 1.3 %collective-permute-start.11 = (f32[3,8,2048]{2,1,0:T(8,128)S(1)}, f32[3,8,2048]{2,1,0:T(8,128)S(1)}, u32[]{:S(2)}, u32[]{:S(2)}) collective-permute-start(f32[3,8,2048]{2,1,0:T(8,128)S(1)} %get-tuple-element.44), channel_id=1, source_target_pairs={{0,1},{1,0},{2,3},{3,2},{4,5},{5,4},{6,7},{7,6},{8,9},{9,8},{10,11... | collective-permute-start | bytes 589832 | tf_op jit(solution)/shard_map/ppermute | solution.py:394
  64.3 6.1 %shard_map.72 = (f32[3,8,2048]{2,1,0:T(8,128)S(1)}, f32[3,8,2048]{2,1,0:T(8,128)S(1)}, f32[8,128]{1,0:T(8,128)S(1)}) custom-call(f32[3,8,4096]{2,1,0:T(8,128)S(1)} %get-tuple-element.42.refs_0_, f32[3,8,4096]{2,1,0:T(8,128)S(1)} %collective-permute-done.9.refs_1_, f32[3,8,2304]{2,1,0:T(8,128)S(1)} %collective-permute-done.2.refs_2_, ...), custom_call_target="tpu_custom_call" | custom-call | bytes 270000 | tf_op jit(solution)/shard_map/pallas_call | solution.py:293
  70.4 3.9 %collective-permute-start.16 = (f32[8,128]{1,0:T(8,128)S(1)}, f32[8,128]{1,0:T(8,128)S(1)}, u32[]{:S(2)}, u32[]{:S(2)}) collective-permute-start(f32[8,128]{1,0:T(8,128)S(1)} %add_add_fusion.1), channel_id=1, source_target_pairs={{0,6},{1,7},{2,0},{3,1},{4,2},{5,3},{6,4},{7,5},{8,14},{9,15},{10,... | collective-permute-start | bytes 12296 | tf_op jit(solution)/shard_map/ppermute | solution.py:399
  74.3 0.6 collective-permute-start.14
  74.9 0.7 collective-permute-done.16
  75.6 4.1 %collective-permute-done.15 = f32[8,128]{1,0:T(8,128)S(1)} collective-permute-done((f32[8,128]{1,0:T(8,128)S(1)}, f32[8,128]{1,0:T(8,128)S(1)}, u32[]{:S(2)}, u32[]{:S(2)}) %collective-permute-start.15) | collective-permute-done | bytes 4128 | tf_op jit(solution)/shard_map/ppermute | solution.py:399
  79.7 0.9 %collective-permute-done.13.refs_5_ = f32[3,8,2048]{2,1,0:T(8,128)S(1)} collective-permute-done((f32[3,8,2048]{2,1,0:T(8,128)S(1)}, f32[3,8,2048]{2,1,0:T(8,128)S(1)}, u32[]{:S(2)}, u32[]{:S(2)}) %collective-permute-start.13) | collective-permute-done | bytes 196640 | tf_op jit(solution)/shard_map/ppermute | solution.py:394
  80.6 1.3 %shard_map.73 = f32[4,3,8,4096]{3,2,1,0:T(8,128)} custom-call(f32[3,8,4096]{2,1,0:T(8,128)S(1)} %get-tuple-element.38.refs_0_, f32[3,8,4096]{2,1,0:T(8,128)S(1)} %collective-permute-done.8.refs_1_, f32[3,8,2048]{2,1,0:T(8,128)S(1)} %get-tuple-element.43.refs_2_, f32[3,8,2048]{2,1,0:T(8,128)S(1)} %collective-permute-done.11.refs_3_, ...), custom_call_target="tpu_custom_call" | custom-call | bytes 300000 | tf_op jit(solution)/shard_map/pallas_call | solution.py:326
  81.9 2.3 %collective-permute-done.17 = f32[8,128]{1,0:T(8,128)S(1)} collective-permute-done((f32[8,128]{1,0:T(8,128)S(1)}, f32[8,128]{1,0:T(8,128)S(1)}, u32[]{:S(2)}, u32[]{:S(2)}) %collective-permute-start.17) | collective-permute-done | bytes 4128 | tf_op jit(solution)/shard_map/ppermute | solution.py:407
  84.2 0.5 multiply_bitcast_fusion
  (26 shorter events, 0.3 us)
Async XLA Ops:
  0.6 3.8 %collective-permute-start = (f32[4,3,8,4096]{3,2,1,0:T(8,128)}, f32[4,3,8,4096]{3,2,1,0:T(8,128)S(1)}, u32[]{:S(2)}, u32[]{:S(2)}) collective-permute-start(f32[4,3,8,4096]{3,2,1,0:T(8,128)} %own.1), channel_id=1, source_target_pairs={{0,8},{8,0},{1,9},{9,1},{2,10},{10,2},{3,11},{11,3},{4,12},{12,4},... | collective-permute-start | bytes 4718600 | tf_op jit(solution)/shard_map/ppermute | solution.py:352
  1.1 1.4 %copy-start = (f32[4,3,8,4096]{3,2,1,0:T(8,128)S(1)}, f32[4,3,8,4096]{3,2,1,0:T(8,128)}, u32[]{:S(2)}) copy-start(f32[4,3,8,4096]{3,2,1,0:T(8,128)} %own.1) | copy-start | bytes 4718596
  2.6 0.7 copy-start.5
  3.2 1.4 %copy-start.1 = (f32[4,3,8,4096]{3,2,1,0:T(8,128)S(1)}, f32[4,3,8,4096]{3,2,1,0:T(8,128)}, u32[]{:S(2)}) copy-start(f32[4,3,8,4096]{3,2,1,0:T(8,128)} %own.1) | copy-start | bytes 4718596
  4.6 0.7 copy-start.2
  5.3 0.7 copy-start.3
  6.0 0.7 copy-start.4
  7.5 12.6 %collective-permute-start.1 = (f32[3,8,4224]{2,1,0:T(8,128)S(1)}, f32[3,8,4224]{2,1,0:T(8,128)S(1)}, u32[]{:S(2)}, u32[]{:S(2)}) collective-permute-start(f32[3,8,4224]{2,1,0:T(8,128)S(1)} %get-tuple-element.31), channel_id=1, source_target_pairs={{0,1},{1,0},{2,3},{3,2},{4,5},{5,4},{6,7},{7,6},{8,9},{9,8},{10,11... | collective-permute-start | bytes 1216520 | tf_op jit(solution)/shard_map/ppermute | solution.py:374
  10.2 26.1 %collective-permute-start.4 = (f32[3,8,4096]{2,1,0:T(8,128)S(1)}, f32[3,8,4096]{2,1,0:T(8,128)S(1)}, u32[]{:S(2)}, u32[]{:S(2)}) collective-permute-start(f32[3,8,4096]{2,1,0:T(8,128)S(1)} %get-tuple-element.34.refs_0_), channel_id=1, source_target_pairs={{0,6},{1,3},{2,0},{3,5},{4,2},{5,7},{6,4},{7,1},{8,14},{9,11},{10,... | collective-permute-start | bytes 1179656 | tf_op jit(solution)/shard_map/ppermute | solution.py:373
  20.1 27.0 %collective-permute-start.5 = (f32[3,8,4224]{2,1,0:T(8,128)S(1)}, f32[3,8,4224]{2,1,0:T(8,128)S(1)}, u32[]{:S(2)}, u32[]{:S(2)}) collective-permute-start(f32[3,8,4224]{2,1,0:T(8,128)S(1)} %collective-permute-done.1.refs_2_.refs_7_.refs_9_), channel_id=1, source_target_pairs={{0,2},{1,7},{2,4},{3,1},{4,6},{5,3},{6,0},{7,5},{8,10},{9,15},{10,... | collective-permute-start | bytes 1216520 | tf_op jit(solution)/shard_map/ppermute | solution.py:375
  21.9 14.3 %collective-permute-start.6 = (f32[6,8,512]{2,1,0:T(8,128)S(1)}, f32[6,8,512]{2,1,0:T(8,128)S(1)}, u32[]{:S(2)}, u32[]{:S(2)}) collective-permute-start(f32[6,8,512]{2,1,0:T(8,128)S(1)} %get-tuple-element.35), channel_id=1, source_target_pairs={{0,2},{1,7},{2,4},{3,1},{4,6},{5,3},{6,0},{7,5},{8,10},{9,15},{10,... | collective-permute-start | bytes 294920 | tf_op jit(solution)/shard_map/ppermute | solution.py:362
  23.5 12.8 %collective-permute-start.7 = (f32[6,8,512]{2,1,0:T(8,128)S(1)}, f32[6,8,512]{2,1,0:T(8,128)S(1)}, u32[]{:S(2)}, u32[]{:S(2)}) collective-permute-start(f32[6,8,512]{2,1,0:T(8,128)S(1)} %get-tuple-element.36), channel_id=1, source_target_pairs={{0,3},{1,6},{2,5},{3,0},{4,7},{5,2},{6,1},{7,4},{8,11},{9,14},{10,... | collective-permute-start | bytes 294920 | tf_op jit(solution)/shard_map/ppermute | solution.py:363
  26.9 14.8 %collective-permute-start.2 = (f32[3,8,2304]{2,1,0:T(8,128)S(1)}, f32[3,8,2304]{2,1,0:T(8,128)S(1)}, u32[]{:S(2)}, u32[]{:S(2)}) collective-permute-start(f32[3,8,2304]{2,1,0:T(8,128)S(1)} %get-tuple-element.32), channel_id=1, source_target_pairs={{0,1},{1,0},{2,3},{3,2},{4,5},{5,4},{6,7},{7,6},{8,9},{9,8},{10,11... | collective-permute-start | bytes 663560 | tf_op jit(solution)/shard_map/ppermute | solution.py:374
  36.3 20.6 %collective-permute-start.9 = (f32[3,8,4096]{2,1,0:T(8,128)S(1)}, f32[3,8,4096]{2,1,0:T(8,128)S(1)}, u32[]{:S(2)}, u32[]{:S(2)}) collective-permute-start(f32[3,8,4096]{2,1,0:T(8,128)S(1)} %get-tuple-element.42.refs_0_), channel_id=1, source_target_pairs={{0,6},{1,3},{2,0},{3,5},{4,2},{5,7},{6,4},{7,1},{8,14},{9,11},{10,... | collective-permute-start | bytes 1179656 | tf_op jit(solution)/shard_map/ppermute | solution.py:373
  41.7 5.4 %collective-permute-start.3 = (f32[3,8,1792]{2,1,0:T(8,128)S(1)}, f32[3,8,1792]{2,1,0:T(8,128)S(1)}, u32[]{:S(2)}, u32[]{:S(2)}) collective-permute-start(f32[3,8,1792]{2,1,0:T(8,128)S(1)} %get-tuple-element.33), channel_id=1, source_target_pairs={{0,1},{1,0},{2,3},{3,2},{4,5},{5,4},{6,7},{7,6},{8,9},{9,8},{10,11... | collective-permute-start | bytes 516104 | tf_op jit(solution)/shard_map/ppermute | solution.py:374
  41.7 15.1 %collective-permute-start.10 = (f32[3,8,2304]{2,1,0:T(8,128)S(1)}, f32[3,8,2304]{2,1,0:T(8,128)S(1)}, u32[]{:S(2)}, u32[]{:S(2)}) collective-permute-start(f32[3,8,2304]{2,1,0:T(8,128)S(1)} %collective-permute-done.2.refs_2_), channel_id=1, source_target_pairs={{0,2},{1,7},{2,4},{3,1},{4,6},{5,3},{6,0},{7,5},{8,10},{9,15},{10,... | collective-permute-start | bytes 663560 | tf_op jit(solution)/shard_map/ppermute | solution.py:375
  47.1 17.1 %collective-permute-start.12 = (f32[3,8,1792]{2,1,0:T(8,128)S(1)}, f32[3,8,1792]{2,1,0:T(8,128)S(1)}, u32[]{:S(2)}, u32[]{:S(2)}) collective-permute-start(f32[3,8,1792]{2,1,0:T(8,128)S(1)} %collective-permute-done.3.refs_3_), channel_id=1, source_target_pairs={{0,2},{1,7},{2,4},{3,1},{4,6},{5,3},{6,0},{7,5},{8,10},{9,15},{10,... | collective-permute-start | bytes 516104 | tf_op jit(solution)/shard_map/ppermute | solution.py:375
  56.0 14.4 %collective-permute-start.8 = (f32[3,8,4096]{2,1,0:T(8,128)S(1)}, f32[3,8,4096]{2,1,0:T(8,128)S(1)}, u32[]{:S(2)}, u32[]{:S(2)}) collective-permute-start(f32[3,8,4096]{2,1,0:T(8,128)S(1)} %get-tuple-element.39), channel_id=1, source_target_pairs={{0,1},{1,0},{2,3},{3,2},{4,5},{5,4},{6,7},{7,6},{8,9},{9,8},{10,11... | collective-permute-start | bytes 1179656 | tf_op jit(solution)/shard_map/ppermute | solution.py:394
  63.0 7.4 %collective-permute-start.11 = (f32[3,8,2048]{2,1,0:T(8,128)S(1)}, f32[3,8,2048]{2,1,0:T(8,128)S(1)}, u32[]{:S(2)}, u32[]{:S(2)}) collective-permute-start(f32[3,8,2048]{2,1,0:T(8,128)S(1)} %get-tuple-element.44), channel_id=1, source_target_pairs={{0,1},{1,0},{2,3},{3,2},{4,5},{5,4},{6,7},{7,6},{8,9},{9,8},{10,11... | collective-permute-start | bytes 589832 | tf_op jit(solution)/shard_map/ppermute | solution.py:394
  70.4 5.2 %collective-permute-start.16 = (f32[8,128]{1,0:T(8,128)S(1)}, f32[8,128]{1,0:T(8,128)S(1)}, u32[]{:S(2)}, u32[]{:S(2)}) collective-permute-start(f32[8,128]{1,0:T(8,128)S(1)} %add_add_fusion.1), channel_id=1, source_target_pairs={{0,6},{1,7},{2,0},{3,1},{4,2},{5,3},{6,4},{7,5},{8,14},{9,15},{10,... | collective-permute-start | bytes 12296 | tf_op jit(solution)/shard_map/ppermute | solution.py:399
  74.3 5.4 %collective-permute-start.15 = (f32[8,128]{1,0:T(8,128)S(1)}, f32[8,128]{1,0:T(8,128)S(1)}, u32[]{:S(2)}, u32[]{:S(2)}) collective-permute-start(f32[8,128]{1,0:T(8,128)S(1)} %add_add_fusion.1), channel_id=1, source_target_pairs={{0,2},{1,3},{2,4},{3,5},{4,6},{5,7},{6,0},{7,1},{8,10},{9,11},{10,... | collective-permute-start | bytes 12296 | tf_op jit(solution)/shard_map/ppermute | solution.py:399
  74.3 5.4 %collective-permute-start.14 = (f32[8,128]{1,0:T(8,128)S(1)}, f32[8,128]{1,0:T(8,128)S(1)}, u32[]{:S(2)}, u32[]{:S(2)}) collective-permute-start(f32[8,128]{1,0:T(8,128)S(1)} %add_add_fusion.1), channel_id=1, source_target_pairs={{0,4},{1,5},{2,6},{3,7},{4,0},{5,1},{6,2},{7,3},{8,12},{9,13},{10,... | collective-permute-start | bytes 12296 | tf_op jit(solution)/shard_map/ppermute | solution.py:399
  74.9 5.7 %collective-permute-start.13 = (f32[3,8,2048]{2,1,0:T(8,128)S(1)}, f32[3,8,2048]{2,1,0:T(8,128)S(1)}, u32[]{:S(2)}, u32[]{:S(2)}) collective-permute-start(f32[3,8,2048]{2,1,0:T(8,128)S(1)} %get-tuple-element.46), channel_id=1, source_target_pairs={{0,1},{1,0},{2,3},{3,2},{4,5},{5,4},{6,7},{7,6},{8,9},{9,8},{10,11... | collective-permute-start | bytes 589832 | tf_op jit(solution)/shard_map/ppermute | solution.py:394
  80.6 3.6 %collective-permute-start.17 = (f32[8,128]{1,0:T(8,128)S(1)}, f32[8,128]{1,0:T(8,128)S(1)}, u32[]{:S(2)}, u32[]{:S(2)}) collective-permute-start(f32[8,128]{1,0:T(8,128)S(1)} %add_add_fusion), channel_id=1, source_target_pairs={{0,1},{1,0},{2,3},{3,2},{4,5},{5,4},{6,7},{7,6},{8,9},{9,8},{10,11... | collective-permute-start | bytes 12296 | tf_op jit(solution)/shard_map/ppermute | solution.py:407

commit v9 on v7

--- a/solution.py
+++ b/solution.py
@@ -361,14 +361,16 @@
     for k in range(half):
         giving, keeping = tuple(given[k]), kept[k]
         if k:
-            *giving, keeping = after((*giving, keeping), first)
+            giving = after(giving, first)
+        got.append([lax.ppermute(g, "strip", swap) for g in giving])
+        if k:
+            (keeping,) = after((keeping,), (got[k][0], obs_got))
         direct.append(lax.ppermute(keeping, "strip", straight))
-        got.append([lax.ppermute(g, "strip", swap) for g in giving])
         passed.append([lax.ppermute(g, "strip", onward) for g in got[k]])
         if first is None:
-            first = (direct[0], got[0], near, far, obs_got)
+            first = (got[0], near, far)
     for k, p in pieces:
-        (own,) = after((kept[k],), got[-1])
+        (own,) = after((kept[k],), (got[-1], misfits[-1:]))
         keep, send, misfit = forecast(
             own,
             got[k][: p + 1],

time: 76.5 us -> 77.8 us (1.017)
  waiting for transfers between devices: 16 us -> 17.5 us
    ppermute x3, starting transfers between devices: 4.05 us -> 8.53 us  [local(): lax.ppermute(total, 'strip', moved(step, step))]
    ppermute x3, waiting for transfers between devices: 10.9 us -> 8.61 us  [local(): got.append([lax.ppermute(g, 'strip', swap) for g in giving])]
    ppermute x3, waiting for transfers between devices: 0.01 us -> 1.94 us  [local(): blocks.append((keep, lax.ppermute(send, 'strip', swap)))]
    ppermute x1, starting transfers between devices: 1.98 us -> 0.18 us  [local(): theirs = lax.ppermute(total, 'strip', swap)]
    ppermute x3, starting transfers between devices: 4.36 us -> 2.66 us  [local(): blocks.append((keep, lax.ppermute(send, 'strip', swap)))]
    ppermute x1, starting transfers between devices: 0.01 us -> 1.58 us  [local(): near = lax.ppermute(near, 'strip', onward)]
    ppermute x3, waiting for transfers between devices: 0.01 us -> 1.49 us  [local(): passed.append([lax.ppermute(g, 'strip', onward) for g in got[k]])]
    ppermute x2, starting transfers between devices: 10.6 us -> 9.14 us  [local(): direct.append(lax.ppermute(keeping, 'strip', straight))]
  transfers between devices with their start and end apart: 19 -> 19, of which waited for: 6 -> 8; matrix products, arithmetic and copies ran while one was open for 0% -> 0% of each run, Pallas kernels for 31% -> 30%
where the time goes in v9:
time: 77.8 us; the launch traced here: 77.7 us
  starting transfers between devices  32.3 us (42%)
  Pallas kernels  24.2 us (31%)
  waiting for transfers between devices  17.5 us (22%)
  local copies, waits for them, and re-layouts  2.24 us (3%)
    pallas_call x3, Pallas kernels, forecast(): pl.pallas_call(functools.partial(forecast_kernel, worked=worked, kept=kep...  21 us
    ppermute x2, starting transfers between devices, local(): direct.append(lax.ppermute(keeping, 'strip', straight))  9.14 us
    ppermute x3, waiting for transfers between devices, local(): got.append([lax.ppermute(g, 'strip', swap) for g in giving])  8.61 us
    ppermute x3, starting transfers between devices, local(): lax.ppermute(total, 'strip', moved(step, step))  8.53 us
    ppermute x3, starting transfers between devices, local(): got.append([lax.ppermute(g, 'strip', swap) for g in giving])  4.48 us
    ppermute x3, waiting for transfers between devices, local(): lax.ppermute(total, 'strip', moved(step, step))  3.5 us
    ppermute x3, starting transfers between devices, local(): blocks.append((keep, lax.ppermute(send, 'strip', swap)))  2.66 us
    ppermute x3, starting transfers between devices, local(): passed.append([lax.ppermute(g, 'strip', onward) for g in got[k]])  2.63 us
  transfers between devices with their start and end apart: 19, of which 8 were waited for; matrix products, arithmetic and copies ran while one was open for 0% of the time, Pallas kernels for 30%

profile of v9, /device:TPU:0, one launch (start us, length us, event | category | flops | bytes accessed | tf_op | source)
XLA Modules:
  0.0 77.7 jit_solution(15600025654991538613)
XLA Ops:
  0.6 0.5 collective-permute-start
  1.1 1.4 %copy-done = f32[4,3,8,4096]{3,2,1,0:T(8,128)S(1)} copy-done((f32[4,3,8,4096]{3,2,1,0:T(8,128)S(1)}, f32[4,3,8,4096]{3,2,1,0:T(8,128)}, u32[]{:S(2)}) %copy-start) | copy-done | bytes 1572888
  2.6 0.7 copy-done.2
  3.2 1.2 %shard_map.68.index = s32[4]{0:T(128)S(1)} custom-call(s32[8]{0:T(128)S(1)} %copy-done.2, f32[4,3,8,4096]{3,2,1,0:T(8,128)S(1)} %copy-done), custom_call_target="tpu_custom_call" | custom-call | tf_op jit(solution)/shard_map/pallas_call | solution.py:66
  4.5 0.2 copy-done.1
  4.6 0.8 %shard_map.69 = (f32[3,8,4096]{2,1,0:T(8,128)S(1)}, f32[3,8,4096]{2,1,0:T(8,128)S(1)}, f32[3,8,4096]{2,1,0:T(8,128)S(1)}, f32[3,8,2304]{2,1,0:T(8,128)S(1)}, f32...) custom-call(s32[4]{0:T(128)S(1)} %shard_map.68.index, f32[4,3,8,4096]{3,2,1,0:T(8,128)S(1)} %copy-done.1, ...), custom_call_target="tpu_custom_call" | custom-call | tf_op jit(solution)/shard_map/pallas_call | solution.py:130
  5.4 2.7 %collective-permute-start.1 = (f32[3,8,4096]{2,1,0:T(8,128)S(1)}, f32[3,8,4096]{2,1,0:T(8,128)S(1)}, u32[]{:S(2)}, u32[]{:S(2)}) collective-permute-start(f32[3,8,4096]{2,1,0:T(8,128)S(1)} %get-tuple-element.30), channel_id=1, source_target_pairs={{0,1},{1,0},{2,3},{3,2},{4,5},{5,4},{6,7},{7,6},{8,9},{9,8},{10,11... | collective-permute-start | bytes 1179656 | tf_op jit(solution)/shard_map/ppermute | solution.py:365
  8.1 1.6 %collective-permute-start.2 = (f32[6,8,512]{2,1,0:T(8,128)S(1)}, f32[6,8,512]{2,1,0:T(8,128)S(1)}, u32[]{:S(2)}, u32[]{:S(2)}) collective-permute-start(f32[6,8,512]{2,1,0:T(8,128)S(1)} %get-tuple-element.31), channel_id=1, source_target_pairs={{0,2},{1,7},{2,4},{3,1},{4,6},{5,3},{6,0},{7,5},{8,10},{9,15},{10,... | collective-permute-start | bytes 294920 | tf_op jit(solution)/shard_map/ppermute | solution.py:353
  9.8 5.8 %collective-permute-start.6 = (f32[3,8,4096]{2,1,0:T(8,128)S(1)}, f32[3,8,4096]{2,1,0:T(8,128)S(1)}, u32[]{:S(2)}, u32[]{:S(2)}) collective-permute-start(f32[3,8,4096]{2,1,0:T(8,128)S(1)} %get-tuple-element.35.refs_0_), channel_id=1, source_target_pairs={{0,6},{1,3},{2,0},{3,5},{4,2},{5,7},{6,4},{7,1},{8,14},{9,11},{10,... | collective-permute-start | bytes 1179656 | tf_op jit(solution)/shard_map/ppermute | solution.py:368
  15.6 4.3 %collective-permute-done.1.refs_2_ = f32[3,8,4096]{2,1,0:T(8,128)S(1)} collective-permute-done((f32[3,8,4096]{2,1,0:T(8,128)S(1)}, f32[3,8,4096]{2,1,0:T(8,128)S(1)}, u32[]{:S(2)}, u32[]{:S(2)}) %collective-permute-start.1) | collective-permute-done | bytes 393248 | tf_op jit(solution)/shard_map/ppermute | solution.py:365
  19.9 1.7 %collective-permute-start.4 = (f32[3,8,2304]{2,1,0:T(8,128)S(1)}, f32[3,8,2304]{2,1,0:T(8,128)S(1)}, u32[]{:S(2)}, u32[]{:S(2)}) collective-permute-start(f32[3,8,2304]{2,1,0:T(8,128)S(1)} %get-tuple-element.33), channel_id=1, source_target_pairs={{0,1},{1,0},{2,3},{3,2},{4,5},{5,4},{6,7},{7,6},{8,9},{9,8},{10,11... | collective-permute-start | bytes 663560 | tf_op jit(solution)/shard_map/ppermute | solution.py:365
  21.6 1.6 %collective-permute-start.7 = (f32[3,8,4096]{2,1,0:T(8,128)S(1)}, f32[3,8,4096]{2,1,0:T(8,128)S(1)}, u32[]{:S(2)}, u32[]{:S(2)}) collective-permute-start(f32[3,8,4096]{2,1,0:T(8,128)S(1)} %collective-permute-done.1.refs_2_), channel_id=1, source_target_pairs={{0,2},{1,7},{2,4},{3,1},{4,6},{5,3},{6,0},{7,5},{8,10},{9,15},{10,... | collective-permute-start | bytes 1179656 | tf_op jit(solution)/shard_map/ppermute | solution.py:369
  23.2 2.6 %collective-permute-start.8 = (f32[3,8,128]{2,1,0:T(8,128)S(1)}, f32[3,8,128]{2,1,0:T(8,128)S(1)}, u32[]{:S(2)}, u32[]{:S(2)}) collective-permute-start(f32[3,8,128]{2,1,0:T(8,128)S(1)} %pad_maximum_fusion.refs_6_.refs_8_), channel_id=1, source_target_pairs={{0,1},{1,0},{2,3},{3,2},{4,5},{5,4},{6,7},{7,6},{8,9},{9,8},{10,11... | collective-permute-start | bytes 36872 | tf_op jit(solution)/shard_map/ppermute | solution.py:356
  25.8 1.7 %collective-permute-done.8.refs_7_.refs_9_ = f32[3,8,128]{2,1,0:T(8,128)S(1)} collective-permute-done((f32[3,8,128]{2,1,0:T(8,128)S(1)}, f32[3,8,128]{2,1,0:T(8,128)S(1)}, u32[]{:S(2)}, u32[]{:S(2)}) %collective-permute-start.8) | collective-permute-done | bytes 12320 | tf_op jit(solution)/shard_map/ppermute | solution.py:356
  27.5 3.4 %collective-permute-start.10 = (f32[3,8,4096]{2,1,0:T(8,128)S(1)}, f32[3,8,4096]{2,1,0:T(8,128)S(1)}, u32[]{:S(2)}, u32[]{:S(2)}) collective-permute-start(f32[3,8,4096]{2,1,0:T(8,128)S(1)} %get-tuple-element.45.refs_0_), channel_id=1, source_target_pairs={{0,6},{1,3},{2,0},{3,5},{4,2},{5,7},{6,4},{7,1},{8,14},{9,11},{10,... | collective-permute-start | bytes 1179656 | tf_op jit(solution)/shard_map/ppermute | solution.py:368
  30.8 1.1 %collective-permute-start.11 = (f32[3,8,2304]{2,1,0:T(8,128)S(1)}, f32[3,8,2304]{2,1,0:T(8,128)S(1)}, u32[]{:S(2)}, u32[]{:S(2)}) collective-permute-start(f32[3,8,2304]{2,1,0:T(8,128)S(1)} %collective-permute-done.4.refs_2_), channel_id=1, source_target_pairs={{0,2},{1,7},{2,4},{3,1},{4,6},{5,3},{6,0},{7,5},{8,10},{9,15},{10,... | collective-permute-start | bytes 663560 | tf_op jit(solution)/shard_map/ppermute | solution.py:369
  31.9 4.3 %collective-permute-done.5.refs_3_ = f32[3,8,1792]{2,1,0:T(8,128)S(1)} collective-permute-done((f32[3,8,1792]{2,1,0:T(8,128)S(1)}, f32[3,8,1792]{2,1,0:T(8,128)S(1)}, u32[]{:S(2)}, u32[]{:S(2)}) %collective-permute-start.5) | collective-permute-done | bytes 172064 | tf_op jit(solution)/shard_map/ppermute | solution.py:365
  36.3 8.9 %shard_map.70 = (f32[3,8,4096]{2,1,0:T(8,128)S(1)}, f32[3,8,4096]{2,1,0:T(8,128)S(1)}, f32[8,128]{1,0:T(8,128)S(1)}) custom-call(f32[3,8,4096]{2,1,0:T(8,128)S(1)} %get-tuple-element.35.refs_0_, f32[3,8,4096]{2,1,0:T(8,128)S(1)} %collective-permute-done.6.refs_1_, f32[3,8,4096]{2,1,0:T(8,128)S(1)} %collective-permute-done.1.refs_2_, ...), custom_call_target="tpu_custom_call" | custom-call | bytes 480000 | tf_op jit(solution)/shard_map/pallas_call | solution.py:282
  45.1 2.5 %collective-permute-start.9 = (f32[3,8,4096]{2,1,0:T(8,128)S(1)}, f32[3,8,4096]{2,1,0:T(8,128)S(1)}, u32[]{:S(2)}, u32[]{:S(2)}) collective-permute-start(f32[3,8,4096]{2,1,0:T(8,128)S(1)} %get-tuple-element.37), channel_id=1, source_target_pairs={{0,1},{1,0},{2,3},{3,2},{4,5},{5,4},{6,7},{7,6},{8,9},{9,8},{10,11... | collective-permute-start | bytes 1179656 | tf_op jit(solution)/shard_map/ppermute | solution.py:389
  47.7 1.5 %collective-permute-done.11.refs_3_.refs_4_ = f32[3,8,2304]{2,1,0:T(8,128)S(1)} collective-permute-done((f32[3,8,2304]{2,1,0:T(8,128)S(1)}, f32[3,8,2304]{2,1,0:T(8,128)S(1)}, u32[]{:S(2)}, u32[]{:S(2)}) %collective-permute-start.11) | collective-permute-done | bytes 221216 | tf_op jit(solution)/shard_map/ppermute | solution.py:369
  49.2 6.1 %shard_map.71 = (f32[3,8,2048]{2,1,0:T(8,128)S(1)}, f32[3,8,2048]{2,1,0:T(8,128)S(1)}, f32[8,128]{1,0:T(8,128)S(1)}) custom-call(f32[3,8,4096]{2,1,0:T(8,128)S(1)} %get-tuple-element.45.refs_0_, f32[3,8,4096]{2,1,0:T(8,128)S(1)} %collective-permute-done.10.refs_1_, f32[3,8,2304]{2,1,0:T(8,128)S(1)} %collective-permute-done.4.refs_2_, ...), custom_call_target="tpu_custom_call" | custom-call | bytes 270000 | tf_op jit(solution)/shard_map/pallas_call | solution.py:282
  55.3 6.1 %shard_map.72 = (f32[3,8,2048]{2,1,0:T(8,128)S(1)}, f32[3,8,2048]{2,1,0:T(8,128)S(1)}, f32[8,128]{1,0:T(8,128)S(1)}) custom-call(f32[3,8,4096]{2,1,0:T(8,128)S(1)} %get-tuple-element.45.refs_0_, f32[3,8,4096]{2,1,0:T(8,128)S(1)} %collective-permute-done.10.refs_1_, f32[3,8,2304]{2,1,0:T(8,128)S(1)} %collective-permute-done.4.refs_2_, ...), custom_call_target="tpu_custom_call" | custom-call | bytes 270000 | tf_op jit(solution)/shard_map/pallas_call | solution.py:282
  61.5 4.1 %collective-permute-start.16 = (f32[8,128]{1,0:T(8,128)S(1)}, f32[8,128]{1,0:T(8,128)S(1)}, u32[]{:S(2)}, u32[]{:S(2)}) collective-permute-start(f32[8,128]{1,0:T(8,128)S(1)} %add_add_fusion.1), channel_id=1, source_target_pairs={{0,2},{1,3},{2,4},{3,5},{4,6},{5,7},{6,0},{7,1},{8,10},{9,11},{10,... | collective-permute-start | bytes 12296 | tf_op jit(solution)/shard_map/ppermute | solution.py:394
  65.5 3.5 %collective-permute-start.17 = (f32[8,128]{1,0:T(8,128)S(1)}, f32[8,128]{1,0:T(8,128)S(1)}, u32[]{:S(2)}, u32[]{:S(2)}) collective-permute-start(f32[8,128]{1,0:T(8,128)S(1)} %add_add_fusion.1), channel_id=1, source_target_pairs={{0,6},{1,7},{2,0},{3,1},{4,2},{5,3},{6,4},{7,5},{8,14},{9,15},{10,... | collective-permute-start | bytes 12296 | tf_op jit(solution)/shard_map/ppermute | solution.py:394
  69.0 1.0 %collective-permute-start.15 = (f32[8,128]{1,0:T(8,128)S(1)}, f32[8,128]{1,0:T(8,128)S(1)}, u32[]{:S(2)}, u32[]{:S(2)}) collective-permute-start(f32[8,128]{1,0:T(8,128)S(1)} %add_add_fusion.1), channel_id=1, source_target_pairs={{0,4},{1,5},{2,6},{3,7},{4,0},{5,1},{6,2},{7,3},{8,12},{9,13},{10,... | collective-permute-start | bytes 12296 | tf_op jit(solution)/shard_map/ppermute | solution.py:394
  70.0 0.5 collective-permute-done.16
  70.6 3.0 %collective-permute-done.15 = f32[8,128]{1,0:T(8,128)S(1)} collective-permute-done((f32[8,128]{1,0:T(8,128)S(1)}, f32[8,128]{1,0:T(8,128)S(1)}, u32[]{:S(2)}, u32[]{:S(2)}) %collective-permute-start.15) | collective-permute-done | bytes 4128 | tf_op jit(solution)/shard_map/ppermute | solution.py:394
  73.5 0.2 collective-permute-start.18
  73.7 1.9 %collective-permute-done.14.refs_5_ = f32[3,8,2048]{2,1,0:T(8,128)S(1)} collective-permute-done((f32[3,8,2048]{2,1,0:T(8,128)S(1)}, f32[3,8,2048]{2,1,0:T(8,128)S(1)}, u32[]{:S(2)}, u32[]{:S(2)}) %collective-permute-start.14) | collective-permute-done | bytes 196640 | tf_op jit(solution)/shard_map/ppermute | solution.py:389
  75.7 1.3 %shard_map.73 = f32[4,3,8,4096]{3,2,1,0:T(8,128)} custom-call(f32[3,8,4096]{2,1,0:T(8,128)S(1)} %get-tuple-element.36.refs_0_, f32[3,8,4096]{2,1,0:T(8,128)S(1)} %collective-permute-done.9.refs_1_, f32[3,8,2048]{2,1,0:T(8,128)S(1)} %get-tuple-element.42.refs_2_, f32[3,8,2048]{2,1,0:T(8,128)S(1)} %collective-permute-done.12.refs_3_, ...), custom_call_target="tpu_custom_call" | custom-call | bytes 300000 | tf_op jit(solution)/shard_map/pallas_call | solution.py:315
  76.9 0.2 collective-permute-done.18
  77.2 0.5 multiply_bitcast_fusion.1
  (32 shorter events, 0.3 us)
Async XLA Ops:
  0.6 3.8 %collective-permute-start = (f32[4,3,8,4096]{3,2,1,0:T(8,128)}, f32[4,3,8,4096]{3,2,1,0:T(8,128)S(1)}, u32[]{:S(2)}, u32[]{:S(2)}) collective-permute-start(f32[4,3,8,4096]{3,2,1,0:T(8,128)} %own.1), channel_id=1, source_target_pairs={{0,8},{8,0},{1,9},{9,1},{2,10},{10,2},{3,11},{11,3},{4,12},{12,4},... | collective-permute-start | bytes 4718600 | tf_op jit(solution)/shard_map/ppermute | solution.py:341
  1.1 1.4 %copy-start = (f32[4,3,8,4096]{3,2,1,0:T(8,128)S(1)}, f32[4,3,8,4096]{3,2,1,0:T(8,128)}, u32[]{:S(2)}) copy-start(f32[4,3,8,4096]{3,2,1,0:T(8,128)} %own.1) | copy-start | bytes 4718596
  2.6 0.7 copy-start.2
  3.2 1.4 %copy-start.1 = (f32[4,3,8,4096]{3,2,1,0:T(8,128)S(1)}, f32[4,3,8,4096]{3,2,1,0:T(8,128)}, u32[]{:S(2)}) copy-start(f32[4,3,8,4096]{3,2,1,0:T(8,128)} %own.1) | copy-start | bytes 4718596
  4.4 5.3 %copy-start.3 = (f32[8,128]{1,0:T(8,128)S(1)}, f32[8,128]{1,0:T(8,128)}, u32[]{:S(2)}) copy-start(f32[8,128]{1,0:T(8,128)} %param.9) | copy-start | bytes 12292
  4.4 18.8 %copy-start.4 = (s32[8,128]{1,0:T(8,128)S(1)}, s32[8,128]{1,0:T(8,128)}, u32[]{:S(2)}) copy-start(s32[8,128]{1,0:T(8,128)} %param.8) | copy-start | bytes 12292
  4.4 18.8 %copy-start.5 = (f32[8,128]{1,0:T(8,128)S(1)}, f32[8,128]{1,0:T(8,128)}, u32[]{:S(2)}) copy-start(f32[8,128]{1,0:T(8,128)} %param.7) | copy-start | bytes 12292
  5.4 14.5 %collective-permute-start.1 = (f32[3,8,4096]{2,1,0:T(8,128)S(1)}, f32[3,8,4096]{2,1,0:T(8,128)S(1)}, u32[]{:S(2)}, u32[]{:S(2)}) collective-permute-start(f32[3,8,4096]{2,1,0:T(8,128)S(1)} %get-tuple-element.30), channel_id=1, source_target_pairs={{0,1},{1,0},{2,3},{3,2},{4,5},{5,4},{6,7},{7,6},{8,9},{9,8},{10,11... | collective-permute-start | bytes 1179656 | tf_op jit(solution)/shard_map/ppermute | solution.py:365
  8.1 7.5 %collective-permute-start.2 = (f32[6,8,512]{2,1,0:T(8,128)S(1)}, f32[6,8,512]{2,1,0:T(8,128)S(1)}, u32[]{:S(2)}, u32[]{:S(2)}) collective-permute-start(f32[6,8,512]{2,1,0:T(8,128)S(1)} %get-tuple-element.31), channel_id=1, source_target_pairs={{0,2},{1,7},{2,4},{3,1},{4,6},{5,3},{6,0},{7,5},{8,10},{9,15},{10,... | collective-permute-start | bytes 294920 | tf_op jit(solution)/shard_map/ppermute | solution.py:353
  9.7 5.9 %collective-permute-start.3 = (f32[6,8,512]{2,1,0:T(8,128)S(1)}, f32[6,8,512]{2,1,0:T(8,128)S(1)}, u32[]{:S(2)}, u32[]{:S(2)}) collective-permute-start(f32[6,8,512]{2,1,0:T(8,128)S(1)} %get-tuple-element.32), channel_id=1, source_target_pairs={{0,3},{1,6},{2,5},{3,0},{4,7},{5,2},{6,1},{7,4},{8,11},{9,14},{10,... | collective-permute-start | bytes 294920 | tf_op jit(solution)/shard_map/ppermute | solution.py:354
  9.8 26.4 %collective-permute-start.6 = (f32[3,8,4096]{2,1,0:T(8,128)S(1)}, f32[3,8,4096]{2,1,0:T(8,128)S(1)}, u32[]{:S(2)}, u32[]{:S(2)}) collective-permute-start(f32[3,8,4096]{2,1,0:T(8,128)S(1)} %get-tuple-element.35.refs_0_), channel_id=1, source_target_pairs={{0,6},{1,3},{2,0},{3,5},{4,2},{5,7},{6,4},{7,1},{8,14},{9,11},{10,... | collective-permute-start | bytes 1179656 | tf_op jit(solution)/shard_map/ppermute | solution.py:368
  19.9 7.6 %collective-permute-start.4 = (f32[3,8,2304]{2,1,0:T(8,128)S(1)}, f32[3,8,2304]{2,1,0:T(8,128)S(1)}, u32[]{:S(2)}, u32[]{:S(2)}) collective-permute-start(f32[3,8,2304]{2,1,0:T(8,128)S(1)} %get-tuple-element.33), channel_id=1, source_target_pairs={{0,1},{1,0},{2,3},{3,2},{4,5},{5,4},{6,7},{7,6},{8,9},{9,8},{10,11... | collective-permute-start | bytes 663560 | tf_op jit(solution)/shard_map/ppermute | solution.py:365
  21.6 14.7 %collective-permute-start.7 = (f32[3,8,4096]{2,1,0:T(8,128)S(1)}, f32[3,8,4096]{2,1,0:T(8,128)S(1)}, u32[]{:S(2)}, u32[]{:S(2)}) collective-permute-start(f32[3,8,4096]{2,1,0:T(8,128)S(1)} %collective-permute-done.1.refs_2_), channel_id=1, source_target_pairs={{0,2},{1,7},{2,4},{3,1},{4,6},{5,3},{6,0},{7,5},{8,10},{9,15},{10,... | collective-permute-start | bytes 1179656 | tf_op jit(solution)/shard_map/ppermute | solution.py:369
  23.2 4.3 %collective-permute-start.8 = (f32[3,8,128]{2,1,0:T(8,128)S(1)}, f32[3,8,128]{2,1,0:T(8,128)S(1)}, u32[]{:S(2)}, u32[]{:S(2)}) collective-permute-start(f32[3,8,128]{2,1,0:T(8,128)S(1)} %pad_maximum_fusion.refs_6_.refs_8_), channel_id=1, source_target_pairs={{0,1},{1,0},{2,3},{3,2},{4,5},{5,4},{6,7},{7,6},{8,9},{9,8},{10,11... | collective-permute-start | bytes 36872 | tf_op jit(solution)/shard_map/ppermute | solution.py:356
  27.5 21.7 %collective-permute-start.10 = (f32[3,8,4096]{2,1,0:T(8,128)S(1)}, f32[3,8,4096]{2,1,0:T(8,128)S(1)}, u32[]{:S(2)}, u32[]{:S(2)}) collective-permute-start(f32[3,8,4096]{2,1,0:T(8,128)S(1)} %get-tuple-element.45.refs_0_), channel_id=1, source_target_pairs={{0,6},{1,3},{2,0},{3,5},{4,2},{5,7},{6,4},{7,1},{8,14},{9,11},{10,... | collective-permute-start | bytes 1179656 | tf_op jit(solution)/shard_map/ppermute | solution.py:368
  30.8 5.4 %collective-permute-start.5 = (f32[3,8,1792]{2,1,0:T(8,128)S(1)}, f32[3,8,1792]{2,1,0:T(8,128)S(1)}, u32[]{:S(2)}, u32[]{:S(2)}) collective-permute-start(f32[3,8,1792]{2,1,0:T(8,128)S(1)} %get-tuple-element.34), channel_id=1, source_target_pairs={{0,1},{1,0},{2,3},{3,2},{4,5},{5,4},{6,7},{7,6},{8,9},{9,8},{10,11... | collective-permute-start | bytes 516104 | tf_op jit(solution)/shard_map/ppermute | solution.py:365
  30.8 18.3 %collective-permute-start.11 = (f32[3,8,2304]{2,1,0:T(8,128)S(1)}, f32[3,8,2304]{2,1,0:T(8,128)S(1)}, u32[]{:S(2)}, u32[]{:S(2)}) collective-permute-start(f32[3,8,2304]{2,1,0:T(8,128)S(1)} %collective-permute-done.4.refs_2_), channel_id=1, source_target_pairs={{0,2},{1,7},{2,4},{3,1},{4,6},{5,3},{6,0},{7,5},{8,10},{9,15},{10,... | collective-permute-start | bytes 663560 | tf_op jit(solution)/shard_map/ppermute | solution.py:369
  36.3 19.1 %collective-permute-start.13 = (f32[3,8,1792]{2,1,0:T(8,128)S(1)}, f32[3,8,1792]{2,1,0:T(8,128)S(1)}, u32[]{:S(2)}, u32[]{:S(2)}) collective-permute-start(f32[3,8,1792]{2,1,0:T(8,128)S(1)} %collective-permute-done.5.refs_3_), channel_id=1, source_target_pairs={{0,2},{1,7},{2,4},{3,1},{4,6},{5,3},{6,0},{7,5},{8,10},{9,15},{10,... | collective-permute-start | bytes 516104 | tf_op jit(solution)/shard_map/ppermute | solution.py:369
  45.1 16.3 %collective-permute-start.9 = (f32[3,8,4096]{2,1,0:T(8,128)S(1)}, f32[3,8,4096]{2,1,0:T(8,128)S(1)}, u32[]{:S(2)}, u32[]{:S(2)}) collective-permute-start(f32[3,8,4096]{2,1,0:T(8,128)S(1)} %get-tuple-element.37), channel_id=1, source_target_pairs={{0,1},{1,0},{2,3},{3,2},{4,5},{5,4},{6,7},{7,6},{8,9},{9,8},{10,11... | collective-permute-start | bytes 1179656 | tf_op jit(solution)/shard_map/ppermute | solution.py:389
  55.2 6.2 %collective-permute-start.12 = (f32[3,8,2048]{2,1,0:T(8,128)S(1)}, f32[3,8,2048]{2,1,0:T(8,128)S(1)}, u32[]{:S(2)}, u32[]{:S(2)}) collective-permute-start(f32[3,8,2048]{2,1,0:T(8,128)S(1)} %get-tuple-element.43), channel_id=1, source_target_pairs={{0,1},{1,0},{2,3},{3,2},{4,5},{5,4},{6,7},{7,6},{8,9},{9,8},{10,11... | collective-permute-start | bytes 589832 | tf_op jit(solution)/shard_map/ppermute | solution.py:389
  61.5 9.1 %collective-permute-start.16 = (f32[8,128]{1,0:T(8,128)S(1)}, f32[8,128]{1,0:T(8,128)S(1)}, u32[]{:S(2)}, u32[]{:S(2)}) collective-permute-start(f32[8,128]{1,0:T(8,128)S(1)} %add_add_fusion.1), channel_id=1, source_target_pairs={{0,2},{1,3},{2,4},{3,5},{4,6},{5,7},{6,0},{7,1},{8,10},{9,11},{10,... | collective-permute-start | bytes 12296 | tf_op jit(solution)/shard_map/ppermute | solution.py:394
  65.5 5.0 %collective-permute-start.17 = (f32[8,128]{1,0:T(8,128)S(1)}, f32[8,128]{1,0:T(8,128)S(1)}, u32[]{:S(2)}, u32[]{:S(2)}) collective-permute-start(f32[8,128]{1,0:T(8,128)S(1)} %add_add_fusion.1), channel_id=1, source_target_pairs={{0,6},{1,7},{2,0},{3,1},{4,2},{5,3},{6,4},{7,5},{8,14},{9,15},{10,... | collective-permute-start | bytes 12296 | tf_op jit(solution)/shard_map/ppermute | solution.py:394
  69.0 4.5 %collective-permute-start.15 = (f32[8,128]{1,0:T(8,128)S(1)}, f32[8,128]{1,0:T(8,128)S(1)}, u32[]{:S(2)}, u32[]{:S(2)}) collective-permute-start(f32[8,128]{1,0:T(8,128)S(1)} %add_add_fusion.1), channel_id=1, source_target_pairs={{0,4},{1,5},{2,6},{3,7},{4,0},{5,1},{6,2},{7,3},{8,12},{9,13},{10,... | collective-permute-start | bytes 12296 | tf_op jit(solution)/shard_map/ppermute | solution.py:394
  70.0 5.7 %collective-permute-start.14 = (f32[3,8,2048]{2,1,0:T(8,128)S(1)}, f32[3,8,2048]{2,1,0:T(8,128)S(1)}, u32[]{:S(2)}, u32[]{:S(2)}) collective-permute-start(f32[3,8,2048]{2,1,0:T(8,128)S(1)} %get-tuple-element.47), channel_id=1, source_target_pairs={{0,1},{1,0},{2,3},{3,2},{4,5},{5,4},{6,7},{7,6},{8,9},{9,8},{10,11... | collective-permute-start | bytes 589832 | tf_op jit(solution)/shard_map/ppermute | solution.py:389
  73.5 3.6 %collective-permute-start.18 = (f32[8,128]{1,0:T(8,128)S(1)}, f32[8,128]{1,0:T(8,128)S(1)}, u32[]{:S(2)}, u32[]{:S(2)}) collective-permute-start(f32[8,128]{1,0:T(8,128)S(1)} %add_add_fusion), channel_id=1, source_target_pairs={{0,1},{1,0},{2,3},{3,2},{4,5},{5,4},{6,7},{7,6},{8,9},{9,8},{10,11... | collective-permute-start | bytes 12296 | tf_op jit(solution)/shard_map/ppermute | solution.py:401

commit v10 on v9

--- a/solution.py
+++ b/solution.py
@@ -364,7 +364,7 @@
             giving = after(giving, first)
         got.append([lax.ppermute(g, "strip", swap) for g in giving])
         if k:
-            (keeping,) = after((keeping,), (got[k][0], obs_got))
+            (keeping,) = after((keeping,), (got[k], obs_got))
         direct.append(lax.ppermute(keeping, "strip", straight))
         passed.append([lax.ppermute(g, "strip", onward) for g in got[k]])
         if first is None:

time: 77.8 us -> 75.3 us (0.968)
  waiting for transfers between devices: 17.5 us -> 15.7 us
    ppermute x3, waiting for transfers between devices: 8.61 us -> 4.27 us  [local(): got.append([lax.ppermute(g, 'strip', swap) for g in giving])]
    ppermute x3, starting transfers between devices: 8.53 us -> 4.96 us  [local(): lax.ppermute(total, 'strip', moved(step, step))]
    ppermute x3, waiting for transfers between devices: 1.49 us -> 3.73 us  [local(): passed.append([lax.ppermute(g, 'strip', onward) for g in got[k]])]
    ppermute x1, waiting for transfers between devices: 1.67 us -> 3.61 us  [local(): obs_got = lax.ppermute(obs_own, 'strip', swap)]
    ppermute x3, waiting for transfers between devices: 1.94 us -> 0.25 us  [local(): blocks.append((keep, lax.ppermute(send, 'strip', swap)))]
    ppermute x1, starting transfers between devices: 0.18 us -> 1.41 us  [local(): theirs = lax.ppermute(total, 'strip', swap)]
    ppermute x1, starting transfers between devices: 2.61 us -> 3.6 us  [local(): obs_got = lax.ppermute(obs_own, 'strip', swap)]
    ppermute x3, starting transfers between devices: 2.66 us -> 3.61 us  [local(): blocks.append((keep, lax.ppermute(send, 'strip', swap)))]
  transfers between devices with their start and end apart: 19 -> 19, of which waited for: 8 -> 8; matrix products, arithmetic and copies ran while one was open for 0% -> 0% of each run, Pallas kernels for 30% -> 31%
where the time goes in v10:
time: 75.3 us; the launch traced here: 75.1 us
  starting transfers between devices  31.6 us (42%)
  Pallas kernels  24.2 us (32%)
  waiting for transfers between devices  15.7 us (21%)
  local copies, waits for them, and re-layouts  2.24 us (3%)
  between operations  0.77 us (1%)
    pallas_call x3, Pallas kernels, forecast(): pl.pallas_call(functools.partial(forecast_kernel, worked=worked, kept=kep...  21 us
    ppermute x2, starting transfers between devices, local(): direct.append(lax.ppermute(keeping, 'strip', straight))  9.38 us
    ppermute x3, starting transfers between devices, local(): lax.ppermute(total, 'strip', moved(step, step))  4.96 us
    ppermute x3, starting transfers between devices, local(): got.append([lax.ppermute(g, 'strip', swap) for g in giving])  4.76 us
    ppermute x3, waiting for transfers between devices, local(): got.append([lax.ppermute(g, 'strip', swap) for g in giving])  4.27 us
    ppermute x3, waiting for transfers between devices, local(): passed.append([lax.ppermute(g, 'strip', onward) for g in got[k]])  3.73 us
    ppermute x1, waiting for transfers between devices, local(): obs_got = lax.ppermute(obs_own, 'strip', swap)  3.61 us
    ppermute x3, starting transfers between devices, local(): blocks.append((keep, lax.ppermute(send, 'strip', swap)))  3.61 us
  transfers between devices with their start and end apart: 19, of which 8 were waited for; matrix products, arithmetic and copies ran while one was open for 0% of the time, Pallas kernels for 31%

profile of v10, /device:TPU:0, one launch (start us, length us, event | category | flops | bytes accessed | tf_op | source)
XLA Modules:
  0.0 75.1 jit_solution(4895901931933881242)
XLA Ops:
  0.6 0.5 collective-permute-start
  1.1 1.4 %copy-done = f32[4,3,8,4096]{3,2,1,0:T(8,128)S(1)} copy-done((f32[4,3,8,4096]{3,2,1,0:T(8,128)S(1)}, f32[4,3,8,4096]{3,2,1,0:T(8,128)}, u32[]{:S(2)}) %copy-start) | copy-done | bytes 1572888
  2.6 0.7 copy-done.2
  3.2 1.2 %shard_map.68.index = s32[4]{0:T(128)S(1)} custom-call(s32[8]{0:T(128)S(1)} %copy-done.2, f32[4,3,8,4096]{3,2,1,0:T(8,128)S(1)} %copy-done), custom_call_target="tpu_custom_call" | custom-call | tf_op jit(solution)/shard_map/pallas_call | solution.py:66
  4.5 0.2 copy-done.1
  4.6 0.8 %shard_map.69 = (f32[3,8,4096]{2,1,0:T(8,128)S(1)}, f32[3,8,4096]{2,1,0:T(8,128)S(1)}, f32[3,8,4096]{2,1,0:T(8,128)S(1)}, f32[3,8,2304]{2,1,0:T(8,128)S(1)}, f32...) custom-call(s32[4]{0:T(128)S(1)} %shard_map.68.index, f32[4,3,8,4096]{3,2,1,0:T(8,128)S(1)} %copy-done.1, ...), custom_call_target="tpu_custom_call" | custom-call | tf_op jit(solution)/shard_map/pallas_call | solution.py:130
  5.4 2.7 %collective-permute-start.1 = (f32[3,8,4096]{2,1,0:T(8,128)S(1)}, f32[3,8,4096]{2,1,0:T(8,128)S(1)}, u32[]{:S(2)}, u32[]{:S(2)}) collective-permute-start(f32[3,8,4096]{2,1,0:T(8,128)S(1)} %get-tuple-element.30), channel_id=1, source_target_pairs={{0,1},{1,0},{2,3},{3,2},{4,5},{5,4},{6,7},{7,6},{8,9},{9,8},{10,11... | collective-permute-start | bytes 1179656 | tf_op jit(solution)/shard_map/ppermute | solution.py:365
  8.1 1.6 %collective-permute-start.2 = (f32[6,8,512]{2,1,0:T(8,128)S(1)}, f32[6,8,512]{2,1,0:T(8,128)S(1)}, u32[]{:S(2)}, u32[]{:S(2)}) collective-permute-start(f32[6,8,512]{2,1,0:T(8,128)S(1)} %get-tuple-element.31), channel_id=1, source_target_pairs={{0,2},{1,7},{2,4},{3,1},{4,6},{5,3},{6,0},{7,5},{8,10},{9,15},{10,... | collective-permute-start | bytes 294920 | tf_op jit(solution)/shard_map/ppermute | solution.py:353
  9.8 5.8 %collective-permute-start.6 = (f32[3,8,4096]{2,1,0:T(8,128)S(1)}, f32[3,8,4096]{2,1,0:T(8,128)S(1)}, u32[]{:S(2)}, u32[]{:S(2)}) collective-permute-start(f32[3,8,4096]{2,1,0:T(8,128)S(1)} %get-tuple-element.35.refs_0_), channel_id=1, source_target_pairs={{0,6},{1,3},{2,0},{3,5},{4,2},{5,7},{6,4},{7,1},{8,14},{9,11},{10,... | collective-permute-start | bytes 1179656 | tf_op jit(solution)/shard_map/ppermute | solution.py:368
  15.6 4.3 %collective-permute-done.1.refs_2_ = f32[3,8,4096]{2,1,0:T(8,128)S(1)} collective-permute-done((f32[3,8,4096]{2,1,0:T(8,128)S(1)}, f32[3,8,4096]{2,1,0:T(8,128)S(1)}, u32[]{:S(2)}, u32[]{:S(2)}) %collective-permute-start.1) | collective-permute-done | bytes 393248 | tf_op jit(solution)/shard_map/ppermute | solution.py:365
  19.9 1.7 %collective-permute-start.4 = (f32[3,8,2304]{2,1,0:T(8,128)S(1)}, f32[3,8,2304]{2,1,0:T(8,128)S(1)}, u32[]{:S(2)}, u32[]{:S(2)}) collective-permute-start(f32[3,8,2304]{2,1,0:T(8,128)S(1)} %get-tuple-element.33), channel_id=1, source_target_pairs={{0,1},{1,0},{2,3},{3,2},{4,5},{5,4},{6,7},{7,6},{8,9},{9,8},{10,11... | collective-permute-start | bytes 663560 | tf_op jit(solution)/shard_map/ppermute | solution.py:365
  21.6 0.3 collective-permute-start.5
  21.9 1.8 %collective-permute-start.7 = (f32[3,8,4096]{2,1,0:T(8,128)S(1)}, f32[3,8,4096]{2,1,0:T(8,128)S(1)}, u32[]{:S(2)}, u32[]{:S(2)}) collective-permute-start(f32[3,8,4096]{2,1,0:T(8,128)S(1)} %collective-permute-done.1.refs_2_), channel_id=1, source_target_pairs={{0,2},{1,7},{2,4},{3,1},{4,6},{5,3},{6,0},{7,5},{8,10},{9,15},{10,... | collective-permute-start | bytes 1179656 | tf_op jit(solution)/shard_map/ppermute | solution.py:369
  23.7 3.6 %collective-permute-start.8 = (f32[3,8,128]{2,1,0:T(8,128)S(1)}, f32[3,8,128]{2,1,0:T(8,128)S(1)}, u32[]{:S(2)}, u32[]{:S(2)}) collective-permute-start(f32[3,8,128]{2,1,0:T(8,128)S(1)} %pad_maximum_fusion.refs_6_.refs_8_), channel_id=1, source_target_pairs={{0,1},{1,0},{2,3},{3,2},{4,5},{5,4},{6,7},{7,6},{8,9},{9,8},{10,11... | collective-permute-start | bytes 36872 | tf_op jit(solution)/shard_map/ppermute | solution.py:356
  27.3 3.6 %collective-permute-done.8.refs_7_.refs_9_ = f32[3,8,128]{2,1,0:T(8,128)S(1)} collective-permute-done((f32[3,8,128]{2,1,0:T(8,128)S(1)}, f32[3,8,128]{2,1,0:T(8,128)S(1)}, u32[]{:S(2)}, u32[]{:S(2)}) %collective-permute-start.8) | collective-permute-done | bytes 12320 | tf_op jit(solution)/shard_map/ppermute | solution.py:356
  30.9 3.6 %collective-permute-start.10 = (f32[3,8,4096]{2,1,0:T(8,128)S(1)}, f32[3,8,4096]{2,1,0:T(8,128)S(1)}, u32[]{:S(2)}, u32[]{:S(2)}) collective-permute-start(f32[3,8,4096]{2,1,0:T(8,128)S(1)} %get-tuple-element.45.refs_0_), channel_id=1, source_target_pairs={{0,6},{1,3},{2,0},{3,5},{4,2},{5,7},{6,4},{7,1},{8,14},{9,11},{10,... | collective-permute-start | bytes 1179656 | tf_op jit(solution)/shard_map/ppermute | solution.py:368
  34.5 1.0 %collective-permute-done.7.refs_3_ = f32[3,8,4096]{2,1,0:T(8,128)S(1)} collective-permute-done((f32[3,8,4096]{2,1,0:T(8,128)S(1)}, f32[3,8,4096]{2,1,0:T(8,128)S(1)}, u32[]{:S(2)}, u32[]{:S(2)}) %collective-permute-start.7) | collective-permute-done | bytes 393248 | tf_op jit(solution)/shard_map/ppermute | solution.py:369
  35.5 8.8 %shard_map.70 = (f32[3,8,4096]{2,1,0:T(8,128)S(1)}, f32[3,8,4096]{2,1,0:T(8,128)S(1)}, f32[8,128]{1,0:T(8,128)S(1)}) custom-call(f32[3,8,4096]{2,1,0:T(8,128)S(1)} %get-tuple-element.35.refs_0_, f32[3,8,4096]{2,1,0:T(8,128)S(1)} %collective-permute-done.6.refs_1_, f32[3,8,4096]{2,1,0:T(8,128)S(1)} %collective-permute-done.1.refs_2_, ...), custom_call_target="tpu_custom_call" | custom-call | bytes 480000 | tf_op jit(solution)/shard_map/pallas_call | solution.py:282
  44.4 2.6 %collective-permute-start.9 = (f32[3,8,4096]{2,1,0:T(8,128)S(1)}, f32[3,8,4096]{2,1,0:T(8,128)S(1)}, u32[]{:S(2)}, u32[]{:S(2)}) collective-permute-start(f32[3,8,4096]{2,1,0:T(8,128)S(1)} %get-tuple-element.37), channel_id=1, source_target_pairs={{0,1},{1,0},{2,3},{3,2},{4,5},{5,4},{6,7},{7,6},{8,9},{9,8},{10,11... | collective-permute-start | bytes 1179656 | tf_op jit(solution)/shard_map/ppermute | solution.py:389
  47.0 2.7 %collective-permute-done.11.refs_3_.refs_4_ = f32[3,8,2304]{2,1,0:T(8,128)S(1)} collective-permute-done((f32[3,8,2304]{2,1,0:T(8,128)S(1)}, f32[3,8,2304]{2,1,0:T(8,128)S(1)}, u32[]{:S(2)}, u32[]{:S(2)}) %collective-permute-start.11) | collective-permute-done | bytes 221216 | tf_op jit(solution)/shard_map/ppermute | solution.py:369
  49.8 6.1 %shard_map.71 = (f32[3,8,2048]{2,1,0:T(8,128)S(1)}, f32[3,8,2048]{2,1,0:T(8,128)S(1)}, f32[8,128]{1,0:T(8,128)S(1)}) custom-call(f32[3,8,4096]{2,1,0:T(8,128)S(1)} %get-tuple-element.45.refs_0_, f32[3,8,4096]{2,1,0:T(8,128)S(1)} %collective-permute-done.10.refs_1_, f32[3,8,2304]{2,1,0:T(8,128)S(1)} %collective-permute-done.4.refs_2_, ...), custom_call_target="tpu_custom_call" | custom-call | bytes 270000 | tf_op jit(solution)/shard_map/pallas_call | solution.py:282
  55.9 6.1 %shard_map.72 = (f32[3,8,2048]{2,1,0:T(8,128)S(1)}, f32[3,8,2048]{2,1,0:T(8,128)S(1)}, f32[8,128]{1,0:T(8,128)S(1)}) custom-call(f32[3,8,4096]{2,1,0:T(8,128)S(1)} %get-tuple-element.45.refs_0_, f32[3,8,4096]{2,1,0:T(8,128)S(1)} %collective-permute-done.10.refs_1_, f32[3,8,2304]{2,1,0:T(8,128)S(1)} %collective-permute-done.4.refs_2_, ...), custom_call_target="tpu_custom_call" | custom-call | bytes 270000 | tf_op jit(solution)/shard_map/pallas_call | solution.py:282
  62.0 1.1 %collective-permute-start.16 = (f32[8,128]{1,0:T(8,128)S(1)}, f32[8,128]{1,0:T(8,128)S(1)}, u32[]{:S(2)}, u32[]{:S(2)}) collective-permute-start(f32[8,128]{1,0:T(8,128)S(1)} %add_add_fusion.1), channel_id=1, source_target_pairs={{0,2},{1,3},{2,4},{3,5},{4,6},{5,7},{6,0},{7,1},{8,10},{9,11},{10,... | collective-permute-start | bytes 12296 | tf_op jit(solution)/shard_map/ppermute | solution.py:394
  63.2 3.3 %collective-permute-start.17 = (f32[8,128]{1,0:T(8,128)S(1)}, f32[8,128]{1,0:T(8,128)S(1)}, u32[]{:S(2)}, u32[]{:S(2)}) collective-permute-start(f32[8,128]{1,0:T(8,128)S(1)} %add_add_fusion.1), channel_id=1, source_target_pairs={{0,6},{1,7},{2,0},{3,1},{4,2},{5,3},{6,4},{7,5},{8,14},{9,15},{10,... | collective-permute-start | bytes 12296 | tf_op jit(solution)/shard_map/ppermute | solution.py:394
  66.5 0.5 collective-permute-start.15
  67.0 0.9 %collective-permute-start.14 = (f32[3,8,2048]{2,1,0:T(8,128)S(1)}, f32[3,8,2048]{2,1,0:T(8,128)S(1)}, u32[]{:S(2)}, u32[]{:S(2)}) collective-permute-start(f32[3,8,2048]{2,1,0:T(8,128)S(1)} %get-tuple-element.47), channel_id=1, source_target_pairs={{0,1},{1,0},{2,3},{3,2},{4,5},{5,4},{6,7},{7,6},{8,9},{9,8},{10,11... | collective-permute-start | bytes 589832 | tf_op jit(solution)/shard_map/ppermute | solution.py:389
  68.0 3.0 %collective-permute-done.15 = f32[8,128]{1,0:T(8,128)S(1)} collective-permute-done((f32[8,128]{1,0:T(8,128)S(1)}, f32[8,128]{1,0:T(8,128)S(1)}, u32[]{:S(2)}, u32[]{:S(2)}) %collective-permute-start.15) | collective-permute-done | bytes 4128 | tf_op jit(solution)/shard_map/ppermute | solution.py:394
  71.0 1.4 %collective-permute-start.18 = (f32[8,128]{1,0:T(8,128)S(1)}, f32[8,128]{1,0:T(8,128)S(1)}, u32[]{:S(2)}, u32[]{:S(2)}) collective-permute-start(f32[8,128]{1,0:T(8,128)S(1)} %add_add_fusion), channel_id=1, source_target_pairs={{0,1},{1,0},{2,3},{3,2},{4,5},{5,4},{6,7},{7,6},{8,9},{9,8},{10,11... | collective-permute-start | bytes 12296 | tf_op jit(solution)/shard_map/ppermute | solution.py:401
  72.4 0.2 collective-permute-done.14.refs_5_
  72.7 1.3 %shard_map.73 = f32[4,3,8,4096]{3,2,1,0:T(8,128)} custom-call(f32[3,8,4096]{2,1,0:T(8,128)S(1)} %get-tuple-element.36.refs_0_, f32[3,8,4096]{2,1,0:T(8,128)S(1)} %collective-permute-done.9.refs_1_, f32[3,8,2048]{2,1,0:T(8,128)S(1)} %get-tuple-element.42.refs_2_, f32[3,8,2048]{2,1,0:T(8,128)S(1)} %collective-permute-done.12.refs_3_, ...), custom_call_target="tpu_custom_call" | custom-call | bytes 300000 | tf_op jit(solution)/shard_map/pallas_call | solution.py:315
  73.9 0.7 collective-permute-done.18
  74.6 0.5 multiply_bitcast_fusion.1
  (32 shorter events, 0.4 us)
Async XLA Ops:
  0.6 3.8 %collective-permute-start = (f32[4,3,8,4096]{3,2,1,0:T(8,128)}, f32[4,3,8,4096]{3,2,1,0:T(8,128)S(1)}, u32[]{:S(2)}, u32[]{:S(2)}) collective-permute-start(f32[4,3,8,4096]{3,2,1,0:T(8,128)} %own.1), channel_id=1, source_target_pairs={{0,8},{8,0},{1,9},{9,1},{2,10},{10,2},{3,11},{11,3},{4,12},{12,4},... | collective-permute-start | bytes 4718600 | tf_op jit(solution)/shard_map/ppermute | solution.py:341
  1.1 1.4 %copy-start = (f32[4,3,8,4096]{3,2,1,0:T(8,128)S(1)}, f32[4,3,8,4096]{3,2,1,0:T(8,128)}, u32[]{:S(2)}) copy-start(f32[4,3,8,4096]{3,2,1,0:T(8,128)} %own.1) | copy-start | bytes 4718596
  2.6 0.7 copy-start.2
  3.2 1.4 %copy-start.1 = (f32[4,3,8,4096]{3,2,1,0:T(8,128)S(1)}, f32[4,3,8,4096]{3,2,1,0:T(8,128)}, u32[]{:S(2)}) copy-start(f32[4,3,8,4096]{3,2,1,0:T(8,128)} %own.1) | copy-start | bytes 4718596
  4.4 5.3 %copy-start.3 = (f32[8,128]{1,0:T(8,128)S(1)}, f32[8,128]{1,0:T(8,128)}, u32[]{:S(2)}) copy-start(f32[8,128]{1,0:T(8,128)} %param.9) | copy-start | bytes 12292
  4.4 19.3 %copy-start.4 = (s32[8,128]{1,0:T(8,128)S(1)}, s32[8,128]{1,0:T(8,128)}, u32[]{:S(2)}) copy-start(s32[8,128]{1,0:T(8,128)} %param.8) | copy-start | bytes 12292
  4.4 19.3 %copy-start.5 = (f32[8,128]{1,0:T(8,128)S(1)}, f32[8,128]{1,0:T(8,128)}, u32[]{:S(2)}) copy-start(f32[8,128]{1,0:T(8,128)} %param.7) | copy-start | bytes 12292
  5.4 14.5 %collective-permute-start.1 = (f32[3,8,4096]{2,1,0:T(8,128)S(1)}, f32[3,8,4096]{2,1,0:T(8,128)S(1)}, u32[]{:S(2)}, u32[]{:S(2)}) collective-permute-start(f32[3,8,4096]{2,1,0:T(8,128)S(1)} %get-tuple-element.30), channel_id=1, source_target_pairs={{0,1},{1,0},{2,3},{3,2},{4,5},{5,4},{6,7},{7,6},{8,9},{9,8},{10,11... | collective-permute-start | bytes 1179656 | tf_op jit(solution)/shard_map/ppermute | solution.py:365
  8.1 7.5 %collective-permute-start.2 = (f32[6,8,512]{2,1,0:T(8,128)S(1)}, f32[6,8,512]{2,1,0:T(8,128)S(1)}, u32[]{:S(2)}, u32[]{:S(2)}) collective-permute-start(f32[6,8,512]{2,1,0:T(8,128)S(1)} %get-tuple-element.31), channel_id=1, source_target_pairs={{0,2},{1,7},{2,4},{3,1},{4,6},{5,3},{6,0},{7,5},{8,10},{9,15},{10,... | collective-permute-start | bytes 294920 | tf_op jit(solution)/shard_map/ppermute | solution.py:353
  9.7 5.9 %collective-permute-start.3 = (f32[6,8,512]{2,1,0:T(8,128)S(1)}, f32[6,8,512]{2,1,0:T(8,128)S(1)}, u32[]{:S(2)}, u32[]{:S(2)}) collective-permute-start(f32[6,8,512]{2,1,0:T(8,128)S(1)} %get-tuple-element.32), channel_id=1, source_target_pairs={{0,3},{1,6},{2,5},{3,0},{4,7},{5,2},{6,1},{7,4},{8,11},{9,14},{10,... | collective-permute-start | bytes 294920 | tf_op jit(solution)/shard_map/ppermute | solution.py:354
  9.8 24.7 %collective-permute-start.6 = (f32[3,8,4096]{2,1,0:T(8,128)S(1)}, f32[3,8,4096]{2,1,0:T(8,128)S(1)}, u32[]{:S(2)}, u32[]{:S(2)}) collective-permute-start(f32[3,8,4096]{2,1,0:T(8,128)S(1)} %get-tuple-element.35.refs_0_), channel_id=1, source_target_pairs={{0,6},{1,3},{2,0},{3,5},{4,2},{5,7},{6,4},{7,1},{8,14},{9,11},{10,... | collective-permute-start | bytes 1179656 | tf_op jit(solution)/shard_map/ppermute | solution.py:368
  19.9 11.1 %collective-permute-start.4 = (f32[3,8,2304]{2,1,0:T(8,128)S(1)}, f32[3,8,2304]{2,1,0:T(8,128)S(1)}, u32[]{:S(2)}, u32[]{:S(2)}) collective-permute-start(f32[3,8,2304]{2,1,0:T(8,128)S(1)} %get-tuple-element.33), channel_id=1, source_target_pairs={{0,1},{1,0},{2,3},{3,2},{4,5},{5,4},{6,7},{7,6},{8,9},{9,8},{10,11... | collective-permute-start | bytes 663560 | tf_op jit(solution)/shard_map/ppermute | solution.py:365
  21.6 9.3 %collective-permute-start.5 = (f32[3,8,1792]{2,1,0:T(8,128)S(1)}, f32[3,8,1792]{2,1,0:T(8,128)S(1)}, u32[]{:S(2)}, u32[]{:S(2)}) collective-permute-start(f32[3,8,1792]{2,1,0:T(8,128)S(1)} %get-tuple-element.34), channel_id=1, source_target_pairs={{0,1},{1,0},{2,3},{3,2},{4,5},{5,4},{6,7},{7,6},{8,9},{9,8},{10,11... | collective-permute-start | bytes 516104 | tf_op jit(solution)/shard_map/ppermute | solution.py:365
  21.9 13.6 %collective-permute-start.7 = (f32[3,8,4096]{2,1,0:T(8,128)S(1)}, f32[3,8,4096]{2,1,0:T(8,128)S(1)}, u32[]{:S(2)}, u32[]{:S(2)}) collective-permute-start(f32[3,8,4096]{2,1,0:T(8,128)S(1)} %collective-permute-done.1.refs_2_), channel_id=1, source_target_pairs={{0,2},{1,7},{2,4},{3,1},{4,6},{5,3},{6,0},{7,5},{8,10},{9,15},{10,... | collective-permute-start | bytes 1179656 | tf_op jit(solution)/shard_map/ppermute | solution.py:369
  23.7 7.2 %collective-permute-start.8 = (f32[3,8,128]{2,1,0:T(8,128)S(1)}, f32[3,8,128]{2,1,0:T(8,128)S(1)}, u32[]{:S(2)}, u32[]{:S(2)}) collective-permute-start(f32[3,8,128]{2,1,0:T(8,128)S(1)} %pad_maximum_fusion.refs_6_.refs_8_), channel_id=1, source_target_pairs={{0,1},{1,0},{2,3},{3,2},{4,5},{5,4},{6,7},{7,6},{8,9},{9,8},{10,11... | collective-permute-start | bytes 36872 | tf_op jit(solution)/shard_map/ppermute | solution.py:356
  30.9 18.8 %collective-permute-start.10 = (f32[3,8,4096]{2,1,0:T(8,128)S(1)}, f32[3,8,4096]{2,1,0:T(8,128)S(1)}, u32[]{:S(2)}, u32[]{:S(2)}) collective-permute-start(f32[3,8,4096]{2,1,0:T(8,128)S(1)} %get-tuple-element.45.refs_0_), channel_id=1, source_target_pairs={{0,6},{1,3},{2,0},{3,5},{4,2},{5,7},{6,4},{7,1},{8,14},{9,11},{10,... | collective-permute-start | bytes 1179656 | tf_op jit(solution)/shard_map/ppermute | solution.py:368
  34.5 15.2 %collective-permute-start.11 = (f32[3,8,2304]{2,1,0:T(8,128)S(1)}, f32[3,8,2304]{2,1,0:T(8,128)S(1)}, u32[]{:S(2)}, u32[]{:S(2)}) collective-permute-start(f32[3,8,2304]{2,1,0:T(8,128)S(1)} %collective-permute-done.4.refs_2_), channel_id=1, source_target_pairs={{0,2},{1,7},{2,4},{3,1},{4,6},{5,3},{6,0},{7,5},{8,10},{9,15},{10,... | collective-permute-start | bytes 663560 | tf_op jit(solution)/shard_map/ppermute | solution.py:369
  34.5 21.4 %collective-permute-start.13 = (f32[3,8,1792]{2,1,0:T(8,128)S(1)}, f32[3,8,1792]{2,1,0:T(8,128)S(1)}, u32[]{:S(2)}, u32[]{:S(2)}) collective-permute-start(f32[3,8,1792]{2,1,0:T(8,128)S(1)} %collective-permute-done.5.refs_3_), channel_id=1, source_target_pairs={{0,2},{1,7},{2,4},{3,1},{4,6},{5,3},{6,0},{7,5},{8,10},{9,15},{10,... | collective-permute-start | bytes 516104 | tf_op jit(solution)/shard_map/ppermute | solution.py:369
  44.4 17.6 %collective-permute-start.9 = (f32[3,8,4096]{2,1,0:T(8,128)S(1)}, f32[3,8,4096]{2,1,0:T(8,128)S(1)}, u32[]{:S(2)}, u32[]{:S(2)}) collective-permute-start(f32[3,8,4096]{2,1,0:T(8,128)S(1)} %get-tuple-element.37), channel_id=1, source_target_pairs={{0,1},{1,0},{2,3},{3,2},{4,5},{5,4},{6,7},{7,6},{8,9},{9,8},{10,11... | collective-permute-start | bytes 1179656 | tf_op jit(solution)/shard_map/ppermute | solution.py:389
  55.8 6.2 %collective-permute-start.12 = (f32[3,8,2048]{2,1,0:T(8,128)S(1)}, f32[3,8,2048]{2,1,0:T(8,128)S(1)}, u32[]{:S(2)}, u32[]{:S(2)}) collective-permute-start(f32[3,8,2048]{2,1,0:T(8,128)S(1)} %get-tuple-element.43), channel_id=1, source_target_pairs={{0,1},{1,0},{2,3},{3,2},{4,5},{5,4},{6,7},{7,6},{8,9},{9,8},{10,11... | collective-permute-start | bytes 589832 | tf_op jit(solution)/shard_map/ppermute | solution.py:389
  62.0 6.0 %collective-permute-start.16 = (f32[8,128]{1,0:T(8,128)S(1)}, f32[8,128]{1,0:T(8,128)S(1)}, u32[]{:S(2)}, u32[]{:S(2)}) collective-permute-start(f32[8,128]{1,0:T(8,128)S(1)} %add_add_fusion.1), channel_id=1, source_target_pairs={{0,2},{1,3},{2,4},{3,5},{4,6},{5,7},{6,0},{7,1},{8,10},{9,11},{10,... | collective-permute-start | bytes 12296 | tf_op jit(solution)/shard_map/ppermute | solution.py:394
  63.2 4.9 %collective-permute-start.17 = (f32[8,128]{1,0:T(8,128)S(1)}, f32[8,128]{1,0:T(8,128)S(1)}, u32[]{:S(2)}, u32[]{:S(2)}) collective-permute-start(f32[8,128]{1,0:T(8,128)S(1)} %add_add_fusion.1), channel_id=1, source_target_pairs={{0,6},{1,7},{2,0},{3,1},{4,2},{5,3},{6,4},{7,5},{8,14},{9,15},{10,... | collective-permute-start | bytes 12296 | tf_op jit(solution)/shard_map/ppermute | solution.py:394
  66.5 4.5 %collective-permute-start.15 = (f32[8,128]{1,0:T(8,128)S(1)}, f32[8,128]{1,0:T(8,128)S(1)}, u32[]{:S(2)}, u32[]{:S(2)}) collective-permute-start(f32[8,128]{1,0:T(8,128)S(1)} %add_add_fusion.1), channel_id=1, source_target_pairs={{0,4},{1,5},{2,6},{3,7},{4,0},{5,1},{6,2},{7,3},{8,12},{9,13},{10,... | collective-permute-start | bytes 12296 | tf_op jit(solution)/shard_map/ppermute | solution.py:394
  67.0 5.7 %collective-permute-start.14 = (f32[3,8,2048]{2,1,0:T(8,128)S(1)}, f32[3,8,2048]{2,1,0:T(8,128)S(1)}, u32[]{:S(2)}, u32[]{:S(2)}) collective-permute-start(f32[3,8,2048]{2,1,0:T(8,128)S(1)} %get-tuple-element.47), channel_id=1, source_target_pairs={{0,1},{1,0},{2,3},{3,2},{4,5},{5,4},{6,7},{7,6},{8,9},{9,8},{10,11... | collective-permute-start | bytes 589832 | tf_op jit(solution)/shard_map/ppermute | solution.py:389
  71.0 3.6 %collective-permute-start.18 = (f32[8,128]{1,0:T(8,128)S(1)}, f32[8,128]{1,0:T(8,128)S(1)}, u32[]{:S(2)}, u32[]{:S(2)}) collective-permute-start(f32[8,128]{1,0:T(8,128)S(1)} %add_add_fusion), channel_id=1, source_target_pairs={{0,1},{1,0},{2,3},{3,2},{4,5},{5,4},{6,7},{7,6},{8,9},{9,8},{10,11... | collective-permute-start | bytes 12296 | tf_op jit(solution)/shard_map/ppermute | solution.py:401

commit v11 on v10

--- a/solution.py
+++ b/solution.py
@@ -390,18 +390,17 @@
         misfits.append(misfit)
     total = sum(misfits[1:], misfits[0])
     (total,) = after((total,), [b[1] for b in blocks[:-1]])
+    state = gather(blocks, pieces, ncol, half)
     if strips == 8:
         turn = [lax.ppermute(total, "strip", moved(step, step)) for step in (2, 4, 6)]
+        *turn, total = after((*turn, total), state)
         total = (total + turn[1]) + (turn[0] + turn[2])
     else:
         step = 2
         while step < strips:
             total = total + lax.ppermute(total, "strip", [(i, i ^ step) for i in range(strips)])
             step *= 2
-    theirs = lax.ppermute(total, "strip", swap)
-    state = gather(blocks, pieces, ncol, half)
-    theirs, total = after((theirs, total), state)
-    total = total + theirs
+    total = total + lax.ppermute(total, "strip", swap)
     log_weights = (-0.5 / (total_rows * obs_cols.shape[1])) * total[0, :members]
     return (state, log_weights)
 

time: 75.3 us -> 75 us (level)
  waiting for transfers between devices: 15.7 us -> 14.7 us
    ppermute x3, waiting for transfers between devices: 3.09 us -> 1.47 us  [local(): lax.ppermute(total, 'strip', moved(step, step))]
    ppermute x3, starting transfers between devices: 3.61 us -> 4.75 us  [local(): blocks.append((keep, lax.ppermute(send, 'strip', swap)))]
    ppermute x3, starting transfers between devices: 4.96 us -> 3.88 us  [local(): lax.ppermute(total, 'strip', moved(step, step))]
    ppermute x1, waiting for transfers between devices: 0.69 us -> 1.62 us  [local(): total = total + lax.ppermute(total, 'strip', swap)]
where the time goes in v11:
time: 75 us; the launch traced here: 74.8 us
  starting transfers between devices  32.3 us (43%)
  Pallas kernels  24.2 us (32%)
  waiting for transfers between devices  14.7 us (20%)
  local copies, waits for them, and re-layouts  2.24 us (3%)
  between operations  0.75 us (1%)
    pallas_call x3, Pallas kernels, forecast(): pl.pallas_call(functools.partial(forecast_kernel, worked=worked, kept=kep...  21 us
    ppermute x2, starting transfers between devices, local(): direct.append(lax.ppermute(keeping, 'strip', straight))  9.38 us
    ppermute x3, starting transfers between devices, local(): got.append([lax.ppermute(g, 'strip', swap) for g in giving])  4.76 us
    ppermute x3, starting transfers between devices, local(): blocks.append((keep, lax.ppermute(send, 'strip', swap)))  4.75 us
    ppermute x3, waiting for transfers between devices, local(): got.append([lax.ppermute(g, 'strip', swap) for g in giving])  4.27 us
    ppermute x3, starting transfers between devices, local(): lax.ppermute(total, 'strip', moved(step, step))  3.88 us
    ppermute x3, waiting for transfers between devices, local(): passed.append([lax.ppermute(g, 'strip', onward) for g in got[k]])  3.73 us
    ppermute x1, waiting for transfers between devices, local(): obs_got = lax.ppermute(obs_own, 'strip', swap)  3.61 us
  transfers between devices with their start and end apart: 19, of which 8 were waited for; matrix products, arithmetic and copies ran while one was open for 0% of the time, Pallas kernels for 31%

profile of v11, /device:TPU:0, one launch (start us, length us, event | category | flops | bytes accessed | tf_op | source)
XLA Modules:
  0.0 74.8 jit_solution(10212603089737182983)
XLA Ops:
  0.6 0.5 collective-permute-start
  1.1 1.4 %copy-done = f32[4,3,8,4096]{3,2,1,0:T(8,128)S(1)} copy-done((f32[4,3,8,4096]{3,2,1,0:T(8,128)S(1)}, f32[4,3,8,4096]{3,2,1,0:T(8,128)}, u32[]{:S(2)}) %copy-start) | copy-done | bytes 1572888
  2.6 0.7 copy-done.2
  3.2 1.2 %shard_map.68.index = s32[4]{0:T(128)S(1)} custom-call(s32[8]{0:T(128)S(1)} %copy-done.2, f32[4,3,8,4096]{3,2,1,0:T(8,128)S(1)} %copy-done), custom_call_target="tpu_custom_call" | custom-call | tf_op jit(solution)/shard_map/pallas_call | solution.py:66
  4.5 0.2 copy-done.1
  4.6 0.8 %shard_map.69 = (f32[3,8,4096]{2,1,0:T(8,128)S(1)}, f32[3,8,4096]{2,1,0:T(8,128)S(1)}, f32[3,8,4096]{2,1,0:T(8,128)S(1)}, f32[3,8,2304]{2,1,0:T(8,128)S(1)}, f32...) custom-call(s32[4]{0:T(128)S(1)} %shard_map.68.index, f32[4,3,8,4096]{3,2,1,0:T(8,128)S(1)} %copy-done.1, ...), custom_call_target="tpu_custom_call" | custom-call | tf_op jit(solution)/shard_map/pallas_call | solution.py:130
  5.4 2.7 %collective-permute-start.1 = (f32[3,8,4096]{2,1,0:T(8,128)S(1)}, f32[3,8,4096]{2,1,0:T(8,128)S(1)}, u32[]{:S(2)}, u32[]{:S(2)}) collective-permute-start(f32[3,8,4096]{2,1,0:T(8,128)S(1)} %get-tuple-element.32), channel_id=1, source_target_pairs={{0,1},{1,0},{2,3},{3,2},{4,5},{5,4},{6,7},{7,6},{8,9},{9,8},{10,11... | collective-permute-start | bytes 1179656 | tf_op jit(solution)/shard_map/ppermute | solution.py:365
  8.1 1.6 %collective-permute-start.2 = (f32[6,8,512]{2,1,0:T(8,128)S(1)}, f32[6,8,512]{2,1,0:T(8,128)S(1)}, u32[]{:S(2)}, u32[]{:S(2)}) collective-permute-start(f32[6,8,512]{2,1,0:T(8,128)S(1)} %get-tuple-element.33), channel_id=1, source_target_pairs={{0,2},{1,7},{2,4},{3,1},{4,6},{5,3},{6,0},{7,5},{8,10},{9,15},{10,... | collective-permute-start | bytes 294920 | tf_op jit(solution)/shard_map/ppermute | solution.py:353
  9.8 5.8 %collective-permute-start.6 = (f32[3,8,4096]{2,1,0:T(8,128)S(1)}, f32[3,8,4096]{2,1,0:T(8,128)S(1)}, u32[]{:S(2)}, u32[]{:S(2)}) collective-permute-start(f32[3,8,4096]{2,1,0:T(8,128)S(1)} %get-tuple-element.37.refs_0_), channel_id=1, source_target_pairs={{0,6},{1,3},{2,0},{3,5},{4,2},{5,7},{6,4},{7,1},{8,14},{9,11},{10,... | collective-permute-start | bytes 1179656 | tf_op jit(solution)/shard_map/ppermute | solution.py:368
  15.6 4.3 %collective-permute-done.1.refs_2_ = f32[3,8,4096]{2,1,0:T(8,128)S(1)} collective-permute-done((f32[3,8,4096]{2,1,0:T(8,128)S(1)}, f32[3,8,4096]{2,1,0:T(8,128)S(1)}, u32[]{:S(2)}, u32[]{:S(2)}) %collective-permute-start.1) | collective-permute-done | bytes 393248 | tf_op jit(solution)/shard_map/ppermute | solution.py:365
  19.9 1.7 %collective-permute-start.4 = (f32[3,8,2304]{2,1,0:T(8,128)S(1)}, f32[3,8,2304]{2,1,0:T(8,128)S(1)}, u32[]{:S(2)}, u32[]{:S(2)}) collective-permute-start(f32[3,8,2304]{2,1,0:T(8,128)S(1)} %get-tuple-element.35), channel_id=1, source_target_pairs={{0,1},{1,0},{2,3},{3,2},{4,5},{5,4},{6,7},{7,6},{8,9},{9,8},{10,11... | collective-permute-start | bytes 663560 | tf_op jit(solution)/shard_map/ppermute | solution.py:365
  21.6 0.3 collective-permute-start.5
  21.9 1.8 %collective-permute-start.7 = (f32[3,8,4096]{2,1,0:T(8,128)S(1)}, f32[3,8,4096]{2,1,0:T(8,128)S(1)}, u32[]{:S(2)}, u32[]{:S(2)}) collective-permute-start(f32[3,8,4096]{2,1,0:T(8,128)S(1)} %collective-permute-done.1.refs_2_), channel_id=1, source_target_pairs={{0,2},{1,7},{2,4},{3,1},{4,6},{5,3},{6,0},{7,5},{8,10},{9,15},{10,... | collective-permute-start | bytes 1179656 | tf_op jit(solution)/shard_map/ppermute | solution.py:369
  23.7 3.6 %collective-permute-start.8 = (f32[3,8,128]{2,1,0:T(8,128)S(1)}, f32[3,8,128]{2,1,0:T(8,128)S(1)}, u32[]{:S(2)}, u32[]{:S(2)}) collective-permute-start(f32[3,8,128]{2,1,0:T(8,128)S(1)} %pad_maximum_fusion.refs_6_.refs_8_), channel_id=1, source_target_pairs={{0,1},{1,0},{2,3},{3,2},{4,5},{5,4},{6,7},{7,6},{8,9},{9,8},{10,11... | collective-permute-start | bytes 36872 | tf_op jit(solution)/shard_map/ppermute | solution.py:356
  27.3 3.6 %collective-permute-done.8.refs_7_.refs_9_ = f32[3,8,128]{2,1,0:T(8,128)S(1)} collective-permute-done((f32[3,8,128]{2,1,0:T(8,128)S(1)}, f32[3,8,128]{2,1,0:T(8,128)S(1)}, u32[]{:S(2)}, u32[]{:S(2)}) %collective-permute-start.8) | collective-permute-done | bytes 12320 | tf_op jit(solution)/shard_map/ppermute | solution.py:356
  30.9 3.6 %collective-permute-start.10 = (f32[3,8,4096]{2,1,0:T(8,128)S(1)}, f32[3,8,4096]{2,1,0:T(8,128)S(1)}, u32[]{:S(2)}, u32[]{:S(2)}) collective-permute-start(f32[3,8,4096]{2,1,0:T(8,128)S(1)} %get-tuple-element.47.refs_0_), channel_id=1, source_target_pairs={{0,6},{1,3},{2,0},{3,5},{4,2},{5,7},{6,4},{7,1},{8,14},{9,11},{10,... | collective-permute-start | bytes 1179656 | tf_op jit(solution)/shard_map/ppermute | solution.py:368
  34.5 1.0 %collective-permute-done.7.refs_3_ = f32[3,8,4096]{2,1,0:T(8,128)S(1)} collective-permute-done((f32[3,8,4096]{2,1,0:T(8,128)S(1)}, f32[3,8,4096]{2,1,0:T(8,128)S(1)}, u32[]{:S(2)}, u32[]{:S(2)}) %collective-permute-start.7) | collective-permute-done | bytes 393248 | tf_op jit(solution)/shard_map/ppermute | solution.py:369
  35.5 8.8 %shard_map.70 = (f32[3,8,4096]{2,1,0:T(8,128)S(1)}, f32[3,8,4096]{2,1,0:T(8,128)S(1)}, f32[8,128]{1,0:T(8,128)S(1)}) custom-call(f32[3,8,4096]{2,1,0:T(8,128)S(1)} %get-tuple-element.37.refs_0_, f32[3,8,4096]{2,1,0:T(8,128)S(1)} %collective-permute-done.6.refs_1_, f32[3,8,4096]{2,1,0:T(8,128)S(1)} %collective-permute-done.1.refs_2_, ...), custom_call_target="tpu_custom_call" | custom-call | bytes 480000 | tf_op jit(solution)/shard_map/pallas_call | solution.py:282
  44.4 2.6 %collective-permute-start.9 = (f32[3,8,4096]{2,1,0:T(8,128)S(1)}, f32[3,8,4096]{2,1,0:T(8,128)S(1)}, u32[]{:S(2)}, u32[]{:S(2)}) collective-permute-start(f32[3,8,4096]{2,1,0:T(8,128)S(1)} %get-tuple-element.39), channel_id=1, source_target_pairs={{0,1},{1,0},{2,3},{3,2},{4,5},{5,4},{6,7},{7,6},{8,9},{9,8},{10,11... | collective-permute-start | bytes 1179656 | tf_op jit(solution)/shard_map/ppermute | solution.py:389
  47.0 2.7 %collective-permute-done.11.refs_3_.refs_4_ = f32[3,8,2304]{2,1,0:T(8,128)S(1)} collective-permute-done((f32[3,8,2304]{2,1,0:T(8,128)S(1)}, f32[3,8,2304]{2,1,0:T(8,128)S(1)}, u32[]{:S(2)}, u32[]{:S(2)}) %collective-permute-start.11) | collective-permute-done | bytes 221216 | tf_op jit(solution)/shard_map/ppermute | solution.py:369
  49.8 6.1 %shard_map.71 = (f32[3,8,2048]{2,1,0:T(8,128)S(1)}, f32[3,8,2048]{2,1,0:T(8,128)S(1)}, f32[8,128]{1,0:T(8,128)S(1)}) custom-call(f32[3,8,4096]{2,1,0:T(8,128)S(1)} %get-tuple-element.47.refs_0_, f32[3,8,4096]{2,1,0:T(8,128)S(1)} %collective-permute-done.10.refs_1_, f32[3,8,2304]{2,1,0:T(8,128)S(1)} %collective-permute-done.4.refs_2_, ...), custom_call_target="tpu_custom_call" | custom-call | bytes 270000 | tf_op jit(solution)/shard_map/pallas_call | solution.py:282
  55.9 6.1 %shard_map.72 = (f32[3,8,2048]{2,1,0:T(8,128)S(1)}, f32[3,8,2048]{2,1,0:T(8,128)S(1)}, f32[8,128]{1,0:T(8,128)S(1)}) custom-call(f32[3,8,4096]{2,1,0:T(8,128)S(1)} %get-tuple-element.47.refs_0_, f32[3,8,4096]{2,1,0:T(8,128)S(1)} %collective-permute-done.10.refs_1_, f32[3,8,2304]{2,1,0:T(8,128)S(1)} %collective-permute-done.4.refs_2_, ...), custom_call_target="tpu_custom_call" | custom-call | bytes 270000 | tf_op jit(solution)/shard_map/pallas_call | solution.py:282
  62.0 2.1 %collective-permute-start.14 = (f32[3,8,2048]{2,1,0:T(8,128)S(1)}, f32[3,8,2048]{2,1,0:T(8,128)S(1)}, u32[]{:S(2)}, u32[]{:S(2)}) collective-permute-start(f32[3,8,2048]{2,1,0:T(8,128)S(1)} %get-tuple-element.49), channel_id=1, source_target_pairs={{0,1},{1,0},{2,3},{3,2},{4,5},{5,4},{6,7},{7,6},{8,9},{9,8},{10,11... | collective-permute-start | bytes 589832 | tf_op jit(solution)/shard_map/ppermute | solution.py:389
  64.1 1.1 %collective-permute-start.15 = (f32[8,128]{1,0:T(8,128)S(1)}, f32[8,128]{1,0:T(8,128)S(1)}, u32[]{:S(2)}, u32[]{:S(2)}) collective-permute-start(f32[8,128]{1,0:T(8,128)S(1)} %add_add_fusion.1), channel_id=1, source_target_pairs={{0,2},{1,3},{2,4},{3,5},{4,6},{5,7},{6,0},{7,1},{8,10},{9,11},{10,... | collective-permute-start | bytes 12296 | tf_op jit(solution)/shard_map/ppermute | solution.py:395
  65.2 1.9 %collective-permute-start.16 = (f32[8,128]{1,0:T(8,128)S(1)}, f32[8,128]{1,0:T(8,128)S(1)}, u32[]{:S(2)}, u32[]{:S(2)}) collective-permute-start(f32[8,128]{1,0:T(8,128)S(1)} %add_add_fusion.1), channel_id=1, source_target_pairs={{0,4},{1,5},{2,6},{3,7},{4,0},{5,1},{6,2},{7,3},{8,12},{9,13},{10,... | collective-permute-start | bytes 12296 | tf_op jit(solution)/shard_map/ppermute | solution.py:395
  67.1 0.9 %collective-permute-start.17 = (f32[8,128]{1,0:T(8,128)S(1)}, f32[8,128]{1,0:T(8,128)S(1)}, u32[]{:S(2)}, u32[]{:S(2)}) collective-permute-start(f32[8,128]{1,0:T(8,128)S(1)} %add_add_fusion.1), channel_id=1, source_target_pairs={{0,6},{1,7},{2,0},{3,1},{4,2},{5,3},{6,4},{7,5},{8,14},{9,15},{10,... | collective-permute-start | bytes 12296 | tf_op jit(solution)/shard_map/ppermute | solution.py:395
  68.0 1.3 %shard_map.73 = f32[4,3,8,4096]{3,2,1,0:T(8,128)} custom-call(f32[3,8,4096]{2,1,0:T(8,128)S(1)} %get-tuple-element.38.refs_0_, f32[3,8,4096]{2,1,0:T(8,128)S(1)} %collective-permute-done.9.refs_1_, f32[3,8,2048]{2,1,0:T(8,128)S(1)} %get-tuple-element.44.refs_2_, f32[3,8,2048]{2,1,0:T(8,128)S(1)} %collective-permute-done.12.refs_3_, ...), custom_call_target="tpu_custom_call" | custom-call | bytes 300000 | tf_op jit(solution)/shard_map/pallas_call | solution.py:315
  69.2 0.3 collective-permute-done.15
  69.7 1.0 %collective-permute-done.17 = f32[8,128]{1,0:T(8,128)S(1)} collective-permute-done((f32[8,128]{1,0:T(8,128)S(1)}, f32[8,128]{1,0:T(8,128)S(1)}, u32[]{:S(2)}, u32[]{:S(2)}) %collective-permute-start.17) | collective-permute-done | bytes 4128 | tf_op jit(solution)/shard_map/ppermute | solution.py:395
  70.7 2.0 %collective-permute-start.18 = (f32[8,128]{1,0:T(8,128)S(1)}, f32[8,128]{1,0:T(8,128)S(1)}, u32[]{:S(2)}, u32[]{:S(2)}) collective-permute-start(f32[8,128]{1,0:T(8,128)S(1)} %add_add_fusion), channel_id=1, source_target_pairs={{0,1},{1,0},{2,3},{3,2},{4,5},{5,4},{6,7},{7,6},{8,9},{9,8},{10,11... | collective-permute-start | bytes 12296 | tf_op jit(solution)/shard_map/ppermute | solution.py:403
  72.7 1.6 %collective-permute-done.18 = f32[8,128]{1,0:T(8,128)S(1)} collective-permute-done((f32[8,128]{1,0:T(8,128)S(1)}, f32[8,128]{1,0:T(8,128)S(1)}, u32[]{:S(2)}, u32[]{:S(2)}) %collective-permute-start.18) | collective-permute-done | bytes 4128 | tf_op jit(solution)/shard_map/ppermute | solution.py:403
  74.3 0.5 multiply_bitcast_fusion.1
  (32 shorter events, 0.4 us)
Async XLA Ops:
  0.6 3.8 %collective-permute-start = (f32[4,3,8,4096]{3,2,1,0:T(8,128)}, f32[4,3,8,4096]{3,2,1,0:T(8,128)S(1)}, u32[]{:S(2)}, u32[]{:S(2)}) collective-permute-start(f32[4,3,8,4096]{3,2,1,0:T(8,128)} %own.1), channel_id=1, source_target_pairs={{0,8},{8,0},{1,9},{9,1},{2,10},{10,2},{3,11},{11,3},{4,12},{12,4},... | collective-permute-start | bytes 4718600 | tf_op jit(solution)/shard_map/ppermute | solution.py:341
  1.1 1.4 %copy-start = (f32[4,3,8,4096]{3,2,1,0:T(8,128)S(1)}, f32[4,3,8,4096]{3,2,1,0:T(8,128)}, u32[]{:S(2)}) copy-start(f32[4,3,8,4096]{3,2,1,0:T(8,128)} %own.1) | copy-start | bytes 4718596
  2.6 0.7 copy-start.2
  3.2 1.4 %copy-start.1 = (f32[4,3,8,4096]{3,2,1,0:T(8,128)S(1)}, f32[4,3,8,4096]{3,2,1,0:T(8,128)}, u32[]{:S(2)}) copy-start(f32[4,3,8,4096]{3,2,1,0:T(8,128)} %own.1) | copy-start | bytes 4718596
  4.4 5.3 %copy-start.3 = (f32[8,128]{1,0:T(8,128)S(1)}, f32[8,128]{1,0:T(8,128)}, u32[]{:S(2)}) copy-start(f32[8,128]{1,0:T(8,128)} %param.9) | copy-start | bytes 12292
  4.4 19.3 %copy-start.4 = (s32[8,128]{1,0:T(8,128)S(1)}, s32[8,128]{1,0:T(8,128)}, u32[]{:S(2)}) copy-start(s32[8,128]{1,0:T(8,128)} %param.8) | copy-start | bytes 12292
  4.4 19.3 %copy-start.5 = (f32[8,128]{1,0:T(8,128)S(1)}, f32[8,128]{1,0:T(8,128)}, u32[]{:S(2)}) copy-start(f32[8,128]{1,0:T(8,128)} %param.7) | copy-start | bytes 12292
  5.4 14.5 %collective-permute-start.1 = (f32[3,8,4096]{2,1,0:T(8,128)S(1)}, f32[3,8,4096]{2,1,0:T(8,128)S(1)}, u32[]{:S(2)}, u32[]{:S(2)}) collective-permute-start(f32[3,8,4096]{2,1,0:T(8,128)S(1)} %get-tuple-element.32), channel_id=1, source_target_pairs={{0,1},{1,0},{2,3},{3,2},{4,5},{5,4},{6,7},{7,6},{8,9},{9,8},{10,11... | collective-permute-start | bytes 1179656 | tf_op jit(solution)/shard_map/ppermute | solution.py:365
  8.1 7.5 %collective-permute-start.2 = (f32[6,8,512]{2,1,0:T(8,128)S(1)}, f32[6,8,512]{2,1,0:T(8,128)S(1)}, u32[]{:S(2)}, u32[]{:S(2)}) collective-permute-start(f32[6,8,512]{2,1,0:T(8,128)S(1)} %get-tuple-element.33), channel_id=1, source_target_pairs={{0,2},{1,7},{2,4},{3,1},{4,6},{5,3},{6,0},{7,5},{8,10},{9,15},{10,... | collective-permute-start | bytes 294920 | tf_op jit(solution)/shard_map/ppermute | solution.py:353
  9.7 5.9 %collective-permute-start.3 = (f32[6,8,512]{2,1,0:T(8,128)S(1)}, f32[6,8,512]{2,1,0:T(8,128)S(1)}, u32[]{:S(2)}, u32[]{:S(2)}) collective-permute-start(f32[6,8,512]{2,1,0:T(8,128)S(1)} %get-tuple-element.34), channel_id=1, source_target_pairs={{0,3},{1,6},{2,5},{3,0},{4,7},{5,2},{6,1},{7,4},{8,11},{9,14},{10,... | collective-permute-start | bytes 294920 | tf_op jit(solution)/shard_map/ppermute | solution.py:354
  9.8 24.7 %collective-permute-start.6 = (f32[3,8,4096]{2,1,0:T(8,128)S(1)}, f32[3,8,4096]{2,1,0:T(8,128)S(1)}, u32[]{:S(2)}, u32[]{:S(2)}) collective-permute-start(f32[3,8,4096]{2,1,0:T(8,128)S(1)} %get-tuple-element.37.refs_0_), channel_id=1, source_target_pairs={{0,6},{1,3},{2,0},{3,5},{4,2},{5,7},{6,4},{7,1},{8,14},{9,11},{10,... | collective-permute-start | bytes 1179656 | tf_op jit(solution)/shard_map/ppermute | solution.py:368
  19.9 11.1 %collective-permute-start.4 = (f32[3,8,2304]{2,1,0:T(8,128)S(1)}, f32[3,8,2304]{2,1,0:T(8,128)S(1)}, u32[]{:S(2)}, u32[]{:S(2)}) collective-permute-start(f32[3,8,2304]{2,1,0:T(8,128)S(1)} %get-tuple-element.35), channel_id=1, source_target_pairs={{0,1},{1,0},{2,3},{3,2},{4,5},{5,4},{6,7},{7,6},{8,9},{9,8},{10,11... | collective-permute-start | bytes 663560 | tf_op jit(solution)/shard_map/ppermute | solution.py:365
  21.6 9.3 %collective-permute-start.5 = (f32[3,8,1792]{2,1,0:T(8,128)S(1)}, f32[3,8,1792]{2,1,0:T(8,128)S(1)}, u32[]{:S(2)}, u32[]{:S(2)}) collective-permute-start(f32[3,8,1792]{2,1,0:T(8,128)S(1)} %get-tuple-element.36), channel_id=1, source_target_pairs={{0,1},{1,0},{2,3},{3,2},{4,5},{5,4},{6,7},{7,6},{8,9},{9,8},{10,11... | collective-permute-start | bytes 516104 | tf_op jit(solution)/shard_map/ppermute | solution.py:365
  21.9 13.6 %collective-permute-start.7 = (f32[3,8,4096]{2,1,0:T(8,128)S(1)}, f32[3,8,4096]{2,1,0:T(8,128)S(1)}, u32[]{:S(2)}, u32[]{:S(2)}) collective-permute-start(f32[3,8,4096]{2,1,0:T(8,128)S(1)} %collective-permute-done.1.refs_2_), channel_id=1, source_target_pairs={{0,2},{1,7},{2,4},{3,1},{4,6},{5,3},{6,0},{7,5},{8,10},{9,15},{10,... | collective-permute-start | bytes 1179656 | tf_op jit(solution)/shard_map/ppermute | solution.py:369
  23.7 7.2 %collective-permute-start.8 = (f32[3,8,128]{2,1,0:T(8,128)S(1)}, f32[3,8,128]{2,1,0:T(8,128)S(1)}, u32[]{:S(2)}, u32[]{:S(2)}) collective-permute-start(f32[3,8,128]{2,1,0:T(8,128)S(1)} %pad_maximum_fusion.refs_6_.refs_8_), channel_id=1, source_target_pairs={{0,1},{1,0},{2,3},{3,2},{4,5},{5,4},{6,7},{7,6},{8,9},{9,8},{10,11... | collective-permute-start | bytes 36872 | tf_op jit(solution)/shard_map/ppermute | solution.py:356
  30.9 18.8 %collective-permute-start.10 = (f32[3,8,4096]{2,1,0:T(8,128)S(1)}, f32[3,8,4096]{2,1,0:T(8,128)S(1)}, u32[]{:S(2)}, u32[]{:S(2)}) collective-permute-start(f32[3,8,4096]{2,1,0:T(8,128)S(1)} %get-tuple-element.47.refs_0_), channel_id=1, source_target_pairs={{0,6},{1,3},{2,0},{3,5},{4,2},{5,7},{6,4},{7,1},{8,14},{9,11},{10,... | collective-permute-start | bytes 1179656 | tf_op jit(solution)/shard_map/ppermute | solution.py:368
  34.5 15.2 %collective-permute-start.11 = (f32[3,8,2304]{2,1,0:T(8,128)S(1)}, f32[3,8,2304]{2,1,0:T(8,128)S(1)}, u32[]{:S(2)}, u32[]{:S(2)}) collective-permute-start(f32[3,8,2304]{2,1,0:T(8,128)S(1)} %collective-permute-done.4.refs_2_), channel_id=1, source_target_pairs={{0,2},{1,7},{2,4},{3,1},{4,6},{5,3},{6,0},{7,5},{8,10},{9,15},{10,... | collective-permute-start | bytes 663560 | tf_op jit(solution)/shard_map/ppermute | solution.py:369
  34.5 21.4 %collective-permute-start.13 = (f32[3,8,1792]{2,1,0:T(8,128)S(1)}, f32[3,8,1792]{2,1,0:T(8,128)S(1)}, u32[]{:S(2)}, u32[]{:S(2)}) collective-permute-start(f32[3,8,1792]{2,1,0:T(8,128)S(1)} %collective-permute-done.5.refs_3_), channel_id=1, source_target_pairs={{0,2},{1,7},{2,4},{3,1},{4,6},{5,3},{6,0},{7,5},{8,10},{9,15},{10,... | collective-permute-start | bytes 516104 | tf_op jit(solution)/shard_map/ppermute | solution.py:369
  44.4 19.7 %collective-permute-start.9 = (f32[3,8,4096]{2,1,0:T(8,128)S(1)}, f32[3,8,4096]{2,1,0:T(8,128)S(1)}, u32[]{:S(2)}, u32[]{:S(2)}) collective-permute-start(f32[3,8,4096]{2,1,0:T(8,128)S(1)} %get-tuple-element.39), channel_id=1, source_target_pairs={{0,1},{1,0},{2,3},{3,2},{4,5},{5,4},{6,7},{7,6},{8,9},{9,8},{10,11... | collective-permute-start | bytes 1179656 | tf_op jit(solution)/shard_map/ppermute | solution.py:389
  55.8 8.2 %collective-permute-start.12 = (f32[3,8,2048]{2,1,0:T(8,128)S(1)}, f32[3,8,2048]{2,1,0:T(8,128)S(1)}, u32[]{:S(2)}, u32[]{:S(2)}) collective-permute-start(f32[3,8,2048]{2,1,0:T(8,128)S(1)} %get-tuple-element.45), channel_id=1, source_target_pairs={{0,1},{1,0},{2,3},{3,2},{4,5},{5,4},{6,7},{7,6},{8,9},{9,8},{10,11... | collective-permute-start | bytes 589832 | tf_op jit(solution)/shard_map/ppermute | solution.py:389
  62.0 6.0 %collective-permute-start.14 = (f32[3,8,2048]{2,1,0:T(8,128)S(1)}, f32[3,8,2048]{2,1,0:T(8,128)S(1)}, u32[]{:S(2)}, u32[]{:S(2)}) collective-permute-start(f32[3,8,2048]{2,1,0:T(8,128)S(1)} %get-tuple-element.49), channel_id=1, source_target_pairs={{0,1},{1,0},{2,3},{3,2},{4,5},{5,4},{6,7},{7,6},{8,9},{9,8},{10,11... | collective-permute-start | bytes 589832 | tf_op jit(solution)/shard_map/ppermute | solution.py:389
  64.1 5.5 %collective-permute-start.15 = (f32[8,128]{1,0:T(8,128)S(1)}, f32[8,128]{1,0:T(8,128)S(1)}, u32[]{:S(2)}, u32[]{:S(2)}) collective-permute-start(f32[8,128]{1,0:T(8,128)S(1)} %add_add_fusion.1), channel_id=1, source_target_pairs={{0,2},{1,3},{2,4},{3,5},{4,6},{5,7},{6,0},{7,1},{8,10},{9,11},{10,... | collective-permute-start | bytes 12296 | tf_op jit(solution)/shard_map/ppermute | solution.py:395
  65.2 4.5 %collective-permute-start.16 = (f32[8,128]{1,0:T(8,128)S(1)}, f32[8,128]{1,0:T(8,128)S(1)}, u32[]{:S(2)}, u32[]{:S(2)}) collective-permute-start(f32[8,128]{1,0:T(8,128)S(1)} %add_add_fusion.1), channel_id=1, source_target_pairs={{0,4},{1,5},{2,6},{3,7},{4,0},{5,1},{6,2},{7,3},{8,12},{9,13},{10,... | collective-permute-start | bytes 12296 | tf_op jit(solution)/shard_map/ppermute | solution.py:395
  67.1 3.6 %collective-permute-start.17 = (f32[8,128]{1,0:T(8,128)S(1)}, f32[8,128]{1,0:T(8,128)S(1)}, u32[]{:S(2)}, u32[]{:S(2)}) collective-permute-start(f32[8,128]{1,0:T(8,128)S(1)} %add_add_fusion.1), channel_id=1, source_target_pairs={{0,6},{1,7},{2,0},{3,1},{4,2},{5,3},{6,4},{7,5},{8,14},{9,15},{10,... | collective-permute-start | bytes 12296 | tf_op jit(solution)/shard_map/ppermute | solution.py:395
  70.7 3.6 %collective-permute-start.18 = (f32[8,128]{1,0:T(8,128)S(1)}, f32[8,128]{1,0:T(8,128)S(1)}, u32[]{:S(2)}, u32[]{:S(2)}) collective-permute-start(f32[8,128]{1,0:T(8,128)S(1)} %add_add_fusion), channel_id=1, source_target_pairs={{0,1},{1,0},{2,3},{3,2},{4,5},{5,4},{6,7},{7,6},{8,9},{9,8},{10,11... | collective-permute-start | bytes 12296 | tf_op jit(solution)/shard_map/ppermute | solution.py:403

commit v12 on v11

--- a/solution.py
+++ b/solution.py
@@ -31,7 +31,7 @@
     every = list(range(ncol))
     if slot < slots - 1:
         return ((every, every, every),)
-    cut = ncol // 2 + 2
+    cut = ncol * 11 // 16
     return (
         (every[:cut], every[:cut], every[1 : cut - 1]),
         (every[cut:], every[cut - 2 :] + [0, 1], every[cut - 1 :] + [0]),

time: 75 us -> 75.1 us (level)
  waiting for transfers between devices: 14.7 us -> 19.6 us
  starting transfers between devices: 32.3 us -> 27.5 us
    ppermute x1, starting transfers between devices: 3.6 us -> 0.09 us  [local(): obs_got = lax.ppermute(obs_own, 'strip', swap)]
    ppermute x3, waiting for transfers between devices: 3.73 us -> 6.18 us  [local(): passed.append([lax.ppermute(g, 'strip', onward) for g in got[k]])]
    ppermute x3, starting transfers between devices: 4.76 us -> 7.02 us  [local(): got.append([lax.ppermute(g, 'strip', swap) for g in giving])]
    ppermute x3, starting transfers between devices: 4.75 us -> 2.95 us  [local(): blocks.append((keep, lax.ppermute(send, 'strip', swap)))]
    ppermute x1, waiting for transfers between devices: 1.62 us -> 3.16 us  [local(): total = total + lax.ppermute(total, 'strip', swap)]
    ppermute x1, starting transfers between devices: 1.99 us -> 0.45 us  [local(): total = total + lax.ppermute(total, 'strip', swap)]
    ppermute x1, waiting for transfers between devices: 3.61 us -> 5.1 us  [local(): obs_got = lax.ppermute(obs_own, 'strip', swap)]
where the time goes in v12:
time: 75.1 us; the launch traced here: 74.9 us
  starting transfers between devices  27.5 us (37%)
  Pallas kernels  24.2 us (32%)
  waiting for transfers between devices  19.6 us (26%)
  local copies, waits for them, and re-layouts  2.24 us (3%)
    pallas_call x3, Pallas kernels, forecast(): pl.pallas_call(functools.partial(forecast_kernel, worked=worked, kept=kep...  21 us
    ppermute x2, starting transfers between devices, local(): direct.append(lax.ppermute(keeping, 'strip', straight))  9.38 us
    ppermute x3, starting transfers between devices, local(): got.append([lax.ppermute(g, 'strip', swap) for g in giving])  7.02 us
    ppermute x3, waiting for transfers between devices, local(): passed.append([lax.ppermute(g, 'strip', onward) for g in got[k]])  6.18 us
    ppermute x1, waiting for transfers between devices, local(): obs_got = lax.ppermute(obs_own, 'strip', swap)  5.1 us
    ppermute x3, waiting for transfers between devices, local(): got.append([lax.ppermute(g, 'strip', swap) for g in giving])  4.27 us
    ppermute x3, starting transfers between devices, local(): lax.ppermute(total, 'strip', moved(step, step))  3.88 us
    ppermute x1, waiting for transfers between devices, local(): total = total + lax.ppermute(total, 'strip', swap)  3.16 us
  transfers between devices with their start and end apart: 19, of which 8 were waited for; matrix products, arithmetic and copies ran while one was open for 0% of the time, Pallas kernels for 31%

profile of v12, /device:TPU:0, one launch (start us, length us, event | category | flops | bytes accessed | tf_op | source)
XLA Modules:
  0.0 74.9 jit_solution(10175314523100778418)
XLA Ops:
  0.6 0.5 collective-permute-start
  1.1 1.4 %copy-done = f32[4,3,8,4096]{3,2,1,0:T(8,128)S(1)} copy-done((f32[4,3,8,4096]{3,2,1,0:T(8,128)S(1)}, f32[4,3,8,4096]{3,2,1,0:T(8,128)}, u32[]{:S(2)}) %copy-start) | copy-done | bytes 1572888
  2.6 0.7 copy-done.2
  3.2 1.2 %shard_map.68.index = s32[4]{0:T(128)S(1)} custom-call(s32[8]{0:T(128)S(1)} %copy-done.2, f32[4,3,8,4096]{3,2,1,0:T(8,128)S(1)} %copy-done), custom_call_target="tpu_custom_call" | custom-call | tf_op jit(solution)/shard_map/pallas_call | solution.py:66
  4.5 0.2 copy-done.1
  4.6 0.8 %shard_map.69 = (f32[3,8,4096]{2,1,0:T(8,128)S(1)}, f32[3,8,4096]{2,1,0:T(8,128)S(1)}, f32[3,8,4096]{2,1,0:T(8,128)S(1)}, f32[3,8,2816]{2,1,0:T(8,128)S(1)}, f32...) custom-call(s32[4]{0:T(128)S(1)} %shard_map.68.index, f32[4,3,8,4096]{3,2,1,0:T(8,128)S(1)} %copy-done.1, ...), custom_call_target="tpu_custom_call" | custom-call | tf_op jit(solution)/shard_map/pallas_call | solution.py:130
  5.4 2.7 %collective-permute-start.1 = (f32[3,8,4096]{2,1,0:T(8,128)S(1)}, f32[3,8,4096]{2,1,0:T(8,128)S(1)}, u32[]{:S(2)}, u32[]{:S(2)}) collective-permute-start(f32[3,8,4096]{2,1,0:T(8,128)S(1)} %get-tuple-element.32), channel_id=1, source_target_pairs={{0,1},{1,0},{2,3},{3,2},{4,5},{5,4},{6,7},{7,6},{8,9},{9,8},{10,11... | collective-permute-start | bytes 1179656 | tf_op jit(solution)/shard_map/ppermute | solution.py:365
  8.1 1.6 %collective-permute-start.2 = (f32[6,8,512]{2,1,0:T(8,128)S(1)}, f32[6,8,512]{2,1,0:T(8,128)S(1)}, u32[]{:S(2)}, u32[]{:S(2)}) collective-permute-start(f32[6,8,512]{2,1,0:T(8,128)S(1)} %get-tuple-element.33), channel_id=1, source_target_pairs={{0,2},{1,7},{2,4},{3,1},{4,6},{5,3},{6,0},{7,5},{8,10},{9,15},{10,... | collective-permute-start | bytes 294920 | tf_op jit(solution)/shard_map/ppermute | solution.py:353
  9.8 5.8 %collective-permute-start.6 = (f32[3,8,4096]{2,1,0:T(8,128)S(1)}, f32[3,8,4096]{2,1,0:T(8,128)S(1)}, u32[]{:S(2)}, u32[]{:S(2)}) collective-permute-start(f32[3,8,4096]{2,1,0:T(8,128)S(1)} %get-tuple-element.37.refs_0_), channel_id=1, source_target_pairs={{0,6},{1,3},{2,0},{3,5},{4,2},{5,7},{6,4},{7,1},{8,14},{9,11},{10,... | collective-permute-start | bytes 1179656 | tf_op jit(solution)/shard_map/ppermute | solution.py:368
  15.6 4.3 %collective-permute-done.1.refs_2_ = f32[3,8,4096]{2,1,0:T(8,128)S(1)} collective-permute-done((f32[3,8,4096]{2,1,0:T(8,128)S(1)}, f32[3,8,4096]{2,1,0:T(8,128)S(1)}, u32[]{:S(2)}, u32[]{:S(2)}) %collective-permute-start.1) | collective-permute-done | bytes 393248 | tf_op jit(solution)/shard_map/ppermute | solution.py:365
  19.9 1.7 %collective-permute-start.4 = (f32[3,8,2816]{2,1,0:T(8,128)S(1)}, f32[3,8,2816]{2,1,0:T(8,128)S(1)}, u32[]{:S(2)}, u32[]{:S(2)}) collective-permute-start(f32[3,8,2816]{2,1,0:T(8,128)S(1)} %get-tuple-element.35), channel_id=1, source_target_pairs={{0,1},{1,0},{2,3},{3,2},{4,5},{5,4},{6,7},{7,6},{8,9},{9,8},{10,11... | collective-permute-start | bytes 811016 | tf_op jit(solution)/shard_map/ppermute | solution.py:365
  21.6 1.6 %collective-permute-start.7 = (f32[3,8,4096]{2,1,0:T(8,128)S(1)}, f32[3,8,4096]{2,1,0:T(8,128)S(1)}, u32[]{:S(2)}, u32[]{:S(2)}) collective-permute-start(f32[3,8,4096]{2,1,0:T(8,128)S(1)} %collective-permute-done.1.refs_2_), channel_id=1, source_target_pairs={{0,2},{1,7},{2,4},{3,1},{4,6},{5,3},{6,0},{7,5},{8,10},{9,15},{10,... | collective-permute-start | bytes 1179656 | tf_op jit(solution)/shard_map/ppermute | solution.py:369
  23.2 2.5 %collective-permute-start.5 = (f32[3,8,1280]{2,1,0:T(8,128)S(1)}, f32[3,8,1280]{2,1,0:T(8,128)S(1)}, u32[]{:S(2)}, u32[]{:S(2)}) collective-permute-start(f32[3,8,1280]{2,1,0:T(8,128)S(1)} %get-tuple-element.36), channel_id=1, source_target_pairs={{0,1},{1,0},{2,3},{3,2},{4,5},{5,4},{6,7},{7,6},{8,9},{9,8},{10,11... | collective-permute-start | bytes 368648 | tf_op jit(solution)/shard_map/ppermute | solution.py:365
  25.8 5.1 %collective-permute-done.8.refs_7_.refs_9_ = f32[3,8,128]{2,1,0:T(8,128)S(1)} collective-permute-done((f32[3,8,128]{2,1,0:T(8,128)S(1)}, f32[3,8,128]{2,1,0:T(8,128)S(1)}, u32[]{:S(2)}, u32[]{:S(2)}) %collective-permute-start.8) | collective-permute-done | bytes 12320 | tf_op jit(solution)/shard_map/ppermute | solution.py:356
  30.9 3.6 %collective-permute-start.10 = (f32[3,8,4096]{2,1,0:T(8,128)S(1)}, f32[3,8,4096]{2,1,0:T(8,128)S(1)}, u32[]{:S(2)}, u32[]{:S(2)}) collective-permute-start(f32[3,8,4096]{2,1,0:T(8,128)S(1)} %get-tuple-element.47.refs_0_), channel_id=1, source_target_pairs={{0,6},{1,3},{2,0},{3,5},{4,2},{5,7},{6,4},{7,1},{8,14},{9,11},{10,... | collective-permute-start | bytes 1179656 | tf_op jit(solution)/shard_map/ppermute | solution.py:368
  34.5 1.0 %collective-permute-done.7.refs_3_ = f32[3,8,4096]{2,1,0:T(8,128)S(1)} collective-permute-done((f32[3,8,4096]{2,1,0:T(8,128)S(1)}, f32[3,8,4096]{2,1,0:T(8,128)S(1)}, u32[]{:S(2)}, u32[]{:S(2)}) %collective-permute-start.7) | collective-permute-done | bytes 393248 | tf_op jit(solution)/shard_map/ppermute | solution.py:369
  35.5 8.8 %shard_map.70 = (f32[3,8,4096]{2,1,0:T(8,128)S(1)}, f32[3,8,4096]{2,1,0:T(8,128)S(1)}, f32[8,128]{1,0:T(8,128)S(1)}) custom-call(f32[3,8,4096]{2,1,0:T(8,128)S(1)} %get-tuple-element.37.refs_0_, f32[3,8,4096]{2,1,0:T(8,128)S(1)} %collective-permute-done.6.refs_1_, f32[3,8,4096]{2,1,0:T(8,128)S(1)} %collective-permute-done.1.refs_2_, ...), custom_call_target="tpu_custom_call" | custom-call | bytes 480000 | tf_op jit(solution)/shard_map/pallas_call | solution.py:282
  44.4 0.8 %collective-permute-start.9 = (f32[3,8,4096]{2,1,0:T(8,128)S(1)}, f32[3,8,4096]{2,1,0:T(8,128)S(1)}, u32[]{:S(2)}, u32[]{:S(2)}) collective-permute-start(f32[3,8,4096]{2,1,0:T(8,128)S(1)} %get-tuple-element.39), channel_id=1, source_target_pairs={{0,1},{1,0},{2,3},{3,2},{4,5},{5,4},{6,7},{7,6},{8,9},{9,8},{10,11... | collective-permute-start | bytes 1179656 | tf_op jit(solution)/shard_map/ppermute | solution.py:389
  45.2 5.2 %collective-permute-done.11.refs_3_.refs_4_ = f32[3,8,2816]{2,1,0:T(8,128)S(1)} collective-permute-done((f32[3,8,2816]{2,1,0:T(8,128)S(1)}, f32[3,8,2816]{2,1,0:T(8,128)S(1)}, u32[]{:S(2)}, u32[]{:S(2)}) %collective-permute-start.11) | collective-permute-done | bytes 270368 | tf_op jit(solution)/shard_map/ppermute | solution.py:369
  50.4 6.9 %shard_map.71 = (f32[3,8,2560]{2,1,0:T(8,128)S(1)}, f32[3,8,2560]{2,1,0:T(8,128)S(1)}, f32[8,128]{1,0:T(8,128)S(1)}) custom-call(f32[3,8,4096]{2,1,0:T(8,128)S(1)} %get-tuple-element.47.refs_0_, f32[3,8,4096]{2,1,0:T(8,128)S(1)} %collective-permute-done.10.refs_1_, f32[3,8,2816]{2,1,0:T(8,128)S(1)} %collective-permute-done.4.refs_2_, ...), custom_call_target="tpu_custom_call" | custom-call | bytes 330000 | tf_op jit(solution)/shard_map/pallas_call | solution.py:282
  57.4 5.3 %shard_map.72 = (f32[3,8,1536]{2,1,0:T(8,128)S(1)}, f32[3,8,1536]{2,1,0:T(8,128)S(1)}, f32[8,128]{1,0:T(8,128)S(1)}) custom-call(f32[3,8,4096]{2,1,0:T(8,128)S(1)} %get-tuple-element.47.refs_0_, f32[3,8,4096]{2,1,0:T(8,128)S(1)} %collective-permute-done.10.refs_1_, f32[3,8,2816]{2,1,0:T(8,128)S(1)} %collective-permute-done.4.refs_2_, ...), custom_call_target="tpu_custom_call" | custom-call | bytes 210000 | tf_op jit(solution)/shard_map/pallas_call | solution.py:282
  62.7 2.1 %collective-permute-start.14 = (f32[3,8,1536]{2,1,0:T(8,128)S(1)}, f32[3,8,1536]{2,1,0:T(8,128)S(1)}, u32[]{:S(2)}, u32[]{:S(2)}) collective-permute-start(f32[3,8,1536]{2,1,0:T(8,128)S(1)} %get-tuple-element.49), channel_id=1, source_target_pairs={{0,1},{1,0},{2,3},{3,2},{4,5},{5,4},{6,7},{7,6},{8,9},{9,8},{10,11... | collective-permute-start | bytes 442376 | tf_op jit(solution)/shard_map/ppermute | solution.py:389
  64.7 1.0 %collective-permute-start.15 = (f32[8,128]{1,0:T(8,128)S(1)}, f32[8,128]{1,0:T(8,128)S(1)}, u32[]{:S(2)}, u32[]{:S(2)}) collective-permute-start(f32[8,128]{1,0:T(8,128)S(1)} %add_add_fusion.1), channel_id=1, source_target_pairs={{0,2},{1,3},{2,4},{3,5},{4,6},{5,7},{6,0},{7,1},{8,10},{9,11},{10,... | collective-permute-start | bytes 12296 | tf_op jit(solution)/shard_map/ppermute | solution.py:395
  65.7 1.2 %collective-permute-start.16 = (f32[8,128]{1,0:T(8,128)S(1)}, f32[8,128]{1,0:T(8,128)S(1)}, u32[]{:S(2)}, u32[]{:S(2)}) collective-permute-start(f32[8,128]{1,0:T(8,128)S(1)} %add_add_fusion.1), channel_id=1, source_target_pairs={{0,4},{1,5},{2,6},{3,7},{4,0},{5,1},{6,2},{7,3},{8,12},{9,13},{10,... | collective-permute-start | bytes 12296 | tf_op jit(solution)/shard_map/ppermute | solution.py:395
  66.9 1.7 %collective-permute-start.17 = (f32[8,128]{1,0:T(8,128)S(1)}, f32[8,128]{1,0:T(8,128)S(1)}, u32[]{:S(2)}, u32[]{:S(2)}) collective-permute-start(f32[8,128]{1,0:T(8,128)S(1)} %add_add_fusion.1), channel_id=1, source_target_pairs={{0,6},{1,7},{2,0},{3,1},{4,2},{5,3},{6,4},{7,5},{8,14},{9,15},{10,... | collective-permute-start | bytes 12296 | tf_op jit(solution)/shard_map/ppermute | solution.py:395
  68.6 1.3 %shard_map.73 = f32[4,3,8,4096]{3,2,1,0:T(8,128)} custom-call(f32[3,8,4096]{2,1,0:T(8,128)S(1)} %get-tuple-element.38.refs_0_, f32[3,8,4096]{2,1,0:T(8,128)S(1)} %collective-permute-done.9.refs_1_, f32[3,8,2560]{2,1,0:T(8,128)S(1)} %get-tuple-element.44.refs_2_, f32[3,8,2560]{2,1,0:T(8,128)S(1)} %collective-permute-done.12.refs_3_, ...), custom_call_target="tpu_custom_call" | custom-call | bytes 300000 | tf_op jit(solution)/shard_map/pallas_call | solution.py:315
  69.9 0.3 collective-permute-done.15
  70.2 0.1 collective-permute-done.16
  70.3 0.5 collective-permute-done.17
  70.8 0.5 collective-permute-start.18
  71.2 3.2 %collective-permute-done.18 = f32[8,128]{1,0:T(8,128)S(1)} collective-permute-done((f32[8,128]{1,0:T(8,128)S(1)}, f32[8,128]{1,0:T(8,128)S(1)}, u32[]{:S(2)}, u32[]{:S(2)}) %collective-permute-start.18) | collective-permute-done | bytes 4128 | tf_op jit(solution)/shard_map/ppermute | solution.py:403
  74.4 0.5 multiply_bitcast_fusion.1
  (32 shorter events, 0.3 us)
Async XLA Ops:
  0.6 3.8 %collective-permute-start = (f32[4,3,8,4096]{3,2,1,0:T(8,128)}, f32[4,3,8,4096]{3,2,1,0:T(8,128)S(1)}, u32[]{:S(2)}, u32[]{:S(2)}) collective-permute-start(f32[4,3,8,4096]{3,2,1,0:T(8,128)} %own.1), channel_id=1, source_target_pairs={{0,8},{8,0},{1,9},{9,1},{2,10},{10,2},{3,11},{11,3},{4,12},{12,4},... | collective-permute-start | bytes 4718600 | tf_op jit(solution)/shard_map/ppermute | solution.py:341
  1.1 1.4 %copy-start = (f32[4,3,8,4096]{3,2,1,0:T(8,128)S(1)}, f32[4,3,8,4096]{3,2,1,0:T(8,128)}, u32[]{:S(2)}) copy-start(f32[4,3,8,4096]{3,2,1,0:T(8,128)} %own.1) | copy-start | bytes 4718596
  2.6 0.7 copy-start.2
  3.2 1.4 %copy-start.1 = (f32[4,3,8,4096]{3,2,1,0:T(8,128)S(1)}, f32[4,3,8,4096]{3,2,1,0:T(8,128)}, u32[]{:S(2)}) copy-start(f32[4,3,8,4096]{3,2,1,0:T(8,128)} %own.1) | copy-start | bytes 4718596
  4.4 5.3 %copy-start.3 = (f32[8,128]{1,0:T(8,128)S(1)}, f32[8,128]{1,0:T(8,128)}, u32[]{:S(2)}) copy-start(f32[8,128]{1,0:T(8,128)} %param.9) | copy-start | bytes 12292
  4.4 18.8 %copy-start.4 = (s32[8,128]{1,0:T(8,128)S(1)}, s32[8,128]{1,0:T(8,128)}, u32[]{:S(2)}) copy-start(s32[8,128]{1,0:T(8,128)} %param.8) | copy-start | bytes 12292
  4.4 21.3 %copy-start.5 = (f32[8,128]{1,0:T(8,128)S(1)}, f32[8,128]{1,0:T(8,128)}, u32[]{:S(2)}) copy-start(f32[8,128]{1,0:T(8,128)} %param.7) | copy-start | bytes 12292
  5.4 14.5 %collective-permute-start.1 = (f32[3,8,4096]{2,1,0:T(8,128)S(1)}, f32[3,8,4096]{2,1,0:T(8,128)S(1)}, u32[]{:S(2)}, u32[]{:S(2)}) collective-permute-start(f32[3,8,4096]{2,1,0:T(8,128)S(1)} %get-tuple-element.32), channel_id=1, source_target_pairs={{0,1},{1,0},{2,3},{3,2},{4,5},{5,4},{6,7},{7,6},{8,9},{9,8},{10,11... | collective-permute-start | bytes 1179656 | tf_op jit(solution)/shard_map/ppermute | solution.py:365
  8.1 7.5 %collective-permute-start.2 = (f32[6,8,512]{2,1,0:T(8,128)S(1)}, f32[6,8,512]{2,1,0:T(8,128)S(1)}, u32[]{:S(2)}, u32[]{:S(2)}) collective-permute-start(f32[6,8,512]{2,1,0:T(8,128)S(1)} %get-tuple-element.33), channel_id=1, source_target_pairs={{0,2},{1,7},{2,4},{3,1},{4,6},{5,3},{6,0},{7,5},{8,10},{9,15},{10,... | collective-permute-start | bytes 294920 | tf_op jit(solution)/shard_map/ppermute | solution.py:353
  9.7 5.9 %collective-permute-start.3 = (f32[6,8,512]{2,1,0:T(8,128)S(1)}, f32[6,8,512]{2,1,0:T(8,128)S(1)}, u32[]{:S(2)}, u32[]{:S(2)}) collective-permute-start(f32[6,8,512]{2,1,0:T(8,128)S(1)} %get-tuple-element.34), channel_id=1, source_target_pairs={{0,3},{1,6},{2,5},{3,0},{4,7},{5,2},{6,1},{7,4},{8,11},{9,14},{10,... | collective-permute-start | bytes 294920 | tf_op jit(solution)/shard_map/ppermute | solution.py:354
  9.8 24.7 %collective-permute-start.6 = (f32[3,8,4096]{2,1,0:T(8,128)S(1)}, f32[3,8,4096]{2,1,0:T(8,128)S(1)}, u32[]{:S(2)}, u32[]{:S(2)}) collective-permute-start(f32[3,8,4096]{2,1,0:T(8,128)S(1)} %get-tuple-element.37.refs_0_), channel_id=1, source_target_pairs={{0,6},{1,3},{2,0},{3,5},{4,2},{5,7},{6,4},{7,1},{8,14},{9,11},{10,... | collective-permute-start | bytes 1179656 | tf_op jit(solution)/shard_map/ppermute | solution.py:368
  19.9 11.1 %collective-permute-start.4 = (f32[3,8,2816]{2,1,0:T(8,128)S(1)}, f32[3,8,2816]{2,1,0:T(8,128)S(1)}, u32[]{:S(2)}, u32[]{:S(2)}) collective-permute-start(f32[3,8,2816]{2,1,0:T(8,128)S(1)} %get-tuple-element.35), channel_id=1, source_target_pairs={{0,1},{1,0},{2,3},{3,2},{4,5},{5,4},{6,7},{7,6},{8,9},{9,8},{10,11... | collective-permute-start | bytes 811016 | tf_op jit(solution)/shard_map/ppermute | solution.py:365
  21.6 13.9 %collective-permute-start.7 = (f32[3,8,4096]{2,1,0:T(8,128)S(1)}, f32[3,8,4096]{2,1,0:T(8,128)S(1)}, u32[]{:S(2)}, u32[]{:S(2)}) collective-permute-start(f32[3,8,4096]{2,1,0:T(8,128)S(1)} %collective-permute-done.1.refs_2_), channel_id=1, source_target_pairs={{0,2},{1,7},{2,4},{3,1},{4,6},{5,3},{6,0},{7,5},{8,10},{9,15},{10,... | collective-permute-start | bytes 1179656 | tf_op jit(solution)/shard_map/ppermute | solution.py:369
  23.2 7.7 %collective-permute-start.5 = (f32[3,8,1280]{2,1,0:T(8,128)S(1)}, f32[3,8,1280]{2,1,0:T(8,128)S(1)}, u32[]{:S(2)}, u32[]{:S(2)}) collective-permute-start(f32[3,8,1280]{2,1,0:T(8,128)S(1)} %get-tuple-element.36), channel_id=1, source_target_pairs={{0,1},{1,0},{2,3},{3,2},{4,5},{5,4},{6,7},{7,6},{8,9},{9,8},{10,11... | collective-permute-start | bytes 368648 | tf_op jit(solution)/shard_map/ppermute | solution.py:365
  25.7 5.2 %collective-permute-start.8 = (f32[3,8,128]{2,1,0:T(8,128)S(1)}, f32[3,8,128]{2,1,0:T(8,128)S(1)}, u32[]{:S(2)}, u32[]{:S(2)}) collective-permute-start(f32[3,8,128]{2,1,0:T(8,128)S(1)} %pad_maximum_fusion.refs_6_.refs_8_), channel_id=1, source_target_pairs={{0,1},{1,0},{2,3},{3,2},{4,5},{5,4},{6,7},{7,6},{8,9},{9,8},{10,11... | collective-permute-start | bytes 36872 | tf_op jit(solution)/shard_map/ppermute | solution.py:356
  30.9 19.5 %collective-permute-start.10 = (f32[3,8,4096]{2,1,0:T(8,128)S(1)}, f32[3,8,4096]{2,1,0:T(8,128)S(1)}, u32[]{:S(2)}, u32[]{:S(2)}) collective-permute-start(f32[3,8,4096]{2,1,0:T(8,128)S(1)} %get-tuple-element.47.refs_0_), channel_id=1, source_target_pairs={{0,6},{1,3},{2,0},{3,5},{4,2},{5,7},{6,4},{7,1},{8,14},{9,11},{10,... | collective-permute-start | bytes 1179656 | tf_op jit(solution)/shard_map/ppermute | solution.py:368
  34.5 15.9 %collective-permute-start.11 = (f32[3,8,2816]{2,1,0:T(8,128)S(1)}, f32[3,8,2816]{2,1,0:T(8,128)S(1)}, u32[]{:S(2)}, u32[]{:S(2)}) collective-permute-start(f32[3,8,2816]{2,1,0:T(8,128)S(1)} %collective-permute-done.4.refs_2_), channel_id=1, source_target_pairs={{0,2},{1,7},{2,4},{3,1},{4,6},{5,3},{6,0},{7,5},{8,10},{9,15},{10,... | collective-permute-start | bytes 811016 | tf_op jit(solution)/shard_map/ppermute | solution.py:369
  44.4 20.3 %collective-permute-start.9 = (f32[3,8,4096]{2,1,0:T(8,128)S(1)}, f32[3,8,4096]{2,1,0:T(8,128)S(1)}, u32[]{:S(2)}, u32[]{:S(2)}) collective-permute-start(f32[3,8,4096]{2,1,0:T(8,128)S(1)} %get-tuple-element.39), channel_id=1, source_target_pairs={{0,1},{1,0},{2,3},{3,2},{4,5},{5,4},{6,7},{7,6},{8,9},{9,8},{10,11... | collective-permute-start | bytes 1179656 | tf_op jit(solution)/shard_map/ppermute | solution.py:389
  45.2 12.2 %collective-permute-start.13 = (f32[3,8,1280]{2,1,0:T(8,128)S(1)}, f32[3,8,1280]{2,1,0:T(8,128)S(1)}, u32[]{:S(2)}, u32[]{:S(2)}) collective-permute-start(f32[3,8,1280]{2,1,0:T(8,128)S(1)} %collective-permute-done.5.refs_3_), channel_id=1, source_target_pairs={{0,2},{1,7},{2,4},{3,1},{4,6},{5,3},{6,0},{7,5},{8,10},{9,15},{10,... | collective-permute-start | bytes 368648 | tf_op jit(solution)/shard_map/ppermute | solution.py:369
  57.3 7.5 %collective-permute-start.12 = (f32[3,8,2560]{2,1,0:T(8,128)S(1)}, f32[3,8,2560]{2,1,0:T(8,128)S(1)}, u32[]{:S(2)}, u32[]{:S(2)}) collective-permute-start(f32[3,8,2560]{2,1,0:T(8,128)S(1)} %get-tuple-element.45), channel_id=1, source_target_pairs={{0,1},{1,0},{2,3},{3,2},{4,5},{5,4},{6,7},{7,6},{8,9},{9,8},{10,11... | collective-permute-start | bytes 737288 | tf_op jit(solution)/shard_map/ppermute | solution.py:389
  62.7 6.0 %collective-permute-start.14 = (f32[3,8,1536]{2,1,0:T(8,128)S(1)}, f32[3,8,1536]{2,1,0:T(8,128)S(1)}, u32[]{:S(2)}, u32[]{:S(2)}) collective-permute-start(f32[3,8,1536]{2,1,0:T(8,128)S(1)} %get-tuple-element.49), channel_id=1, source_target_pairs={{0,1},{1,0},{2,3},{3,2},{4,5},{5,4},{6,7},{7,6},{8,9},{9,8},{10,11... | collective-permute-start | bytes 442376 | tf_op jit(solution)/shard_map/ppermute | solution.py:389
  64.7 5.5 %collective-permute-start.15 = (f32[8,128]{1,0:T(8,128)S(1)}, f32[8,128]{1,0:T(8,128)S(1)}, u32[]{:S(2)}, u32[]{:S(2)}) collective-permute-start(f32[8,128]{1,0:T(8,128)S(1)} %add_add_fusion.1), channel_id=1, source_target_pairs={{0,2},{1,3},{2,4},{3,5},{4,6},{5,7},{6,0},{7,1},{8,10},{9,11},{10,... | collective-permute-start | bytes 12296 | tf_op jit(solution)/shard_map/ppermute | solution.py:395
  65.7 4.6 %collective-permute-start.16 = (f32[8,128]{1,0:T(8,128)S(1)}, f32[8,128]{1,0:T(8,128)S(1)}, u32[]{:S(2)}, u32[]{:S(2)}) collective-permute-start(f32[8,128]{1,0:T(8,128)S(1)} %add_add_fusion.1), channel_id=1, source_target_pairs={{0,4},{1,5},{2,6},{3,7},{4,0},{5,1},{6,2},{7,3},{8,12},{9,13},{10,... | collective-permute-start | bytes 12296 | tf_op jit(solution)/shard_map/ppermute | solution.py:395
  66.9 3.8 %collective-permute-start.17 = (f32[8,128]{1,0:T(8,128)S(1)}, f32[8,128]{1,0:T(8,128)S(1)}, u32[]{:S(2)}, u32[]{:S(2)}) collective-permute-start(f32[8,128]{1,0:T(8,128)S(1)} %add_add_fusion.1), channel_id=1, source_target_pairs={{0,6},{1,7},{2,0},{3,1},{4,2},{5,3},{6,4},{7,5},{8,14},{9,15},{10,... | collective-permute-start | bytes 12296 | tf_op jit(solution)/shard_map/ppermute | solution.py:395
  70.8 3.6 %collective-permute-start.18 = (f32[8,128]{1,0:T(8,128)S(1)}, f32[8,128]{1,0:T(8,128)S(1)}, u32[]{:S(2)}, u32[]{:S(2)}) collective-permute-start(f32[8,128]{1,0:T(8,128)S(1)} %add_add_fusion), channel_id=1, source_target_pairs={{0,1},{1,0},{2,3},{3,2},{4,5},{5,4},{6,7},{7,6},{8,9},{9,8},{10,11... | collective-permute-start | bytes 12296 | tf_op jit(solution)/shard_map/ppermute | solution.py:403
